TPU v7x, 32 devices: a whole 2x2x4 slice. The times are simulated.
32 devices in a mesh: group: 2 (over x), row: 8 (over z, y), col: 2 (over core).
Axes of the slice: x: 2, y: 2, z: 4, core: 2. Of those that a mesh axis runs over, the one named last changes fastest.
Arguments:
- alignment: bfloat16 [128, 256, 256], P(('group', 'row'), 'col'), parts along dimension 0, may hold values from -6 to 6
- ln_gain: float32 [256], replicated, may hold values from 0.5 to 1.5
- ln_bias: float32 [256], replicated, may hold values from -3 to 3
- w_left: bfloat16 [256, 32], replicated, may hold values from -0.375 to 0.375
- b_left: float32 [32], replicated, may hold values from -3 to 3
- w_right: bfloat16 [256, 32], replicated, may hold values from -0.375 to 0.375
- b_right: float32 [32], replicated, may hold values from -3 to 3
- w_out: bfloat16 [1024, 128], replicated, may hold values from -1.5 to 1.5
- b_out: float32 [128], replicated, may hold values from -3 to 3
Outputs:
- pair_update: bfloat16 [512, 256, 128], P(('group', 'row'), 'col'), parts along dimension 0
There are 2 independent parts, one for each index of `group`. A program takes and returns all parts, laid end to end along the dimension named above; an argument that names none is the same for every part. Nothing has to cross between parts.
All inputs are finite; a program needn't handle non-finite values.
Results may differ from a plain program's by a relative error of at most 0.0053.
Values may be sent and summed in bfloat16 or wider, within the bound.
No kernel may reach another device: no remote copies, remote signals or barrier semaphores. Data moves between devices by JAX's collectives and lax.ppermute only.
A program may use at most 128 MiB of HBM per device.

v0:
```python
import math

import jax
import jax.numpy as jnp
from jax import lax
from jax.sharding import PartitionSpec as P

S = 64


def projected_sides(alignment, ln_gain, ln_bias, w_left, b_left, w_right, b_right):
    values = alignment.astype(jnp.float32)
    average = jnp.mean(values, axis=-1, keepdims=True)
    centred = values - average
    variance = jnp.mean(centred * centred, axis=-1, keepdims=True)
    normed = (centred * lax.rsqrt(variance + 1e-05) * ln_gain + ln_bias).astype(jnp.bfloat16)
    left = jnp.einsum("slm,mc->slc", normed, w_left, preferred_element_type=jnp.float32) + b_left
    right = jnp.einsum("slm,mc->slc", normed, w_right, preferred_element_type=jnp.float32) + b_right
    return (left.astype(jnp.bfloat16), right.astype(jnp.bfloat16))


def on_device(alignment, ln_gain, ln_bias, w_left, b_left, w_right, b_right, w_out, b_out):
    left_local, right_local = projected_sides(
        alignment, ln_gain, ln_bias, w_left, b_left, w_right, b_right
    )
    row_count = lax.axis_size("row")
    col_count = lax.axis_size("col")
    half_width = left_local.shape[1]
    rows_here = half_width * col_count // row_count
    left_whole = lax.all_gather(left_local, "col", axis=1, tiled=True)
    left_rows = lax.all_to_all(left_whole, "row", split_axis=1, concat_axis=0, tiled=True)
    right_all = lax.all_gather(right_local, "row", axis=0, tiled=True)
    seq_total = right_all.shape[0]
    width_c = right_all.shape[2]
    out_width = w_out.shape[1]
    column_block = math.gcd(half_width, 128)
    block_count = half_width // column_block
    stacked = right_all.reshape(seq_total, block_count, column_block, width_c).transpose(1, 0, 2, 3)

    def pair_block(right_block):
        outer = (
            jnp.einsum("sic,sje->ijce", left_rows, right_block, preferred_element_type=jnp.float32)
            / S
        )
        flat = outer.astype(jnp.bfloat16).reshape(rows_here * column_block, width_c * width_c)
        update = jnp.dot(flat, w_out, preferred_element_type=jnp.float32) + b_out
        return update.astype(jnp.bfloat16).reshape(rows_here, column_block, out_width)

    results = lax.map(pair_block, stacked)
    return results.transpose(1, 0, 2, 3).reshape(rows_here, half_width, out_width)


def solution(mesh):
    in_specs = (P(("group", "row"), "col", None), P(), P(), P(), P(), P(), P(), P(), P())
    out_specs = P(("group", "row"), "col", None)
    return jax.shard_map(
        on_device, mesh=mesh, in_specs=in_specs, out_specs=out_specs, check_vma=False
    )
```

profile of v0, /device:TPU:0, one launch (start us, length us, event | category | flops | bytes accessed | tf_op | source)
XLA Modules:
  0.0 78.2 jit_solution(6878693020322644634)
XLA Ops:
  0.0 0.0 copy-start
  0.0 1.3 %convert_reduce_fusion = f32[8,128]{1,0:T(8,128)S(1)} fusion(bf16[8,128,256]{2,1,0:T(8,128)(2,1)} %param.9), kind=kLoop, calls=%fused_computation.8 | loop fusion | flops 523264 | bytes 528384 | tf_op jit(solution)/shard_map/reduce_sum | solution.py:13
  1.3 1.4 %fusion.14 = f32[8,128]{1,0:T(8,128)S(1)} fusion(bf16[8,128,256]{2,1,0:T(8,128)(2,1)} %param.9, f32[8,128]{1,0:T(8,128)S(1)} %broadcast_multiply_fusion), kind=kLoop, calls=%fused_computation.15 | loop fusion | flops 1047552 | bytes 532480 | tf_op jit(solution)/shard_map/reduce_sum | solution.py:15
  2.7 1.5 %fusion.13 = bf16[8,128,32]{1,2,0:T(8,128)(2,1)S(1)} fusion(bf16[8,128,256]{2,1,0:T(8,128)(2,1)} %param.9, f32[256]{0:T(256)} %param.11, f32[256]{0:T(256)} %param.10, f32[8,128]{1,0:T(8,128)S(1)} %add_rsqrt_fusion, f32[8,128]{1,0:T(8,128)S(1)} %broadcast_multiply_fusion, f32[32]{0:T(128)} %param.13, bf16[256,32]{0,1:T(8,128)(2,1)} %param.12), kind=kOutput, calls=%fused_computation.14 | convolution fusion | flops 18415616 | bytes 616576 | tf_op jit(solution)/shard_map/slm,mc->slc/dot_general | solution.py:17
  4.3 2.0 %all_gather.7 = bf16[8,256,32]{1,2,0:T(8,128)(2,1)S(1)} all-gather(bf16[8,128,32]{1,2,0:T(8,128)(2,1)S(1)} %fusion.13), channel_id=1, replica_groups=mesh['group'=2,'row'=8,'col'=2] {'col'}, dimensions={1}, use_global_device_ids=true | all-gather | bytes 196608 | tf_op jit(solution)/shard_map/all_gather | solution.py:30
  6.3 0.3 copy.19
  6.6 1.2 %reshape.32 = bf16[8,2,4096]{2,1,0:T(2,128)(2,1)} reshape(bf16[256,8,32]{2,1,0:T(8,128)(2,1)S(1)} %bitcast.33) | data formatting | bytes 262144
  7.8 7.2 %all-to-all-start = ((bf16[8,2,4096]{2,1,0:T(2,128)(2,1)}), bf16[8,2,4096]{2,1,0:T(2,128)(2,1)S(1)}, u32[]{:S(2)}, u32[]{:S(2)}) async-start(bf16[8,2,4096]{2,1,0:T(2,128)(2,1)} %reshape.32), calls=%async_computation | async-start | bytes 262144 | tf_op jit(solution)/shard_map/all_to_all | solution.py:31
  15.0 1.5 %fusion.12 = bf16[8,128,32]{1,2,0:T(8,128)(2,1)S(1)} fusion(bf16[8,128,256]{2,1,0:T(8,128)(2,1)} %param.9, f32[256]{0:T(256)} %param.11, f32[256]{0:T(256)} %param.10, f32[8,128]{1,0:T(8,128)S(1)} %add_rsqrt_fusion, f32[8,128]{1,0:T(8,128)S(1)} %broadcast_multiply_fusion, f32[32]{0:T(128)} %param.15, bf16[256,32]{0,1:T(8,128)(2,1)} %param.14), kind=kOutput, calls=%fused_computation.13 | convolution fusion | flops 18415616 | bytes 616576 | tf_op jit(solution)/shard_map/slm,mc->slc/dot_general | solution.py:18
  16.5 32.1 %all_gather.6 = bf16[64,128,32]{1,2,0:T(8,128)(2,1)S(1)} all-gather(bf16[8,128,32]{1,2,0:T(8,128)(2,1)S(1)} %fusion.12), channel_id=1, replica_groups=mesh['group'=2,'row'=8,'col'=2] {'row'}, dimensions={0}, use_global_device_ids=true | all-gather | bytes 589824 | tf_op jit(solution)/shard_map/all_gather | solution.py:32
  48.6 0.0 all-to-all-done
  48.6 0.3 reshape.33
  48.9 0.1 copy.20
  49.0 0.6 copy.22
  49.6 5.6 %fusion.3 = bf16[32,128,32,32]{1,2,0,3:T(8,128)(2,1)} fusion(bf16[64,128,32,1]{1,2,0,3:T(8,128)(2,1)S(1)} %bitcast.32, bf16[64,32,32]{0,2,1:T(8,128)(2,1)S(1)} %copy.22), kind=kOutput, calls=%fused_computation.4 | convolution fusion | flops 545259520 | bytes 9043968 | tf_op jit(solution)/shard_map/while/body/eval_jaxpr/sic,sje->ijce/dot_general | solution.py:42
  55.1 0.0 copy-start.1
  55.1 9.8 %copy.23 = bf16[32,128,32,32]{1,0,3,2:T(8,128)(2,1)} copy(bf16[32,128,32,32]{1,2,0,3:T(8,128)(2,1)} %fusion.3) | data formatting | bytes 16777216 | tf_op jit(solution)/shard_map/while/body/eval_jaxpr/convert_element_type | solution.py:45
  65.0 0.0 copy-done
  65.0 0.0 copy-done.1
  65.0 13.3 %fusion.7 = bf16[4096,128]{1,0:T(8,128)(2,1)} fusion(bf16[1024,128]{1,0:T(8,128)(2,1)S(1)} %copy-done, bf16[128,8,32,128]{3,2,1,0:T(8,128)(2,1)} %bitcast.31, f32[128]{0:T(128)S(1)} %copy-done.1), kind=kOutput, calls=%fused_computation.6 | convolution fusion | flops 1074790400 | bytes 9699840 | tf_op jit(solution)/shard_map/while/body/eval_jaxpr/dot_general | solution.py:46
  (2 shorter events, 0.0 us)
Async XLA Ops:
  0.0 65.0 %copy-start = (bf16[1024,128]{1,0:T(8,128)(2,1)S(1)}, bf16[1024,128]{1,0:T(8,128)(2,1)}, u32[]{:S(2)}) copy-start(bf16[1024,128]{1,0:T(8,128)(2,1)} %param.16) | copy-start | bytes 786436
  7.8 40.8 %all-to-all-start = ((bf16[8,2,4096]{2,1,0:T(2,128)(2,1)}), bf16[8,2,4096]{2,1,0:T(2,128)(2,1)S(1)}, u32[]{:S(2)}, u32[]{:S(2)}) async-start(bf16[8,2,4096]{2,1,0:T(2,128)(2,1)} %reshape.32), calls=%async_computation | async-start | bytes 262144 | tf_op jit(solution)/shard_map/all_to_all | solution.py:31
  55.1 9.8 %copy-start.1 = (f32[128]{0:T(128)S(1)}, f32[128]{0:T(128)}, u32[]{:S(2)}) copy-start(f32[128]{0:T(128)} %param.17) | copy-start | bytes 1540
where the time goes:
time: 78.6 us; the launch traced here: 78.2 us
  blocking collectives  34.1 us (43%)
  matrix products  21.9 us (28%)
  local copies, waits for them, and re-layouts  12.3 us (16%)
  starting transfers between devices  7.18 us (9%)
  other arithmetic  2.72 us (3%)
    all_gather x1, blocking collectives, on_device(): right_all = lax.all_gather(right_local, 'row', axis=0, tiled=True)  32.1 us
    dot_general x1, matrix products, pair_block(): update = jnp.dot(flat, w_out, preferred_element_type=jnp.float32) + b_out  13.3 us
    convert_element_type x1, local copies, waits for them, and re-layouts, pair_block(): outer.astype(jnp.bfloat16)  9.84 us
    all_to_all x1, starting transfers between devices, on_device(): lax.all_to_all(left_whole, 'row', split_axis=1, concat_axis=0, tiled=True)  7.18 us
    dot_general x1, matrix products, pair_block(): jnp.einsum('sic,sje->ijce', left_rows, right_block, preferred_element_typ...  5.56 us
    all_gather x1, blocking collectives, on_device(): left_whole = lax.all_gather(left_local, 'col', axis=1, tiled=True)  2 us
  transfers between devices with their start and end apart: 1, of which 0 were waited for; matrix products, arithmetic and copies ran while one was open for 2% of the time, Pallas kernels for 0%

commit v1 on v0

v1 whole, which is shorter than its diff:
```python
import functools

import jax
import jax.numpy as jnp
from jax import lax
from jax.experimental import pallas as pl
from jax.experimental.pallas import tpu as pltpu
from jax.sharding import PartitionSpec as P

LANES = 128


def features_kernel(scale, x_ref, gain_ref, bias_ref, wl_ref, bl_ref, wr_ref, br_ref,
                    left_ref, right_ref, normed_ref, left_f32, right_f32):
    seqs, width, channels = x_ref.shape
    c = wl_ref.shape[0]
    fold = LANES // c
    quarter = width // fold
    for s in range(seqs):
        values = x_ref[s].astype(jnp.float32)
        average = jnp.mean(values, axis=-1, keepdims=True)
        centred = values - average
        variance = jnp.mean(centred * centred, axis=-1, keepdims=True)
        normed = centred * lax.rsqrt(variance + 1e-05) * gain_ref[...] + bias_ref[...]
        for h in range(channels // LANES):
            normed_ref[h, s * width:(s + 1) * width] = normed[:, h * LANES:(h + 1) * LANES]
        right = lax.dot_general(wr_ref[...], normed.astype(jnp.bfloat16), (((1,), (1,)), ((), ())),
                                preferred_element_type=jnp.float32) + br_ref[...]
        for b in range(width // LANES):
            right_f32[pl.ds(b * c * seqs + s, c, stride=seqs), :] = right[:, b * LANES:(b + 1) * LANES]
    total = None
    for q in range(fold):
        part = jnp.concatenate(
            [normed_ref[h, pl.ds(q, seqs * quarter, stride=fold), :] for h in range(channels // LANES)], axis=1
        ).astype(jnp.bfloat16)
        zeros = [jnp.zeros((c, channels), jnp.bfloat16)]
        w = jnp.concatenate(zeros * q + [wl_ref[...]] + zeros * (fold - 1 - q), axis=0)
        term = lax.dot_general(part, w, (((1,), (1,)), ((), ())), preferred_element_type=jnp.float32)
        total = term if total is None else total + term
    total = (total + jnp.concatenate([bl_ref[...]] * fold, axis=1)) * scale
    for s in range(seqs):
        left_f32[pl.ds(s, quarter, stride=seqs), :] = total[s * quarter:(s + 1) * quarter]
    left_ref[...] = left_f32[...].astype(jnp.bfloat16)
    right_ref[...] = right_f32[...].astype(jnp.bfloat16)


def features(alignment, ln_gain, ln_bias, w_left, b_left, w_right, b_right, scale):
    seqs, width, channels = alignment.shape
    c = w_left.shape[1]
    left_rows = seqs * width * c // LANES
    right_rows = left_rows
    vmem = pl.BlockSpec(memory_space=pltpu.VMEM)
    return pl.pallas_call(
        functools.partial(features_kernel, scale),
        out_shape=(jax.ShapeDtypeStruct((left_rows, LANES), jnp.bfloat16),
                   jax.ShapeDtypeStruct((right_rows, LANES), jnp.bfloat16)),
        in_specs=[vmem] * 7,
        out_specs=(vmem, vmem),
        scratch_shapes=[pltpu.VMEM((channels // LANES, seqs * width, LANES), jnp.float32),
                        pltpu.VMEM((left_rows, LANES), jnp.float32),
                        pltpu.VMEM((right_rows, LANES), jnp.float32)],
        compiler_params=pltpu.CompilerParams(vmem_limit_bytes=32 * 1024 * 1024),
        name="features",
    )(alignment, ln_gain.reshape(1, -1), ln_bias.reshape(1, -1), w_left.T, b_left.reshape(1, -1),
      w_right.T, b_right.reshape(-1, 1))


def by_sequence(block, f32_ref, inner, seqs):
    sources = f32_ref.shape[0]
    for src in range(sources):
        f32_ref[src] = block(src)
    if seqs % 8 == 0:
        return lambda n: jnp.concatenate(
            [f32_ref[src, n * seqs:(n + 1) * seqs] for src in range(sources)], axis=0)
    flat = f32_ref.reshape(sources * inner * seqs, LANES)
    return lambda n: jnp.concatenate(
        [flat[pl.ds(n * seqs + s, sources, stride=inner * seqs), :] for s in range(seqs)], axis=0)


def pair_kernel(seqs, c, rows_step, recv_ref, w_ref, bias_ref, out_ref,
                left_f32, right_f32, left_t, right_b, w_f32, w_t, outer_ref):
    sources = recv_ref.shape[0]
    rows, width, z = out_ref.shape[0], out_ref.shape[1], out_ref.shape[2]
    left_rows = left_f32.shape[1]
    fold = LANES // c
    blocks = width // LANES
    step = pl.program_id(0)

    @pl.when(step == 0)
    def _():
        left_of = by_sequence(lambda src: recv_ref[src, :left_rows].astype(jnp.float32),
                              left_f32, left_rows // seqs, seqs)
        for k in range(left_rows // seqs):
            left_t[k * LANES:(k + 1) * LANES] = left_of(k).T.astype(jnp.bfloat16)
        for b in range(blocks):
            first = left_rows + b * c * seqs
            right_of = by_sequence(lambda src: recv_ref[src, first:first + c * seqs].astype(jnp.float32),
                                   right_f32, c, seqs)
            for e in range(c):
                at = (b * c + e) * LANES
                right_b[:, at:at + LANES] = right_of(e).astype(jnp.bfloat16)
        w_f32[...] = w_ref[...].astype(jnp.float32)
        for e in range(c):
            w_t[:, e * c:(e + 1) * c] = w_f32[pl.ds(e, c, stride=c), :].T.astype(jnp.bfloat16)

    here = left_t[pl.ds(pl.multiple_of(step * rows_step * c, rows_step * c), rows_step * c), :]
    for b in range(blocks):
        for e in range(0, c, 2):
            at = (b * c + e) * LANES
            outer = jnp.dot(here, right_b[:, at:at + 2 * LANES], preferred_element_type=jnp.float32)
            outer = outer.astype(jnp.bfloat16)
            for half in range(2):
                for i in range(rows_step):
                    outer_ref[i // 2, (e + half) * c:(e + half + 1) * c,
                              (i % 2) * LANES:(i % 2 + 1) * LANES] = (
                        outer[i * c:(i + 1) * c, half * LANES:(half + 1) * LANES])
        for p in range(rows_step // 2):
            update = jnp.dot(w_t[...], outer_ref[p], preferred_element_type=jnp.float32)
            for half in range(2):
                mine = update[:, half * LANES:(half + 1) * LANES].T + bias_ref[...]
                out_ref[2 * p + half, b * LANES:(b + 1) * LANES, :] = mine.astype(out_ref.dtype)


def pairs(received, w_out, b_out, seqs, c, rows, width):
    sources, all_rows, _ = received.shape
    z = w_out.shape[1]
    left_rows = rows * c * seqs // LANES
    rows_step = 8
    vmem = pl.BlockSpec(memory_space=pltpu.VMEM)
    total = sources * seqs
    return pl.pallas_call(
        functools.partial(pair_kernel, seqs, c, rows_step),
        grid=(rows // rows_step,),
        out_shape=jax.ShapeDtypeStruct((rows, width, z), jnp.bfloat16),
        in_specs=[vmem] * 3,
        out_specs=pl.BlockSpec((rows_step, width, z), lambda i: (i, 0, 0)),
        scratch_shapes=[pltpu.VMEM((sources, left_rows, LANES), jnp.float32),
                        pltpu.VMEM((sources, c * seqs, LANES), jnp.float32),
                        pltpu.VMEM((rows * c, total), jnp.bfloat16),
                        pltpu.VMEM((total, width * c), jnp.bfloat16),
                        pltpu.VMEM(w_out.shape, jnp.float32),
                        pltpu.VMEM((z, c * c), jnp.bfloat16),
                        pltpu.VMEM((rows_step // 2, c * c, 2 * LANES), jnp.bfloat16)],
        compiler_params=pltpu.CompilerParams(vmem_limit_bytes=48 * 1024 * 1024),
        name="pairs",
    )(received, w_out, b_out.reshape(1, -1))


def on_device(alignment, ln_gain, ln_bias, w_left, b_left, w_right, b_right, w_out, b_out):
    seqs, width, _ = alignment.shape
    c = w_left.shape[1]
    row_count = lax.axis_size("row")
    col_count = lax.axis_size("col")
    rows = width * col_count // row_count
    left, right = features(alignment, ln_gain, ln_bias, w_left, b_left, w_right, b_right,
                           1.0 / (seqs * row_count))
    left = left.reshape(width // rows, rows * c * seqs // LANES, LANES)
    left = lax.all_gather(left, "col", axis=0, tiled=True)
    send = jnp.concatenate(
        [left, jnp.broadcast_to(right[None], (row_count,) + right.shape)], axis=1)
    received = lax.all_to_all(send, "row", split_axis=0, concat_axis=0, tiled=True)
    return pairs(received, w_out, b_out, seqs, c, rows, width)


def solution(mesh):
    in_specs = (P(("group", "row"), "col", None), P(), P(), P(), P(), P(), P(), P(), P())
    out_specs = P(("group", "row"), "col", None)
    return jax.shard_map(
        on_device, mesh=mesh, in_specs=in_specs, out_specs=out_specs, check_vma=False
    )
```

time: 78.6 us -> 39.7 us (0.51)
  matrix products: 21.9 us -> 0 us
  starting transfers between devices: 7.18 us -> 0 us
  local copies, waits for them, and re-layouts: 12.3 us -> 5.3 us
  blocking collectives: 34.1 us -> 27.1 us
  Pallas kernels: 0 us -> 6.78 us
  other arithmetic: 2.72 us -> 0.04 us
    all_gather x2 -> x1, blocking collectives: 34.1 us -> 2 us  [on_device(): left = lax.all_gather(left, 'col', axis=0, tiled=True)]
    all_to_all x0 -> x1, blocking collectives: none -> 25.1 us  [on_device(): lax.all_to_all(send, 'row', split_axis=0, concat_axis=0, tiled=True)]
    dot_general x4 -> x0, matrix products: 21.9 us -> none  [the longest x1 13.3 us: pair_block(): update = jnp.dot(flat, w_out, preferred_element_type=jnp.float32) + b_out]
    convert_element_type x1 -> x0, local copies, waits for them, and re-layouts: 9.84 us -> none  [pair_block(): outer.astype(jnp.bfloat16)]
    all_to_all x1 -> x0, starting transfers between devices: 7.18 us -> none  [on_device(): lax.all_to_all(left_whole, 'row', split_axis=1, concat_axis=0, tiled=True)]
    pallas_call x0 -> x2, Pallas kernels: none -> 6.78 us  [the longest x1 5.98 us: pairs(): pl.pallas_call(functools.partial(pair_kernel, seqs, c, rows_step), grid=(...]
    unnamed x6 -> x16, local copies, waits for them, and re-layouts: 1.43 us -> 4.5 us
    reduce_sum x2 -> x0, other arithmetic: 2.71 us -> none  [the longest x1 1.41 us: projected_sides(): variance = jnp.mean(centred * centred, axis=-1, keepdims=True)]
  transfers between devices with their start and end apart: 1 -> 0, of which waited for: 0 -> 0; matrix products, arithmetic and copies ran while one was open for 2% -> 0% of each run, Pallas kernels for 0% -> 0%
where the time goes in v1:
time: 39.7 us; the launch traced here: 39.3 us
  blocking collectives  27.1 us (68%)
  Pallas kernels  6.78 us (17%)
  local copies, waits for them, and re-layouts  5.3 us (13%)
    all_to_all x1, blocking collectives, on_device(): lax.all_to_all(send, 'row', split_axis=0, concat_axis=0, tiled=True)  25.1 us
    pallas_call x1, Pallas kernels, pairs(): pl.pallas_call(functools.partial(pair_kernel, seqs, c, rows_step), grid=(...  5.98 us
    unnamed x16, local copies, waits for them, and re-layouts  4.5 us
    all_gather x1, blocking collectives, on_device(): left = lax.all_gather(left, 'col', axis=0, tiled=True)  2 us
    pallas_call x1, Pallas kernels, features(): pl.pallas_call(functools.partial(features_kernel, scale), out_shape=(jax....  0.8 us

profile of v1, /device:TPU:0, one launch (start us, length us, event | category | flops | bytes accessed | tf_op | source)
XLA Modules:
  0.0 39.3 jit_solution(7968081942680105276)
XLA Ops:
  0.0 0.7 %copy.11.br_ref = f32[32,1]{1,0:T(8,128)S(1)} copy(f32[32,1]{0,1:T(1,128)} %bitcast.15) | data formatting | bytes 256 | tf_op jit(solution)/shard_map/reshape | solution.py:65
  0.7 0.0 copy-start
  0.7 1.0 %copy-done = bf16[8,128,256]{2,1,0:T(8,128)(2,1)S(1)} copy-done((bf16[8,128,256]{2,1,0:T(8,128)(2,1)S(1)}, bf16[8,128,256]{2,1,0:T(8,128)(2,1)}, u32[]{:S(2)}) %copy-start) | copy-done | bytes 524312
  1.8 0.0 copy-start.2
  1.8 0.7 %copy-done.2 = bf16[256,32]{0,1:T(8,128)(2,1)S(1)} copy-done((bf16[256,32]{0,1:T(8,128)(2,1)S(1)}, bf16[256,32]{0,1:T(8,128)(2,1)}, u32[]{:S(2)}) %copy-start.2) | copy-done | bytes 16408
  2.5 0.0 copy-start.3
  2.5 0.7 %copy-done.3 = bf16[256,32]{0,1:T(8,128)(2,1)S(1)} copy-done((bf16[256,32]{0,1:T(8,128)(2,1)S(1)}, bf16[256,32]{0,1:T(8,128)(2,1)}, u32[]{:S(2)}) %copy-start.3) | copy-done | bytes 16408
  3.2 0.0 copy-start.4
  3.2 0.7 %copy-done.4 = f32[256]{0:T(256)S(1)} copy-done((f32[256]{0:T(256)S(1)}, f32[256]{0:T(256)}, u32[]{:S(2)}) %copy-start.4) | copy-done | bytes 1048
  3.9 0.0 copy-start.5
  3.9 0.7 %copy-done.5 = f32[256]{0:T(256)S(1)} copy-done((f32[256]{0:T(256)S(1)}, f32[256]{0:T(256)}, u32[]{:S(2)}) %copy-start.5) | copy-done | bytes 1048
  4.6 0.0 copy-start.7
  4.6 0.7 %copy-done.7 = f32[32]{0:T(128)S(1)} copy-done((f32[32]{0:T(128)S(1)}, f32[32]{0:T(128)}, u32[]{:S(2)}) %copy-start.7) | copy-done | bytes 152
  5.2 0.8 %features.1 = (bf16[256,128]{1,0:T(8,128)(2,1)S(1)}, bf16[256,128]{1,0:T(8,128)(2,1)S(1)}) custom-call(bf16[8,128,256]{2,1,0:T(8,128)(2,1)S(1)} %copy-done, f32[1,256]{1,0:T(1,128)S(1)} %bitcast.11, f32[1,256]{1,0:T(1,128)S(1)} %bitcast.12, bf16[32,256]{1,0:T(8,128)(2,1)S(1)} %bitcast.9, f32[1,32]{1,0:T(1,128)S(1)} %bitcast.14, ...), custom_call_target="tpu_custom_call" | custom-call | tf_op jit(solution)/shard_map/features/pallas_call | solution.py:53
  6.0 2.0 %all_gather.3 = bf16[8,64,128]{2,1,0:T(8,128)(2,1)S(1)} all-gather(bf16[4,64,128]{2,1,0:T(8,128)(2,1)S(1)} %bitcast.8), channel_id=1, replica_groups=mesh['group'=2,'row'=8,'col'=2] {'col'}, dimensions={0}, use_global_device_ids=true | all-gather | bytes 196608 | tf_op jit(solution)/shard_map/all_gather | solution.py:158
  8.0 0.1 broadcast_in_dim.2
  8.1 0.0 copy-start.1
  8.1 0.0 copy-start.6
  8.2 25.1 %all_to_all.5.recv_ref = bf16[8,320,128]{2,1,0:T(8,128)(2,1)S(1)} all-to-all(bf16[8,320,128]{2,1,0:T(8,128)(2,1)S(1)} %pad_maximum_fusion), channel_id=1, replica_groups=mesh['group'=2,'row'=8,'col'=2] {'row'}, dimensions={0} | all-to-all | bytes 1310720 | tf_op jit(solution)/shard_map/all_to_all | solution.py:161
  33.3 0.0 copy-done.1
  33.3 0.0 copy-done.6
  33.3 6.0 %pairs.1 = bf16[32,128,128]{2,1,0:T(8,128)(2,1)} custom-call(bf16[8,320,128]{2,1,0:T(8,128)(2,1)S(1)} %all_to_all.5.recv_ref, bf16[1024,128]{1,0:T(8,128)(2,1)S(1)} %copy-done.1, f32[1,128]{1,0:T(1,128)S(1)} %bitcast.13), custom_call_target="tpu_custom_call" | custom-call | tf_op jit(solution)/shard_map/pairs/pallas_call | solution.py:131
  (1 shorter events, 0.0 us)
Async XLA Ops:
  0.7 1.0 %copy-start = (bf16[8,128,256]{2,1,0:T(8,128)(2,1)S(1)}, bf16[8,128,256]{2,1,0:T(8,128)(2,1)}, u32[]{:S(2)}) copy-start(bf16[8,128,256]{2,1,0:T(8,128)(2,1)} %x_ref.1) | copy-start | bytes 1572868
  1.8 0.7 %copy-start.2 = (bf16[256,32]{0,1:T(8,128)(2,1)S(1)}, bf16[256,32]{0,1:T(8,128)(2,1)}, u32[]{:S(2)}) copy-start(bf16[256,32]{0,1:T(8,128)(2,1)} %param.12) | copy-start | bytes 49156
  2.5 0.7 %copy-start.3 = (bf16[256,32]{0,1:T(8,128)(2,1)S(1)}, bf16[256,32]{0,1:T(8,128)(2,1)}, u32[]{:S(2)}) copy-start(bf16[256,32]{0,1:T(8,128)(2,1)} %param.14) | copy-start | bytes 49156
  3.2 0.7 %copy-start.4 = (f32[256]{0:T(256)S(1)}, f32[256]{0:T(256)}, u32[]{:S(2)}) copy-start(f32[256]{0:T(256)} %param.10) | copy-start | bytes 3076
  3.9 0.7 %copy-start.5 = (f32[256]{0:T(256)S(1)}, f32[256]{0:T(256)}, u32[]{:S(2)}) copy-start(f32[256]{0:T(256)} %param.11) | copy-start | bytes 3076
  4.6 0.7 %copy-start.7 = (f32[32]{0:T(128)S(1)}, f32[32]{0:T(128)}, u32[]{:S(2)}) copy-start(f32[32]{0:T(128)} %param.13) | copy-start | bytes 388
  8.1 25.2 %copy-start.1 = (bf16[1024,128]{1,0:T(8,128)(2,1)S(1)}, bf16[1024,128]{1,0:T(8,128)(2,1)}, u32[]{:S(2)}) copy-start(bf16[1024,128]{1,0:T(8,128)(2,1)} %w_ref.1) | copy-start | bytes 786436
  8.1 25.2 %copy-start.6 = (f32[128]{0:T(128)S(1)}, f32[128]{0:T(128)}, u32[]{:S(2)}) copy-start(f32[128]{0:T(128)} %param.17) | copy-start | bytes 1540

commit v2 on v1

--- a/solution.py
+++ b/solution.py
@@ -16,6 +16,7 @@
     c = wl_ref.shape[0]
     fold = LANES // c
     quarter = width // fold
+    right_bias = jnp.broadcast_to(br_ref[...], (LANES, c)).T[:, :1]
     for s in range(seqs):
         values = x_ref[s].astype(jnp.float32)
         average = jnp.mean(values, axis=-1, keepdims=True)
@@ -25,7 +26,7 @@
         for h in range(channels // LANES):
             normed_ref[h, s * width:(s + 1) * width] = normed[:, h * LANES:(h + 1) * LANES]
         right = lax.dot_general(wr_ref[...], normed.astype(jnp.bfloat16), (((1,), (1,)), ((), ())),
-                                preferred_element_type=jnp.float32) + br_ref[...]
+                                preferred_element_type=jnp.float32) + right_bias
         for b in range(width // LANES):
             right_f32[pl.ds(b * c * seqs + s, c, stride=seqs), :] = right[:, b * LANES:(b + 1) * LANES]
     total = None
@@ -47,22 +48,24 @@
 def features(alignment, ln_gain, ln_bias, w_left, b_left, w_right, b_right, scale):
     seqs, width, channels = alignment.shape
     c = w_left.shape[1]
-    left_rows = seqs * width * c // LANES
-    right_rows = left_rows
-    vmem = pl.BlockSpec(memory_space=pltpu.VMEM)
+    rows = seqs * width * c // LANES
+    whole = [pl.BlockSpec(shape, lambda i, n=len(shape): (0,) * n)
+             for shape in (alignment.shape, (1, channels), (1, channels), (c, channels), (1, c),
+                           (c, channels), (1, c))]
+    side = pl.BlockSpec((rows, LANES), lambda i: (0, 0))
     return pl.pallas_call(
         functools.partial(features_kernel, scale),
-        out_shape=(jax.ShapeDtypeStruct((left_rows, LANES), jnp.bfloat16),
-                   jax.ShapeDtypeStruct((right_rows, LANES), jnp.bfloat16)),
-        in_specs=[vmem] * 7,
-        out_specs=(vmem, vmem),
+        grid=(1,),
+        out_shape=(jax.ShapeDtypeStruct((rows, LANES), jnp.bfloat16),) * 2,
+        in_specs=whole,
+        out_specs=(side, side),
         scratch_shapes=[pltpu.VMEM((channels // LANES, seqs * width, LANES), jnp.float32),
-                        pltpu.VMEM((left_rows, LANES), jnp.float32),
-                        pltpu.VMEM((right_rows, LANES), jnp.float32)],
-        compiler_params=pltpu.CompilerParams(vmem_limit_bytes=32 * 1024 * 1024),
+                        pltpu.VMEM((rows, LANES), jnp.float32),
+                        pltpu.VMEM((rows, LANES), jnp.float32)],
+        compiler_params=pltpu.CompilerParams(vmem_limit_bytes=60 * 1024 * 1024),
         name="features",
     )(alignment, ln_gain.reshape(1, -1), ln_bias.reshape(1, -1), w_left.T, b_left.reshape(1, -1),
-      w_right.T, b_right.reshape(-1, 1))
+      w_right.T, b_right.reshape(1, -1))
 
 
 def by_sequence(block, f32_ref, inner, seqs):
@@ -77,25 +80,25 @@
         [flat[pl.ds(n * seqs + s, sources, stride=inner * seqs), :] for s in range(seqs)], axis=0)
 
 
-def pair_kernel(seqs, c, rows_step, recv_ref, w_ref, bias_ref, out_ref,
-                left_f32, right_f32, left_t, right_b, w_f32, w_t, outer_ref):
-    sources = recv_ref.shape[0]
+def pair_kernel(seqs, c, rows_step, order_ref, left_ref, w_ref, bias_ref, *refs):
+    sources = left_ref.shape[0]
+    right_refs = refs[:sources]
+    out_ref, left_f32, right_f32, left_t, right_b, w_f32, w_t, outer_ref = refs[sources:]
     rows, width, z = out_ref.shape[0], out_ref.shape[1], out_ref.shape[2]
     left_rows = left_f32.shape[1]
-    fold = LANES // c
     blocks = width // LANES
     step = pl.program_id(0)
 
     @pl.when(step == 0)
     def _():
-        left_of = by_sequence(lambda src: recv_ref[src, :left_rows].astype(jnp.float32),
+        left_of = by_sequence(lambda src: left_ref[order_ref[src]].astype(jnp.float32),
                               left_f32, left_rows // seqs, seqs)
         for k in range(left_rows // seqs):
             left_t[k * LANES:(k + 1) * LANES] = left_of(k).T.astype(jnp.bfloat16)
         for b in range(blocks):
-            first = left_rows + b * c * seqs
-            right_of = by_sequence(lambda src: recv_ref[src, first:first + c * seqs].astype(jnp.float32),
-                                   right_f32, c, seqs)
+            right_of = by_sequence(
+                lambda src: right_refs[src][b * c * seqs:(b + 1) * c * seqs].astype(jnp.float32),
+                right_f32, c, seqs)
             for e in range(c):
                 at = (b * c + e) * LANES
                 right_b[:, at:at + LANES] = right_of(e).astype(jnp.bfloat16)
@@ -121,18 +124,19 @@
                 out_ref[2 * p + half, b * LANES:(b + 1) * LANES, :] = mine.astype(out_ref.dtype)
 
 
-def pairs(received, w_out, b_out, seqs, c, rows, width):
-    sources, all_rows, _ = received.shape
+def pairs(order, left, rights, w_out, b_out, seqs, c, width):
+    sources, left_rows, _ = left.shape
     z = w_out.shape[1]
-    left_rows = rows * c * seqs // LANES
+    rows = left_rows * LANES // (c * seqs)
     rows_step = 8
-    vmem = pl.BlockSpec(memory_space=pltpu.VMEM)
     total = sources * seqs
+    operands = (left, w_out, b_out.reshape(1, -1), *rights)
     return pl.pallas_call(
         functools.partial(pair_kernel, seqs, c, rows_step),
         grid=(rows // rows_step,),
         out_shape=jax.ShapeDtypeStruct((rows, width, z), jnp.bfloat16),
-        in_specs=[vmem] * 3,
+        in_specs=[pl.BlockSpec(memory_space=pltpu.SMEM)]
+        + [pl.BlockSpec(a.shape, lambda i, n=a.ndim: (0,) * n) for a in operands],
         out_specs=pl.BlockSpec((rows_step, width, z), lambda i: (i, 0, 0)),
         scratch_shapes=[pltpu.VMEM((sources, left_rows, LANES), jnp.float32),
                         pltpu.VMEM((sources, c * seqs, LANES), jnp.float32),
@@ -143,7 +147,13 @@
                         pltpu.VMEM((rows_step // 2, c * c, 2 * LANES), jnp.bfloat16)],
         compiler_params=pltpu.CompilerParams(vmem_limit_bytes=48 * 1024 * 1024),
         name="pairs",
-    )(received, w_out, b_out.reshape(1, -1))
+    )(order, *operands)
+
+
+def ring_of(count):
+    if count % 2 == 0 and count <= 8:
+        return list(range(0, count, 2)) + list(range(count - 1, 0, -2))
+    return list(range(count))
 
 
 def on_device(alignment, ln_gain, ln_bias, w_left, b_left, w_right, b_right, w_out, b_out):
@@ -152,14 +162,27 @@
     row_count = lax.axis_size("row")
     col_count = lax.axis_size("col")
     rows = width * col_count // row_count
+    ring = ring_of(row_count)
     left, right = features(alignment, ln_gain, ln_bias, w_left, b_left, w_right, b_right,
                            1.0 / (seqs * row_count))
+
+    forth = [(ring[i], ring[(i + 1) % row_count]) for i in range(row_count)]
+    back = [(b, a) for a, b in forth]
+    rights = {0: right}
+    for step in range(1, row_count // 2 + 1):
+        rights[-step % row_count] = lax.ppermute(rights[(1 - step) % row_count], "row", forth)
+        if 2 * step < row_count:
+            rights[step] = lax.ppermute(rights[step - 1], "row", back)
+    place = [0] * row_count
+    for i, r in enumerate(ring):
+        place[r] = i
+    around = [[ring[(place[r] + t) % row_count] for t in range(row_count)] for r in range(row_count)]
+    order = jnp.array(around, jnp.int32)[lax.axis_index("row")]
+
     left = left.reshape(width // rows, rows * c * seqs // LANES, LANES)
     left = lax.all_gather(left, "col", axis=0, tiled=True)
-    send = jnp.concatenate(
-        [left, jnp.broadcast_to(right[None], (row_count,) + right.shape)], axis=1)
-    received = lax.all_to_all(send, "row", split_axis=0, concat_axis=0, tiled=True)
-    return pairs(received, w_out, b_out, seqs, c, rows, width)
+    left = lax.all_to_all(left, "row", split_axis=0, concat_axis=0, tiled=True)
+    return pairs(order, left, [rights[t] for t in range(row_count)], w_out, b_out, seqs, c, width)
 
 
 def solution(mesh):

time: 39.7 us -> 36.2 us (0.912)
  blocking collectives: 27.1 us -> 3.36 us
  starting transfers between devices: 0 us -> 15 us
  waiting for transfers between devices: 0 us -> 7.64 us
  local copies, waits for them, and re-layouts: 5.3 us -> 0.7 us
  Pallas kernels: 6.78 us -> 9.08 us
    all_to_all x1 -> x0, blocking collectives: 25.1 us -> none  [on_device(): lax.all_to_all(send, 'row', split_axis=0, concat_axis=0, tiled=True)]
    ppermute x0 -> x7, starting transfers between devices: none -> 10.1 us  [the longest x4 7.08 us: on_device(): lax.ppermute(rights[(1 - step) % row_count], 'row', forth)]
    ppermute x0 -> x7, waiting for transfers between devices: none -> 7.64 us  [the longest x3 5.12 us: on_device(): rights[step] = lax.ppermute(rights[step - 1], 'row', back)]
    all_to_all x0 -> x1, starting transfers between devices: none -> 4.95 us  [on_device(): left = lax.all_to_all(left, 'row', split_axis=0, concat_axis=0, tiled=True)]
    unnamed x16 -> x6, local copies, waits for them, and re-layouts: 4.5 us -> 0.01 us
    pallas_call x1, Pallas kernels: 0.8 us -> 2.51 us  [features(): pl.pallas_call(functools.partial(features_kernel, scale), grid=(1,), out_...]
    all_gather x1, blocking collectives: 2 us -> 3.36 us  [on_device(): left = lax.all_gather(left, 'col', axis=0, tiled=True)]
    reshape x1 -> x0, local copies, waits for them, and re-layouts: 0.74 us -> none  [features(): b_right.reshape(-1, 1)]
  transfers between devices with their start and end apart: 0 -> 8, of which waited for: 0 -> 4; matrix products, arithmetic and copies ran while one was open for 0% -> 2% of each run, Pallas kernels for 0% -> 0%
where the time goes in v2:
time: 36.2 us; the launch traced here: 35.8 us
  starting transfers between devices  15 us (41%)
  Pallas kernels  9.08 us (25%)
  waiting for transfers between devices  7.64 us (21%)
  blocking collectives  3.36 us (9%)
  local copies, waits for them, and re-layouts  0.7 us (2%)
    ppermute x4, starting transfers between devices, on_device(): lax.ppermute(rights[(1 - step) % row_count], 'row', forth)  7.08 us
    pallas_call x1, Pallas kernels, pairs(): pl.pallas_call(functools.partial(pair_kernel, seqs, c, rows_step), grid=(...  6.57 us
    ppermute x3, waiting for transfers between devices, on_device(): rights[step] = lax.ppermute(rights[step - 1], 'row', back)  5.12 us
    all_to_all x1, starting transfers between devices, on_device(): left = lax.all_to_all(left, 'row', split_axis=0, concat_axis=0, tiled=True)  4.95 us
    all_gather x1, blocking collectives, on_device(): left = lax.all_gather(left, 'col', axis=0, tiled=True)  3.36 us
    ppermute x3, starting transfers between devices, on_device(): rights[step] = lax.ppermute(rights[step - 1], 'row', back)  2.98 us
    ppermute x4, waiting for transfers between devices, on_device(): lax.ppermute(rights[(1 - step) % row_count], 'row', forth)  2.52 us
    pallas_call x1, Pallas kernels, features(): pl.pallas_call(functools.partial(features_kernel, scale), grid=(1,), out_...  2.51 us
  transfers between devices with their start and end apart: 8, of which 4 were waited for; matrix products, arithmetic and copies ran while one was open for 2% of the time, Pallas kernels for 0%

profile of v2, /device:TPU:0, one launch (start us, length us, event | category | flops | bytes accessed | tf_op | source)
XLA Modules:
  0.0 35.8 jit_solution(3201210084375343422)
XLA Ops:
  0.0 2.5 %features.1 = (bf16[256,128]{1,0:T(8,128)(2,1)}, bf16[256,128]{1,0:T(8,128)(2,1)}) custom-call(bf16[8,128,256]{2,1,0:T(8,128)(2,1)} %x_ref.1, f32[1,256]{1,0:T(1,128)} %bitcast.14, f32[1,256]{1,0:T(1,128)} %bitcast.15, bf16[32,256]{1,0:T(8,128)(2,1)} %bitcast.12, f32[1,32]{1,0:T(1,128)} %bitcast.16, bf16[32,256]{1,0:T(8,128)(2,1)} %bitcast.13, f32[1,32]{1,0:T(1,128)} %bitcast.17), custom_call_target="tpu_custom_call" | custom-call | tf_op jit(solution)/shard_map/features/pallas_call | solution.py:56
  2.5 0.0 copy-start
  2.5 3.0 %collective-permute-start.3 = (bf16[256,128]{1,0:T(8,128)(2,1)}, bf16[256,128]{1,0:T(8,128)(2,1)S(1)}, u32[]{:S(2)}, u32[]{:S(2)}) collective-permute-start(bf16[256,128]{1,0:T(8,128)(2,1)} %get-tuple-element.8.refs_0_), channel_id=1, source_target_pairs={{0,4},{4,8},{8,12},{12,14},{14,10},{10,6},{6,2},{2,0},{1,5},{5,9},... | collective-permute-start | bytes 196616 | tf_op jit(solution)/shard_map/ppermute | solution.py:173
  5.5 0.0 collective-permute-start
  5.5 2.4 %collective-permute-done.3.refs_7_ = bf16[256,128]{1,0:T(8,128)(2,1)S(1)} collective-permute-done((bf16[256,128]{1,0:T(8,128)(2,1)}, bf16[256,128]{1,0:T(8,128)(2,1)S(1)}, u32[]{:S(2)}, u32[]{:S(2)}) %collective-permute-start.3) | collective-permute-done | bytes 65568 | tf_op jit(solution)/shard_map/ppermute | solution.py:173
  7.9 2.1 %collective-permute-start.4 = (bf16[256,128]{1,0:T(8,128)(2,1)S(1)}, bf16[256,128]{1,0:T(8,128)(2,1)S(1)}, u32[]{:S(2)}, u32[]{:S(2)}) collective-permute-start(bf16[256,128]{1,0:T(8,128)(2,1)S(1)} %collective-permute-done.3.refs_7_), channel_id=1, source_target_pairs={{0,4},{4,8},{8,12},{12,14},{14,10},{10,6},{6,2},{2,0},{1,5},{5,9},... | collective-permute-start | bytes 196616 | tf_op jit(solution)/shard_map/ppermute | solution.py:173
  10.0 3.4 %all_gather.3 = bf16[8,64,128]{2,1,0:T(8,128)(2,1)} all-gather(bf16[4,64,128]{2,1,0:T(8,128)(2,1)} %bitcast.11), channel_id=1, replica_groups=mesh['group'=2,'row'=8,'col'=2] {'col'}, dimensions={0}, use_global_device_ids=true | all-gather | bytes 196608 | tf_op jit(solution)/shard_map/all_gather | solution.py:183
  13.4 5.0 %all-to-all-start = ((bf16[8,64,128]{2,1,0:T(8,128)(2,1)}), bf16[8,64,128]{2,1,0:T(8,128)(2,1)S(1)}, u32[]{:S(2)}, u32[]{:S(2)}) async-start(bf16[8,64,128]{2,1,0:T(8,128)(2,1)} %all_gather.3), calls=%async_computation | async-start | bytes 262144 | tf_op jit(solution)/shard_map/all_to_all | solution.py:184
  18.3 0.0 collective-permute-done.refs_1_
  18.3 2.0 %collective-permute-start.1 = (bf16[256,128]{1,0:T(8,128)(2,1)S(1)}, bf16[256,128]{1,0:T(8,128)(2,1)S(1)}, u32[]{:S(2)}, u32[]{:S(2)}) collective-permute-start(bf16[256,128]{1,0:T(8,128)(2,1)S(1)} %collective-permute-done.refs_1_), channel_id=1, source_target_pairs={{4,0},{8,4},{12,8},{14,12},{10,14},{6,10},{2,6},{0,2},{5,1},{9,5},... | collective-permute-start | bytes 196616 | tf_op jit(solution)/shard_map/ppermute | solution.py:175
  20.3 0.0 collective-permute-done.4.refs_6_
  20.4 0.1 collective-permute-start.5
  20.4 3.6 %collective-permute-done.1.refs_2_ = bf16[256,128]{1,0:T(8,128)(2,1)S(1)} collective-permute-done((bf16[256,128]{1,0:T(8,128)(2,1)S(1)}, bf16[256,128]{1,0:T(8,128)(2,1)S(1)}, u32[]{:S(2)}, u32[]{:S(2)}) %collective-permute-start.1) | collective-permute-done | bytes 65568 | tf_op jit(solution)/shard_map/ppermute | solution.py:175
  24.0 1.0 %collective-permute-start.2 = (bf16[256,128]{1,0:T(8,128)(2,1)S(1)}, bf16[256,128]{1,0:T(8,128)(2,1)S(1)}, u32[]{:S(2)}, u32[]{:S(2)}) collective-permute-start(bf16[256,128]{1,0:T(8,128)(2,1)S(1)} %collective-permute-done.1.refs_2_), channel_id=1, source_target_pairs={{4,0},{8,4},{12,8},{14,12},{10,14},{6,10},{2,6},{0,2},{5,1},{9,5},... | collective-permute-start | bytes 196616 | tf_op jit(solution)/shard_map/ppermute | solution.py:175
  25.0 0.0 collective-permute-done.5.refs_5_
  25.0 1.9 %collective-permute-start.6 = (bf16[256,128]{1,0:T(8,128)(2,1)S(1)}, bf16[256,128]{1,0:T(8,128)(2,1)S(1)}, u32[]{:S(2)}, u32[]{:S(2)}) collective-permute-start(bf16[256,128]{1,0:T(8,128)(2,1)S(1)} %collective-permute-done.5.refs_5_), channel_id=1, source_target_pairs={{0,4},{4,8},{8,12},{12,14},{14,10},{10,6},{6,2},{2,0},{1,5},{5,9},... | collective-permute-start | bytes 196616 | tf_op jit(solution)/shard_map/ppermute | solution.py:173
  26.9 0.7 %dynamic-slice_bitcast_fusion.order_ref = s32[8]{0:T(128)S(1)} fusion(s32[8,8]{1,0:T(8,128)} %constant.12.clone, s32[]{:T(128)S(6)} %select_n.3), kind=kLoop, calls=%fused_computation | loop fusion | bytes 68 | tf_op jit(solution)/shard_map/squeeze | solution.py:180
  27.6 1.5 %collective-permute-done.2.refs_3_ = bf16[256,128]{1,0:T(8,128)(2,1)S(1)} collective-permute-done((bf16[256,128]{1,0:T(8,128)(2,1)S(1)}, bf16[256,128]{1,0:T(8,128)(2,1)S(1)}, u32[]{:S(2)}, u32[]{:S(2)}) %collective-permute-start.2) | collective-permute-done | bytes 65568 | tf_op jit(solution)/shard_map/ppermute | solution.py:175
  29.1 0.0 all-to-all-done.left_ref
  29.1 0.1 collective-permute-done.6.refs_4_
  29.2 0.0 copy-done
  29.2 0.0 copy-done.1
  29.2 0.0 copy-done.2
  29.2 6.6 %pairs.1 = bf16[32,128,128]{2,1,0:T(8,128)(2,1)} custom-call(s32[8]{0:T(128)S(1)} %dynamic-slice_bitcast_fusion.order_ref, bf16[8,64,128]{2,1,0:T(8,128)(2,1)S(1)} %all-to-all-done.left_ref, bf16[1024,128]{1,0:T(8,128)(2,1)S(1)} %copy-done, f32[1,128]{1,0:T(1,128)S(1)} %bitcast.10, bf16[256,128]{1,0:T(8,128)(2,1)S(1)} %copy-done.1, ...), custom_call_target="tpu_custom_call" | custom-call | tf_op jit(solution)/shard_map/pairs/pallas_call | solution.py:134
  (2 shorter events, 0.0 us)
Async XLA Ops:
  2.5 26.7 %copy-start = (bf16[1024,128]{1,0:T(8,128)(2,1)S(1)}, bf16[1024,128]{1,0:T(8,128)(2,1)}, u32[]{:S(2)}) copy-start(bf16[1024,128]{1,0:T(8,128)(2,1)} %w_ref.1) | copy-start | bytes 786436
  2.5 5.4 %collective-permute-start.3 = (bf16[256,128]{1,0:T(8,128)(2,1)}, bf16[256,128]{1,0:T(8,128)(2,1)S(1)}, u32[]{:S(2)}, u32[]{:S(2)}) collective-permute-start(bf16[256,128]{1,0:T(8,128)(2,1)} %get-tuple-element.8.refs_0_), channel_id=1, source_target_pairs={{0,4},{4,8},{8,12},{12,14},{14,10},{10,6},{6,2},{2,0},{1,5},{5,9},... | collective-permute-start | bytes 196616 | tf_op jit(solution)/shard_map/ppermute | solution.py:173
  5.5 12.8 %collective-permute-start = (bf16[256,128]{1,0:T(8,128)(2,1)}, bf16[256,128]{1,0:T(8,128)(2,1)S(1)}, u32[]{:S(2)}, u32[]{:S(2)}) collective-permute-start(bf16[256,128]{1,0:T(8,128)(2,1)} %get-tuple-element.8.refs_0_), channel_id=1, source_target_pairs={{4,0},{8,4},{12,8},{14,12},{10,14},{6,10},{2,6},{0,2},{5,1},{9,5},... | collective-permute-start | bytes 196616 | tf_op jit(solution)/shard_map/ppermute | solution.py:175
  7.9 12.4 %collective-permute-start.4 = (bf16[256,128]{1,0:T(8,128)(2,1)S(1)}, bf16[256,128]{1,0:T(8,128)(2,1)S(1)}, u32[]{:S(2)}, u32[]{:S(2)}) collective-permute-start(bf16[256,128]{1,0:T(8,128)(2,1)S(1)} %collective-permute-done.3.refs_7_), channel_id=1, source_target_pairs={{0,4},{4,8},{8,12},{12,14},{14,10},{10,6},{6,2},{2,0},{1,5},{5,9},... | collective-permute-start | bytes 196616 | tf_op jit(solution)/shard_map/ppermute | solution.py:173
  13.4 15.9 %copy-start.1 = (bf16[256,128]{1,0:T(8,128)(2,1)S(1)}, bf16[256,128]{1,0:T(8,128)(2,1)}, u32[]{:S(2)}) copy-start(bf16[256,128]{1,0:T(8,128)(2,1)} %get-tuple-element.8.refs_0_) | copy-start | bytes 196612
  13.4 15.7 %all-to-all-start = ((bf16[8,64,128]{2,1,0:T(8,128)(2,1)}), bf16[8,64,128]{2,1,0:T(8,128)(2,1)S(1)}, u32[]{:S(2)}, u32[]{:S(2)}) async-start(bf16[8,64,128]{2,1,0:T(8,128)(2,1)} %all_gather.3), calls=%async_computation | async-start | bytes 262144 | tf_op jit(solution)/shard_map/all_to_all | solution.py:184
  18.3 5.7 %collective-permute-start.1 = (bf16[256,128]{1,0:T(8,128)(2,1)S(1)}, bf16[256,128]{1,0:T(8,128)(2,1)S(1)}, u32[]{:S(2)}, u32[]{:S(2)}) collective-permute-start(bf16[256,128]{1,0:T(8,128)(2,1)S(1)} %collective-permute-done.refs_1_), channel_id=1, source_target_pairs={{4,0},{8,4},{12,8},{14,12},{10,14},{6,10},{2,6},{0,2},{5,1},{9,5},... | collective-permute-start | bytes 196616 | tf_op jit(solution)/shard_map/ppermute | solution.py:175
  20.4 4.6 %collective-permute-start.5 = (bf16[256,128]{1,0:T(8,128)(2,1)S(1)}, bf16[256,128]{1,0:T(8,128)(2,1)S(1)}, u32[]{:S(2)}, u32[]{:S(2)}) collective-permute-start(bf16[256,128]{1,0:T(8,128)(2,1)S(1)} %collective-permute-done.4.refs_6_), channel_id=1, source_target_pairs={{0,4},{4,8},{8,12},{12,14},{14,10},{10,6},{6,2},{2,0},{1,5},{5,9},... | collective-permute-start | bytes 196616 | tf_op jit(solution)/shard_map/ppermute | solution.py:173
  24.0 5.1 %collective-permute-start.2 = (bf16[256,128]{1,0:T(8,128)(2,1)S(1)}, bf16[256,128]{1,0:T(8,128)(2,1)S(1)}, u32[]{:S(2)}, u32[]{:S(2)}) collective-permute-start(bf16[256,128]{1,0:T(8,128)(2,1)S(1)} %collective-permute-done.1.refs_2_), channel_id=1, source_target_pairs={{4,0},{8,4},{12,8},{14,12},{10,14},{6,10},{2,6},{0,2},{5,1},{9,5},... | collective-permute-start | bytes 196616 | tf_op jit(solution)/shard_map/ppermute | solution.py:175
  25.0 4.3 %collective-permute-start.6 = (bf16[256,128]{1,0:T(8,128)(2,1)S(1)}, bf16[256,128]{1,0:T(8,128)(2,1)S(1)}, u32[]{:S(2)}, u32[]{:S(2)}) collective-permute-start(bf16[256,128]{1,0:T(8,128)(2,1)S(1)} %collective-permute-done.5.refs_5_), channel_id=1, source_target_pairs={{0,4},{4,8},{8,12},{12,14},{14,10},{10,6},{6,2},{2,0},{1,5},{5,9},... | collective-permute-start | bytes 196616 | tf_op jit(solution)/shard_map/ppermute | solution.py:173
  27.6 1.7 %copy-start.2 = (f32[128]{0:T(128)S(1)}, f32[128]{0:T(128)}, u32[]{:S(2)}) copy-start(f32[128]{0:T(128)} %param.18) | copy-start | bytes 1540

commit v3 on v2

--- a/solution.py
+++ b/solution.py
@@ -10,8 +10,9 @@
 LANES = 128
 
 
-def features_kernel(scale, x_ref, gain_ref, bias_ref, wl_ref, bl_ref, wr_ref, br_ref,
-                    left_ref, right_ref, normed_ref, left_f32, right_f32):
+def features_kernel(scale, col_count, x_ref, gain_ref, bias_ref, wl_ref, bl_ref, wr_ref, br_ref,
+                    right_ref, *refs):
+    left_refs, (normed_ref, left_f32, right_f32) = refs[:-3], refs[-3:]
     seqs, width, channels = x_ref.shape
     c = wl_ref.shape[0]
     fold = LANES // c
@@ -41,24 +42,33 @@
     total = (total + jnp.concatenate([bl_ref[...]] * fold, axis=1)) * scale
     for s in range(seqs):
         left_f32[pl.ds(s, quarter, stride=seqs), :] = total[s * quarter:(s + 1) * quarter]
-    left_ref[...] = left_f32[...].astype(jnp.bfloat16)
+    here = lax.axis_index("row")
+    for k, left_ref in enumerate(left_refs):
+        rows = left_ref.shape[0]
+        chip = lax.rem(here + k, len(left_refs)) // col_count
+        left_ref[...] = left_f32[pl.ds(pl.multiple_of(chip * rows, rows), rows), :].astype(jnp.bfloat16)
     right_ref[...] = right_f32[...].astype(jnp.bfloat16)
 
 
-def features(alignment, ln_gain, ln_bias, w_left, b_left, w_right, b_right, scale):
+def features(alignment, ln_gain, ln_bias, w_left, b_left, w_right, b_right, row_count, col_count):
     seqs, width, channels = alignment.shape
     c = w_left.shape[1]
     rows = seqs * width * c // LANES
     whole = [pl.BlockSpec(shape, lambda i, n=len(shape): (0,) * n)
              for shape in (alignment.shape, (1, channels), (1, channels), (c, channels), (1, c),
                            (c, channels), (1, c))]
-    side = pl.BlockSpec((rows, LANES), lambda i: (0, 0))
+    part = rows * col_count // row_count
+
+    def side(n):
+        return pl.BlockSpec((n, LANES), lambda i: (0, 0))
+
     return pl.pallas_call(
-        functools.partial(features_kernel, scale),
+        functools.partial(features_kernel, 1.0 / (seqs * row_count), col_count),
         grid=(1,),
-        out_shape=(jax.ShapeDtypeStruct((rows, LANES), jnp.bfloat16),) * 2,
+        out_shape=[jax.ShapeDtypeStruct((rows, LANES), jnp.bfloat16)]
+        + [jax.ShapeDtypeStruct((part, LANES), jnp.bfloat16)] * row_count,
         in_specs=whole,
-        out_specs=(side, side),
+        out_specs=[side(rows)] + [side(part)] * row_count,
         scratch_shapes=[pltpu.VMEM((channels // LANES, seqs * width, LANES), jnp.float32),
                         pltpu.VMEM((rows, LANES), jnp.float32),
                         pltpu.VMEM((rows, LANES), jnp.float32)],
@@ -68,10 +78,10 @@
       w_right.T, b_right.reshape(1, -1))
 
 
-def by_sequence(block, f32_ref, inner, seqs):
+def by_sequence(block, source_of, f32_ref, inner, seqs):
     sources = f32_ref.shape[0]
     for src in range(sources):
-        f32_ref[src] = block(src)
+        f32_ref[source_of(src)] = block(src)
     if seqs % 8 == 0:
         return lambda n: jnp.concatenate(
             [f32_ref[src, n * seqs:(n + 1) * seqs] for src in range(sources)], axis=0)
@@ -80,10 +90,10 @@
         [flat[pl.ds(n * seqs + s, sources, stride=inner * seqs), :] for s in range(seqs)], axis=0)
 
 
-def pair_kernel(seqs, c, rows_step, order_ref, left_ref, w_ref, bias_ref, *refs):
-    sources = left_ref.shape[0]
-    right_refs = refs[:sources]
-    out_ref, left_f32, right_f32, left_t, right_b, w_f32, w_t, outer_ref = refs[sources:]
+def pair_kernel(seqs, c, rows_step, col_count, steps, w_ref, bias_ref, *refs):
+    sources = len(steps)
+    left_refs, right_refs, refs = refs[:sources], refs[sources:2 * sources], refs[2 * sources:]
+    out_ref, left_f32, right_f32, left_t, right_b, w_f32, w_t, outer_ref = refs
     rows, width, z = out_ref.shape[0], out_ref.shape[1], out_ref.shape[2]
     left_rows = left_f32.shape[1]
     blocks = width // LANES
@@ -91,14 +101,17 @@
 
     @pl.when(step == 0)
     def _():
-        left_of = by_sequence(lambda src: left_ref[order_ref[src]].astype(jnp.float32),
+        here, core = lax.axis_index("row"), lax.axis_index("col")
+        place = lax.rem(here, sources // col_count) * col_count + core
+        left_of = by_sequence(lambda k: left_refs[k][...].astype(jnp.float32),
+                              lambda k: lax.rem(place - k + sources, sources),
                               left_f32, left_rows // seqs, seqs)
         for k in range(left_rows // seqs):
             left_t[k * LANES:(k + 1) * LANES] = left_of(k).T.astype(jnp.bfloat16)
         for b in range(blocks):
             right_of = by_sequence(
-                lambda src: right_refs[src][b * c * seqs:(b + 1) * c * seqs].astype(jnp.float32),
-                right_f32, c, seqs)
+                lambda n: right_refs[n][b * c * seqs:(b + 1) * c * seqs].astype(jnp.float32),
+                lambda n: source_at(here, steps[n], sources), right_f32, c, seqs)
             for e in range(c):
                 at = (b * c + e) * LANES
                 right_b[:, at:at + LANES] = right_of(e).astype(jnp.bfloat16)
@@ -124,19 +137,19 @@
                 out_ref[2 * p + half, b * LANES:(b + 1) * LANES, :] = mine.astype(out_ref.dtype)
 
 
-def pairs(order, left, rights, w_out, b_out, seqs, c, width):
-    sources, left_rows, _ = left.shape
+def pairs(lefts, rights, w_out, b_out, seqs, c, width, col_count):
+    sources, left_rows = len(lefts), lefts[0].shape[0]
     z = w_out.shape[1]
     rows = left_rows * LANES // (c * seqs)
     rows_step = 8
     total = sources * seqs
-    operands = (left, w_out, b_out.reshape(1, -1), *rights)
+    steps = list(rights)
+    operands = (w_out, b_out.reshape(1, -1), *lefts, *rights.values())
     return pl.pallas_call(
-        functools.partial(pair_kernel, seqs, c, rows_step),
+        functools.partial(pair_kernel, seqs, c, rows_step, col_count, steps),
         grid=(rows // rows_step,),
         out_shape=jax.ShapeDtypeStruct((rows, width, z), jnp.bfloat16),
-        in_specs=[pl.BlockSpec(memory_space=pltpu.SMEM)]
-        + [pl.BlockSpec(a.shape, lambda i, n=a.ndim: (0,) * n) for a in operands],
+        in_specs=[pl.BlockSpec(a.shape, lambda i, n=a.ndim: (0,) * n) for a in operands],
         out_specs=pl.BlockSpec((rows_step, width, z), lambda i: (i, 0, 0)),
         scratch_shapes=[pltpu.VMEM((sources, left_rows, LANES), jnp.float32),
                         pltpu.VMEM((sources, c * seqs, LANES), jnp.float32),
@@ -147,13 +160,23 @@
                         pltpu.VMEM((rows_step // 2, c * c, 2 * LANES), jnp.bfloat16)],
         compiler_params=pltpu.CompilerParams(vmem_limit_bytes=48 * 1024 * 1024),
         name="pairs",
-    )(order, *operands)
-
-
-def ring_of(count):
-    if count % 2 == 0 and count <= 8:
-        return list(range(0, count, 2)) + list(range(count - 1, 0, -2))
-    return list(range(count))
+    )(*operands)
+
+
+def pair_width(count):
+    return 2 if count % 2 == 0 else 1
+
+
+def source_at(here, step, count):
+    across = pair_width(count)
+    along = count // across
+    z, y = here // across, here % across
+    z = (z ^ step[0]) if along & (along - 1) == 0 else (z + step[0]) % along
+    return z * across + (y + step[1]) % across
+
+
+def fetch(array, step, count):
+    return lax.ppermute(array, "row", [(source_at(r, step, count), r) for r in range(count)])
 
 
 def on_device(alignment, ln_gain, ln_bias, w_left, b_left, w_right, b_right, w_out, b_out):
@@ -161,28 +184,29 @@
     c = w_left.shape[1]
     row_count = lax.axis_size("row")
     col_count = lax.axis_size("col")
-    rows = width * col_count // row_count
-    ring = ring_of(row_count)
-    left, right = features(alignment, ln_gain, ln_bias, w_left, b_left, w_right, b_right,
-                           1.0 / (seqs * row_count))
-
-    forth = [(ring[i], ring[(i + 1) % row_count]) for i in range(row_count)]
-    back = [(b, a) for a, b in forth]
-    rights = {0: right}
-    for step in range(1, row_count // 2 + 1):
-        rights[-step % row_count] = lax.ppermute(rights[(1 - step) % row_count], "row", forth)
-        if 2 * step < row_count:
-            rights[step] = lax.ppermute(rights[step - 1], "row", back)
-    place = [0] * row_count
-    for i, r in enumerate(ring):
-        place[r] = i
-    around = [[ring[(place[r] + t) % row_count] for t in range(row_count)] for r in range(row_count)]
-    order = jnp.array(around, jnp.int32)[lax.axis_index("row")]
-
-    left = left.reshape(width // rows, rows * c * seqs // LANES, LANES)
-    left = lax.all_gather(left, "col", axis=0, tiled=True)
-    left = lax.all_to_all(left, "row", split_axis=0, concat_axis=0, tiled=True)
-    return pairs(order, left, [rights[t] for t in range(row_count)], w_out, b_out, seqs, c, width)
+    right, *lefts = features(alignment, ln_gain, ln_bias, w_left, b_left, w_right, b_right,
+                             row_count, col_count)
+
+    across = pair_width(row_count)
+    along = row_count // across
+    rights = {(0, 0): right}
+    for a in reversed(range(1, along)):
+        rights[a, 0] = fetch(right, (a, 0), row_count)
+    if across == 2:
+        for a in range(along):
+            rights[a, 1] = fetch(rights[a, 0], (0, 1), row_count)
+
+    chips = row_count // col_count
+    received = []
+    for k, left in enumerate(lefts):
+        moves = []
+        for r in range(row_count):
+            for core in range(col_count):
+                place = (r + k) % row_count
+                to = (core * chips + place // col_count) * col_count + place % col_count
+                moves.append((r * col_count + core, to))
+        received.append(lax.ppermute(left, ("row", "col"), moves))
+    return pairs(received, rights, w_out, b_out, seqs, c, width, col_count)
 
 
 def solution(mesh):

time: 36.2 us -> 56.8 us (1.57)
  starting transfers between devices: 15 us -> 28.6 us
  waiting for transfers between devices: 7.64 us -> 18 us
  blocking collectives: 3.36 us -> 0 us
    ppermute x7 -> x15, starting transfers between devices: 10.1 us -> 28.6 us  [the longest x8 18.9 us: on_device(): received.append(lax.ppermute(left, ('row', 'col'), moves))]
    ppermute x7 -> x15, waiting for transfers between devices: 7.64 us -> 18 us  [the longest x8 17.9 us: on_device(): received.append(lax.ppermute(left, ('row', 'col'), moves))]
    all_to_all x1 -> x0, starting transfers between devices: 4.95 us -> none  [on_device(): left = lax.all_to_all(left, 'row', split_axis=0, concat_axis=0, tiled=True)]
    all_gather x1 -> x0, blocking collectives: 3.36 us -> none  [on_device(): left = lax.all_gather(left, 'col', axis=0, tiled=True)]
    unnamed x6 -> x8, local copies, waits for them, and re-layouts: 0.01 us -> 0.85 us
    squeeze x1 -> x0, local copies, waits for them, and re-layouts: 0.69 us -> none  [on_device(): order = jnp.array(around, jnp.int32)[lax.axis_index('row')]]
  transfers between devices with their start and end apart: 8 -> 15, of which waited for: 4 -> 6; matrix products, arithmetic and copies ran while one was open for 2% -> 0% of each run, Pallas kernels for 0% -> 0%
where the time goes in v3:
time: 56.8 us; the launch traced here: 56.2 us
  starting transfers between devices  28.6 us (50%)
  waiting for transfers between devices  18 us (32%)
  Pallas kernels  8.72 us (15%)
  local copies, waits for them, and re-layouts  0.85 us (1%)
    ppermute x8, starting transfers between devices, on_device(): received.append(lax.ppermute(left, ('row', 'col'), moves))  18.9 us
    ppermute x8, waiting for transfers between devices, on_device(): received.append(lax.ppermute(left, ('row', 'col'), moves))  17.9 us
    ppermute x7, starting transfers between devices, fetch(): lax.ppermute(array, 'row', [(source_at(r, step, count), r) for r in range...  9.74 us
    pallas_call x1, Pallas kernels, pairs(): pl.pallas_call(functools.partial(pair_kernel, seqs, c, rows_step, col_cou...  6.14 us
    pallas_call x1, Pallas kernels, features(): pl.pallas_call(functools.partial(features_kernel, 1.0 / (seqs * row_count...  2.58 us
  transfers between devices with their start and end apart: 15, of which 6 were waited for; matrix products, arithmetic and copies ran while one was open for 0% of the time, Pallas kernels for 0%

profile of v3, /device:TPU:0, one launch (start us, length us, event | category | flops | bytes accessed | tf_op | source)
XLA Modules:
  0.0 56.2 jit_solution(7635665805857486235)
XLA Ops:
  0.0 2.6 %features.1 = (bf16[256,128]{1,0:T(8,128)(2,1)}, bf16[64,128]{1,0:T(8,128)(2,1)}, bf16[64,128]{1,0:T(8,128)(2,1)}, bf16[64,128]{1,0:T(8,128)(2,1)}, bf16[64,128]...) custom-call(bf16[8,128,256]{2,1,0:T(8,128)(2,1)} %x_ref.1, ...), custom_call_target="tpu_custom_call" | custom-call | tf_op jit(solution)/shard_map/features/pallas_call | solution.py:65
  2.6 3.1 %collective-permute-start.10 = (bf16[256,128]{1,0:T(8,128)(2,1)}, bf16[256,128]{1,0:T(8,128)(2,1)S(1)}, u32[]{:S(2)}, u32[]{:S(2)}) collective-permute-start(bf16[256,128]{1,0:T(8,128)(2,1)} %get-tuple-element.22.refs_8_), channel_id=1, source_target_pairs={{4,0},{6,2},{0,4},{2,6},{12,8},{14,10},{8,12},{10,14},{5,1},{7,3},... | collective-permute-start | bytes 196616 | tf_op jit(solution)/shard_map/ppermute | solution.py:179
  5.7 2.6 %collective-permute-start.9 = (bf16[256,128]{1,0:T(8,128)(2,1)}, bf16[256,128]{1,0:T(8,128)(2,1)S(1)}, u32[]{:S(2)}, u32[]{:S(2)}) collective-permute-start(bf16[256,128]{1,0:T(8,128)(2,1)} %get-tuple-element.22.refs_8_), channel_id=1, source_target_pairs={{8,0},{10,2},{12,4},{14,6},{0,8},{2,10},{4,12},{6,14},{9,1},{11,3}... | collective-permute-start | bytes 196616 | tf_op jit(solution)/shard_map/ppermute | solution.py:179
  8.3 1.4 %collective-permute-start = (bf16[64,128]{1,0:T(8,128)(2,1)}, bf16[64,128]{1,0:T(8,128)(2,1)S(1)}, u32[]{:S(2)}, u32[]{:S(2)}) collective-permute-start(bf16[64,128]{1,0:T(8,128)(2,1)} %get-tuple-element.14), channel_id=1, source_target_pairs={{0,0},{1,8},{2,1},{3,9},{4,2},{5,10},{6,3},{7,11},{8,4},{9,12},{10... | collective-permute-start | bytes 49160 | tf_op jit(solution)/shard_map/ppermute | solution.py:208
  9.7 4.5 %collective-permute-start.1 = (bf16[64,128]{1,0:T(8,128)(2,1)}, bf16[64,128]{1,0:T(8,128)(2,1)S(1)}, u32[]{:S(2)}, u32[]{:S(2)}) collective-permute-start(bf16[64,128]{1,0:T(8,128)(2,1)} %get-tuple-element.15), channel_id=1, source_target_pairs={{0,1},{1,9},{2,2},{3,10},{4,3},{5,11},{6,4},{7,12},{8,5},{9,13},{1... | collective-permute-start | bytes 49160 | tf_op jit(solution)/shard_map/ppermute | solution.py:208
  14.1 4.5 %collective-permute-start.2 = (bf16[64,128]{1,0:T(8,128)(2,1)}, bf16[64,128]{1,0:T(8,128)(2,1)S(1)}, u32[]{:S(2)}, u32[]{:S(2)}) collective-permute-start(bf16[64,128]{1,0:T(8,128)(2,1)} %get-tuple-element.16), channel_id=1, source_target_pairs={{0,2},{1,10},{2,3},{3,11},{4,4},{5,12},{6,5},{7,13},{8,6},{9,14},{... | collective-permute-start | bytes 49160 | tf_op jit(solution)/shard_map/ppermute | solution.py:208
  18.7 0.2 collective-permute-done.1.refs_1_
  18.8 2.5 %collective-permute-start.3 = (bf16[64,128]{1,0:T(8,128)(2,1)}, bf16[64,128]{1,0:T(8,128)(2,1)S(1)}, u32[]{:S(2)}, u32[]{:S(2)}) collective-permute-start(bf16[64,128]{1,0:T(8,128)(2,1)} %get-tuple-element.17), channel_id=1, source_target_pairs={{0,3},{1,11},{2,4},{3,12},{4,5},{5,13},{6,6},{7,14},{8,7},{9,15},{... | collective-permute-start | bytes 49160 | tf_op jit(solution)/shard_map/ppermute | solution.py:208
  21.3 0.5 collective-permute-done.2.refs_2_
  21.8 0.2 collective-permute-start.4
  21.9 4.7 %collective-permute-done.3.refs_3_ = bf16[64,128]{1,0:T(8,128)(2,1)S(1)} collective-permute-done((bf16[64,128]{1,0:T(8,128)(2,1)}, bf16[64,128]{1,0:T(8,128)(2,1)S(1)}, u32[]{:S(2)}, u32[]{:S(2)}) %collective-permute-start.3) | collective-permute-done | bytes 16416 | tf_op jit(solution)/shard_map/ppermute | solution.py:208
  26.6 0.4 collective-permute-start.11
  27.0 1.6 %collective-permute-start.12 = (bf16[256,128]{1,0:T(8,128)(2,1)S(1)}, bf16[256,128]{1,0:T(8,128)(2,1)S(1)}, u32[]{:S(2)}, u32[]{:S(2)}) collective-permute-start(bf16[256,128]{1,0:T(8,128)(2,1)S(1)} %collective-permute-done.10.refs_11_), channel_id=1, source_target_pairs={{2,0},{0,2},{6,4},{4,6},{10,8},{8,10},{14,12},{12,14},{3,1},{1,3},... | collective-permute-start | bytes 196616 | tf_op jit(solution)/shard_map/ppermute | solution.py:179
  28.6 0.4 collective-permute-start.13
  29.0 1.6 %collective-permute-start.14 = (bf16[256,128]{1,0:T(8,128)(2,1)S(1)}, bf16[256,128]{1,0:T(8,128)(2,1)S(1)}, u32[]{:S(2)}, u32[]{:S(2)}) collective-permute-start(bf16[256,128]{1,0:T(8,128)(2,1)S(1)} %collective-permute-done.8.refs_9_), channel_id=1, source_target_pairs={{2,0},{0,2},{6,4},{4,6},{10,8},{8,10},{14,12},{12,14},{3,1},{1,3},... | collective-permute-start | bytes 196616 | tf_op jit(solution)/shard_map/ppermute | solution.py:179
  30.7 1.9 %collective-permute-start.5 = (bf16[64,128]{1,0:T(8,128)(2,1)}, bf16[64,128]{1,0:T(8,128)(2,1)S(1)}, u32[]{:S(2)}, u32[]{:S(2)}) collective-permute-start(bf16[64,128]{1,0:T(8,128)(2,1)} %get-tuple-element.19), channel_id=1, source_target_pairs={{0,5},{1,13},{2,6},{3,14},{4,7},{5,15},{6,0},{7,8},{8,1},{9,9},{10... | collective-permute-start | bytes 49160 | tf_op jit(solution)/shard_map/ppermute | solution.py:208
  32.6 4.9 %collective-permute-done.5.refs_5_ = bf16[64,128]{1,0:T(8,128)(2,1)S(1)} collective-permute-done((bf16[64,128]{1,0:T(8,128)(2,1)}, bf16[64,128]{1,0:T(8,128)(2,1)S(1)}, u32[]{:S(2)}, u32[]{:S(2)}) %collective-permute-start.5) | collective-permute-done | bytes 16416 | tf_op jit(solution)/shard_map/ppermute | solution.py:208
  37.4 1.9 %collective-permute-start.6 = (bf16[64,128]{1,0:T(8,128)(2,1)}, bf16[64,128]{1,0:T(8,128)(2,1)S(1)}, u32[]{:S(2)}, u32[]{:S(2)}) collective-permute-start(bf16[64,128]{1,0:T(8,128)(2,1)} %get-tuple-element.20), channel_id=1, source_target_pairs={{0,6},{1,14},{2,7},{3,15},{4,0},{5,8},{6,1},{7,9},{8,2},{9,10},{10... | collective-permute-start | bytes 49160 | tf_op jit(solution)/shard_map/ppermute | solution.py:208
  39.4 3.9 %collective-permute-done.6.refs_6_ = bf16[64,128]{1,0:T(8,128)(2,1)S(1)} collective-permute-done((bf16[64,128]{1,0:T(8,128)(2,1)}, bf16[64,128]{1,0:T(8,128)(2,1)S(1)}, u32[]{:S(2)}, u32[]{:S(2)}) %collective-permute-start.6) | collective-permute-done | bytes 16416 | tf_op jit(solution)/shard_map/ppermute | solution.py:208
  43.3 2.0 %collective-permute-start.7 = (bf16[64,128]{1,0:T(8,128)(2,1)S(1)}, bf16[64,128]{1,0:T(8,128)(2,1)S(1)}, u32[]{:S(2)}, u32[]{:S(2)}) collective-permute-start(bf16[64,128]{1,0:T(8,128)(2,1)S(1)} %copy-done.3), channel_id=1, source_target_pairs={{0,7},{1,15},{2,0},{3,8},{4,1},{5,9},{6,2},{7,10},{8,3},{9,11},{10... | collective-permute-start | bytes 49160 | tf_op jit(solution)/shard_map/ppermute | solution.py:208
  45.3 3.9 %collective-permute-done.7.refs_7_ = bf16[64,128]{1,0:T(8,128)(2,1)S(1)} collective-permute-done((bf16[64,128]{1,0:T(8,128)(2,1)S(1)}, bf16[64,128]{1,0:T(8,128)(2,1)S(1)}, u32[]{:S(2)}, u32[]{:S(2)}) %collective-permute-start.7) | collective-permute-done | bytes 16416 | tf_op jit(solution)/shard_map/ppermute | solution.py:208
  49.3 0.0 copy-start.1
  49.3 0.8 %copy-done.1 = bf16[256,128]{1,0:T(8,128)(2,1)S(1)} copy-done((bf16[256,128]{1,0:T(8,128)(2,1)S(1)}, bf16[256,128]{1,0:T(8,128)(2,1)}, u32[]{:S(2)}) %copy-start.1) | copy-done | bytes 65560
  50.1 6.1 %pairs.1 = bf16[32,128,128]{2,1,0:T(8,128)(2,1)} custom-call(bf16[1024,128]{1,0:T(8,128)(2,1)S(1)} %copy-done, f32[1,128]{1,0:T(1,128)S(1)} %bitcast.7, bf16[64,128]{1,0:T(8,128)(2,1)S(1)} %collective-permute-done.refs_0_, bf16[64,128]{1,0:T(8,128)(2,1)S(1)} %collective-permute-done.1.refs_1_, bf16[64,128]{1,0:T(8,128)(2,1)S(1)} %collective-permute-done.2.refs_2_, ...), custom_call_target="tpu_custom_call" | custom-call | tf_op jit(solution)/shard_map/pairs/pallas_call | solution.py:148
  (16 shorter events, 0.0 us)
Async XLA Ops:
  0.0 49.2 %copy-start = (bf16[1024,128]{1,0:T(8,128)(2,1)S(1)}, bf16[1024,128]{1,0:T(8,128)(2,1)}, u32[]{:S(2)}) copy-start(bf16[1024,128]{1,0:T(8,128)(2,1)} %w_ref.1) | copy-start | bytes 786436
  2.6 40.7 %copy-start.3 = (bf16[64,128]{1,0:T(8,128)(2,1)S(1)}, bf16[64,128]{1,0:T(8,128)(2,1)}, u32[]{:S(2)}) copy-start(bf16[64,128]{1,0:T(8,128)(2,1)} %get-tuple-element.21) | copy-start | bytes 49156
  2.6 24.4 %collective-permute-start.10 = (bf16[256,128]{1,0:T(8,128)(2,1)}, bf16[256,128]{1,0:T(8,128)(2,1)S(1)}, u32[]{:S(2)}, u32[]{:S(2)}) collective-permute-start(bf16[256,128]{1,0:T(8,128)(2,1)} %get-tuple-element.22.refs_8_), channel_id=1, source_target_pairs={{4,0},{6,2},{0,4},{2,6},{12,8},{14,10},{8,12},{10,14},{5,1},{7,3},... | collective-permute-start | bytes 196616 | tf_op jit(solution)/shard_map/ppermute | solution.py:179
  5.7 22.9 %collective-permute-start.9 = (bf16[256,128]{1,0:T(8,128)(2,1)}, bf16[256,128]{1,0:T(8,128)(2,1)S(1)}, u32[]{:S(2)}, u32[]{:S(2)}) collective-permute-start(bf16[256,128]{1,0:T(8,128)(2,1)} %get-tuple-element.22.refs_8_), channel_id=1, source_target_pairs={{8,0},{10,2},{12,4},{14,6},{0,8},{2,10},{4,12},{6,14},{9,1},{11,3}... | collective-permute-start | bytes 196616 | tf_op jit(solution)/shard_map/ppermute | solution.py:179
  8.3 20.7 %collective-permute-start.8 = (bf16[256,128]{1,0:T(8,128)(2,1)}, bf16[256,128]{1,0:T(8,128)(2,1)S(1)}, u32[]{:S(2)}, u32[]{:S(2)}) collective-permute-start(bf16[256,128]{1,0:T(8,128)(2,1)} %get-tuple-element.22.refs_8_), channel_id=1, source_target_pairs={{12,0},{14,2},{8,4},{10,6},{4,8},{6,10},{0,12},{2,14},{13,1},{15,3... | collective-permute-start | bytes 196616 | tf_op jit(solution)/shard_map/ppermute | solution.py:179
  8.3 5.8 %collective-permute-start = (bf16[64,128]{1,0:T(8,128)(2,1)}, bf16[64,128]{1,0:T(8,128)(2,1)S(1)}, u32[]{:S(2)}, u32[]{:S(2)}) collective-permute-start(bf16[64,128]{1,0:T(8,128)(2,1)} %get-tuple-element.14), channel_id=1, source_target_pairs={{0,0},{1,8},{2,1},{3,9},{4,2},{5,10},{6,3},{7,11},{8,4},{9,12},{10... | collective-permute-start | bytes 49160 | tf_op jit(solution)/shard_map/ppermute | solution.py:208
  9.7 9.2 %collective-permute-start.1 = (bf16[64,128]{1,0:T(8,128)(2,1)}, bf16[64,128]{1,0:T(8,128)(2,1)S(1)}, u32[]{:S(2)}, u32[]{:S(2)}) collective-permute-start(bf16[64,128]{1,0:T(8,128)(2,1)} %get-tuple-element.15), channel_id=1, source_target_pairs={{0,1},{1,9},{2,2},{3,10},{4,3},{5,11},{6,4},{7,12},{8,5},{9,13},{1... | collective-permute-start | bytes 49160 | tf_op jit(solution)/shard_map/ppermute | solution.py:208
  14.1 7.6 %collective-permute-start.2 = (bf16[64,128]{1,0:T(8,128)(2,1)}, bf16[64,128]{1,0:T(8,128)(2,1)S(1)}, u32[]{:S(2)}, u32[]{:S(2)}) collective-permute-start(bf16[64,128]{1,0:T(8,128)(2,1)} %get-tuple-element.16), channel_id=1, source_target_pairs={{0,2},{1,10},{2,3},{3,11},{4,4},{5,12},{6,5},{7,13},{8,6},{9,14},{... | collective-permute-start | bytes 49160 | tf_op jit(solution)/shard_map/ppermute | solution.py:208
  18.8 7.8 %collective-permute-start.3 = (bf16[64,128]{1,0:T(8,128)(2,1)}, bf16[64,128]{1,0:T(8,128)(2,1)S(1)}, u32[]{:S(2)}, u32[]{:S(2)}) collective-permute-start(bf16[64,128]{1,0:T(8,128)(2,1)} %get-tuple-element.17), channel_id=1, source_target_pairs={{0,3},{1,11},{2,4},{3,12},{4,5},{5,13},{6,6},{7,14},{8,7},{9,15},{... | collective-permute-start | bytes 49160 | tf_op jit(solution)/shard_map/ppermute | solution.py:208
  21.8 8.9 %collective-permute-start.4 = (bf16[64,128]{1,0:T(8,128)(2,1)}, bf16[64,128]{1,0:T(8,128)(2,1)S(1)}, u32[]{:S(2)}, u32[]{:S(2)}) collective-permute-start(bf16[64,128]{1,0:T(8,128)(2,1)} %get-tuple-element.18), channel_id=1, source_target_pairs={{0,4},{1,12},{2,5},{3,13},{4,6},{5,14},{6,7},{7,15},{8,0},{9,8},{1... | collective-permute-start | bytes 49160 | tf_op jit(solution)/shard_map/ppermute | solution.py:208
  26.6 22.6 %collective-permute-start.11 = (bf16[256,128]{1,0:T(8,128)(2,1)}, bf16[256,128]{1,0:T(8,128)(2,1)S(1)}, u32[]{:S(2)}, u32[]{:S(2)}) collective-permute-start(bf16[256,128]{1,0:T(8,128)(2,1)} %get-tuple-element.22.refs_8_), channel_id=1, source_target_pairs={{2,0},{0,2},{6,4},{4,6},{10,8},{8,10},{14,12},{12,14},{3,1},{1,3},... | collective-permute-start | bytes 196616 | tf_op jit(solution)/shard_map/ppermute | solution.py:179
  27.0 22.2 %collective-permute-start.12 = (bf16[256,128]{1,0:T(8,128)(2,1)S(1)}, bf16[256,128]{1,0:T(8,128)(2,1)S(1)}, u32[]{:S(2)}, u32[]{:S(2)}) collective-permute-start(bf16[256,128]{1,0:T(8,128)(2,1)S(1)} %collective-permute-done.10.refs_11_), channel_id=1, source_target_pairs={{2,0},{0,2},{6,4},{4,6},{10,8},{8,10},{14,12},{12,14},{3,1},{1,3},... | collective-permute-start | bytes 196616 | tf_op jit(solution)/shard_map/ppermute | solution.py:179
  28.6 20.6 %collective-permute-start.13 = (bf16[256,128]{1,0:T(8,128)(2,1)S(1)}, bf16[256,128]{1,0:T(8,128)(2,1)S(1)}, u32[]{:S(2)}, u32[]{:S(2)}) collective-permute-start(bf16[256,128]{1,0:T(8,128)(2,1)S(1)} %collective-permute-done.9.refs_10_), channel_id=1, source_target_pairs={{2,0},{0,2},{6,4},{4,6},{10,8},{8,10},{14,12},{12,14},{3,1},{1,3},... | collective-permute-start | bytes 196616 | tf_op jit(solution)/shard_map/ppermute | solution.py:179
  29.0 20.2 %collective-permute-start.14 = (bf16[256,128]{1,0:T(8,128)(2,1)S(1)}, bf16[256,128]{1,0:T(8,128)(2,1)S(1)}, u32[]{:S(2)}, u32[]{:S(2)}) collective-permute-start(bf16[256,128]{1,0:T(8,128)(2,1)S(1)} %collective-permute-done.8.refs_9_), channel_id=1, source_target_pairs={{2,0},{0,2},{6,4},{4,6},{10,8},{8,10},{14,12},{12,14},{3,1},{1,3},... | collective-permute-start | bytes 196616 | tf_op jit(solution)/shard_map/ppermute | solution.py:179
  30.7 6.8 %collective-permute-start.5 = (bf16[64,128]{1,0:T(8,128)(2,1)}, bf16[64,128]{1,0:T(8,128)(2,1)S(1)}, u32[]{:S(2)}, u32[]{:S(2)}) collective-permute-start(bf16[64,128]{1,0:T(8,128)(2,1)} %get-tuple-element.19), channel_id=1, source_target_pairs={{0,5},{1,13},{2,6},{3,14},{4,7},{5,15},{6,0},{7,8},{8,1},{9,9},{10... | collective-permute-start | bytes 49160 | tf_op jit(solution)/shard_map/ppermute | solution.py:208
  37.4 5.8 %collective-permute-start.6 = (bf16[64,128]{1,0:T(8,128)(2,1)}, bf16[64,128]{1,0:T(8,128)(2,1)S(1)}, u32[]{:S(2)}, u32[]{:S(2)}) collective-permute-start(bf16[64,128]{1,0:T(8,128)(2,1)} %get-tuple-element.20), channel_id=1, source_target_pairs={{0,6},{1,14},{2,7},{3,15},{4,0},{5,8},{6,1},{7,9},{8,2},{9,10},{10... | collective-permute-start | bytes 49160 | tf_op jit(solution)/shard_map/ppermute | solution.py:208
  43.3 6.0 %copy-start.2 = (f32[128]{0:T(128)S(1)}, f32[128]{0:T(128)}, u32[]{:S(2)}) copy-start(f32[128]{0:T(128)} %param.17) | copy-start | bytes 1540
  43.3 5.9 %collective-permute-start.7 = (bf16[64,128]{1,0:T(8,128)(2,1)S(1)}, bf16[64,128]{1,0:T(8,128)(2,1)S(1)}, u32[]{:S(2)}, u32[]{:S(2)}) collective-permute-start(bf16[64,128]{1,0:T(8,128)(2,1)S(1)} %copy-done.3), channel_id=1, source_target_pairs={{0,7},{1,15},{2,0},{3,8},{4,1},{5,9},{6,2},{7,10},{8,3},{9,11},{10... | collective-permute-start | bytes 49160 | tf_op jit(solution)/shard_map/ppermute | solution.py:208
  49.3 0.8 %copy-start.1 = (bf16[256,128]{1,0:T(8,128)(2,1)S(1)}, bf16[256,128]{1,0:T(8,128)(2,1)}, u32[]{:S(2)}) copy-start(bf16[256,128]{1,0:T(8,128)(2,1)} %get-tuple-element.22.refs_8_) | copy-start | bytes 196612

commit v4 on v3

--- a/solution.py
+++ b/solution.py
@@ -10,9 +10,8 @@
 LANES = 128
 
 
-def features_kernel(scale, col_count, x_ref, gain_ref, bias_ref, wl_ref, bl_ref, wr_ref, br_ref,
-                    right_ref, *refs):
-    left_refs, (normed_ref, left_f32, right_f32) = refs[:-3], refs[-3:]
+def features_kernel(scale, x_ref, gain_ref, bias_ref, wl_ref, bl_ref, wr_ref, br_ref,
+                    left_ref, right_ref, normed_ref, left_f32, right_f32):
     seqs, width, channels = x_ref.shape
     c = wl_ref.shape[0]
     fold = LANES // c
@@ -42,33 +41,27 @@
     total = (total + jnp.concatenate([bl_ref[...]] * fold, axis=1)) * scale
     for s in range(seqs):
         left_f32[pl.ds(s, quarter, stride=seqs), :] = total[s * quarter:(s + 1) * quarter]
-    here = lax.axis_index("row")
-    for k, left_ref in enumerate(left_refs):
-        rows = left_ref.shape[0]
-        chip = lax.rem(here + k, len(left_refs)) // col_count
-        left_ref[...] = left_f32[pl.ds(pl.multiple_of(chip * rows, rows), rows), :].astype(jnp.bfloat16)
+    left = left_f32[...].astype(jnp.bfloat16)
+    for copy in range(left_ref.shape[0]):
+        left_ref[copy] = left
     right_ref[...] = right_f32[...].astype(jnp.bfloat16)
 
 
-def features(alignment, ln_gain, ln_bias, w_left, b_left, w_right, b_right, row_count, col_count):
+def features(alignment, ln_gain, ln_bias, w_left, b_left, w_right, b_right, row_count, copies):
     seqs, width, channels = alignment.shape
     c = w_left.shape[1]
     rows = seqs * width * c // LANES
     whole = [pl.BlockSpec(shape, lambda i, n=len(shape): (0,) * n)
              for shape in (alignment.shape, (1, channels), (1, channels), (c, channels), (1, c),
                            (c, channels), (1, c))]
-    part = rows * col_count // row_count
-
-    def side(n):
-        return pl.BlockSpec((n, LANES), lambda i: (0, 0))
-
     return pl.pallas_call(
-        functools.partial(features_kernel, 1.0 / (seqs * row_count), col_count),
+        functools.partial(features_kernel, 1.0 / (seqs * row_count)),
         grid=(1,),
-        out_shape=[jax.ShapeDtypeStruct((rows, LANES), jnp.bfloat16)]
-        + [jax.ShapeDtypeStruct((part, LANES), jnp.bfloat16)] * row_count,
+        out_shape=(jax.ShapeDtypeStruct((copies, rows, LANES), jnp.bfloat16),
+                   jax.ShapeDtypeStruct((rows, LANES), jnp.bfloat16)),
         in_specs=whole,
-        out_specs=[side(rows)] + [side(part)] * row_count,
+        out_specs=(pl.BlockSpec((copies, rows, LANES), lambda i: (0, 0, 0)),
+                   pl.BlockSpec((rows, LANES), lambda i: (0, 0))),
         scratch_shapes=[pltpu.VMEM((channels // LANES, seqs * width, LANES), jnp.float32),
                         pltpu.VMEM((rows, LANES), jnp.float32),
                         pltpu.VMEM((rows, LANES), jnp.float32)],
@@ -90,9 +83,9 @@
         [flat[pl.ds(n * seqs + s, sources, stride=inner * seqs), :] for s in range(seqs)], axis=0)
 
 
-def pair_kernel(seqs, c, rows_step, col_count, steps, w_ref, bias_ref, *refs):
+def pair_kernel(seqs, c, rows_step, col_count, steps, w_ref, bias_ref, mine_ref, other_ref, *refs):
     sources = len(steps)
-    left_refs, right_refs, refs = refs[:sources], refs[sources:2 * sources], refs[2 * sources:]
+    right_refs, refs = refs[:sources], refs[sources:]
     out_ref, left_f32, right_f32, left_t, right_b, w_f32, w_t, outer_ref = refs
     rows, width, z = out_ref.shape[0], out_ref.shape[1], out_ref.shape[2]
     left_rows = left_f32.shape[1]
@@ -102,10 +95,10 @@
     @pl.when(step == 0)
     def _():
         here, core = lax.axis_index("row"), lax.axis_index("col")
-        place = lax.rem(here, sources // col_count) * col_count + core
-        left_of = by_sequence(lambda k: left_refs[k][...].astype(jnp.float32),
-                              lambda k: lax.rem(place - k + sources, sources),
-                              left_f32, left_rows // seqs, seqs)
+        mine = here // (sources // col_count) == core
+        left_of = by_sequence(
+            lambda n: jnp.where(mine, mine_ref[n].astype(jnp.float32), other_ref[n].astype(jnp.float32)),
+            lambda n: n, left_f32, left_rows // seqs, seqs)
         for k in range(left_rows // seqs):
             left_t[k * LANES:(k + 1) * LANES] = left_of(k).T.astype(jnp.bfloat16)
         for b in range(blocks):
@@ -138,7 +131,7 @@
 
 
 def pairs(lefts, rights, w_out, b_out, seqs, c, width, col_count):
-    sources, left_rows = len(lefts), lefts[0].shape[0]
+    sources, left_rows, _ = lefts[0].shape
     z = w_out.shape[1]
     rows = left_rows * LANES // (c * seqs)
     rows_step = 8
@@ -184,8 +177,8 @@
     c = w_left.shape[1]
     row_count = lax.axis_size("row")
     col_count = lax.axis_size("col")
-    right, *lefts = features(alignment, ln_gain, ln_bias, w_left, b_left, w_right, b_right,
-                             row_count, col_count)
+    left, right = features(alignment, ln_gain, ln_bias, w_left, b_left, w_right, b_right,
+                           row_count, col_count)
 
     across = pair_width(row_count)
     along = row_count // across
@@ -196,17 +189,10 @@
         for a in range(along):
             rights[a, 1] = fetch(rights[a, 0], (0, 1), row_count)
 
-    chips = row_count // col_count
-    received = []
-    for k, left in enumerate(lefts):
-        moves = []
-        for r in range(row_count):
-            for core in range(col_count):
-                place = (r + k) % row_count
-                to = (core * chips + place // col_count) * col_count + place % col_count
-                moves.append((r * col_count + core, to))
-        received.append(lax.ppermute(left, ("row", "col"), moves))
-    return pairs(received, rights, w_out, b_out, seqs, c, width, col_count)
+    left = left.reshape(row_count, -1, LANES)
+    mine = lax.all_to_all(left, "row", split_axis=0, concat_axis=0, tiled=True)
+    other = lax.ppermute(mine, "col", [(i, (i + 1) % col_count) for i in range(col_count)])
+    return pairs((mine, other), rights, w_out, b_out, seqs, c, width, col_count)
 
 
 def solution(mesh):

time: 56.8 us -> 34.4 us (0.61)
  starting transfers between devices: 28.6 us -> 15.9 us
  waiting for transfers between devices: 18 us -> 8.69 us
    ppermute x8 -> x1, starting transfers between devices: 18.9 us -> 0.01 us  [on_device(): lax.ppermute(mine, 'col', [(i, (i + 1) % col_count) for i in range(col_co...]
    ppermute x8 -> x1, waiting for transfers between devices: 17.9 us -> 0.01 us  [on_device(): lax.ppermute(mine, 'col', [(i, (i + 1) % col_count) for i in range(col_co...]
    all_to_all x0 -> x1, starting transfers between devices: none -> 7.41 us  [on_device(): mine = lax.all_to_all(left, 'row', split_axis=0, concat_axis=0, tiled=True)]
    ppermute x7, waiting for transfers between devices: 0.02 us -> 4.87 us  [fetch(): lax.ppermute(array, 'row', [(source_at(r, step, count), r) for r in range...]
    all_to_all x0 -> x1, waiting for transfers between devices: none -> 3.81 us  [on_device(): mine = lax.all_to_all(left, 'row', split_axis=0, concat_axis=0, tiled=True)]
    ppermute x7, starting transfers between devices: 9.74 us -> 8.51 us  [fetch(): lax.ppermute(array, 'row', [(source_at(r, step, count), r) for r in range...]
  transfers between devices with their start and end apart: 15 -> 9, of which waited for: 6 -> 5; matrix products, arithmetic and copies ran while one was open for 0% -> 0% of each run, Pallas kernels for 0% -> 0%
where the time goes in v4:
time: 34.4 us; the launch traced here: 34.1 us
  starting transfers between devices  15.9 us (46%)
  waiting for transfers between devices  8.69 us (25%)
  Pallas kernels  8.64 us (25%)
  local copies, waits for them, and re-layouts  0.84 us (2%)
    ppermute x7, starting transfers between devices, fetch(): lax.ppermute(array, 'row', [(source_at(r, step, count), r) for r in range...  8.51 us
    all_to_all x1, starting transfers between devices, on_device(): mine = lax.all_to_all(left, 'row', split_axis=0, concat_axis=0, tiled=True)  7.41 us
    pallas_call x1, Pallas kernels, pairs(): pl.pallas_call(functools.partial(pair_kernel, seqs, c, rows_step, col_cou...  6.1 us
    ppermute x7, waiting for transfers between devices, fetch(): lax.ppermute(array, 'row', [(source_at(r, step, count), r) for r in range...  4.87 us
    all_to_all x1, waiting for transfers between devices, on_device(): mine = lax.all_to_all(left, 'row', split_axis=0, concat_axis=0, tiled=True)  3.81 us
    pallas_call x1, Pallas kernels, features(): pl.pallas_call(functools.partial(features_kernel, 1.0 / (seqs * row_count...  2.54 us
    unnamed x6, local copies, waits for them, and re-layouts  0.84 us
  transfers between devices with their start and end apart: 9, of which 5 were waited for; matrix products, arithmetic and copies ran while one was open for 0% of the time, Pallas kernels for 0%

profile of v4, /device:TPU:0, one launch (start us, length us, event | category | flops | bytes accessed | tf_op | source)
XLA Modules:
  0.0 34.1 jit_solution(16562900218681766629)
XLA Ops:
  0.0 2.5 %features.1 = (bf16[2,256,128]{2,1,0:T(8,128)(2,1)}, bf16[256,128]{1,0:T(8,128)(2,1)}) custom-call(bf16[8,128,256]{2,1,0:T(8,128)(2,1)} %x_ref.1, f32[1,256]{1,0:T(1,128)} %bitcast.12, f32[1,256]{1,0:T(1,128)} %bitcast.13, bf16[32,256]{1,0:T(8,128)(2,1)} %bitcast.10, f32[1,32]{1,0:T(1,128)} %bitcast.14, bf16[32,256]{1,0:T(8,128)(2,1)} %bitcast.11, ...), custom_call_target="tpu_custom_call" | custom-call | tf_op jit(solution)/shard_map/features/pallas_call | solution.py:57
  2.5 7.4 %all-to-all-start = ((bf16[8,64,128]{2,1,0:T(8,128)(2,1)}), bf16[8,64,128]{2,1,0:T(8,128)(2,1)S(1)}, u32[]{:S(2)}, u32[]{:S(2)}) async-start(bf16[8,64,128]{2,1,0:T(8,128)(2,1)} %bitcast.9), calls=%async_computation | async-start | bytes 262144 | tf_op jit(solution)/shard_map/all_to_all | solution.py:193
  10.0 2.0 %collective-permute-start.3 = (bf16[256,128]{1,0:T(8,128)(2,1)}, bf16[256,128]{1,0:T(8,128)(2,1)S(1)}, u32[]{:S(2)}, u32[]{:S(2)}) collective-permute-start(bf16[256,128]{1,0:T(8,128)(2,1)} %get-tuple-element.8.refs_0_), channel_id=1, source_target_pairs={{4,0},{6,2},{0,4},{2,6},{12,8},{14,10},{8,12},{10,14},{5,1},{7,3},... | collective-permute-start | bytes 196616 | tf_op jit(solution)/shard_map/ppermute | solution.py:172
  12.0 2.4 %collective-permute-start.2 = (bf16[256,128]{1,0:T(8,128)(2,1)}, bf16[256,128]{1,0:T(8,128)(2,1)S(1)}, u32[]{:S(2)}, u32[]{:S(2)}) collective-permute-start(bf16[256,128]{1,0:T(8,128)(2,1)} %get-tuple-element.8.refs_0_), channel_id=1, source_target_pairs={{8,0},{10,2},{12,4},{14,6},{0,8},{2,10},{4,12},{6,14},{9,1},{11,3}... | collective-permute-start | bytes 196616 | tf_op jit(solution)/shard_map/ppermute | solution.py:172
  14.3 0.1 collective-permute-start.1
  14.4 3.8 %all-to-all-done.mine_ref = bf16[8,64,128]{2,1,0:T(8,128)(2,1)S(1)} async-done(((bf16[8,64,128]{2,1,0:T(8,128)(2,1)}), bf16[8,64,128]{2,1,0:T(8,128)(2,1)S(1)}, u32[]{:S(2)}, u32[]{:S(2)}) %all-to-all-start) | async-done | bytes 131104 | tf_op jit(solution)/shard_map/all_to_all | solution.py:193
  18.2 0.0 collective-permute-start
  18.2 1.0 %collective-permute-start.4 = (bf16[256,128]{1,0:T(8,128)(2,1)}, bf16[256,128]{1,0:T(8,128)(2,1)S(1)}, u32[]{:S(2)}, u32[]{:S(2)}) collective-permute-start(bf16[256,128]{1,0:T(8,128)(2,1)} %get-tuple-element.8.refs_0_), channel_id=1, source_target_pairs={{2,0},{0,2},{6,4},{4,6},{10,8},{8,10},{14,12},{12,14},{3,1},{1,3},... | collective-permute-start | bytes 196616 | tf_op jit(solution)/shard_map/ppermute | solution.py:172
  19.2 0.0 collective-permute-done.3.refs_3_
  19.2 1.0 %collective-permute-start.5 = (bf16[256,128]{1,0:T(8,128)(2,1)S(1)}, bf16[256,128]{1,0:T(8,128)(2,1)S(1)}, u32[]{:S(2)}, u32[]{:S(2)}) collective-permute-start(bf16[256,128]{1,0:T(8,128)(2,1)S(1)} %collective-permute-done.3.refs_3_), channel_id=1, source_target_pairs={{2,0},{0,2},{6,4},{4,6},{10,8},{8,10},{14,12},{12,14},{3,1},{1,3},... | collective-permute-start | bytes 196616 | tf_op jit(solution)/shard_map/ppermute | solution.py:172
  20.3 1.2 %collective-permute-done.2.refs_2_ = bf16[256,128]{1,0:T(8,128)(2,1)S(1)} collective-permute-done((bf16[256,128]{1,0:T(8,128)(2,1)}, bf16[256,128]{1,0:T(8,128)(2,1)S(1)}, u32[]{:S(2)}, u32[]{:S(2)}) %collective-permute-start.2) | collective-permute-done | bytes 65568 | tf_op jit(solution)/shard_map/ppermute | solution.py:172
  21.4 1.3 %collective-permute-start.6 = (bf16[256,128]{1,0:T(8,128)(2,1)S(1)}, bf16[256,128]{1,0:T(8,128)(2,1)S(1)}, u32[]{:S(2)}, u32[]{:S(2)}) collective-permute-start(bf16[256,128]{1,0:T(8,128)(2,1)S(1)} %collective-permute-done.2.refs_2_), channel_id=1, source_target_pairs={{2,0},{0,2},{6,4},{4,6},{10,8},{8,10},{14,12},{12,14},{3,1},{1,3},... | collective-permute-start | bytes 196616 | tf_op jit(solution)/shard_map/ppermute | solution.py:172
  22.7 0.0 collective-permute-done.1.refs_1_
  22.7 0.7 %collective-permute-start.7 = (bf16[256,128]{1,0:T(8,128)(2,1)S(1)}, bf16[256,128]{1,0:T(8,128)(2,1)S(1)}, u32[]{:S(2)}, u32[]{:S(2)}) collective-permute-start(bf16[256,128]{1,0:T(8,128)(2,1)S(1)} %collective-permute-done.1.refs_1_), channel_id=1, source_target_pairs={{2,0},{0,2},{6,4},{4,6},{10,8},{8,10},{14,12},{12,14},{3,1},{1,3},... | collective-permute-start | bytes 196616 | tf_op jit(solution)/shard_map/ppermute | solution.py:172
  23.5 0.0 collective-permute-done.4.refs_4_
  23.5 1.3 %collective-permute-done.5.refs_5_ = bf16[256,128]{1,0:T(8,128)(2,1)S(1)} collective-permute-done((bf16[256,128]{1,0:T(8,128)(2,1)S(1)}, bf16[256,128]{1,0:T(8,128)(2,1)S(1)}, u32[]{:S(2)}, u32[]{:S(2)}) %collective-permute-start.5) | collective-permute-done | bytes 65568 | tf_op jit(solution)/shard_map/ppermute | solution.py:172
  24.7 1.7 %collective-permute-done.6.refs_6_ = bf16[256,128]{1,0:T(8,128)(2,1)S(1)} collective-permute-done((bf16[256,128]{1,0:T(8,128)(2,1)S(1)}, bf16[256,128]{1,0:T(8,128)(2,1)S(1)}, u32[]{:S(2)}, u32[]{:S(2)}) %collective-permute-start.6) | collective-permute-done | bytes 65568 | tf_op jit(solution)/shard_map/ppermute | solution.py:172
  26.5 0.7 %collective-permute-done.7.refs_7_ = bf16[256,128]{1,0:T(8,128)(2,1)S(1)} collective-permute-done((bf16[256,128]{1,0:T(8,128)(2,1)S(1)}, bf16[256,128]{1,0:T(8,128)(2,1)S(1)}, u32[]{:S(2)}, u32[]{:S(2)}) %collective-permute-start.7) | collective-permute-done | bytes 65568 | tf_op jit(solution)/shard_map/ppermute | solution.py:172
  27.2 0.0 collective-permute-done.other_ref
  27.2 0.0 copy-done
  27.2 0.0 copy-done.2
  27.2 0.0 copy-start.1
  27.2 0.8 %copy-done.1 = bf16[256,128]{1,0:T(8,128)(2,1)S(1)} copy-done((bf16[256,128]{1,0:T(8,128)(2,1)S(1)}, bf16[256,128]{1,0:T(8,128)(2,1)}, u32[]{:S(2)}) %copy-start.1) | copy-done | bytes 65560
  28.0 6.1 %pairs.1 = bf16[32,128,128]{2,1,0:T(8,128)(2,1)} custom-call(bf16[1024,128]{1,0:T(8,128)(2,1)S(1)} %copy-done, f32[1,128]{1,0:T(1,128)S(1)} %bitcast.8, bf16[8,64,128]{2,1,0:T(8,128)(2,1)S(1)} %all-to-all-done.mine_ref, bf16[8,64,128]{2,1,0:T(8,128)(2,1)S(1)} %collective-permute-done.other_ref, bf16[256,128]{1,0:T(8,128)(2,1)S(1)} %copy-done.1, ...), custom_call_target="tpu_custom_call" | custom-call | tf_op jit(solution)/shard_map/pairs/pallas_call | solution.py:141
  (2 shorter events, 0.0 us)
Async XLA Ops:
  2.5 24.6 %copy-start = (bf16[1024,128]{1,0:T(8,128)(2,1)S(1)}, bf16[1024,128]{1,0:T(8,128)(2,1)}, u32[]{:S(2)}) copy-start(bf16[1024,128]{1,0:T(8,128)(2,1)} %w_ref.1) | copy-start | bytes 786436
  2.5 15.7 %all-to-all-start = ((bf16[8,64,128]{2,1,0:T(8,128)(2,1)}), bf16[8,64,128]{2,1,0:T(8,128)(2,1)S(1)}, u32[]{:S(2)}, u32[]{:S(2)}) async-start(bf16[8,64,128]{2,1,0:T(8,128)(2,1)} %bitcast.9), calls=%async_computation | async-start | bytes 262144 | tf_op jit(solution)/shard_map/all_to_all | solution.py:193
  10.0 17.2 %copy-start.2 = (f32[128]{0:T(128)S(1)}, f32[128]{0:T(128)}, u32[]{:S(2)}) copy-start(f32[128]{0:T(128)} %param.17) | copy-start | bytes 1540
  10.0 9.3 %collective-permute-start.3 = (bf16[256,128]{1,0:T(8,128)(2,1)}, bf16[256,128]{1,0:T(8,128)(2,1)S(1)}, u32[]{:S(2)}, u32[]{:S(2)}) collective-permute-start(bf16[256,128]{1,0:T(8,128)(2,1)} %get-tuple-element.8.refs_0_), channel_id=1, source_target_pairs={{4,0},{6,2},{0,4},{2,6},{12,8},{14,10},{8,12},{10,14},{5,1},{7,3},... | collective-permute-start | bytes 196616 | tf_op jit(solution)/shard_map/ppermute | solution.py:172
  12.0 9.4 %collective-permute-start.2 = (bf16[256,128]{1,0:T(8,128)(2,1)}, bf16[256,128]{1,0:T(8,128)(2,1)S(1)}, u32[]{:S(2)}, u32[]{:S(2)}) collective-permute-start(bf16[256,128]{1,0:T(8,128)(2,1)} %get-tuple-element.8.refs_0_), channel_id=1, source_target_pairs={{8,0},{10,2},{12,4},{14,6},{0,8},{2,10},{4,12},{6,14},{9,1},{11,3}... | collective-permute-start | bytes 196616 | tf_op jit(solution)/shard_map/ppermute | solution.py:172
  14.3 8.4 %collective-permute-start.1 = (bf16[256,128]{1,0:T(8,128)(2,1)}, bf16[256,128]{1,0:T(8,128)(2,1)S(1)}, u32[]{:S(2)}, u32[]{:S(2)}) collective-permute-start(bf16[256,128]{1,0:T(8,128)(2,1)} %get-tuple-element.8.refs_0_), channel_id=1, source_target_pairs={{12,0},{14,2},{8,4},{10,6},{4,8},{6,10},{0,12},{2,14},{13,1},{15,3... | collective-permute-start | bytes 196616 | tf_op jit(solution)/shard_map/ppermute | solution.py:172
  18.2 8.9 %collective-permute-start = (bf16[8,64,128]{2,1,0:T(8,128)(2,1)S(1)}, bf16[8,64,128]{2,1,0:T(8,128)(2,1)S(1)}, u32[]{:S(2)}, u32[]{:S(2)}) collective-permute-start(bf16[8,64,128]{2,1,0:T(8,128)(2,1)S(1)} %all-to-all-done.mine_ref), channel_id=1, source_target_pairs={{0,1},{1,0},{2,3},{3,2},{4,5},{5,4},{6,7},{7,6},{8,9},{9,8},{10,11... | collective-permute-start | bytes 393224 | tf_op jit(solution)/shard_map/ppermute | solution.py:194
  18.2 5.2 %collective-permute-start.4 = (bf16[256,128]{1,0:T(8,128)(2,1)}, bf16[256,128]{1,0:T(8,128)(2,1)S(1)}, u32[]{:S(2)}, u32[]{:S(2)}) collective-permute-start(bf16[256,128]{1,0:T(8,128)(2,1)} %get-tuple-element.8.refs_0_), channel_id=1, source_target_pairs={{2,0},{0,2},{6,4},{4,6},{10,8},{8,10},{14,12},{12,14},{3,1},{1,3},... | collective-permute-start | bytes 196616 | tf_op jit(solution)/shard_map/ppermute | solution.py:172
  19.2 5.5 %collective-permute-start.5 = (bf16[256,128]{1,0:T(8,128)(2,1)S(1)}, bf16[256,128]{1,0:T(8,128)(2,1)S(1)}, u32[]{:S(2)}, u32[]{:S(2)}) collective-permute-start(bf16[256,128]{1,0:T(8,128)(2,1)S(1)} %collective-permute-done.3.refs_3_), channel_id=1, source_target_pairs={{2,0},{0,2},{6,4},{4,6},{10,8},{8,10},{14,12},{12,14},{3,1},{1,3},... | collective-permute-start | bytes 196616 | tf_op jit(solution)/shard_map/ppermute | solution.py:172
  21.4 5.0 %collective-permute-start.6 = (bf16[256,128]{1,0:T(8,128)(2,1)S(1)}, bf16[256,128]{1,0:T(8,128)(2,1)S(1)}, u32[]{:S(2)}, u32[]{:S(2)}) collective-permute-start(bf16[256,128]{1,0:T(8,128)(2,1)S(1)} %collective-permute-done.2.refs_2_), channel_id=1, source_target_pairs={{2,0},{0,2},{6,4},{4,6},{10,8},{8,10},{14,12},{12,14},{3,1},{1,3},... | collective-permute-start | bytes 196616 | tf_op jit(solution)/shard_map/ppermute | solution.py:172
  22.7 4.4 %collective-permute-start.7 = (bf16[256,128]{1,0:T(8,128)(2,1)S(1)}, bf16[256,128]{1,0:T(8,128)(2,1)S(1)}, u32[]{:S(2)}, u32[]{:S(2)}) collective-permute-start(bf16[256,128]{1,0:T(8,128)(2,1)S(1)} %collective-permute-done.1.refs_1_), channel_id=1, source_target_pairs={{2,0},{0,2},{6,4},{4,6},{10,8},{8,10},{14,12},{12,14},{3,1},{1,3},... | collective-permute-start | bytes 196616 | tf_op jit(solution)/shard_map/ppermute | solution.py:172
  27.2 0.8 %copy-start.1 = (bf16[256,128]{1,0:T(8,128)(2,1)S(1)}, bf16[256,128]{1,0:T(8,128)(2,1)}, u32[]{:S(2)}) copy-start(bf16[256,128]{1,0:T(8,128)(2,1)} %get-tuple-element.8.refs_0_) | copy-start | bytes 196612

commit v5 on v1

v5 whole, which is shorter than its diff:
```python
import functools

import jax
import jax.numpy as jnp
from jax import lax
from jax.experimental import pallas as pl
from jax.experimental.pallas import tpu as pltpu
from jax.sharding import PartitionSpec as P

LANES = 128
HALVES = 2
VMEM_LIMIT = 60 * 1024 * 1024


def whole(shape):
    return pl.BlockSpec(shape, lambda i: (0,) * len(shape))


def features_kernel(scale, x_ref, gain_ref, bias_ref, wl_ref, bl_ref, wr_ref, br_ref,
                    left_ref, right_ref, normed_ref, left_f32, right_f32):
    seqs, width, channels = x_ref.shape
    c = wl_ref.shape[0]
    part = c // HALVES
    blocks = width // LANES
    fold = LANES // c
    quarter = width // fold
    right_bias = jnp.broadcast_to(br_ref[...], (LANES, c)).T[:, :1]
    for s in range(seqs):
        values = x_ref[s].astype(jnp.float32)
        average = jnp.mean(values, axis=-1, keepdims=True)
        centred = values - average
        variance = jnp.mean(centred * centred, axis=-1, keepdims=True)
        normed = centred * lax.rsqrt(variance + 1e-05) * gain_ref[...] + bias_ref[...]
        for h in range(channels // LANES):
            normed_ref[h, s * width:(s + 1) * width] = normed[:, h * LANES:(h + 1) * LANES]
        right = lax.dot_general(wr_ref[...], normed.astype(jnp.bfloat16), (((1,), (1,)), ((), ())),
                                preferred_element_type=jnp.float32) + right_bias
        for h in range(HALVES):
            for b in range(blocks):
                right_f32[pl.ds((h * blocks + b) * part * seqs + s, part, stride=seqs), :] = (
                    right[h * part:(h + 1) * part, b * LANES:(b + 1) * LANES])
    total = None
    for q in range(fold):
        rows = jnp.concatenate(
            [normed_ref[h, pl.ds(q, seqs * quarter, stride=fold), :] for h in range(channels // LANES)], axis=1
        ).astype(jnp.bfloat16)
        zeros = [jnp.zeros((c, channels), jnp.bfloat16)]
        w = jnp.concatenate(zeros * q + [wl_ref[...]] + zeros * (fold - 1 - q), axis=0)
        term = lax.dot_general(rows, w, (((1,), (1,)), ((), ())), preferred_element_type=jnp.float32)
        total = term if total is None else total + term
    total = (total + jnp.concatenate([bl_ref[...]] * fold, axis=1)) * scale
    for s in range(seqs):
        left_f32[pl.ds(s, quarter, stride=seqs), :] = total[s * quarter:(s + 1) * quarter]
    left_ref[...] = left_f32[...].astype(jnp.bfloat16)
    right_ref[...] = right_f32[...].astype(jnp.bfloat16)


def features(alignment, ln_gain, ln_bias, w_left, b_left, w_right, b_right, scale):
    seqs, width, channels = alignment.shape
    c = w_left.shape[1]
    rows = seqs * width * c // LANES
    operands = (alignment, ln_gain.reshape(1, -1), ln_bias.reshape(1, -1), w_left.T, b_left.reshape(1, -1),
                w_right.T, b_right.reshape(1, -1))
    return pl.pallas_call(
        functools.partial(features_kernel, scale),
        grid=(1,),
        out_shape=(jax.ShapeDtypeStruct((rows, LANES), jnp.bfloat16),) * 2,
        in_specs=[whole(a.shape) for a in operands],
        out_specs=(whole((rows, LANES)),) * 2,
        scratch_shapes=[pltpu.VMEM((channels // LANES, seqs * width, LANES), jnp.float32),
                        pltpu.VMEM((rows, LANES), jnp.float32),
                        pltpu.VMEM((rows, LANES), jnp.float32)],
        compiler_params=pltpu.CompilerParams(vmem_limit_bytes=VMEM_LIMIT),
        name="features",
    )(*operands)


def repeat_kernel(left_ref, after_ref, out_ref):
    for copy in range(out_ref.shape[0]):
        out_ref[copy] = left_ref[...]


def repeat_after(left, after, copies):
    return pl.pallas_call(
        repeat_kernel,
        grid=(1,),
        out_shape=jax.ShapeDtypeStruct((copies,) + left.shape, left.dtype),
        in_specs=[whole(left.shape), pl.BlockSpec(memory_space=pl.ANY)],
        out_specs=whole((copies,) + left.shape),
        compiler_params=pltpu.CompilerParams(vmem_limit_bytes=VMEM_LIMIT),
        name="repeat",
    )(left, after)


def sequence_rows(block, f32_ref, inner, seqs):
    sources = f32_ref.shape[0]
    for n in range(sources):
        f32_ref[n] = block(n)
    if seqs % 8 == 0:
        return lambda m: jnp.concatenate(
            [f32_ref[n, m * seqs:(m + 1) * seqs] for n in range(sources)], axis=0)
    flat = f32_ref.reshape(sources * inner * seqs, LANES)
    return lambda m: jnp.concatenate(
        [flat[pl.ds(m * seqs + s, sources, stride=inner * seqs), :] for s in range(seqs)], axis=0)


def prepare_kernel(seqs, c, col_count, steps, mine_ref, other_ref, w_ref, left_ref, weights_ref,
                   left_f32, w_f32):
    sources, left_rows, _ = mine_ref.shape
    here, core = lax.axis_index("row"), lax.axis_index("col")
    mine = here // (sources // col_count) == core

    def block(n):
        source = source_at(here, steps[n], sources)
        return jnp.where(mine, mine_ref[source].astype(jnp.float32), other_ref[source].astype(jnp.float32))

    left_of = sequence_rows(block, left_f32, left_rows // seqs, seqs)
    for k in range(left_rows // seqs):
        left_ref[k * LANES:(k + 1) * LANES] = left_of(k).T.astype(jnp.bfloat16)
    w_f32[...] = w_ref[...].astype(jnp.float32)
    for e in range(c):
        weights_ref[:, e * c:(e + 1) * c] = w_f32[pl.ds(e, c, stride=c), :].T.astype(jnp.bfloat16)


def prepare(mine, other, w_out, steps, seqs, c, col_count):
    sources, left_rows, _ = mine.shape
    shapes = ((left_rows // seqs * LANES, sources * seqs), (w_out.shape[1], w_out.shape[0]))
    operands = (mine, other, w_out)
    return pl.pallas_call(
        functools.partial(prepare_kernel, seqs, c, col_count, steps),
        grid=(1,),
        out_shape=[jax.ShapeDtypeStruct(shape, jnp.bfloat16) for shape in shapes],
        in_specs=[whole(a.shape) for a in operands],
        out_specs=[whole(shape) for shape in shapes],
        scratch_shapes=[pltpu.VMEM(mine.shape, jnp.float32), pltpu.VMEM(w_out.shape, jnp.float32)],
        name="prepare",
    )(*operands)


def pair_kernel(seqs, c, first, last, left_ref, weights_ref, near_ref, far_ref, *refs):
    if not first:
        so_far_ref, refs = refs[0], refs[1:]
    if last:
        bias_ref, refs = refs[0], refs[1:]
    out_ref, right_f32, right_b, outer_ref = refs
    rows_step = out_ref.shape[0]
    along = near_ref.shape[0]
    part = right_f32.shape[1] // seqs
    blocks = right_b.shape[1] // LANES // part

    @pl.when(pl.program_id(0) == 0)
    def _():
        for b in range(blocks):
            at = b * part * seqs
            right_of = sequence_rows(
                lambda n: (near_ref if n < along else far_ref)[n % along, at:at + part * seqs].astype(jnp.float32),
                right_f32, part, seqs)
            for e in range(part):
                lanes = (b * part + e) * LANES
                right_b[:, lanes:lanes + LANES] = right_of(e).astype(jnp.bfloat16)

    for b in range(blocks):
        for e in range(0, part, 2):
            at = (b * part + e) * LANES
            outer = jnp.dot(left_ref[...], right_b[:, at:at + 2 * LANES], preferred_element_type=jnp.float32)
            outer = outer.astype(jnp.bfloat16)
            for half in range(2):
                for i in range(rows_step):
                    outer_ref[i // 2, (e + half) * c:(e + half + 1) * c,
                              (i % 2) * LANES:(i % 2 + 1) * LANES] = (
                        outer[i * c:(i + 1) * c, half * LANES:(half + 1) * LANES])
        for p in range(rows_step // 2):
            update = jnp.dot(weights_ref[...], outer_ref[p], preferred_element_type=jnp.float32)
            for half in range(2):
                mine = update[:, half * LANES:(half + 1) * LANES]
                i = 2 * p + half
                if not first:
                    mine = mine + so_far_ref[i, b]
                if last:
                    out_ref[i, b * LANES:(b + 1) * LANES, :] = (mine.T + bias_ref[...]).astype(out_ref.dtype)
                else:
                    out_ref[i, b] = mine


def pairs(half, left, weights, near, far, so_far, bias, seqs, c, width):
    along = near.shape[0]
    sources = 2 * along
    z = weights.shape[0]
    part = c // HALVES
    blocks = width // LANES
    rows = left.shape[0] // c
    rows_step = 8
    total = sources * seqs
    first, last = so_far is None, bias is not None
    sums = pl.BlockSpec((rows_step, blocks, z, LANES), lambda i: (i, 0, 0, 0))
    operands = [left, weights, near, far]
    in_specs = [pl.BlockSpec((rows_step * c, total), lambda i: (i, 0)),
                pl.BlockSpec((z, part * c), lambda i: (0, half)), whole(near.shape), whole(far.shape)]
    if not first:
        operands.append(so_far)
        in_specs.append(sums)
    if last:
        operands.append(bias.reshape(1, -1))
        in_specs.append(whole((1, z)))
    if last:
        out_shape = jax.ShapeDtypeStruct((rows, width, z), jnp.bfloat16)
        out_spec = pl.BlockSpec((rows_step, width, z), lambda i: (i, 0, 0))
    else:
        out_shape = jax.ShapeDtypeStruct((rows, blocks, z, LANES), jnp.float32)
        out_spec = sums
    return pl.pallas_call(
        functools.partial(pair_kernel, seqs, c, first, last),
        grid=(rows // rows_step,),
        out_shape=out_shape,
        in_specs=in_specs,
        out_specs=out_spec,
        scratch_shapes=[pltpu.VMEM((sources, part * seqs, LANES), jnp.float32),
                        pltpu.VMEM((total, width * part), jnp.bfloat16),
                        pltpu.VMEM((rows_step // 2, part * c, 2 * LANES), jnp.bfloat16)],
        compiler_params=pltpu.CompilerParams(vmem_limit_bytes=32 * 1024 * 1024),
        cost_estimate=pl.CostEstimate(flops=2 * rows * c * width * part * (total + z),
                                      bytes_accessed=4 * rows * width * z, transcendentals=0),
        name="pairs",
    )(*operands)


def source_at(here, step, count):
    along = count // 2
    n, across = here // 2, here % 2
    n = (n ^ step[0]) if along & (along - 1) == 0 else (n + step[0]) % along
    return n * 2 + (across + step[1]) % 2


def fetch(array, step, count):
    return lax.ppermute(array, "row", [(source_at(r, step, count), r) for r in range(count)])


def on_device(alignment, ln_gain, ln_bias, w_left, b_left, w_right, b_right, w_out, b_out):
    seqs, width, _ = alignment.shape
    c = w_left.shape[1]
    row_count = lax.axis_size("row")
    col_count = lax.axis_size("col")
    along = row_count // 2
    left, right = features(alignment, ln_gain, ln_bias, w_left, b_left, w_right, b_right,
                           1.0 / (seqs * row_count))

    blocks = [right] + [fetch(right, (a, 0), row_count) for a in range(1, along)]
    left = repeat_after(left, blocks[1], col_count).reshape(row_count, -1, LANES)
    mine = lax.all_to_all(left, "row", split_axis=0, concat_axis=0, tiled=True)
    other = lax.ppermute(mine, "col", [(i, (i + 1) % col_count) for i in range(col_count)])
    steps = [(a, b) for b in range(2) for a in range(along)]
    left, weights = prepare(mine, other, w_out, steps, seqs, c, col_count)

    rows = right.shape[0] // HALVES
    near = [jnp.stack([block[h * rows:(h + 1) * rows] for block in blocks]) for h in range(HALVES)]
    far = [fetch(part, (0, 1), row_count) for part in near]
    sums = None
    for h in range(HALVES):
        sums = pairs(h, left, weights, near[h], far[h], sums, b_out if h == HALVES - 1 else None, seqs, c, width)
    return sums


def solution(mesh):
    in_specs = (P(("group", "row"), "col", None), P(), P(), P(), P(), P(), P(), P(), P())
    out_specs = P(("group", "row"), "col", None)
    return jax.shard_map(
        on_device, mesh=mesh, in_specs=in_specs, out_specs=out_specs, check_vma=False
    )
```

time: 39.7 us -> 40.7 us (1.025)
  blocking collectives: 27.1 us -> 0 us
  starting transfers between devices: 0 us -> 13.4 us
  waiting for transfers between devices: 0 us -> 8.61 us
  Pallas kernels: 6.78 us -> 13.3 us
  local copies, waits for them, and re-layouts: 5.3 us -> 4.76 us
    all_to_all x1 -> x0, blocking collectives: 25.1 us -> none  [on_device(): lax.all_to_all(send, 'row', split_axis=0, concat_axis=0, tiled=True)]
    ppermute x0 -> x6, starting transfers between devices: none -> 7.98 us  [the longest x5 7.98 us: fetch(): lax.ppermute(array, 'row', [(source_at(r, step, count), r) for r in range...]
    pallas_call x2 -> x5, Pallas kernels: 6.78 us -> 13.3 us  [the longest x2 6.54 us: pairs(): pl.pallas_call(functools.partial(pair_kernel, seqs, c, first, last), grid...]
    all_to_all x0 -> x1, starting transfers between devices: none -> 5.44 us  [on_device(): mine = lax.all_to_all(left, 'row', split_axis=0, concat_axis=0, tiled=True)]
    all_to_all x0 -> x1, waiting for transfers between devices: none -> 4.39 us  [on_device(): mine = lax.all_to_all(left, 'row', split_axis=0, concat_axis=0, tiled=True)]
    ppermute x0 -> x6, waiting for transfers between devices: none -> 4.22 us  [the longest x5 3.17 us: fetch(): lax.ppermute(array, 'row', [(source_at(r, step, count), r) for r in range...]
    all_gather x1 -> x0, blocking collectives: 2 us -> none  [on_device(): left = lax.all_gather(left, 'col', axis=0, tiled=True)]
    another operation x0 -> x4, local copies, waits for them, and re-layouts: none -> 1.59 us  [on_device(): jnp.stack([block[h * rows:(h + 1) * rows] for block in blocks])]
  transfers between devices with their start and end apart: 0 -> 7, of which waited for: 0 -> 3; matrix products, arithmetic and copies ran while one was open for 0% -> 4% of each run, Pallas kernels for 0% -> 17%
where the time goes in v5:
time: 40.7 us; the launch traced here: 40.2 us
  starting transfers between devices  13.4 us (33%)
  Pallas kernels  13.3 us (33%)
  waiting for transfers between devices  8.61 us (21%)
  local copies, waits for them, and re-layouts  4.76 us (12%)
    ppermute x5, starting transfers between devices, fetch(): lax.ppermute(array, 'row', [(source_at(r, step, count), r) for r in range...  7.98 us
    pallas_call x2, Pallas kernels, pairs(): pl.pallas_call(functools.partial(pair_kernel, seqs, c, first, last), grid...  6.54 us
    all_to_all x1, starting transfers between devices, on_device(): mine = lax.all_to_all(left, 'row', split_axis=0, concat_axis=0, tiled=True)  5.44 us
    all_to_all x1, waiting for transfers between devices, on_device(): mine = lax.all_to_all(left, 'row', split_axis=0, concat_axis=0, tiled=True)  4.39 us
    ppermute x5, waiting for transfers between devices, fetch(): lax.ppermute(array, 'row', [(source_at(r, step, count), r) for r in range...  3.17 us
    unnamed x12, local copies, waits for them, and re-layouts  3.17 us
    pallas_call x1, Pallas kernels, prepare(): pl.pallas_call(functools.partial(prepare_kernel, seqs, c, col_count, step...  2.74 us
    pallas_call x1, Pallas kernels, features(): pl.pallas_call(functools.partial(features_kernel, scale), grid=(1,), out_...  2.5 us
  transfers between devices with their start and end apart: 7, of which 3 were waited for; matrix products, arithmetic and copies ran while one was open for 4% of the time, Pallas kernels for 17%

profile of v5, /device:TPU:0, one launch (start us, length us, event | category | flops | bytes accessed | tf_op | source)
XLA Modules:
  0.0 40.2 jit_solution(4436894598567796247)
XLA Ops:
  0.0 2.5 %features.1 = (bf16[256,128]{1,0:T(8,128)(2,1)}, bf16[256,128]{1,0:T(8,128)(2,1)}) custom-call(bf16[8,128,256]{2,1,0:T(8,128)(2,1)} %x_ref.1, f32[1,256]{1,0:T(1,128)} %bitcast.28, f32[1,256]{1,0:T(1,128)} %bitcast.29, bf16[32,256]{1,0:T(8,128)(2,1)} %bitcast.26, f32[1,32]{1,0:T(1,128)} %bitcast.30, bf16[32,256]{1,0:T(8,128)(2,1)} %bitcast.27, f32[1,32]{1,0:T(1,128)} %bitcast.31), custom_call_target="tpu_custom_call" | custom-call | tf_op jit(solution)/shard_map/features/pallas_call | solution.py:64
  2.5 5.0 %collective-permute-start.3 = (bf16[256,128]{1,0:T(8,128)(2,1)}, bf16[256,128]{1,0:T(8,128)(2,1)S(1)}, u32[]{:S(2)}, u32[]{:S(2)}) collective-permute-start(bf16[256,128]{1,0:T(8,128)(2,1)} %get-tuple-element.10), channel_id=1, source_target_pairs={{12,0},{14,2},{8,4},{10,6},{4,8},{6,10},{0,12},{2,14},{13,1},{15,3... | collective-permute-start | bytes 196616 | tf_op jit(solution)/shard_map/ppermute | solution.py:235
  7.5 0.0 collective-permute-start.2
  7.5 0.6 %collective-permute-start = (bf16[256,128]{1,0:T(8,128)(2,1)}, bf16[256,128]{1,0:T(8,128)(2,1)S(1)}, u32[]{:S(2)}, u32[]{:S(2)}) collective-permute-start(bf16[256,128]{1,0:T(8,128)(2,1)} %get-tuple-element.10), channel_id=1, source_target_pairs={{4,0},{6,2},{0,4},{2,6},{12,8},{14,10},{8,12},{10,14},{5,1},{7,3},... | collective-permute-start | bytes 196616 | tf_op jit(solution)/shard_map/ppermute | solution.py:235
  8.1 0.8 %slice_bitcast_fusion.6 = (bf16[1,128,128]{2,1,0:T(8,128)(2,1)S(1)}, bf16[1,128,128]{2,1,0:T(8,128)(2,1)S(1)}) fusion(bf16[256,128]{1,0:T(8,128)(2,1)} %get-tuple-element.10), kind=kLoop, calls=%fused_computation.8 | loop fusion | bytes 131072 | tf_op jit(solution)/shard_map/stack | solution.py:255
  8.9 3.2 %collective-permute-done.after_ref = bf16[256,128]{1,0:T(8,128)(2,1)S(1)} collective-permute-done((bf16[256,128]{1,0:T(8,128)(2,1)}, bf16[256,128]{1,0:T(8,128)(2,1)S(1)}, u32[]{:S(2)}, u32[]{:S(2)}) %collective-permute-start) | collective-permute-done | bytes 65568 | tf_op jit(solution)/shard_map/ppermute | solution.py:235
  12.1 0.6 %copy-done.4 = bf16[256,128]{1,0:T(8,128)(2,1)} copy-done((bf16[256,128]{1,0:T(8,128)(2,1)}, bf16[256,128]{1,0:T(8,128)(2,1)S(1)}, u32[]{:S(2)}) %copy-start.4) | copy-done | bytes 65560
  12.7 1.5 %repeat.1 = bf16[2,256,128]{2,1,0:T(8,128)(2,1)} custom-call(bf16[256,128]{1,0:T(8,128)(2,1)} %get-tuple-element.9.left_ref, bf16[256,128]{1,0:T(8,128)(2,1)} %copy-done.4), custom_call_target="tpu_custom_call" | custom-call | tf_op jit(solution)/shard_map/repeat/pallas_call | solution.py:84
  14.2 5.4 %all-to-all-start = ((bf16[8,64,128]{2,1,0:T(8,128)(2,1)}), bf16[8,64,128]{2,1,0:T(8,128)(2,1)S(1)}, u32[]{:S(2)}, u32[]{:S(2)}) async-start(bf16[8,64,128]{2,1,0:T(8,128)(2,1)} %bitcast.25), calls=%async_computation | async-start | bytes 262144 | tf_op jit(solution)/shard_map/all_to_all | solution.py:249
  19.6 0.8 %slice_bitcast_fusion.2 = (bf16[1,128,128]{2,1,0:T(8,128)(2,1)S(1)}, bf16[1,128,128]{2,1,0:T(8,128)(2,1)S(1)}) fusion(bf16[256,128]{1,0:T(8,128)(2,1)} %copy-done.4), kind=kLoop, calls=%fused_computation.4 | loop fusion | bytes 131072 | tf_op jit(solution)/shard_map/stack | solution.py:255
  20.4 0.0 collective-permute-done.3
  20.4 0.0 copy-start.2
  20.5 0.0 collective-permute-done.2
  20.5 2.1 %collective-permute-start.5 = (bf16[4,128,128]{2,1,0:T(8,128)(2,1)S(1)}, bf16[4,128,128]{2,1,0:T(8,128)(2,1)S(1)}, u32[]{:S(2)}, u32[]{:S(2)}) collective-permute-start(bf16[4,128,128]{2,1,0:T(8,128)(2,1)S(1)} %pad_maximum_fusion.1.near_ref), channel_id=1, source_target_pairs={{2,0},{0,2},{6,4},{4,6},{10,8},{8,10},{14,12},{12,14},{3,1},{1,3},... | collective-permute-start | bytes 393224 | tf_op jit(solution)/shard_map/ppermute | solution.py:235
  22.6 4.4 %all-to-all-done.mine_ref = bf16[8,64,128]{2,1,0:T(8,128)(2,1)S(1)} async-done(((bf16[8,64,128]{2,1,0:T(8,128)(2,1)}), bf16[8,64,128]{2,1,0:T(8,128)(2,1)S(1)}, u32[]{:S(2)}, u32[]{:S(2)}) %all-to-all-start) | async-done | bytes 131104 | tf_op jit(solution)/shard_map/all_to_all | solution.py:249
  27.0 0.3 collective-permute-start.4
  27.3 1.0 %collective-permute-done.1.other_ref = bf16[8,64,128]{2,1,0:T(8,128)(2,1)S(1)} collective-permute-done((bf16[8,64,128]{2,1,0:T(8,128)(2,1)S(1)}, bf16[8,64,128]{2,1,0:T(8,128)(2,1)S(1)}, u32[]{:S(2)}, u32[]{:S(2)}) %collective-permute-start.1) | collective-permute-done | bytes 131104 | tf_op jit(solution)/shard_map/ppermute | solution.py:250
  28.3 0.6 %copy-done.5 = bf16[8,64,128]{2,1,0:T(8,128)(2,1)} copy-done((bf16[8,64,128]{2,1,0:T(8,128)(2,1)}, bf16[8,64,128]{2,1,0:T(8,128)(2,1)S(1)}, u32[]{:S(2)}) %copy-start.5) | copy-done | bytes 131096
  29.0 2.7 %prepare.1 = (bf16[1024,64]{1,0:T(8,128)(2,1)}, bf16[128,1024]{1,0:T(8,128)(2,1)}) custom-call(bf16[8,64,128]{2,1,0:T(8,128)(2,1)} %copy-done.3, bf16[8,64,128]{2,1,0:T(8,128)(2,1)} %copy-done.5, bf16[1024,128]{1,0:T(8,128)(2,1)} %w_ref.1), custom_call_target="tpu_custom_call" | custom-call | tf_op jit(solution)/shard_map/prepare/pallas_call | solution.py:129
  31.7 0.9 %copy-done = bf16[1024,64]{1,0:T(8,128)(2,1)S(1)} copy-done((bf16[1024,64]{1,0:T(8,128)(2,1)S(1)}, bf16[1024,64]{1,0:T(8,128)(2,1)}, u32[]{:S(2)}) %copy-start) | copy-done | bytes 131096
  32.7 0.9 %copy-done.1 = bf16[128,1024]{1,0:T(8,128)(2,1)S(1)} copy-done((bf16[128,1024]{1,0:T(8,128)(2,1)S(1)}, bf16[128,1024]{1,0:T(8,128)(2,1)}, u32[]{:S(2)}) %copy-start.1) | copy-done | bytes 262168
  33.6 2.7 %pairs.2.refs_0_ = f32[32,1,128,128]{3,2,1,0:T(8,128)S(1)} custom-call(bf16[1024,64]{1,0:T(8,128)(2,1)S(1)} %copy-done, bf16[128,1024]{1,0:T(8,128)(2,1)S(1)} %copy-done.1, bf16[4,128,128]{2,1,0:T(8,128)(2,1)S(1)} %pad_maximum_fusion.1.near_ref, bf16[4,128,128]{2,1,0:T(8,128)(2,1)S(1)} %collective-permute-done.5.far_ref), custom_call_target="tpu_custom_call" | custom-call | flops 805306368 | bytes 2097152 | tf_op jit(solution)/shard_map/pairs/pallas_call | solution.py:211
  36.3 0.0 collective-permute-done.4.far_ref
  36.4 3.8 %pairs.3 = bf16[32,128,128]{2,1,0:T(8,128)(2,1)} custom-call(bf16[1024,64]{1,0:T(8,128)(2,1)S(1)} %copy-done, bf16[128,1024]{1,0:T(8,128)(2,1)S(1)} %copy-done.1, bf16[4,128,128]{2,1,0:T(8,128)(2,1)S(1)} %pad_maximum_fusion.near_ref, bf16[4,128,128]{2,1,0:T(8,128)(2,1)S(1)} %collective-permute-done.4.far_ref, f32[32,1,128,128]{3,2,1,0:T(8,128)S(1)} %pairs.2.refs_0_, ...), custom_call_target="tpu_custom_call" | custom-call | flops 805306368 | bytes 2097152 | tf_op jit(solution)/shard_map/pairs/pallas_call | solution.py:211
  (13 shorter events, 0.1 us)
Async XLA Ops:
  2.5 17.9 %collective-permute-start.3 = (bf16[256,128]{1,0:T(8,128)(2,1)}, bf16[256,128]{1,0:T(8,128)(2,1)S(1)}, u32[]{:S(2)}, u32[]{:S(2)}) collective-permute-start(bf16[256,128]{1,0:T(8,128)(2,1)} %get-tuple-element.10), channel_id=1, source_target_pairs={{12,0},{14,2},{8,4},{10,6},{4,8},{6,10},{0,12},{2,14},{13,1},{15,3... | collective-permute-start | bytes 196616 | tf_op jit(solution)/shard_map/ppermute | solution.py:235
  7.5 12.9 %collective-permute-start.2 = (bf16[256,128]{1,0:T(8,128)(2,1)}, bf16[256,128]{1,0:T(8,128)(2,1)S(1)}, u32[]{:S(2)}, u32[]{:S(2)}) collective-permute-start(bf16[256,128]{1,0:T(8,128)(2,1)} %get-tuple-element.10), channel_id=1, source_target_pairs={{8,0},{10,2},{12,4},{14,6},{0,8},{2,10},{4,12},{6,14},{9,1},{11,3}... | collective-permute-start | bytes 196616 | tf_op jit(solution)/shard_map/ppermute | solution.py:235
  7.5 4.5 %collective-permute-start = (bf16[256,128]{1,0:T(8,128)(2,1)}, bf16[256,128]{1,0:T(8,128)(2,1)S(1)}, u32[]{:S(2)}, u32[]{:S(2)}) collective-permute-start(bf16[256,128]{1,0:T(8,128)(2,1)} %get-tuple-element.10), channel_id=1, source_target_pairs={{4,0},{6,2},{0,4},{2,6},{12,8},{14,10},{8,12},{10,14},{5,1},{7,3},... | collective-permute-start | bytes 196616 | tf_op jit(solution)/shard_map/ppermute | solution.py:235
  12.1 0.6 %copy-start.4 = (bf16[256,128]{1,0:T(8,128)(2,1)}, bf16[256,128]{1,0:T(8,128)(2,1)S(1)}, u32[]{:S(2)}) copy-start(bf16[256,128]{1,0:T(8,128)(2,1)S(1)} %collective-permute-done.after_ref) | copy-start | bytes 196612
  14.2 12.8 %all-to-all-start = ((bf16[8,64,128]{2,1,0:T(8,128)(2,1)}), bf16[8,64,128]{2,1,0:T(8,128)(2,1)S(1)}, u32[]{:S(2)}, u32[]{:S(2)}) async-start(bf16[8,64,128]{2,1,0:T(8,128)(2,1)} %bitcast.25), calls=%async_computation | async-start | bytes 262144 | tf_op jit(solution)/shard_map/all_to_all | solution.py:249
  20.4 15.9 %copy-start.2 = (f32[128]{0:T(128)S(1)}, f32[128]{0:T(128)}, u32[]{:S(2)}) copy-start(f32[128]{0:T(128)} %param.17) | copy-start | bytes 1540
  20.5 11.2 %collective-permute-start.5 = (bf16[4,128,128]{2,1,0:T(8,128)(2,1)S(1)}, bf16[4,128,128]{2,1,0:T(8,128)(2,1)S(1)}, u32[]{:S(2)}, u32[]{:S(2)}) collective-permute-start(bf16[4,128,128]{2,1,0:T(8,128)(2,1)S(1)} %pad_maximum_fusion.1.near_ref), channel_id=1, source_target_pairs={{2,0},{0,2},{6,4},{4,6},{10,8},{8,10},{14,12},{12,14},{3,1},{1,3},... | collective-permute-start | bytes 393224 | tf_op jit(solution)/shard_map/ppermute | solution.py:235
  27.0 1.4 %copy-start.3 = (bf16[8,64,128]{2,1,0:T(8,128)(2,1)}, bf16[8,64,128]{2,1,0:T(8,128)(2,1)S(1)}, u32[]{:S(2)}) copy-start(bf16[8,64,128]{2,1,0:T(8,128)(2,1)S(1)} %all-to-all-done.mine_ref) | copy-start | bytes 393220
  27.0 1.3 %collective-permute-start.1 = (bf16[8,64,128]{2,1,0:T(8,128)(2,1)S(1)}, bf16[8,64,128]{2,1,0:T(8,128)(2,1)S(1)}, u32[]{:S(2)}, u32[]{:S(2)}) collective-permute-start(bf16[8,64,128]{2,1,0:T(8,128)(2,1)S(1)} %all-to-all-done.mine_ref), channel_id=1, source_target_pairs={{0,1},{1,0},{2,3},{3,2},{4,5},{5,4},{6,7},{7,6},{8,9},{9,8},{10,11... | collective-permute-start | bytes 393224 | tf_op jit(solution)/shard_map/ppermute | solution.py:250
  27.0 9.3 %collective-permute-start.4 = (bf16[4,128,128]{2,1,0:T(8,128)(2,1)S(1)}, bf16[4,128,128]{2,1,0:T(8,128)(2,1)S(1)}, u32[]{:S(2)}, u32[]{:S(2)}) collective-permute-start(bf16[4,128,128]{2,1,0:T(8,128)(2,1)S(1)} %pad_maximum_fusion.near_ref), channel_id=1, source_target_pairs={{2,0},{0,2},{6,4},{4,6},{10,8},{8,10},{14,12},{12,14},{3,1},{1,3},... | collective-permute-start | bytes 393224 | tf_op jit(solution)/shard_map/ppermute | solution.py:235
  28.3 0.6 %copy-start.5 = (bf16[8,64,128]{2,1,0:T(8,128)(2,1)}, bf16[8,64,128]{2,1,0:T(8,128)(2,1)S(1)}, u32[]{:S(2)}) copy-start(bf16[8,64,128]{2,1,0:T(8,128)(2,1)S(1)} %collective-permute-done.1.other_ref) | copy-start | bytes 393220
  31.7 1.0 %copy-start = (bf16[1024,64]{1,0:T(8,128)(2,1)S(1)}, bf16[1024,64]{1,0:T(8,128)(2,1)}, u32[]{:S(2)}) copy-start(bf16[1024,64]{1,0:T(8,128)(2,1)} %get-tuple-element.11.left_ref) | copy-start | bytes 393220
  32.7 0.9 %copy-start.1 = (bf16[128,1024]{1,0:T(8,128)(2,1)S(1)}, bf16[128,1024]{1,0:T(8,128)(2,1)}, u32[]{:S(2)}) copy-start(bf16[128,1024]{1,0:T(8,128)(2,1)} %get-tuple-element.12.weights_ref) | copy-start | bytes 786436

commit v6 on v5

v6 whole, which is shorter than its diff:
```python
import functools

import jax
import jax.numpy as jnp
from jax import lax
from jax.experimental import pallas as pl
from jax.experimental.pallas import tpu as pltpu
from jax.sharding import PartitionSpec as P

LANES = 128
VMEM_LIMIT = 60 * 1024 * 1024


def whole(shape):
    return pl.BlockSpec(shape, lambda i: (0,) * len(shape))


def features_kernel(scale, x_ref, gain_ref, bias_ref, wl_ref, bl_ref, wr_ref, br_ref,
                    left_ref, right_ref, normed_ref, left_f32, right_f32):
    seqs, width, channels = x_ref.shape
    c = wl_ref.shape[0]
    blocks = width // LANES
    fold = LANES // c
    quarter = width // fold
    right_bias = jnp.broadcast_to(br_ref[...], (LANES, c)).T[:, :1]
    for s in range(seqs):
        values = x_ref[s].astype(jnp.float32)
        average = jnp.mean(values, axis=-1, keepdims=True)
        centred = values - average
        variance = jnp.mean(centred * centred, axis=-1, keepdims=True)
        normed = centred * lax.rsqrt(variance + 1e-05) * gain_ref[...] + bias_ref[...]
        for h in range(channels // LANES):
            normed_ref[h, s * width:(s + 1) * width] = normed[:, h * LANES:(h + 1) * LANES]
        right = lax.dot_general(wr_ref[...], normed.astype(jnp.bfloat16), (((1,), (1,)), ((), ())),
                                preferred_element_type=jnp.float32) + right_bias
        for b in range(blocks):
            right_f32[pl.ds(b * c * seqs + s, c, stride=seqs), :] = right[:, b * LANES:(b + 1) * LANES]
    total = None
    for q in range(fold):
        rows = jnp.concatenate(
            [normed_ref[h, pl.ds(q, seqs * quarter, stride=fold), :] for h in range(channels // LANES)], axis=1
        ).astype(jnp.bfloat16)
        zeros = [jnp.zeros((c, channels), jnp.bfloat16)]
        w = jnp.concatenate(zeros * q + [wl_ref[...]] + zeros * (fold - 1 - q), axis=0)
        term = lax.dot_general(rows, w, (((1,), (1,)), ((), ())), preferred_element_type=jnp.float32)
        total = term if total is None else total + term
    total = (total + jnp.concatenate([bl_ref[...]] * fold, axis=1)) * scale
    for s in range(seqs):
        left_f32[pl.ds(s, quarter, stride=seqs), :] = total[s * quarter:(s + 1) * quarter]
    along, _, rows, _ = left_ref.shape
    across = lax.rem(lax.axis_index("row"), 2)
    for n in range(along):
        for b in range(2):
            block = lax.rem(n * 2 + lax.rem(across + b, 2), left_f32.shape[0] // rows)
            left_ref[n, b] = left_f32[pl.ds(pl.multiple_of(block * rows, rows), rows), :].astype(jnp.bfloat16)
    right_ref[...] = right_f32[...].astype(jnp.bfloat16)


def features(alignment, ln_gain, ln_bias, w_left, b_left, w_right, b_right, row_count, col_count):
    seqs, width, channels = alignment.shape
    c = w_left.shape[1]
    rows = seqs * width * c // LANES
    shapes = ((row_count // 2, 2, rows * col_count // row_count, LANES), (rows, LANES))
    operands = (alignment, ln_gain.reshape(1, -1), ln_bias.reshape(1, -1), w_left.T, b_left.reshape(1, -1),
                w_right.T, b_right.reshape(1, -1))
    return pl.pallas_call(
        functools.partial(features_kernel, 1.0 / (seqs * row_count)),
        grid=(1,),
        out_shape=[jax.ShapeDtypeStruct(shape, jnp.bfloat16) for shape in shapes],
        in_specs=[whole(a.shape) for a in operands],
        out_specs=[whole(shape) for shape in shapes],
        scratch_shapes=[pltpu.VMEM((channels // LANES, seqs * width, LANES), jnp.float32),
                        pltpu.VMEM((rows, LANES), jnp.float32),
                        pltpu.VMEM((rows, LANES), jnp.float32)],
        compiler_params=pltpu.CompilerParams(vmem_limit_bytes=VMEM_LIMIT),
        name="features",
    )(*operands)


def sequence_rows(block, f32_ref, inner, seqs):
    sources = f32_ref.shape[0]
    for n in range(sources):
        f32_ref[n] = block(n)
    if seqs % 8 == 0:
        return lambda m: jnp.concatenate(
            [f32_ref[n, m * seqs:(m + 1) * seqs] for n in range(sources)], axis=0)
    flat = f32_ref.reshape(sources * inner * seqs, LANES)
    return lambda m: jnp.concatenate(
        [flat[pl.ds(m * seqs + s, sources, stride=inner * seqs), :] for s in range(seqs)], axis=0)


def prepare_kernel(seqs, c, col_count, steps, mine_ref, other_ref, w_ref, own_ref,
                   left_ref, weights_ref, right_ref, left_f32, w_f32):
    sources, left_rows, _ = mine_ref.shape
    along = sources // 2
    here, core = lax.axis_index("row"), lax.axis_index("col")
    mine = here // (sources // col_count) == core

    def block(n):
        source = steps[n][1] * along + source_at(here, steps[n], sources) // 2
        return jnp.where(mine, mine_ref[source].astype(jnp.float32), other_ref[source].astype(jnp.float32))

    left_of = sequence_rows(block, left_f32, left_rows // seqs, seqs)
    for k in range(left_rows // seqs):
        left_ref[k * LANES:(k + 1) * LANES] = left_of(k).T.astype(jnp.bfloat16)
    w_f32[...] = w_ref[...].astype(jnp.float32)
    for e in range(c):
        weights_ref[:, e * c:(e + 1) * c] = w_f32[pl.ds(e, c, stride=c), :].T.astype(jnp.bfloat16)
    right_ref[...] = own_ref[...]


def prepare(mine, other, w_out, right, steps, seqs, c, col_count):
    sources, left_rows, _ = mine.shape
    shapes = ((left_rows // seqs * LANES, sources * seqs), (w_out.shape[1], w_out.shape[0]), right.shape)
    operands = (mine, other, w_out, right)
    return pl.pallas_call(
        functools.partial(prepare_kernel, seqs, c, col_count, steps),
        grid=(1,),
        out_shape=[jax.ShapeDtypeStruct(shape, jnp.bfloat16) for shape in shapes],
        in_specs=[whole(a.shape) for a in operands],
        out_specs=[whole(shape) for shape in shapes],
        scratch_shapes=[pltpu.VMEM(mine.shape, jnp.float32), pltpu.VMEM(w_out.shape, jnp.float32)],
        compiler_params=pltpu.CompilerParams(vmem_limit_bytes=48 * 1024 * 1024),
        name="prepare",
    )(*operands)


def pair_kernel(seqs, c, sources, left_ref, weights_ref, bias_ref, *refs):
    right_refs, (out_ref, right_f32, right_b, outer_ref) = refs[:sources], refs[sources:]
    rows_step = out_ref.shape[0]
    blocks = out_ref.shape[1] // LANES

    @pl.when(pl.program_id(0) == 0)
    def _():
        for b in range(blocks):
            at = b * c * seqs
            right_of = sequence_rows(
                lambda n: right_refs[n][at:at + c * seqs].astype(jnp.float32), right_f32, c, seqs)
            for e in range(c):
                lanes = (b * c + e) * LANES
                right_b[:, lanes:lanes + LANES] = right_of(e).astype(jnp.bfloat16)

    for b in range(blocks):
        for e in range(0, c, 2):
            at = (b * c + e) * LANES
            outer = jnp.dot(left_ref[...], right_b[:, at:at + 2 * LANES], preferred_element_type=jnp.float32)
            outer = outer.astype(jnp.bfloat16)
            for half in range(2):
                for i in range(rows_step):
                    outer_ref[i // 2, (e + half) * c:(e + half + 1) * c,
                              (i % 2) * LANES:(i % 2 + 1) * LANES] = (
                        outer[i * c:(i + 1) * c, half * LANES:(half + 1) * LANES])
        for p in range(rows_step // 2):
            update = jnp.dot(weights_ref[...], outer_ref[p], preferred_element_type=jnp.float32)
            for half in range(2):
                mine = update[:, half * LANES:(half + 1) * LANES].T + bias_ref[...]
                out_ref[2 * p + half, b * LANES:(b + 1) * LANES, :] = mine.astype(out_ref.dtype)


def pairs(left, weights, bias, rights, seqs, c, width):
    sources = len(rights)
    z = weights.shape[0]
    rows = left.shape[0] // c
    rows_step = 8
    total = sources * seqs
    operands = (left, weights, bias.reshape(1, -1), *rights)
    return pl.pallas_call(
        functools.partial(pair_kernel, seqs, c, sources),
        grid=(rows // rows_step,),
        out_shape=jax.ShapeDtypeStruct((rows, width, z), jnp.bfloat16),
        in_specs=[pl.BlockSpec((rows_step * c, total), lambda i: (i, 0))] + [whole(a.shape) for a in operands[1:]],
        out_specs=pl.BlockSpec((rows_step, width, z), lambda i: (i, 0, 0)),
        scratch_shapes=[pltpu.VMEM((sources, c * seqs, LANES), jnp.float32),
                        pltpu.VMEM((total, width * c), jnp.bfloat16),
                        pltpu.VMEM((rows_step // 2, c * c, 2 * LANES), jnp.bfloat16)],
        compiler_params=pltpu.CompilerParams(vmem_limit_bytes=32 * 1024 * 1024),
        cost_estimate=pl.CostEstimate(flops=2 * rows * c * width * c * (total + z),
                                      bytes_accessed=2 * rows * width * z, transcendentals=0),
        name="pairs",
    )(*operands)


def source_at(here, step, count):
    along = count // 2
    n, across = here // 2, here % 2
    n = (n ^ step[0]) if along & (along - 1) == 0 else (n + step[0]) % along
    return n * 2 + (across + step[1]) % 2


def fetch(array, step, count):
    return lax.ppermute(array, "row", [(source_at(r, step, count), r) for r in range(count)])


def on_device(alignment, ln_gain, ln_bias, w_left, b_left, w_right, b_right, w_out, b_out):
    seqs, width, _ = alignment.shape
    c = w_left.shape[1]
    row_count = lax.axis_size("row")
    col_count = lax.axis_size("col")
    along = row_count // 2
    left, right = features(alignment, ln_gain, ln_bias, w_left, b_left, w_right, b_right, row_count, col_count)

    lines = [list(range(y, row_count, 2)) for y in range(2)]
    left = lax.all_to_all(left, "row", split_axis=0, concat_axis=0, axis_index_groups=lines, tiled=True)
    mine = jnp.concatenate([left[:, 0], fetch(left[:, 1], (0, 1), row_count)])
    other = lax.ppermute(mine, "col", [(i, (i + 1) % col_count) for i in range(col_count)])

    near = {0: right}
    for a in reversed(range(1, along)):
        near[a] = fetch(right, (a, 0), row_count)
    far = {a: fetch(near[a], (0, 1), row_count) for a in near}
    steps = [(a, b) for b in range(2) for a in near]
    left, weights, right = prepare(mine, other, w_out, right, steps, seqs, c, col_count)
    near[0] = right
    return pairs(left, weights, b_out, [*near.values(), *far.values()], seqs, c, width)


def solution(mesh):
    in_specs = (P(("group", "row"), "col", None), P(), P(), P(), P(), P(), P(), P(), P())
    out_specs = P(("group", "row"), "col", None)
    return jax.shard_map(
        on_device, mesh=mesh, in_specs=in_specs, out_specs=out_specs, check_vma=False
    )
```

time: 40.7 us -> 40.9 us (level)
  blocking collectives: 0 us -> 12.4 us
  Pallas kernels: 13.3 us -> 8.62 us
  local copies, waits for them, and re-layouts: 4.76 us -> 1.41 us
  starting transfers between devices: 13.4 us -> 10.1 us
  waiting for transfers between devices: 8.61 us -> 8.06 us
    all_to_all x0 -> x1, blocking collectives: none -> 12.4 us  [on_device(): lax.all_to_all(left, 'row', split_axis=0, concat_axis=0, axis_index_group...]
    all_to_all x1 -> x0, starting transfers between devices: 5.44 us -> none  [on_device(): mine = lax.all_to_all(left, 'row', split_axis=0, concat_axis=0, tiled=True)]
    ppermute x5 -> x8, waiting for transfers between devices: 3.17 us -> 8.06 us  [fetch(): lax.ppermute(array, 'row', [(source_at(r, step, count), r) for r in range...]
    all_to_all x1 -> x0, waiting for transfers between devices: 4.39 us -> none  [on_device(): mine = lax.all_to_all(left, 'row', split_axis=0, concat_axis=0, tiled=True)]
    pallas_call x4 -> x2, Pallas kernels: 10.5 us -> 7.62 us  [the longest x1 5.08 us: pairs(): pl.pallas_call(functools.partial(pair_kernel, seqs, c, sources), grid=(ro...]
    ppermute x5 -> x8, starting transfers between devices: 7.98 us -> 10 us  [fetch(): lax.ppermute(array, 'row', [(source_at(r, step, count), r) for r in range...]
    unnamed x12 -> x6, local copies, waits for them, and re-layouts: 3.17 us -> 1.4 us
    pallas_call x1, Pallas kernels: 2.74 us -> 1.01 us  [prepare(): pl.pallas_call(functools.partial(prepare_kernel, seqs, c, col_count, step...]
  transfers between devices with their start and end apart: 7 -> 9, of which waited for: 3 -> 4; matrix products, arithmetic and copies ran while one was open for 4% -> 0% of each run, Pallas kernels for 17% -> 2%
where the time goes in v6:
time: 40.9 us; the launch traced here: 40.6 us
  blocking collectives  12.4 us (30%)
  starting transfers between devices  10.1 us (25%)
  Pallas kernels  8.62 us (21%)
  waiting for transfers between devices  8.06 us (20%)
  local copies, waits for them, and re-layouts  1.41 us (3%)
    all_to_all x1, blocking collectives, on_device(): lax.all_to_all(left, 'row', split_axis=0, concat_axis=0, axis_index_group...  12.4 us
    ppermute x8, starting transfers between devices, fetch(): lax.ppermute(array, 'row', [(source_at(r, step, count), r) for r in range...  10 us
    ppermute x8, waiting for transfers between devices, fetch(): lax.ppermute(array, 'row', [(source_at(r, step, count), r) for r in range...  8.06 us
    pallas_call x1, Pallas kernels, pairs(): pl.pallas_call(functools.partial(pair_kernel, seqs, c, sources), grid=(ro...  5.08 us
    pallas_call x1, Pallas kernels, features(): pl.pallas_call(functools.partial(features_kernel, 1.0 / (seqs * row_count...  2.54 us
    unnamed x6, local copies, waits for them, and re-layouts  1.4 us
    pallas_call x1, Pallas kernels, prepare(): pl.pallas_call(functools.partial(prepare_kernel, seqs, c, col_count, step...  1.01 us
  transfers between devices with their start and end apart: 9, of which 4 were waited for; matrix products, arithmetic and copies ran while one was open for 0% of the time, Pallas kernels for 2%

profile of v6, /device:TPU:0, one launch (start us, length us, event | category | flops | bytes accessed | tf_op | source)
XLA Modules:
  0.0 40.6 jit_solution(3047947418358016185)
XLA Ops:
  0.0 2.5 %features.1 = (bf16[4,2,64,128]{3,2,1,0:T(8,128)(2,1)}, bf16[256,128]{1,0:T(8,128)(2,1)}) custom-call(bf16[8,128,256]{2,1,0:T(8,128)(2,1)} %x_ref.1, f32[1,256]{1,0:T(1,128)} %bitcast.18, f32[1,256]{1,0:T(1,128)} %bitcast.19, bf16[32,256]{1,0:T(8,128)(2,1)} %bitcast.16, f32[1,32]{1,0:T(1,128)} %bitcast.20, bf16[32,256]{1,0:T(8,128)(2,1)} %bitcast.17, ...), custom_call_target="tpu_custom_call" | custom-call | tf_op jit(solution)/shard_map/features/pallas_call | solution.py:66
  2.5 12.4 %all_to_all.5 = bf16[4,2,64,128]{3,2,1,0:T(8,128)(2,1)S(1)} all-to-all(bf16[4,2,64,128]{3,2,1,0:T(8,128)(2,1)} %get-tuple-element.10), channel_id=1, replica_groups={{0,4,8,12},{2,6,10,14},{1,5,9,13},{3,7,11,15},{16,20,24,28},{18,22,26,3..., dimensions={0} | all-to-all | bytes 262144 | tf_op jit(solution)/shard_map/all_to_all | solution.py:203
  14.9 1.6 %collective-permute-start = (bf16[4,64,128]{2,1,0:T(8,128)(2,1)S(1)}, bf16[4,64,128]{2,1,0:T(8,128)(2,1)S(1)}, u32[]{:S(2)}, u32[]{:S(2)}) collective-permute-start(bf16[4,64,128]{2,1,0:T(8,128)(2,1)S(1)} %get-tuple-element.16), channel_id=1, source_target_pairs={{2,0},{0,2},{6,4},{4,6},{10,8},{8,10},{14,12},{12,14},{3,1},{1,3},... | collective-permute-start | bytes 196616 | tf_op jit(solution)/shard_map/ppermute | solution.py:191
  16.5 2.7 %collective-permute-done = bf16[4,64,128]{2,1,0:T(8,128)(2,1)S(1)} collective-permute-done((bf16[4,64,128]{2,1,0:T(8,128)(2,1)S(1)}, bf16[4,64,128]{2,1,0:T(8,128)(2,1)S(1)}, u32[]{:S(2)}, u32[]{:S(2)}) %collective-permute-start) | collective-permute-done | bytes 65568 | tf_op jit(solution)/shard_map/ppermute | solution.py:191
  19.3 0.1 collective-permute-start.1
  19.4 0.7 %copy-done.1 = bf16[256,128]{1,0:T(8,128)(2,1)S(1)} copy-done((bf16[256,128]{1,0:T(8,128)(2,1)S(1)}, bf16[256,128]{1,0:T(8,128)(2,1)}, u32[]{:S(2)}) %copy-start.1) | copy-done | bytes 65560
  20.1 1.1 %collective-permute-start.4 = (bf16[256,128]{1,0:T(8,128)(2,1)S(1)}, bf16[256,128]{1,0:T(8,128)(2,1)S(1)}, u32[]{:S(2)}, u32[]{:S(2)}) collective-permute-start(bf16[256,128]{1,0:T(8,128)(2,1)S(1)} %copy-done.1), channel_id=1, source_target_pairs={{4,0},{6,2},{0,4},{2,6},{12,8},{14,10},{8,12},{10,14},{5,1},{7,3},... | collective-permute-start | bytes 196616 | tf_op jit(solution)/shard_map/ppermute | solution.py:191
  21.2 0.9 %collective-permute-start.3 = (bf16[256,128]{1,0:T(8,128)(2,1)S(1)}, bf16[256,128]{1,0:T(8,128)(2,1)S(1)}, u32[]{:S(2)}, u32[]{:S(2)}) collective-permute-start(bf16[256,128]{1,0:T(8,128)(2,1)S(1)} %copy-done.1), channel_id=1, source_target_pairs={{8,0},{10,2},{12,4},{14,6},{0,8},{2,10},{4,12},{6,14},{9,1},{11,3}... | collective-permute-start | bytes 196616 | tf_op jit(solution)/shard_map/ppermute | solution.py:191
  22.1 2.4 %collective-permute-start.2 = (bf16[256,128]{1,0:T(8,128)(2,1)S(1)}, bf16[256,128]{1,0:T(8,128)(2,1)S(1)}, u32[]{:S(2)}, u32[]{:S(2)}) collective-permute-start(bf16[256,128]{1,0:T(8,128)(2,1)S(1)} %copy-done.1), channel_id=1, source_target_pairs={{12,0},{14,2},{8,4},{10,6},{4,8},{6,10},{0,12},{2,14},{13,1},{15,3... | collective-permute-start | bytes 196616 | tf_op jit(solution)/shard_map/ppermute | solution.py:191
  24.5 1.5 %collective-permute-start.5 = (bf16[256,128]{1,0:T(8,128)(2,1)S(1)}, bf16[256,128]{1,0:T(8,128)(2,1)S(1)}, u32[]{:S(2)}, u32[]{:S(2)}) collective-permute-start(bf16[256,128]{1,0:T(8,128)(2,1)S(1)} %copy-done.1), channel_id=1, source_target_pairs={{2,0},{0,2},{6,4},{4,6},{10,8},{8,10},{14,12},{12,14},{3,1},{1,3},... | collective-permute-start | bytes 196616 | tf_op jit(solution)/shard_map/ppermute | solution.py:191
  26.0 0.0 collective-permute-done.4.refs_3_
  26.0 0.5 %collective-permute-start.8 = (bf16[256,128]{1,0:T(8,128)(2,1)S(1)}, bf16[256,128]{1,0:T(8,128)(2,1)S(1)}, u32[]{:S(2)}, u32[]{:S(2)}) collective-permute-start(bf16[256,128]{1,0:T(8,128)(2,1)S(1)} %collective-permute-done.4.refs_3_), channel_id=1, source_target_pairs={{2,0},{0,2},{6,4},{4,6},{10,8},{8,10},{14,12},{12,14},{3,1},{1,3},... | collective-permute-start | bytes 196616 | tf_op jit(solution)/shard_map/ppermute | solution.py:191
  26.5 2.6 %collective-permute-done.3.refs_2_ = bf16[256,128]{1,0:T(8,128)(2,1)S(1)} collective-permute-done((bf16[256,128]{1,0:T(8,128)(2,1)S(1)}, bf16[256,128]{1,0:T(8,128)(2,1)S(1)}, u32[]{:S(2)}, u32[]{:S(2)}) %collective-permute-start.3) | collective-permute-done | bytes 65568 | tf_op jit(solution)/shard_map/ppermute | solution.py:191
  29.1 1.5 %collective-permute-start.7 = (bf16[256,128]{1,0:T(8,128)(2,1)S(1)}, bf16[256,128]{1,0:T(8,128)(2,1)S(1)}, u32[]{:S(2)}, u32[]{:S(2)}) collective-permute-start(bf16[256,128]{1,0:T(8,128)(2,1)S(1)} %collective-permute-done.3.refs_2_), channel_id=1, source_target_pairs={{2,0},{0,2},{6,4},{4,6},{10,8},{8,10},{14,12},{12,14},{3,1},{1,3},... | collective-permute-start | bytes 196616 | tf_op jit(solution)/shard_map/ppermute | solution.py:191
  30.6 0.0 collective-permute-done.2.refs_1_
  30.6 0.5 %collective-permute-start.6 = (bf16[256,128]{1,0:T(8,128)(2,1)S(1)}, bf16[256,128]{1,0:T(8,128)(2,1)S(1)}, u32[]{:S(2)}, u32[]{:S(2)}) collective-permute-start(bf16[256,128]{1,0:T(8,128)(2,1)S(1)} %collective-permute-done.2.refs_1_), channel_id=1, source_target_pairs={{2,0},{0,2},{6,4},{4,6},{10,8},{8,10},{14,12},{12,14},{3,1},{1,3},... | collective-permute-start | bytes 196616 | tf_op jit(solution)/shard_map/ppermute | solution.py:191
  31.1 0.0 collective-permute-done.1.other_ref
  31.1 1.0 %prepare.1 = (bf16[1024,64]{1,0:T(8,128)(2,1)S(1)}, bf16[128,1024]{1,0:T(8,128)(2,1)S(1)}, bf16[256,128]{1,0:T(8,128)(2,1)S(1)}) custom-call(bf16[8,64,128]{2,1,0:T(8,128)(2,1)S(1)} %pad_maximum_fusion.mine_ref, bf16[8,64,128]{2,1,0:T(8,128)(2,1)S(1)} %collective-permute-done.1.other_ref, bf16[1024,128]{1,0:T(8,128)(2,1)S(1)} %copy-done, ...), custom_call_target="tpu_custom_call" | custom-call | tf_op jit(solution)/shard_map/prepare/pallas_call | solution.py:116
  32.2 0.0 collective-permute-done.5.refs_4_
  32.2 0.0 collective-permute-done.8.refs_7_
  32.2 1.2 %collective-permute-done.7.refs_6_ = bf16[256,128]{1,0:T(8,128)(2,1)S(1)} collective-permute-done((bf16[256,128]{1,0:T(8,128)(2,1)S(1)}, bf16[256,128]{1,0:T(8,128)(2,1)S(1)}, u32[]{:S(2)}, u32[]{:S(2)}) %collective-permute-start.7) | collective-permute-done | bytes 65568 | tf_op jit(solution)/shard_map/ppermute | solution.py:191
  33.4 1.5 %collective-permute-done.6.refs_5_ = bf16[256,128]{1,0:T(8,128)(2,1)S(1)} collective-permute-done((bf16[256,128]{1,0:T(8,128)(2,1)S(1)}, bf16[256,128]{1,0:T(8,128)(2,1)S(1)}, u32[]{:S(2)}, u32[]{:S(2)}) %collective-permute-start.6) | collective-permute-done | bytes 65568 | tf_op jit(solution)/shard_map/ppermute | solution.py:191
  34.9 0.7 %copy-done.2 = f32[128]{0:T(128)S(1)} copy-done((f32[128]{0:T(128)S(1)}, f32[128]{0:T(128)}, u32[]{:S(2)}) %copy-start.2) | copy-done | bytes 536
  35.6 5.1 %pairs.1 = bf16[32,128,128]{2,1,0:T(8,128)(2,1)} custom-call(bf16[1024,64]{1,0:T(8,128)(2,1)S(1)} %get-tuple-element.12.left_ref, bf16[128,1024]{1,0:T(8,128)(2,1)S(1)} %get-tuple-element.13.weights_ref, f32[1,128]{1,0:T(1,128)S(1)} %bitcast.15, bf16[256,128]{1,0:T(8,128)(2,1)S(1)} %get-tuple-element.14.refs_0_, ...), custom_call_target="tpu_custom_call" | custom-call | flops 1610612736 | bytes 1048576 | tf_op jit(solution)/shard_map/pairs/pallas_call | solution.py:167
  (6 shorter events, 0.0 us)
Async XLA Ops:
  14.9 16.2 %copy-start = (bf16[1024,128]{1,0:T(8,128)(2,1)S(1)}, bf16[1024,128]{1,0:T(8,128)(2,1)}, u32[]{:S(2)}) copy-start(bf16[1024,128]{1,0:T(8,128)(2,1)} %w_ref.1) | copy-start | bytes 786436
  14.9 4.3 %collective-permute-start = (bf16[4,64,128]{2,1,0:T(8,128)(2,1)S(1)}, bf16[4,64,128]{2,1,0:T(8,128)(2,1)S(1)}, u32[]{:S(2)}, u32[]{:S(2)}) collective-permute-start(bf16[4,64,128]{2,1,0:T(8,128)(2,1)S(1)} %get-tuple-element.16), channel_id=1, source_target_pairs={{2,0},{0,2},{6,4},{4,6},{10,8},{8,10},{14,12},{12,14},{3,1},{1,3},... | collective-permute-start | bytes 196616 | tf_op jit(solution)/shard_map/ppermute | solution.py:191
  19.3 0.8 %copy-start.1 = (bf16[256,128]{1,0:T(8,128)(2,1)S(1)}, bf16[256,128]{1,0:T(8,128)(2,1)}, u32[]{:S(2)}) copy-start(bf16[256,128]{1,0:T(8,128)(2,1)} %get-tuple-element.11.own_ref) | copy-start | bytes 196612
  19.3 11.9 %collective-permute-start.1 = (bf16[8,64,128]{2,1,0:T(8,128)(2,1)S(1)}, bf16[8,64,128]{2,1,0:T(8,128)(2,1)S(1)}, u32[]{:S(2)}, u32[]{:S(2)}) collective-permute-start(bf16[8,64,128]{2,1,0:T(8,128)(2,1)S(1)} %pad_maximum_fusion.mine_ref), channel_id=1, source_target_pairs={{0,1},{1,0},{2,3},{3,2},{4,5},{5,4},{6,7},{7,6},{8,9},{9,8},{10,11... | collective-permute-start | bytes 393224 | tf_op jit(solution)/shard_map/ppermute | solution.py:205
  20.1 5.9 %collective-permute-start.4 = (bf16[256,128]{1,0:T(8,128)(2,1)S(1)}, bf16[256,128]{1,0:T(8,128)(2,1)S(1)}, u32[]{:S(2)}, u32[]{:S(2)}) collective-permute-start(bf16[256,128]{1,0:T(8,128)(2,1)S(1)} %copy-done.1), channel_id=1, source_target_pairs={{4,0},{6,2},{0,4},{2,6},{12,8},{14,10},{8,12},{10,14},{5,1},{7,3},... | collective-permute-start | bytes 196616 | tf_op jit(solution)/shard_map/ppermute | solution.py:191
  21.2 7.9 %collective-permute-start.3 = (bf16[256,128]{1,0:T(8,128)(2,1)S(1)}, bf16[256,128]{1,0:T(8,128)(2,1)S(1)}, u32[]{:S(2)}, u32[]{:S(2)}) collective-permute-start(bf16[256,128]{1,0:T(8,128)(2,1)S(1)} %copy-done.1), channel_id=1, source_target_pairs={{8,0},{10,2},{12,4},{14,6},{0,8},{2,10},{4,12},{6,14},{9,1},{11,3}... | collective-permute-start | bytes 196616 | tf_op jit(solution)/shard_map/ppermute | solution.py:191
  22.1 8.5 %collective-permute-start.2 = (bf16[256,128]{1,0:T(8,128)(2,1)S(1)}, bf16[256,128]{1,0:T(8,128)(2,1)S(1)}, u32[]{:S(2)}, u32[]{:S(2)}) collective-permute-start(bf16[256,128]{1,0:T(8,128)(2,1)S(1)} %copy-done.1), channel_id=1, source_target_pairs={{12,0},{14,2},{8,4},{10,6},{4,8},{6,10},{0,12},{2,14},{13,1},{15,3... | collective-permute-start | bytes 196616 | tf_op jit(solution)/shard_map/ppermute | solution.py:191
  24.5 7.7 %collective-permute-start.5 = (bf16[256,128]{1,0:T(8,128)(2,1)S(1)}, bf16[256,128]{1,0:T(8,128)(2,1)S(1)}, u32[]{:S(2)}, u32[]{:S(2)}) collective-permute-start(bf16[256,128]{1,0:T(8,128)(2,1)S(1)} %copy-done.1), channel_id=1, source_target_pairs={{2,0},{0,2},{6,4},{4,6},{10,8},{8,10},{14,12},{12,14},{3,1},{1,3},... | collective-permute-start | bytes 196616 | tf_op jit(solution)/shard_map/ppermute | solution.py:191
  26.0 6.1 %collective-permute-start.8 = (bf16[256,128]{1,0:T(8,128)(2,1)S(1)}, bf16[256,128]{1,0:T(8,128)(2,1)S(1)}, u32[]{:S(2)}, u32[]{:S(2)}) collective-permute-start(bf16[256,128]{1,0:T(8,128)(2,1)S(1)} %collective-permute-done.4.refs_3_), channel_id=1, source_target_pairs={{2,0},{0,2},{6,4},{4,6},{10,8},{8,10},{14,12},{12,14},{3,1},{1,3},... | collective-permute-start | bytes 196616 | tf_op jit(solution)/shard_map/ppermute | solution.py:191
  29.1 4.3 %collective-permute-start.7 = (bf16[256,128]{1,0:T(8,128)(2,1)S(1)}, bf16[256,128]{1,0:T(8,128)(2,1)S(1)}, u32[]{:S(2)}, u32[]{:S(2)}) collective-permute-start(bf16[256,128]{1,0:T(8,128)(2,1)S(1)} %collective-permute-done.3.refs_2_), channel_id=1, source_target_pairs={{2,0},{0,2},{6,4},{4,6},{10,8},{8,10},{14,12},{12,14},{3,1},{1,3},... | collective-permute-start | bytes 196616 | tf_op jit(solution)/shard_map/ppermute | solution.py:191
  30.6 4.3 %collective-permute-start.6 = (bf16[256,128]{1,0:T(8,128)(2,1)S(1)}, bf16[256,128]{1,0:T(8,128)(2,1)S(1)}, u32[]{:S(2)}, u32[]{:S(2)}) collective-permute-start(bf16[256,128]{1,0:T(8,128)(2,1)S(1)} %collective-permute-done.2.refs_1_), channel_id=1, source_target_pairs={{2,0},{0,2},{6,4},{4,6},{10,8},{8,10},{14,12},{12,14},{3,1},{1,3},... | collective-permute-start | bytes 196616 | tf_op jit(solution)/shard_map/ppermute | solution.py:191
  34.9 0.7 %copy-start.2 = (f32[128]{0:T(128)S(1)}, f32[128]{0:T(128)}, u32[]{:S(2)}) copy-start(f32[128]{0:T(128)} %param.17) | copy-start | bytes 1540

commit v7 on v6

--- a/solution.py
+++ b/solution.py
@@ -16,7 +16,8 @@
 
 
 def features_kernel(scale, x_ref, gain_ref, bias_ref, wl_ref, bl_ref, wr_ref, br_ref,
-                    left_ref, right_ref, normed_ref, left_f32, right_f32):
+                    *refs):
+    messages, (normed_ref, left_f32, right_f32) = refs[:-3], refs[-3:]
     seqs, width, channels = x_ref.shape
     c = wl_ref.shape[0]
     blocks = width // LANES
@@ -47,20 +48,24 @@
     total = (total + jnp.concatenate([bl_ref[...]] * fold, axis=1)) * scale
     for s in range(seqs):
         left_f32[pl.ds(s, quarter, stride=seqs), :] = total[s * quarter:(s + 1) * quarter]
-    along, _, rows, _ = left_ref.shape
-    across = lax.rem(lax.axis_index("row"), 2)
-    for n in range(along):
-        for b in range(2):
-            block = lax.rem(n * 2 + lax.rem(across + b, 2), left_f32.shape[0] // rows)
-            left_ref[n, b] = left_f32[pl.ds(pl.multiple_of(block * rows, rows), rows), :].astype(jnp.bfloat16)
-    right_ref[...] = right_f32[...].astype(jnp.bfloat16)
+    here = lax.axis_index("row")
+    right = right_f32[...].astype(jnp.bfloat16)
+    count = len(messages)
+    for step, message in zip(steps_of(count), messages):
+        with_right = carries_right(step)
+        left_rows = message.shape[0] - right.shape[0] * with_right
+        block = lax.rem(source_at(here, step, count), left_f32.shape[0] // left_rows)
+        left = left_f32[pl.ds(pl.multiple_of(block * left_rows, left_rows), left_rows), :].astype(jnp.bfloat16)
+        message[message.shape[0] - left_rows:] = left
+        if with_right:
+            message[:right.shape[0]] = right
 
 
 def features(alignment, ln_gain, ln_bias, w_left, b_left, w_right, b_right, row_count, col_count):
     seqs, width, channels = alignment.shape
     c = w_left.shape[1]
     rows = seqs * width * c // LANES
-    shapes = ((row_count // 2, 2, rows * col_count // row_count, LANES), (rows, LANES))
+    shapes = [(rows * carries_right(step) + rows * col_count // row_count, LANES) for step in steps_of(row_count)]
     operands = (alignment, ln_gain.reshape(1, -1), ln_bias.reshape(1, -1), w_left.T, b_left.reshape(1, -1),
                 w_right.T, b_right.reshape(1, -1))
     return pl.pallas_call(
@@ -89,43 +94,39 @@
         [flat[pl.ds(m * seqs + s, sources, stride=inner * seqs), :] for s in range(seqs)], axis=0)
 
 
-def prepare_kernel(seqs, c, col_count, steps, mine_ref, other_ref, w_ref, own_ref,
-                   left_ref, weights_ref, right_ref, left_f32, w_f32):
-    sources, left_rows, _ = mine_ref.shape
-    along = sources // 2
-    here, core = lax.axis_index("row"), lax.axis_index("col")
-    mine = here // (sources // col_count) == core
-
-    def block(n):
-        source = steps[n][1] * along + source_at(here, steps[n], sources) // 2
-        return jnp.where(mine, mine_ref[source].astype(jnp.float32), other_ref[source].astype(jnp.float32))
-
-    left_of = sequence_rows(block, left_f32, left_rows // seqs, seqs)
+def prepare_kernel(seqs, c, left_rows, w_ref, bias_ref, *refs):
+    messages, refs = refs[:-6], refs[-6:]
+    left_ref, weights_ref, right_ref, bias_out_ref, left_f32, w_f32 = refs
+    left_of = sequence_rows(lambda n: messages[n][messages[n].shape[0] - left_rows:].astype(jnp.float32),
+                            left_f32, left_rows // seqs, seqs)
     for k in range(left_rows // seqs):
         left_ref[k * LANES:(k + 1) * LANES] = left_of(k).T.astype(jnp.bfloat16)
     w_f32[...] = w_ref[...].astype(jnp.float32)
     for e in range(c):
         weights_ref[:, e * c:(e + 1) * c] = w_f32[pl.ds(e, c, stride=c), :].T.astype(jnp.bfloat16)
-    right_ref[...] = own_ref[...]
-
-
-def prepare(mine, other, w_out, right, steps, seqs, c, col_count):
-    sources, left_rows, _ = mine.shape
-    shapes = ((left_rows // seqs * LANES, sources * seqs), (w_out.shape[1], w_out.shape[0]), right.shape)
-    operands = (mine, other, w_out, right)
+    right_ref[...] = messages[0][:right_ref.shape[0]]
+    bias_out_ref[...] = bias_ref[...]
+
+
+def prepare(messages, w_out, b_out, seqs, c, left_rows):
+    sources = len(messages)
+    z = w_out.shape[1]
+    outs = [((left_rows // seqs * LANES, sources * seqs), jnp.bfloat16), ((z, w_out.shape[0]), jnp.bfloat16),
+            ((messages[0].shape[0] - left_rows, LANES), jnp.bfloat16), ((1, z), jnp.float32)]
+    operands = (w_out, b_out.reshape(1, -1), *messages)
     return pl.pallas_call(
-        functools.partial(prepare_kernel, seqs, c, col_count, steps),
+        functools.partial(prepare_kernel, seqs, c, left_rows),
         grid=(1,),
-        out_shape=[jax.ShapeDtypeStruct(shape, jnp.bfloat16) for shape in shapes],
+        out_shape=[jax.ShapeDtypeStruct(*out) for out in outs],
         in_specs=[whole(a.shape) for a in operands],
-        out_specs=[whole(shape) for shape in shapes],
-        scratch_shapes=[pltpu.VMEM(mine.shape, jnp.float32), pltpu.VMEM(w_out.shape, jnp.float32)],
+        out_specs=[whole(out[0]) for out in outs],
+        scratch_shapes=[pltpu.VMEM((sources, left_rows, LANES), jnp.float32), pltpu.VMEM(w_out.shape, jnp.float32)],
         compiler_params=pltpu.CompilerParams(vmem_limit_bytes=48 * 1024 * 1024),
         name="prepare",
     )(*operands)
 
 
-def pair_kernel(seqs, c, sources, left_ref, weights_ref, bias_ref, *refs):
+def pair_kernel(seqs, c, sources, col_count, mine_ref, other_ref, weights_ref, bias_ref, *refs):
     right_refs, (out_ref, right_f32, right_b, outer_ref) = refs[:sources], refs[sources:]
     rows_step = out_ref.shape[0]
     blocks = out_ref.shape[1] // LANES
@@ -140,10 +141,12 @@
                 lanes = (b * c + e) * LANES
                 right_b[:, lanes:lanes + LANES] = right_of(e).astype(jnp.bfloat16)
 
+    half = lax.axis_index("row") // (sources // col_count)
+    left = jnp.where(half == lax.axis_index("col"), mine_ref[...], other_ref[...])
     for b in range(blocks):
         for e in range(0, c, 2):
             at = (b * c + e) * LANES
-            outer = jnp.dot(left_ref[...], right_b[:, at:at + 2 * LANES], preferred_element_type=jnp.float32)
+            outer = jnp.dot(left, right_b[:, at:at + 2 * LANES], preferred_element_type=jnp.float32)
             outer = outer.astype(jnp.bfloat16)
             for half in range(2):
                 for i in range(rows_step):
@@ -157,18 +160,18 @@
                 out_ref[2 * p + half, b * LANES:(b + 1) * LANES, :] = mine.astype(out_ref.dtype)
 
 
-def pairs(left, weights, bias, rights, seqs, c, width):
+def pairs(mine, other, weights, bias, rights, seqs, c, width, col_count):
     sources = len(rights)
     z = weights.shape[0]
-    rows = left.shape[0] // c
+    rows = mine.shape[0] // c
     rows_step = 8
     total = sources * seqs
-    operands = (left, weights, bias.reshape(1, -1), *rights)
+    operands = (mine, other, weights, bias, *rights)
     return pl.pallas_call(
-        functools.partial(pair_kernel, seqs, c, sources),
+        functools.partial(pair_kernel, seqs, c, sources, col_count),
         grid=(rows // rows_step,),
         out_shape=jax.ShapeDtypeStruct((rows, width, z), jnp.bfloat16),
-        in_specs=[pl.BlockSpec((rows_step * c, total), lambda i: (i, 0))] + [whole(a.shape) for a in operands[1:]],
+        in_specs=[pl.BlockSpec((rows_step * c, total), lambda i: (i, 0))] * 2 + [whole(a.shape) for a in operands[2:]],
         out_specs=pl.BlockSpec((rows_step, width, z), lambda i: (i, 0, 0)),
         scratch_shapes=[pltpu.VMEM((sources, c * seqs, LANES), jnp.float32),
                         pltpu.VMEM((total, width * c), jnp.bfloat16),
@@ -187,6 +190,14 @@
     return n * 2 + (across + step[1]) % 2
 
 
+def steps_of(count):
+    return [(a, b) for b in range(2) for a in range(count // 2)]
+
+
+def carries_right(step):
+    return step[0] == 0 or step[1] == 0
+
+
 def fetch(array, step, count):
     return lax.ppermute(array, "row", [(source_at(r, step, count), r) for r in range(count)])
 
@@ -196,22 +207,18 @@
     c = w_left.shape[1]
     row_count = lax.axis_size("row")
     col_count = lax.axis_size("col")
-    along = row_count // 2
-    left, right = features(alignment, ln_gain, ln_bias, w_left, b_left, w_right, b_right, row_count, col_count)
-
-    lines = [list(range(y, row_count, 2)) for y in range(2)]
-    left = lax.all_to_all(left, "row", split_axis=0, concat_axis=0, axis_index_groups=lines, tiled=True)
-    mine = jnp.concatenate([left[:, 0], fetch(left[:, 1], (0, 1), row_count)])
+    messages = features(alignment, ln_gain, ln_bias, w_left, b_left, w_right, b_right, row_count, col_count)
+    steps = steps_of(row_count)
+    left_rows = messages[-1].shape[0]
+    right_rows = messages[0].shape[0] - left_rows
+
+    here = {step: message if step == (0, 0) else fetch(message, step, row_count)
+            for step, message in zip(steps, messages)}
+    rights = {step: here[step] if carries_right(step) else fetch(here[step[0], 0][:right_rows], (0, 1), row_count)
+              for step in steps}
+    mine, weights, rights[0, 0], bias = prepare(list(here.values()), w_out, b_out, seqs, c, left_rows)
     other = lax.ppermute(mine, "col", [(i, (i + 1) % col_count) for i in range(col_count)])
-
-    near = {0: right}
-    for a in reversed(range(1, along)):
-        near[a] = fetch(right, (a, 0), row_count)
-    far = {a: fetch(near[a], (0, 1), row_count) for a in near}
-    steps = [(a, b) for b in range(2) for a in near]
-    left, weights, right = prepare(mine, other, w_out, right, steps, seqs, c, col_count)
-    near[0] = right
-    return pairs(left, weights, b_out, [*near.values(), *far.values()], seqs, c, width)
+    return pairs(mine, other, weights, bias, list(rights.values()), seqs, c, width, col_count)
 
 
 def solution(mesh):

time: 40.9 us -> 43.7 us (1.068)
  blocking collectives: 12.4 us -> 0 us
  waiting for transfers between devices: 8.06 us -> 19 us
  starting transfers between devices: 10.1 us -> 14.1 us
    all_to_all x1 -> x0, blocking collectives: 12.4 us -> none  [on_device(): lax.all_to_all(left, 'row', split_axis=0, concat_axis=0, axis_index_group...]
    ppermute x8 -> x10, waiting for transfers between devices: 8.06 us -> 19 us  [fetch(): lax.ppermute(array, 'row', [(source_at(r, step, count), r) for r in range...]
    ppermute x8 -> x10, starting transfers between devices: 10 us -> 14 us  [fetch(): lax.ppermute(array, 'row', [(source_at(r, step, count), r) for r in range...]
  transfers between devices with their start and end apart: 9 -> 11, of which waited for: 4 -> 6; matrix products, arithmetic and copies ran while one was open for 0% -> 0% of each run, Pallas kernels for 2% -> 0%
where the time goes in v7:
time: 43.7 us; the launch traced here: 43.5 us
  waiting for transfers between devices  19 us (43%)
  starting transfers between devices  14.1 us (32%)
  Pallas kernels  8.82 us (20%)
  local copies, waits for them, and re-layouts  1.55 us (4%)
    ppermute x10, waiting for transfers between devices, fetch(): lax.ppermute(array, 'row', [(source_at(r, step, count), r) for r in range...  19 us
    ppermute x10, starting transfers between devices, fetch(): lax.ppermute(array, 'row', [(source_at(r, step, count), r) for r in range...  14 us
    pallas_call x1, Pallas kernels, pairs(): pl.pallas_call(functools.partial(pair_kernel, seqs, c, sources, col_count...  5.17 us
    pallas_call x1, Pallas kernels, features(): pl.pallas_call(functools.partial(features_kernel, 1.0 / (seqs * row_count...  2.67 us
    unnamed x6, local copies, waits for them, and re-layouts  1.53 us
    pallas_call x1, Pallas kernels, prepare(): pl.pallas_call(functools.partial(prepare_kernel, seqs, c, left_rows), gri...  0.98 us
  transfers between devices with their start and end apart: 11, of which 6 were waited for; matrix products, arithmetic and copies ran while one was open for 0% of the time, Pallas kernels for 0%

profile of v7, /device:TPU:0, one launch (start us, length us, event | category | flops | bytes accessed | tf_op | source)
XLA Modules:
  0.0 43.5 jit_solution(13499636906155833327)
XLA Ops:
  0.0 2.7 %features.1 = (bf16[320,128]{1,0:T(8,128)(2,1)}, bf16[320,128]{1,0:T(8,128)(2,1)}, bf16[320,128]{1,0:T(8,128)(2,1)}, bf16[320,128]{1,0:T(8,128)(2,1)}, bf16[320,...) custom-call(bf16[8,128,256]{2,1,0:T(8,128)(2,1)} %x_ref.1, ...), custom_call_target="tpu_custom_call" | custom-call | tf_op jit(solution)/shard_map/features/pallas_call | solution.py:71
  2.7 3.1 %collective-permute-start = (bf16[320,128]{1,0:T(8,128)(2,1)}, bf16[320,128]{1,0:T(8,128)(2,1)S(1)}, u32[]{:S(2)}, u32[]{:S(2)}) collective-permute-start(bf16[320,128]{1,0:T(8,128)(2,1)} %get-tuple-element.18), channel_id=1, source_target_pairs={{4,0},{6,2},{0,4},{2,6},{12,8},{14,10},{8,12},{10,14},{5,1},{7,3},... | collective-permute-start | bytes 245768 | tf_op jit(solution)/shard_map/ppermute | solution.py:202
  5.7 2.6 %collective-permute-start.1 = (bf16[320,128]{1,0:T(8,128)(2,1)}, bf16[320,128]{1,0:T(8,128)(2,1)S(1)}, u32[]{:S(2)}, u32[]{:S(2)}) collective-permute-start(bf16[320,128]{1,0:T(8,128)(2,1)} %get-tuple-element.19), channel_id=1, source_target_pairs={{8,0},{10,2},{12,4},{14,6},{0,8},{2,10},{4,12},{6,14},{9,1},{11,3}... | collective-permute-start | bytes 245768 | tf_op jit(solution)/shard_map/ppermute | solution.py:202
  8.3 1.7 %collective-permute-start.3 = (bf16[320,128]{1,0:T(8,128)(2,1)}, bf16[320,128]{1,0:T(8,128)(2,1)S(1)}, u32[]{:S(2)}, u32[]{:S(2)}) collective-permute-start(bf16[320,128]{1,0:T(8,128)(2,1)} %get-tuple-element.21), channel_id=1, source_target_pairs={{2,0},{0,2},{6,4},{4,6},{10,8},{8,10},{14,12},{12,14},{3,1},{1,3},... | collective-permute-start | bytes 245768 | tf_op jit(solution)/shard_map/ppermute | solution.py:202
  10.1 0.6 %collective-permute-start.4 = (bf16[64,128]{1,0:T(8,128)(2,1)}, bf16[64,128]{1,0:T(8,128)(2,1)S(1)}, u32[]{:S(2)}, u32[]{:S(2)}) collective-permute-start(bf16[64,128]{1,0:T(8,128)(2,1)} %get-tuple-element.22), channel_id=1, source_target_pairs={{6,0},{4,2},{2,4},{0,6},{14,8},{12,10},{10,12},{8,14},{7,1},{5,3},... | collective-permute-start | bytes 49160 | tf_op jit(solution)/shard_map/ppermute | solution.py:202
  10.7 5.3 %collective-permute-done.4.refs_5_ = bf16[64,128]{1,0:T(8,128)(2,1)S(1)} collective-permute-done((bf16[64,128]{1,0:T(8,128)(2,1)}, bf16[64,128]{1,0:T(8,128)(2,1)S(1)}, u32[]{:S(2)}, u32[]{:S(2)}) %collective-permute-start.4) | collective-permute-done | bytes 16416 | tf_op jit(solution)/shard_map/ppermute | solution.py:202
  16.0 1.1 %collective-permute-start.5 = (bf16[64,128]{1,0:T(8,128)(2,1)}, bf16[64,128]{1,0:T(8,128)(2,1)S(1)}, u32[]{:S(2)}, u32[]{:S(2)}) collective-permute-start(bf16[64,128]{1,0:T(8,128)(2,1)} %get-tuple-element.23), channel_id=1, source_target_pairs={{10,0},{8,2},{14,4},{12,6},{2,8},{0,10},{6,12},{4,14},{11,1},{9,3}... | collective-permute-start | bytes 49160 | tf_op jit(solution)/shard_map/ppermute | solution.py:202
  17.1 4.7 %collective-permute-done.5.refs_6_ = bf16[64,128]{1,0:T(8,128)(2,1)S(1)} collective-permute-done((bf16[64,128]{1,0:T(8,128)(2,1)}, bf16[64,128]{1,0:T(8,128)(2,1)S(1)}, u32[]{:S(2)}, u32[]{:S(2)}) %collective-permute-start.5) | collective-permute-done | bytes 16416 | tf_op jit(solution)/shard_map/ppermute | solution.py:202
  21.8 2.7 %collective-permute-start.6 = (bf16[64,128]{1,0:T(8,128)(2,1)}, bf16[64,128]{1,0:T(8,128)(2,1)S(1)}, u32[]{:S(2)}, u32[]{:S(2)}) collective-permute-start(bf16[64,128]{1,0:T(8,128)(2,1)} %get-tuple-element.24), channel_id=1, source_target_pairs={{14,0},{12,2},{10,4},{8,6},{6,8},{4,10},{2,12},{0,14},{15,1},{13,3... | collective-permute-start | bytes 49160 | tf_op jit(solution)/shard_map/ppermute | solution.py:202
  24.5 3.9 %collective-permute-done.6.refs_7_ = bf16[64,128]{1,0:T(8,128)(2,1)S(1)} collective-permute-done((bf16[64,128]{1,0:T(8,128)(2,1)}, bf16[64,128]{1,0:T(8,128)(2,1)S(1)}, u32[]{:S(2)}, u32[]{:S(2)}) %collective-permute-start.6) | collective-permute-done | bytes 16416 | tf_op jit(solution)/shard_map/ppermute | solution.py:202
  28.4 0.0 collective-permute-done.3.refs_4_
  28.4 0.0 copy-start.2
  28.4 0.6 %copy-done.2 = f32[128]{0:T(128)S(1)} copy-done((f32[128]{0:T(128)S(1)}, f32[128]{0:T(128)}, u32[]{:S(2)}) %copy-start.2) | copy-done | bytes 536
  29.1 0.9 %copy-done.1 = bf16[320,128]{1,0:T(8,128)(2,1)S(1)} copy-done((bf16[320,128]{1,0:T(8,128)(2,1)S(1)}, bf16[320,128]{1,0:T(8,128)(2,1)}, u32[]{:S(2)}) %copy-start.1) | copy-done | bytes 81944
  30.0 1.0 %prepare.1 = (bf16[1024,64]{1,0:T(8,128)(2,1)S(1)}, bf16[128,1024]{1,0:T(8,128)(2,1)S(1)}, bf16[256,128]{1,0:T(8,128)(2,1)S(1)}, f32[1,128]{1,0:T(1,128)S(1)}) custom-call(bf16[1024,128]{1,0:T(8,128)(2,1)S(1)} %copy-done, f32[1,128]{1,0:T(1,128)S(1)} %bitcast.7, bf16[320,128]{1,0:T(8,128)(2,1)S(1)} %copy-done.1, ...), custom_call_target="tpu_custom_call" | custom-call | tf_op jit(solution)/shard_map/prepare/pallas_call | solution.py:117
  31.0 0.1 collective-permute-start.7
  31.0 0.1 collective-permute-start.8
  31.1 2.0 %collective-permute-start.9 = (bf16[256,128]{1,0:T(8,128)(2,1)S(1)}, bf16[256,128]{1,0:T(8,128)(2,1)S(1)}, u32[]{:S(2)}, u32[]{:S(2)}) collective-permute-start(bf16[256,128]{1,0:T(8,128)(2,1)S(1)} %slice.13), channel_id=1, source_target_pairs={{2,0},{0,2},{6,4},{4,6},{10,8},{8,10},{14,12},{12,14},{3,1},{1,3},... | collective-permute-start | bytes 196616 | tf_op jit(solution)/shard_map/ppermute | solution.py:202
  33.2 0.1 collective-permute-start.10
  33.2 2.8 %collective-permute-done.8.refs_5_ = bf16[256,128]{1,0:T(8,128)(2,1)S(1)} collective-permute-done((bf16[256,128]{1,0:T(8,128)(2,1)S(1)}, bf16[256,128]{1,0:T(8,128)(2,1)S(1)}, u32[]{:S(2)}, u32[]{:S(2)}) %collective-permute-start.8) | collective-permute-done | bytes 65568 | tf_op jit(solution)/shard_map/ppermute | solution.py:202
  36.0 1.4 %collective-permute-done.9.refs_6_ = bf16[256,128]{1,0:T(8,128)(2,1)S(1)} collective-permute-done((bf16[256,128]{1,0:T(8,128)(2,1)S(1)}, bf16[256,128]{1,0:T(8,128)(2,1)S(1)}, u32[]{:S(2)}, u32[]{:S(2)}) %collective-permute-start.9) | collective-permute-done | bytes 65568 | tf_op jit(solution)/shard_map/ppermute | solution.py:202
  37.4 0.9 %collective-permute-done.10.refs_7_ = bf16[256,128]{1,0:T(8,128)(2,1)S(1)} collective-permute-done((bf16[256,128]{1,0:T(8,128)(2,1)S(1)}, bf16[256,128]{1,0:T(8,128)(2,1)S(1)}, u32[]{:S(2)}, u32[]{:S(2)}) %collective-permute-start.10) | collective-permute-done | bytes 65568 | tf_op jit(solution)/shard_map/ppermute | solution.py:202
  38.4 0.0 collective-permute-done.7.other_ref
  38.4 5.2 %pairs.1 = bf16[32,128,128]{2,1,0:T(8,128)(2,1)} custom-call(bf16[1024,64]{1,0:T(8,128)(2,1)S(1)} %get-tuple-element.25.mine_ref, bf16[1024,64]{1,0:T(8,128)(2,1)S(1)} %collective-permute-done.7.other_ref, bf16[128,1024]{1,0:T(8,128)(2,1)S(1)} %get-tuple-element.26.weights_ref, f32[1,128]{1,0:T(1,128)S(1)} %get-tuple-element.27.bias_ref, ...), custom_call_target="tpu_custom_call" | custom-call | flops 1610612736 | bytes 1048576 | tf_op jit(solution)/shard_map/pairs/pallas_call | solution.py:170
  (10 shorter events, 0.0 us)
Async XLA Ops:
  0.0 28.4 %copy-start = (bf16[1024,128]{1,0:T(8,128)(2,1)S(1)}, bf16[1024,128]{1,0:T(8,128)(2,1)}, u32[]{:S(2)}) copy-start(bf16[1024,128]{1,0:T(8,128)(2,1)} %w_ref.1) | copy-start | bytes 786436
  2.7 25.7 %collective-permute-start = (bf16[320,128]{1,0:T(8,128)(2,1)}, bf16[320,128]{1,0:T(8,128)(2,1)S(1)}, u32[]{:S(2)}, u32[]{:S(2)}) collective-permute-start(bf16[320,128]{1,0:T(8,128)(2,1)} %get-tuple-element.18), channel_id=1, source_target_pairs={{4,0},{6,2},{0,4},{2,6},{12,8},{14,10},{8,12},{10,14},{5,1},{7,3},... | collective-permute-start | bytes 245768 | tf_op jit(solution)/shard_map/ppermute | solution.py:202
  5.7 22.7 %collective-permute-start.1 = (bf16[320,128]{1,0:T(8,128)(2,1)}, bf16[320,128]{1,0:T(8,128)(2,1)S(1)}, u32[]{:S(2)}, u32[]{:S(2)}) collective-permute-start(bf16[320,128]{1,0:T(8,128)(2,1)} %get-tuple-element.19), channel_id=1, source_target_pairs={{8,0},{10,2},{12,4},{14,6},{0,8},{2,10},{4,12},{6,14},{9,1},{11,3}... | collective-permute-start | bytes 245768 | tf_op jit(solution)/shard_map/ppermute | solution.py:202
  8.3 20.1 %collective-permute-start.2 = (bf16[320,128]{1,0:T(8,128)(2,1)}, bf16[320,128]{1,0:T(8,128)(2,1)S(1)}, u32[]{:S(2)}, u32[]{:S(2)}) collective-permute-start(bf16[320,128]{1,0:T(8,128)(2,1)} %get-tuple-element.20), channel_id=1, source_target_pairs={{12,0},{14,2},{8,4},{10,6},{4,8},{6,10},{0,12},{2,14},{13,1},{15,3... | collective-permute-start | bytes 245768 | tf_op jit(solution)/shard_map/ppermute | solution.py:202
  8.3 20.1 %collective-permute-start.3 = (bf16[320,128]{1,0:T(8,128)(2,1)}, bf16[320,128]{1,0:T(8,128)(2,1)S(1)}, u32[]{:S(2)}, u32[]{:S(2)}) collective-permute-start(bf16[320,128]{1,0:T(8,128)(2,1)} %get-tuple-element.21), channel_id=1, source_target_pairs={{2,0},{0,2},{6,4},{4,6},{10,8},{8,10},{14,12},{12,14},{3,1},{1,3},... | collective-permute-start | bytes 245768 | tf_op jit(solution)/shard_map/ppermute | solution.py:202
  10.1 5.9 %collective-permute-start.4 = (bf16[64,128]{1,0:T(8,128)(2,1)}, bf16[64,128]{1,0:T(8,128)(2,1)S(1)}, u32[]{:S(2)}, u32[]{:S(2)}) collective-permute-start(bf16[64,128]{1,0:T(8,128)(2,1)} %get-tuple-element.22), channel_id=1, source_target_pairs={{6,0},{4,2},{2,4},{0,6},{14,8},{12,10},{10,12},{8,14},{7,1},{5,3},... | collective-permute-start | bytes 49160 | tf_op jit(solution)/shard_map/ppermute | solution.py:202
  16.0 5.8 %collective-permute-start.5 = (bf16[64,128]{1,0:T(8,128)(2,1)}, bf16[64,128]{1,0:T(8,128)(2,1)S(1)}, u32[]{:S(2)}, u32[]{:S(2)}) collective-permute-start(bf16[64,128]{1,0:T(8,128)(2,1)} %get-tuple-element.23), channel_id=1, source_target_pairs={{10,0},{8,2},{14,4},{12,6},{2,8},{0,10},{6,12},{4,14},{11,1},{9,3}... | collective-permute-start | bytes 49160 | tf_op jit(solution)/shard_map/ppermute | solution.py:202
  21.8 6.6 %collective-permute-start.6 = (bf16[64,128]{1,0:T(8,128)(2,1)}, bf16[64,128]{1,0:T(8,128)(2,1)S(1)}, u32[]{:S(2)}, u32[]{:S(2)}) collective-permute-start(bf16[64,128]{1,0:T(8,128)(2,1)} %get-tuple-element.24), channel_id=1, source_target_pairs={{14,0},{12,2},{10,4},{8,6},{6,8},{4,10},{2,12},{0,14},{15,1},{13,3... | collective-permute-start | bytes 49160 | tf_op jit(solution)/shard_map/ppermute | solution.py:202
  28.4 0.7 %copy-start.2 = (f32[128]{0:T(128)S(1)}, f32[128]{0:T(128)}, u32[]{:S(2)}) copy-start(f32[128]{0:T(128)} %param.17) | copy-start | bytes 1540
  29.1 0.9 %copy-start.1 = (bf16[320,128]{1,0:T(8,128)(2,1)S(1)}, bf16[320,128]{1,0:T(8,128)(2,1)}, u32[]{:S(2)}) copy-start(bf16[320,128]{1,0:T(8,128)(2,1)} %get-tuple-element.17.refs_0_) | copy-start | bytes 245764
  31.0 7.4 %collective-permute-start.7 = (bf16[1024,64]{1,0:T(8,128)(2,1)S(1)}, bf16[1024,64]{1,0:T(8,128)(2,1)S(1)}, u32[]{:S(2)}, u32[]{:S(2)}) collective-permute-start(bf16[1024,64]{1,0:T(8,128)(2,1)S(1)} %get-tuple-element.25.mine_ref), channel_id=1, source_target_pairs={{0,1},{1,0},{2,3},{3,2},{4,5},{5,4},{6,7},{7,6},{8,9},{9,8},{10,11... | collective-permute-start | bytes 393224 | tf_op jit(solution)/shard_map/ppermute | solution.py:220
  31.0 5.0 %collective-permute-start.8 = (bf16[256,128]{1,0:T(8,128)(2,1)S(1)}, bf16[256,128]{1,0:T(8,128)(2,1)S(1)}, u32[]{:S(2)}, u32[]{:S(2)}) collective-permute-start(bf16[256,128]{1,0:T(8,128)(2,1)S(1)} %slice.12), channel_id=1, source_target_pairs={{2,0},{0,2},{6,4},{4,6},{10,8},{8,10},{14,12},{12,14},{3,1},{1,3},... | collective-permute-start | bytes 196616 | tf_op jit(solution)/shard_map/ppermute | solution.py:202
  31.1 6.3 %collective-permute-start.9 = (bf16[256,128]{1,0:T(8,128)(2,1)S(1)}, bf16[256,128]{1,0:T(8,128)(2,1)S(1)}, u32[]{:S(2)}, u32[]{:S(2)}) collective-permute-start(bf16[256,128]{1,0:T(8,128)(2,1)S(1)} %slice.13), channel_id=1, source_target_pairs={{2,0},{0,2},{6,4},{4,6},{10,8},{8,10},{14,12},{12,14},{3,1},{1,3},... | collective-permute-start | bytes 196616 | tf_op jit(solution)/shard_map/ppermute | solution.py:202
  33.2 5.2 %collective-permute-start.10 = (bf16[256,128]{1,0:T(8,128)(2,1)S(1)}, bf16[256,128]{1,0:T(8,128)(2,1)S(1)}, u32[]{:S(2)}, u32[]{:S(2)}) collective-permute-start(bf16[256,128]{1,0:T(8,128)(2,1)S(1)} %slice.14), channel_id=1, source_target_pairs={{2,0},{0,2},{6,4},{4,6},{10,8},{8,10},{14,12},{12,14},{3,1},{1,3},... | collective-permute-start | bytes 196616 | tf_op jit(solution)/shard_map/ppermute | solution.py:202

commit v8 on v6

--- a/solution.py
+++ b/solution.py
@@ -16,7 +16,8 @@
 
 
 def features_kernel(scale, x_ref, gain_ref, bias_ref, wl_ref, bl_ref, wr_ref, br_ref,
-                    left_ref, right_ref, normed_ref, left_f32, right_f32):
+                    *refs):
+    outs, (normed_ref, left_f32, right_f32) = refs[:-3], refs[-3:]
     seqs, width, channels = x_ref.shape
     c = wl_ref.shape[0]
     blocks = width // LANES
@@ -47,12 +48,12 @@
     total = (total + jnp.concatenate([bl_ref[...]] * fold, axis=1)) * scale
     for s in range(seqs):
         left_f32[pl.ds(s, quarter, stride=seqs), :] = total[s * quarter:(s + 1) * quarter]
-    along, _, rows, _ = left_ref.shape
-    across = lax.rem(lax.axis_index("row"), 2)
-    for n in range(along):
-        for b in range(2):
-            block = lax.rem(n * 2 + lax.rem(across + b, 2), left_f32.shape[0] // rows)
-            left_ref[n, b] = left_f32[pl.ds(pl.multiple_of(block * rows, rows), rows), :].astype(jnp.bfloat16)
+    right_ref, *left_refs = outs
+    here = lax.axis_index("row")
+    for step, left_ref in zip(half_steps(len(left_refs)), left_refs):
+        rows = left_ref.shape[0]
+        block = source_at(here, step) % len(left_refs)
+        left_ref[...] = left_f32[pl.ds(pl.multiple_of(block * rows, rows), rows), :].astype(jnp.bfloat16)
     right_ref[...] = right_f32[...].astype(jnp.bfloat16)
 
 
@@ -60,7 +61,8 @@
     seqs, width, channels = alignment.shape
     c = w_left.shape[1]
     rows = seqs * width * c // LANES
-    shapes = ((row_count // 2, 2, rows * col_count // row_count, LANES), (rows, LANES))
+    chips = row_count // col_count
+    shapes = [(rows, LANES)] + [(rows // chips, LANES)] * chips
     operands = (alignment, ln_gain.reshape(1, -1), ln_bias.reshape(1, -1), w_left.T, b_left.reshape(1, -1),
                 w_right.T, b_right.reshape(1, -1))
     return pl.pallas_call(
@@ -89,16 +91,17 @@
         [flat[pl.ds(m * seqs + s, sources, stride=inner * seqs), :] for s in range(seqs)], axis=0)
 
 
-def prepare_kernel(seqs, c, col_count, steps, mine_ref, other_ref, w_ref, own_ref,
-                   left_ref, weights_ref, right_ref, left_f32, w_f32):
-    sources, left_rows, _ = mine_ref.shape
-    along = sources // 2
-    here, core = lax.axis_index("row"), lax.axis_index("col")
-    mine = here // (sources // col_count) == core
+def prepare_kernel(seqs, c, mine_ref, other_ref, w_ref, bias_ref, own_right_ref,
+                   left_ref, weights_ref, right_ref, bias_out_ref, left_f32, w_f32):
+    sources, left_rows, _ = left_f32.shape
+    chips = sources // 2
+    same_half = lax.axis_index("row") // chips == lax.axis_index("col")
 
     def block(n):
-        source = steps[n][1] * along + source_at(here, steps[n], sources) // 2
-        return jnp.where(mine, mine_ref[source].astype(jnp.float32), other_ref[source].astype(jnp.float32))
+        first = n % chips * left_rows
+        mine = mine_ref[first:first + left_rows].astype(jnp.float32)
+        other = other_ref[first:first + left_rows].astype(jnp.float32)
+        return jnp.where(same_half == (n < chips), mine, other)
 
     left_of = sequence_rows(block, left_f32, left_rows // seqs, seqs)
     for k in range(left_rows // seqs):
@@ -106,20 +109,23 @@
     w_f32[...] = w_ref[...].astype(jnp.float32)
     for e in range(c):
         weights_ref[:, e * c:(e + 1) * c] = w_f32[pl.ds(e, c, stride=c), :].T.astype(jnp.bfloat16)
-    right_ref[...] = own_ref[...]
-
-
-def prepare(mine, other, w_out, right, steps, seqs, c, col_count):
-    sources, left_rows, _ = mine.shape
-    shapes = ((left_rows // seqs * LANES, sources * seqs), (w_out.shape[1], w_out.shape[0]), right.shape)
-    operands = (mine, other, w_out, right)
+    right_ref[...] = own_right_ref[...]
+    bias_out_ref[...] = bias_ref[...]
+
+
+def prepare(mine, other, w_out, b_out, right, sources, seqs, c):
+    left_rows = mine.shape[0] * 2 // sources
+    z = w_out.shape[1]
+    outs = [((left_rows // seqs * LANES, sources * seqs), jnp.bfloat16), ((z, w_out.shape[0]), jnp.bfloat16),
+            (right.shape, jnp.bfloat16), ((1, z), jnp.float32)]
+    operands = (mine, other, w_out, b_out.reshape(1, -1), right)
     return pl.pallas_call(
-        functools.partial(prepare_kernel, seqs, c, col_count, steps),
+        functools.partial(prepare_kernel, seqs, c),
         grid=(1,),
-        out_shape=[jax.ShapeDtypeStruct(shape, jnp.bfloat16) for shape in shapes],
+        out_shape=[jax.ShapeDtypeStruct(*out) for out in outs],
         in_specs=[whole(a.shape) for a in operands],
-        out_specs=[whole(shape) for shape in shapes],
-        scratch_shapes=[pltpu.VMEM(mine.shape, jnp.float32), pltpu.VMEM(w_out.shape, jnp.float32)],
+        out_specs=[whole(out[0]) for out in outs],
+        scratch_shapes=[pltpu.VMEM((sources, left_rows, LANES), jnp.float32), pltpu.VMEM(w_out.shape, jnp.float32)],
         compiler_params=pltpu.CompilerParams(vmem_limit_bytes=48 * 1024 * 1024),
         name="prepare",
     )(*operands)
@@ -163,7 +169,7 @@
     rows = left.shape[0] // c
     rows_step = 8
     total = sources * seqs
-    operands = (left, weights, bias.reshape(1, -1), *rights)
+    operands = (left, weights, bias, *rights)
     return pl.pallas_call(
         functools.partial(pair_kernel, seqs, c, sources),
         grid=(rows // rows_step,),
@@ -180,15 +186,26 @@
     )(*operands)
 
 
-def source_at(here, step, count):
-    along = count // 2
-    n, across = here // 2, here % 2
-    n = (n ^ step[0]) if along & (along - 1) == 0 else (n + step[0]) % along
-    return n * 2 + (across + step[1]) % 2
+def source_at(here, step):
+    return here ^ (2 * step[0] + step[1])
+
+
+def half_steps(chips):
+    return [(a, b) for b in range(2) for a in range(chips // 2)]
 
 
 def fetch(array, step, count):
-    return lax.ppermute(array, "row", [(source_at(r, step, count), r) for r in range(count)])
+    return lax.ppermute(array, "row", [(source_at(r, step), r) for r in range(count)])
+
+
+def fetch_left(array, step, count):
+    chips = count // 2
+    moves = []
+    for r in range(count):
+        for core in range(2):
+            to = source_at(r % chips, step) + core * chips
+            moves.append((2 * r + core, 2 * to + (core if r // chips == core else 1 - core)))
+    return lax.ppermute(array, ("row", "col"), moves)
 
 
 def on_device(alignment, ln_gain, ln_bias, w_left, b_left, w_right, b_right, w_out, b_out):
@@ -196,22 +213,17 @@
     c = w_left.shape[1]
     row_count = lax.axis_size("row")
     col_count = lax.axis_size("col")
-    along = row_count // 2
-    left, right = features(alignment, ln_gain, ln_bias, w_left, b_left, w_right, b_right, row_count, col_count)
-
-    lines = [list(range(y, row_count, 2)) for y in range(2)]
-    left = lax.all_to_all(left, "row", split_axis=0, concat_axis=0, axis_index_groups=lines, tiled=True)
-    mine = jnp.concatenate([left[:, 0], fetch(left[:, 1], (0, 1), row_count)])
-    other = lax.ppermute(mine, "col", [(i, (i + 1) % col_count) for i in range(col_count)])
-
-    near = {0: right}
-    for a in reversed(range(1, along)):
-        near[a] = fetch(right, (a, 0), row_count)
-    far = {a: fetch(near[a], (0, 1), row_count) for a in near}
-    steps = [(a, b) for b in range(2) for a in near]
-    left, weights, right = prepare(mine, other, w_out, right, steps, seqs, c, col_count)
-    near[0] = right
-    return pairs(left, weights, b_out, [*near.values(), *far.values()], seqs, c, width)
+    right, *lefts = features(alignment, ln_gain, ln_bias, w_left, b_left, w_right, b_right, row_count, col_count)
+    chips = row_count // 2
+    along = chips
+
+    near = [right] + [fetch(right, (a, 0), row_count) for a in range(1, along)]
+    far = [fetch(block, (0, 1), row_count) for block in near]
+    mine = jnp.concatenate([fetch_left(left, step, row_count) for step, left in zip(half_steps(chips), lefts)])
+    other = lax.ppermute(mine, "col", [(0, 1), (1, 0)])
+    left, weights, near[0], bias = prepare(mine, other, w_out, b_out, right, row_count, seqs, c)
+    rights = [(near, far)[b][half * (along // 2) + a] for half in range(2) for a, b in half_steps(chips)]
+    return pairs(left, weights, bias, rights, seqs, c, width)
 
 
 def solution(mesh):

time: 40.9 us -> 37.1 us (0.907)
  blocking collectives: 12.4 us -> 0 us
  starting transfers between devices: 10.1 us -> 20.2 us
  local copies, waits for them, and re-layouts: 1.41 us -> 0.04 us
    all_to_all x1 -> x0, blocking collectives: 12.4 us -> none  [on_device(): lax.all_to_all(left, 'row', split_axis=0, concat_axis=0, axis_index_group...]
    ppermute x9 -> x12, starting transfers between devices: 10.1 us -> 20.2 us  [the longest x7 10.4 us: fetch(): lax.ppermute(array, 'row', [(source_at(r, step), r) for r in range(count)])]
    unnamed x6 -> x11, local copies, waits for them, and re-layouts: 1.4 us -> 0.03 us
    ppermute x9 -> x12, waiting for transfers between devices: 8.06 us -> 7.9 us  [the longest x4 4.48 us: fetch_left(): return lax.ppermute(array, ('row', 'col'), moves)]
  transfers between devices with their start and end apart: 9 -> 12, of which waited for: 4 -> 5; matrix products, arithmetic and copies ran while one was open for 0% -> 0% of each run, Pallas kernels for 2% -> 3%
where the time goes in v8:
time: 37.1 us; the launch traced here: 36.8 us
  starting transfers between devices  20.2 us (54%)
  Pallas kernels  8.59 us (23%)
  waiting for transfers between devices  7.9 us (21%)
    ppermute x7, starting transfers between devices, fetch(): lax.ppermute(array, 'row', [(source_at(r, step), r) for r in range(count)])  10.4 us
    ppermute x4, starting transfers between devices, fetch_left(): return lax.ppermute(array, ('row', 'col'), moves)  6.79 us
    pallas_call x1, Pallas kernels, pairs(): pl.pallas_call(functools.partial(pair_kernel, seqs, c, sources), grid=(ro...  5.08 us
    ppermute x4, waiting for transfers between devices, fetch_left(): return lax.ppermute(array, ('row', 'col'), moves)  4.48 us
    ppermute x7, waiting for transfers between devices, fetch(): lax.ppermute(array, 'row', [(source_at(r, step), r) for r in range(count)])  3.42 us
    ppermute x1, starting transfers between devices, on_device(): other = lax.ppermute(mine, 'col', [(0, 1), (1, 0)])  3.09 us
    pallas_call x1, Pallas kernels, features(): pl.pallas_call(functools.partial(features_kernel, 1.0 / (seqs * row_count...  2.53 us
    pallas_call x1, Pallas kernels, prepare(): pl.pallas_call(functools.partial(prepare_kernel, seqs, c), grid=(1,), out...  0.99 us
  transfers between devices with their start and end apart: 12, of which 5 were waited for; matrix products, arithmetic and copies ran while one was open for 0% of the time, Pallas kernels for 3%

profile of v8, /device:TPU:0, one launch (start us, length us, event | category | flops | bytes accessed | tf_op | source)
XLA Modules:
  0.0 36.8 jit_solution(13270179802534310332)
XLA Ops:
  0.0 2.5 %features.1 = (bf16[256,128]{1,0:T(8,128)(2,1)}, bf16[64,128]{1,0:T(8,128)(2,1)}, bf16[64,128]{1,0:T(8,128)(2,1)}, bf16[64,128]{1,0:T(8,128)(2,1)}, bf16[64,128]{1,0:T(8,128)(2,1)}) custom-call(bf16[8,128,256]{2,1,0:T(8,128)(2,1)} %x_ref.1, f32[1,256]{1,0:T(1,128)} %bitcast.10, f32[1,256]{1,0:T(1,128)} %bitcast.11, bf16[32,256]{1,0:T(8,128)(2,1)} %bitcast.8, ...), custom_call_target="tpu_custom_call" | custom-call | tf_op jit(solution)/shard_map/features/pallas_call | solution.py:68
  2.5 1.4 %collective-permute-start = (bf16[64,128]{1,0:T(8,128)(2,1)}, bf16[64,128]{1,0:T(8,128)(2,1)S(1)}, u32[]{:S(2)}, u32[]{:S(2)}) collective-permute-start(bf16[64,128]{1,0:T(8,128)(2,1)} %get-tuple-element.14), channel_id=1, source_target_pairs={{0,0},{1,8},{2,2},{3,10},{4,4},{5,12},{6,6},{7,14},{8,1},{9,9},{10... | collective-permute-start | bytes 49160 | tf_op jit(solution)/shard_map/ppermute | solution.py:208
  3.9 5.7 %collective-permute-start.9 = (bf16[256,128]{1,0:T(8,128)(2,1)}, bf16[256,128]{1,0:T(8,128)(2,1)S(1)}, u32[]{:S(2)}, u32[]{:S(2)}) collective-permute-start(bf16[256,128]{1,0:T(8,128)(2,1)} %get-tuple-element.18.own_right_ref), channel_id=1, source_target_pairs={{12,0},{14,2},{8,4},{10,6},{4,8},{6,10},{0,12},{2,14},{13,1},{15,3... | collective-permute-start | bytes 196616 | tf_op jit(solution)/shard_map/ppermute | solution.py:198
  9.6 0.0 collective-permute-start.8
  9.6 0.6 %collective-permute-start.5 = (bf16[256,128]{1,0:T(8,128)(2,1)}, bf16[256,128]{1,0:T(8,128)(2,1)S(1)}, u32[]{:S(2)}, u32[]{:S(2)}) collective-permute-start(bf16[256,128]{1,0:T(8,128)(2,1)} %get-tuple-element.18.own_right_ref), channel_id=1, source_target_pairs={{4,0},{6,2},{0,4},{2,6},{12,8},{14,10},{8,12},{10,14},{5,1},{7,3},... | collective-permute-start | bytes 196616 | tf_op jit(solution)/shard_map/ppermute | solution.py:198
  10.2 1.4 %collective-permute-start.1 = (bf16[64,128]{1,0:T(8,128)(2,1)}, bf16[64,128]{1,0:T(8,128)(2,1)S(1)}, u32[]{:S(2)}, u32[]{:S(2)}) collective-permute-start(bf16[64,128]{1,0:T(8,128)(2,1)} %get-tuple-element.15), channel_id=1, source_target_pairs={{0,4},{1,12},{2,6},{3,14},{4,0},{5,8},{6,2},{7,10},{8,5},{9,13},{1... | collective-permute-start | bytes 49160 | tf_op jit(solution)/shard_map/ppermute | solution.py:208
  11.6 0.0 collective-permute-done
  11.6 1.5 %collective-permute-start.2 = (bf16[64,128]{1,0:T(8,128)(2,1)}, bf16[64,128]{1,0:T(8,128)(2,1)S(1)}, u32[]{:S(2)}, u32[]{:S(2)}) collective-permute-start(bf16[64,128]{1,0:T(8,128)(2,1)} %get-tuple-element.16), channel_id=1, source_target_pairs={{0,2},{1,10},{2,0},{3,8},{4,6},{5,14},{6,4},{7,12},{8,3},{9,11},{1... | collective-permute-start | bytes 49160 | tf_op jit(solution)/shard_map/ppermute | solution.py:208
  13.1 2.4 %collective-permute-done.1 = bf16[64,128]{1,0:T(8,128)(2,1)S(1)} collective-permute-done((bf16[64,128]{1,0:T(8,128)(2,1)}, bf16[64,128]{1,0:T(8,128)(2,1)S(1)}, u32[]{:S(2)}, u32[]{:S(2)}) %collective-permute-start.1) | collective-permute-done | bytes 16416 | tf_op jit(solution)/shard_map/ppermute | solution.py:208
  15.5 2.5 %collective-permute-start.3 = (bf16[64,128]{1,0:T(8,128)(2,1)S(1)}, bf16[64,128]{1,0:T(8,128)(2,1)S(1)}, u32[]{:S(2)}, u32[]{:S(2)}) collective-permute-start(bf16[64,128]{1,0:T(8,128)(2,1)S(1)} %copy-done.3), channel_id=1, source_target_pairs={{0,6},{1,14},{2,4},{3,12},{4,2},{5,10},{6,0},{7,8},{8,7},{9,15},{1... | collective-permute-start | bytes 49160 | tf_op jit(solution)/shard_map/ppermute | solution.py:208
  18.0 0.0 collective-permute-done.2
  18.1 2.1 %collective-permute-done.3 = bf16[64,128]{1,0:T(8,128)(2,1)S(1)} collective-permute-done((bf16[64,128]{1,0:T(8,128)(2,1)S(1)}, bf16[64,128]{1,0:T(8,128)(2,1)S(1)}, u32[]{:S(2)}, u32[]{:S(2)}) %collective-permute-start.3) | collective-permute-done | bytes 16416 | tf_op jit(solution)/shard_map/ppermute | solution.py:208
  20.2 3.1 %collective-permute-start.4 = (bf16[256,128]{1,0:T(8,128)(2,1)S(1)}, bf16[256,128]{1,0:T(8,128)(2,1)S(1)}, u32[]{:S(2)}, u32[]{:S(2)}) collective-permute-start(bf16[256,128]{1,0:T(8,128)(2,1)S(1)} %constant_dynamic-update-slice_fusion.mine_ref), channel_id=1, source_target_pairs={{0,1},{1,0},{2,3},{3,2},{4,5},{5,4},{6,7},{7,6},{8,9},{9,8},{10,11... | collective-permute-start | bytes 196616 | tf_op jit(solution)/shard_map/ppermute | solution.py:223
  23.3 1.5 %collective-permute-start.6 = (bf16[256,128]{1,0:T(8,128)(2,1)S(1)}, bf16[256,128]{1,0:T(8,128)(2,1)S(1)}, u32[]{:S(2)}, u32[]{:S(2)}) collective-permute-start(bf16[256,128]{1,0:T(8,128)(2,1)S(1)} %copy-done.1), channel_id=1, source_target_pairs={{2,0},{0,2},{6,4},{4,6},{10,8},{8,10},{14,12},{12,14},{3,1},{1,3},... | collective-permute-start | bytes 196616 | tf_op jit(solution)/shard_map/ppermute | solution.py:198
  24.8 0.5 %collective-permute-start.11 = (bf16[256,128]{1,0:T(8,128)(2,1)S(1)}, bf16[256,128]{1,0:T(8,128)(2,1)S(1)}, u32[]{:S(2)}, u32[]{:S(2)}) collective-permute-start(bf16[256,128]{1,0:T(8,128)(2,1)S(1)} %collective-permute-done.9.refs_5_), channel_id=1, source_target_pairs={{2,0},{0,2},{6,4},{4,6},{10,8},{8,10},{14,12},{12,14},{3,1},{1,3},... | collective-permute-start | bytes 196616 | tf_op jit(solution)/shard_map/ppermute | solution.py:198
  25.3 0.0 collective-permute-done.8.refs_4_
  25.3 1.5 %collective-permute-start.10 = (bf16[256,128]{1,0:T(8,128)(2,1)S(1)}, bf16[256,128]{1,0:T(8,128)(2,1)S(1)}, u32[]{:S(2)}, u32[]{:S(2)}) collective-permute-start(bf16[256,128]{1,0:T(8,128)(2,1)S(1)} %collective-permute-done.8.refs_4_), channel_id=1, source_target_pairs={{2,0},{0,2},{6,4},{4,6},{10,8},{8,10},{14,12},{12,14},{3,1},{1,3},... | collective-permute-start | bytes 196616 | tf_op jit(solution)/shard_map/ppermute | solution.py:198
  26.8 0.0 collective-permute-done.5.refs_1_
  26.8 0.5 %collective-permute-start.7 = (bf16[256,128]{1,0:T(8,128)(2,1)S(1)}, bf16[256,128]{1,0:T(8,128)(2,1)S(1)}, u32[]{:S(2)}, u32[]{:S(2)}) collective-permute-start(bf16[256,128]{1,0:T(8,128)(2,1)S(1)} %collective-permute-done.5.refs_1_), channel_id=1, source_target_pairs={{2,0},{0,2},{6,4},{4,6},{10,8},{8,10},{14,12},{12,14},{3,1},{1,3},... | collective-permute-start | bytes 196616 | tf_op jit(solution)/shard_map/ppermute | solution.py:198
  27.3 1.0 %prepare.1 = (bf16[1024,64]{1,0:T(8,128)(2,1)S(1)}, bf16[128,1024]{1,0:T(8,128)(2,1)S(1)}, bf16[256,128]{1,0:T(8,128)(2,1)S(1)}, f32[1,128]{1,0:T(1,128)S(1)}) custom-call(bf16[256,128]{1,0:T(8,128)(2,1)S(1)} %constant_dynamic-update-slice_fusion.mine_ref, bf16[256,128]{1,0:T(8,128)(2,1)S(1)} %collective-permute-done.4.other_ref, ...), custom_call_target="tpu_custom_call" | custom-call | tf_op jit(solution)/shard_map/prepare/pallas_call | solution.py:122
  28.3 1.4 %collective-permute-done.11.refs_7_ = bf16[256,128]{1,0:T(8,128)(2,1)S(1)} collective-permute-done((bf16[256,128]{1,0:T(8,128)(2,1)S(1)}, bf16[256,128]{1,0:T(8,128)(2,1)S(1)}, u32[]{:S(2)}, u32[]{:S(2)}) %collective-permute-start.11) | collective-permute-done | bytes 65568 | tf_op jit(solution)/shard_map/ppermute | solution.py:198
  29.8 1.3 %collective-permute-done.10.refs_6_ = bf16[256,128]{1,0:T(8,128)(2,1)S(1)} collective-permute-done((bf16[256,128]{1,0:T(8,128)(2,1)S(1)}, bf16[256,128]{1,0:T(8,128)(2,1)S(1)}, u32[]{:S(2)}, u32[]{:S(2)}) %collective-permute-start.10) | collective-permute-done | bytes 65568 | tf_op jit(solution)/shard_map/ppermute | solution.py:198
  31.0 0.7 %collective-permute-done.7.refs_3_ = bf16[256,128]{1,0:T(8,128)(2,1)S(1)} collective-permute-done((bf16[256,128]{1,0:T(8,128)(2,1)S(1)}, bf16[256,128]{1,0:T(8,128)(2,1)S(1)}, u32[]{:S(2)}, u32[]{:S(2)}) %collective-permute-start.7) | collective-permute-done | bytes 65568 | tf_op jit(solution)/shard_map/ppermute | solution.py:198
  31.7 5.1 %pairs.1 = bf16[32,128,128]{2,1,0:T(8,128)(2,1)} custom-call(bf16[1024,64]{1,0:T(8,128)(2,1)S(1)} %get-tuple-element.19.left_ref, bf16[128,1024]{1,0:T(8,128)(2,1)S(1)} %get-tuple-element.20.weights_ref, f32[1,128]{1,0:T(1,128)S(1)} %get-tuple-element.21.bias_ref, bf16[256,128]{1,0:T(8,128)(2,1)S(1)} %get-tuple-element.22.refs_0_, ...), custom_call_target="tpu_custom_call" | custom-call | flops 1610612736 | bytes 1048576 | tf_op jit(solution)/shard_map/pairs/pallas_call | solution.py:173
  (15 shorter events, 0.0 us)
Async XLA Ops:
  0.0 27.3 %copy-start = (bf16[1024,128]{1,0:T(8,128)(2,1)S(1)}, bf16[1024,128]{1,0:T(8,128)(2,1)}, u32[]{:S(2)}) copy-start(bf16[1024,128]{1,0:T(8,128)(2,1)} %w_ref.1) | copy-start | bytes 786436
  2.5 9.1 %collective-permute-start = (bf16[64,128]{1,0:T(8,128)(2,1)}, bf16[64,128]{1,0:T(8,128)(2,1)S(1)}, u32[]{:S(2)}, u32[]{:S(2)}) collective-permute-start(bf16[64,128]{1,0:T(8,128)(2,1)} %get-tuple-element.14), channel_id=1, source_target_pairs={{0,0},{1,8},{2,2},{3,10},{4,4},{5,12},{6,6},{7,14},{8,1},{9,9},{10... | collective-permute-start | bytes 49160 | tf_op jit(solution)/shard_map/ppermute | solution.py:208
  3.9 20.9 %collective-permute-start.9 = (bf16[256,128]{1,0:T(8,128)(2,1)}, bf16[256,128]{1,0:T(8,128)(2,1)S(1)}, u32[]{:S(2)}, u32[]{:S(2)}) collective-permute-start(bf16[256,128]{1,0:T(8,128)(2,1)} %get-tuple-element.18.own_right_ref), channel_id=1, source_target_pairs={{12,0},{14,2},{8,4},{10,6},{4,8},{6,10},{0,12},{2,14},{13,1},{15,3... | collective-permute-start | bytes 196616 | tf_op jit(solution)/shard_map/ppermute | solution.py:198
  9.6 15.7 %collective-permute-start.8 = (bf16[256,128]{1,0:T(8,128)(2,1)}, bf16[256,128]{1,0:T(8,128)(2,1)S(1)}, u32[]{:S(2)}, u32[]{:S(2)}) collective-permute-start(bf16[256,128]{1,0:T(8,128)(2,1)} %get-tuple-element.18.own_right_ref), channel_id=1, source_target_pairs={{8,0},{10,2},{12,4},{14,6},{0,8},{2,10},{4,12},{6,14},{9,1},{11,3}... | collective-permute-start | bytes 196616 | tf_op jit(solution)/shard_map/ppermute | solution.py:198
  9.6 17.2 %collective-permute-start.5 = (bf16[256,128]{1,0:T(8,128)(2,1)}, bf16[256,128]{1,0:T(8,128)(2,1)S(1)}, u32[]{:S(2)}, u32[]{:S(2)}) collective-permute-start(bf16[256,128]{1,0:T(8,128)(2,1)} %get-tuple-element.18.own_right_ref), channel_id=1, source_target_pairs={{4,0},{6,2},{0,4},{2,6},{12,8},{14,10},{8,12},{10,14},{5,1},{7,3},... | collective-permute-start | bytes 196616 | tf_op jit(solution)/shard_map/ppermute | solution.py:198
  10.2 5.3 %collective-permute-start.1 = (bf16[64,128]{1,0:T(8,128)(2,1)}, bf16[64,128]{1,0:T(8,128)(2,1)S(1)}, u32[]{:S(2)}, u32[]{:S(2)}) collective-permute-start(bf16[64,128]{1,0:T(8,128)(2,1)} %get-tuple-element.15), channel_id=1, source_target_pairs={{0,4},{1,12},{2,6},{3,14},{4,0},{5,8},{6,2},{7,10},{8,5},{9,13},{1... | collective-permute-start | bytes 49160 | tf_op jit(solution)/shard_map/ppermute | solution.py:208
  11.6 3.9 %copy-start.3 = (bf16[64,128]{1,0:T(8,128)(2,1)S(1)}, bf16[64,128]{1,0:T(8,128)(2,1)}, u32[]{:S(2)}) copy-start(bf16[64,128]{1,0:T(8,128)(2,1)} %get-tuple-element.17) | copy-start | bytes 49156
  11.6 11.6 %copy-start.1 = (bf16[256,128]{1,0:T(8,128)(2,1)S(1)}, bf16[256,128]{1,0:T(8,128)(2,1)}, u32[]{:S(2)}) copy-start(bf16[256,128]{1,0:T(8,128)(2,1)} %get-tuple-element.18.own_right_ref) | copy-start | bytes 196612
  11.6 6.4 %collective-permute-start.2 = (bf16[64,128]{1,0:T(8,128)(2,1)}, bf16[64,128]{1,0:T(8,128)(2,1)S(1)}, u32[]{:S(2)}, u32[]{:S(2)}) collective-permute-start(bf16[64,128]{1,0:T(8,128)(2,1)} %get-tuple-element.16), channel_id=1, source_target_pairs={{0,2},{1,10},{2,0},{3,8},{4,6},{5,14},{6,4},{7,12},{8,3},{9,11},{1... | collective-permute-start | bytes 49160 | tf_op jit(solution)/shard_map/ppermute | solution.py:208
  15.5 4.6 %collective-permute-start.3 = (bf16[64,128]{1,0:T(8,128)(2,1)S(1)}, bf16[64,128]{1,0:T(8,128)(2,1)S(1)}, u32[]{:S(2)}, u32[]{:S(2)}) collective-permute-start(bf16[64,128]{1,0:T(8,128)(2,1)S(1)} %copy-done.3), channel_id=1, source_target_pairs={{0,6},{1,14},{2,4},{3,12},{4,2},{5,10},{6,0},{7,8},{8,7},{9,15},{1... | collective-permute-start | bytes 49160 | tf_op jit(solution)/shard_map/ppermute | solution.py:208
  20.2 7.2 %copy-start.2 = (f32[128]{0:T(128)S(1)}, f32[128]{0:T(128)}, u32[]{:S(2)}) copy-start(f32[128]{0:T(128)} %param.17) | copy-start | bytes 1540
  20.2 7.2 %collective-permute-start.4 = (bf16[256,128]{1,0:T(8,128)(2,1)S(1)}, bf16[256,128]{1,0:T(8,128)(2,1)S(1)}, u32[]{:S(2)}, u32[]{:S(2)}) collective-permute-start(bf16[256,128]{1,0:T(8,128)(2,1)S(1)} %constant_dynamic-update-slice_fusion.mine_ref), channel_id=1, source_target_pairs={{0,1},{1,0},{2,3},{3,2},{4,5},{5,4},{6,7},{7,6},{8,9},{9,8},{10,11... | collective-permute-start | bytes 196616 | tf_op jit(solution)/shard_map/ppermute | solution.py:223
  23.3 5.1 %collective-permute-start.6 = (bf16[256,128]{1,0:T(8,128)(2,1)S(1)}, bf16[256,128]{1,0:T(8,128)(2,1)S(1)}, u32[]{:S(2)}, u32[]{:S(2)}) collective-permute-start(bf16[256,128]{1,0:T(8,128)(2,1)S(1)} %copy-done.1), channel_id=1, source_target_pairs={{2,0},{0,2},{6,4},{4,6},{10,8},{8,10},{14,12},{12,14},{3,1},{1,3},... | collective-permute-start | bytes 196616 | tf_op jit(solution)/shard_map/ppermute | solution.py:198
  24.8 5.0 %collective-permute-start.11 = (bf16[256,128]{1,0:T(8,128)(2,1)S(1)}, bf16[256,128]{1,0:T(8,128)(2,1)S(1)}, u32[]{:S(2)}, u32[]{:S(2)}) collective-permute-start(bf16[256,128]{1,0:T(8,128)(2,1)S(1)} %collective-permute-done.9.refs_5_), channel_id=1, source_target_pairs={{2,0},{0,2},{6,4},{4,6},{10,8},{8,10},{14,12},{12,14},{3,1},{1,3},... | collective-permute-start | bytes 196616 | tf_op jit(solution)/shard_map/ppermute | solution.py:198
  25.3 5.7 %collective-permute-start.10 = (bf16[256,128]{1,0:T(8,128)(2,1)S(1)}, bf16[256,128]{1,0:T(8,128)(2,1)S(1)}, u32[]{:S(2)}, u32[]{:S(2)}) collective-permute-start(bf16[256,128]{1,0:T(8,128)(2,1)S(1)} %collective-permute-done.8.refs_4_), channel_id=1, source_target_pairs={{2,0},{0,2},{6,4},{4,6},{10,8},{8,10},{14,12},{12,14},{3,1},{1,3},... | collective-permute-start | bytes 196616 | tf_op jit(solution)/shard_map/ppermute | solution.py:198
  26.8 4.9 %collective-permute-start.7 = (bf16[256,128]{1,0:T(8,128)(2,1)S(1)}, bf16[256,128]{1,0:T(8,128)(2,1)S(1)}, u32[]{:S(2)}, u32[]{:S(2)}) collective-permute-start(bf16[256,128]{1,0:T(8,128)(2,1)S(1)} %collective-permute-done.5.refs_1_), channel_id=1, source_target_pairs={{2,0},{0,2},{6,4},{4,6},{10,8},{8,10},{14,12},{12,14},{3,1},{1,3},... | collective-permute-start | bytes 196616 | tf_op jit(solution)/shard_map/ppermute | solution.py:198

commit v9 on v8

--- a/solution.py
+++ b/solution.py
@@ -16,8 +16,7 @@
 
 
 def features_kernel(scale, x_ref, gain_ref, bias_ref, wl_ref, bl_ref, wr_ref, br_ref,
-                    *refs):
-    outs, (normed_ref, left_f32, right_f32) = refs[:-3], refs[-3:]
+                    left_ref, right_ref, normed_ref, left_f32, right_f32):
     seqs, width, channels = x_ref.shape
     c = wl_ref.shape[0]
     blocks = width // LANES
@@ -48,12 +47,9 @@
     total = (total + jnp.concatenate([bl_ref[...]] * fold, axis=1)) * scale
     for s in range(seqs):
         left_f32[pl.ds(s, quarter, stride=seqs), :] = total[s * quarter:(s + 1) * quarter]
-    right_ref, *left_refs = outs
-    here = lax.axis_index("row")
-    for step, left_ref in zip(half_steps(len(left_refs)), left_refs):
-        rows = left_ref.shape[0]
-        block = source_at(here, step) % len(left_refs)
-        left_ref[...] = left_f32[pl.ds(pl.multiple_of(block * rows, rows), rows), :].astype(jnp.bfloat16)
+    left = left_f32[...].astype(jnp.bfloat16)
+    for copy in range(left_ref.shape[0]):
+        left_ref[copy] = left
     right_ref[...] = right_f32[...].astype(jnp.bfloat16)
 
 
@@ -61,8 +57,7 @@
     seqs, width, channels = alignment.shape
     c = w_left.shape[1]
     rows = seqs * width * c // LANES
-    chips = row_count // col_count
-    shapes = [(rows, LANES)] + [(rows // chips, LANES)] * chips
+    shapes = ((col_count, rows, LANES), (rows, LANES))
     operands = (alignment, ln_gain.reshape(1, -1), ln_bias.reshape(1, -1), w_left.T, b_left.reshape(1, -1),
                 w_right.T, b_right.reshape(1, -1))
     return pl.pallas_call(
@@ -91,17 +86,15 @@
         [flat[pl.ds(m * seqs + s, sources, stride=inner * seqs), :] for s in range(seqs)], axis=0)
 
 
-def prepare_kernel(seqs, c, mine_ref, other_ref, w_ref, bias_ref, own_right_ref,
+def prepare_kernel(seqs, c, steps, mine_ref, other_ref, w_ref, bias_ref, own_right_ref,
                    left_ref, weights_ref, right_ref, bias_out_ref, left_f32, w_f32):
     sources, left_rows, _ = left_f32.shape
-    chips = sources // 2
-    same_half = lax.axis_index("row") // chips == lax.axis_index("col")
+    here = lax.axis_index("row")
+    same_half = here // (sources // 2) == lax.axis_index("col")
 
     def block(n):
-        first = n % chips * left_rows
-        mine = mine_ref[first:first + left_rows].astype(jnp.float32)
-        other = other_ref[first:first + left_rows].astype(jnp.float32)
-        return jnp.where(same_half == (n < chips), mine, other)
+        source = source_at(here, steps[n])
+        return jnp.where(same_half, mine_ref[source].astype(jnp.float32), other_ref[source].astype(jnp.float32))
 
     left_of = sequence_rows(block, left_f32, left_rows // seqs, seqs)
     for k in range(left_rows // seqs):
@@ -113,14 +106,14 @@
     bias_out_ref[...] = bias_ref[...]
 
 
-def prepare(mine, other, w_out, b_out, right, sources, seqs, c):
-    left_rows = mine.shape[0] * 2 // sources
+def prepare(mine, other, w_out, b_out, right, steps, seqs, c):
+    sources, left_rows, _ = mine.shape
     z = w_out.shape[1]
     outs = [((left_rows // seqs * LANES, sources * seqs), jnp.bfloat16), ((z, w_out.shape[0]), jnp.bfloat16),
             (right.shape, jnp.bfloat16), ((1, z), jnp.float32)]
     operands = (mine, other, w_out, b_out.reshape(1, -1), right)
     return pl.pallas_call(
-        functools.partial(prepare_kernel, seqs, c),
+        functools.partial(prepare_kernel, seqs, c, steps),
         grid=(1,),
         out_shape=[jax.ShapeDtypeStruct(*out) for out in outs],
         in_specs=[whole(a.shape) for a in operands],
@@ -131,17 +124,21 @@
     )(*operands)
 
 
-def pair_kernel(seqs, c, sources, left_ref, weights_ref, bias_ref, *refs):
-    right_refs, (out_ref, right_f32, right_b, outer_ref) = refs[:sources], refs[sources:]
+def pair_kernel(seqs, c, right_at, left_ref, weights_ref, bias_ref, *refs):
+    right_refs, (out_ref, right_f32, right_b, outer_ref) = refs[:-4], refs[-4:]
     rows_step = out_ref.shape[0]
     blocks = out_ref.shape[1] // LANES
+
+    def block_of(n, at):
+        array, first = right_at[n]
+        return right_refs[array][first + at:first + at + c * seqs].astype(jnp.float32)
 
     @pl.when(pl.program_id(0) == 0)
     def _():
         for b in range(blocks):
             at = b * c * seqs
             right_of = sequence_rows(
-                lambda n: right_refs[n][at:at + c * seqs].astype(jnp.float32), right_f32, c, seqs)
+                lambda n: block_of(n, at), right_f32, c, seqs)
             for e in range(c):
                 lanes = (b * c + e) * LANES
                 right_b[:, lanes:lanes + LANES] = right_of(e).astype(jnp.bfloat16)
@@ -163,15 +160,15 @@
                 out_ref[2 * p + half, b * LANES:(b + 1) * LANES, :] = mine.astype(out_ref.dtype)
 
 
-def pairs(left, weights, bias, rights, seqs, c, width):
-    sources = len(rights)
+def pairs(left, weights, bias, rights, right_at, seqs, c, width):
+    sources = len(right_at)
     z = weights.shape[0]
     rows = left.shape[0] // c
     rows_step = 8
     total = sources * seqs
     operands = (left, weights, bias, *rights)
     return pl.pallas_call(
-        functools.partial(pair_kernel, seqs, c, sources),
+        functools.partial(pair_kernel, seqs, c, right_at),
         grid=(rows // rows_step,),
         out_shape=jax.ShapeDtypeStruct((rows, width, z), jnp.bfloat16),
         in_specs=[pl.BlockSpec((rows_step * c, total), lambda i: (i, 0))] + [whole(a.shape) for a in operands[1:]],
@@ -190,22 +187,8 @@
     return here ^ (2 * step[0] + step[1])
 
 
-def half_steps(chips):
-    return [(a, b) for b in range(2) for a in range(chips // 2)]
-
-
 def fetch(array, step, count):
     return lax.ppermute(array, "row", [(source_at(r, step), r) for r in range(count)])
-
-
-def fetch_left(array, step, count):
-    chips = count // 2
-    moves = []
-    for r in range(count):
-        for core in range(2):
-            to = source_at(r % chips, step) + core * chips
-            moves.append((2 * r + core, 2 * to + (core if r // chips == core else 1 - core)))
-    return lax.ppermute(array, ("row", "col"), moves)
 
 
 def on_device(alignment, ln_gain, ln_bias, w_left, b_left, w_right, b_right, w_out, b_out):
@@ -213,17 +196,23 @@
     c = w_left.shape[1]
     row_count = lax.axis_size("row")
     col_count = lax.axis_size("col")
-    right, *lefts = features(alignment, ln_gain, ln_bias, w_left, b_left, w_right, b_right, row_count, col_count)
-    chips = row_count // 2
-    along = chips
-
-    near = [right] + [fetch(right, (a, 0), row_count) for a in range(1, along)]
-    far = [fetch(block, (0, 1), row_count) for block in near]
-    mine = jnp.concatenate([fetch_left(left, step, row_count) for step, left in zip(half_steps(chips), lefts)])
+    left, right = features(alignment, ln_gain, ln_bias, w_left, b_left, w_right, b_right, row_count, col_count)
+    along = row_count // 2
+    rows = right.shape[0]
+
+    across = fetch(right, (0, 1), row_count)
+    line = [fetch(right, (a, 0), row_count) for a in reversed(range(1, along))][::-1]
+
+    left, line[0] = lax.optimization_barrier((left, line[0]))
+    mine = lax.all_to_all(left.reshape(row_count, -1, LANES), "row", split_axis=0, concat_axis=0, tiled=True)
+    mine, across, *line = lax.optimization_barrier((mine, across, *line))
+    far = fetch(jnp.concatenate(line), (0, 1), row_count)
     other = lax.ppermute(mine, "col", [(0, 1), (1, 0)])
-    left, weights, near[0], bias = prepare(mine, other, w_out, b_out, right, row_count, seqs, c)
-    rights = [(near, far)[b][half * (along // 2) + a] for half in range(2) for a, b in half_steps(chips)]
-    return pairs(left, weights, bias, rights, seqs, c, width)
+
+    steps = [(a, b) for b in range(2) for a in range(along)]
+    right_at = [(a, 0) for a in range(along)] + [(along, 0)] + [(along + 1, a * rows) for a in range(along - 1)]
+    left, weights, right, bias = prepare(mine, other, w_out, b_out, right, steps, seqs, c)
+    return pairs(left, weights, bias, [right, *line, across, far], right_at, seqs, c, width)
 
 
 def solution(mesh):

time: 37.1 us -> 36.1 us (0.973)
  starting transfers between devices: 20.2 us -> 16.3 us
  waiting for transfers between devices: 7.9 us -> 10.8 us
    ppermute x4 -> x0, starting transfers between devices: 6.79 us -> none  [fetch_left(): return lax.ppermute(array, ('row', 'col'), moves)]
    all_to_all x0 -> x1, starting transfers between devices: none -> 6.41 us  [on_device(): lax.all_to_all(left.reshape(row_count, -1, LANES), 'row', split_axis=0, c...]
    ppermute x7 -> x5, waiting for transfers between devices: 3.42 us -> 9.5 us  [fetch(): lax.ppermute(array, 'row', [(source_at(r, step), r) for r in range(count)])]
    ppermute x4 -> x0, waiting for transfers between devices: 4.48 us -> none  [fetch_left(): return lax.ppermute(array, ('row', 'col'), moves)]
    ppermute x1, starting transfers between devices: 3.09 us -> 0.01 us  [on_device(): other = lax.ppermute(mine, 'col', [(0, 1), (1, 0)])]
    ppermute x1, waiting for transfers between devices: 0.01 us -> 1.35 us  [on_device(): other = lax.ppermute(mine, 'col', [(0, 1), (1, 0)])]
    ppermute x7 -> x5, starting transfers between devices: 10.4 us -> 9.89 us  [fetch(): lax.ppermute(array, 'row', [(source_at(r, step), r) for r in range(count)])]
  transfers between devices with their start and end apart: 12 -> 7, of which waited for: 5 -> 5; matrix products, arithmetic and copies ran while one was open for 0% -> 0% of each run, Pallas kernels for 3% -> 3%
where the time goes in v9:
time: 36.1 us; the launch traced here: 35.8 us
  starting transfers between devices  16.3 us (45%)
  waiting for transfers between devices  10.8 us (30%)
  Pallas kernels  8.59 us (24%)
    ppermute x5, starting transfers between devices, fetch(): lax.ppermute(array, 'row', [(source_at(r, step), r) for r in range(count)])  9.89 us
    ppermute x5, waiting for transfers between devices, fetch(): lax.ppermute(array, 'row', [(source_at(r, step), r) for r in range(count)])  9.5 us
    all_to_all x1, starting transfers between devices, on_device(): lax.all_to_all(left.reshape(row_count, -1, LANES), 'row', split_axis=0, c...  6.41 us
    pallas_call x1, Pallas kernels, pairs(): pl.pallas_call(functools.partial(pair_kernel, seqs, c, right_at), grid=(r...  5.08 us
    pallas_call x1, Pallas kernels, features(): pl.pallas_call(functools.partial(features_kernel, 1.0 / (seqs * row_count...  2.54 us
    ppermute x1, waiting for transfers between devices, on_device(): other = lax.ppermute(mine, 'col', [(0, 1), (1, 0)])  1.35 us
    pallas_call x1, Pallas kernels, prepare(): pl.pallas_call(functools.partial(prepare_kernel, seqs, c, steps), grid=(1...  0.98 us
  transfers between devices with their start and end apart: 7, of which 5 were waited for; matrix products, arithmetic and copies ran while one was open for 0% of the time, Pallas kernels for 3%

profile of v9, /device:TPU:0, one launch (start us, length us, event | category | flops | bytes accessed | tf_op | source)
XLA Modules:
  0.0 35.8 jit_solution(8841021573898904432)
XLA Ops:
  0.0 2.5 %features.1 = (bf16[2,256,128]{2,1,0:T(8,128)(2,1)}, bf16[256,128]{1,0:T(8,128)(2,1)}) custom-call(bf16[8,128,256]{2,1,0:T(8,128)(2,1)} %x_ref.1, f32[1,256]{1,0:T(1,128)} %bitcast.12, f32[1,256]{1,0:T(1,128)} %bitcast.13, bf16[32,256]{1,0:T(8,128)(2,1)} %bitcast.10, f32[1,32]{1,0:T(1,128)} %bitcast.14, bf16[32,256]{1,0:T(8,128)(2,1)} %bitcast.11, ...), custom_call_target="tpu_custom_call" | custom-call | tf_op jit(solution)/shard_map/features/pallas_call | solution.py:63
  2.5 3.0 %collective-permute-start = (bf16[256,128]{1,0:T(8,128)(2,1)}, bf16[256,128]{1,0:T(8,128)(2,1)S(1)}, u32[]{:S(2)}, u32[]{:S(2)}) collective-permute-start(bf16[256,128]{1,0:T(8,128)(2,1)} %get-tuple-element.19.own_right_ref), channel_id=1, source_target_pairs={{4,0},{6,2},{0,4},{2,6},{12,8},{14,10},{8,12},{10,14},{5,1},{7,3},... | collective-permute-start | bytes 196616 | tf_op jit(solution)/shard_map/ppermute | solution.py:191
  5.6 2.5 %collective-permute-done.refs_1_ = bf16[256,128]{1,0:T(8,128)(2,1)S(1)} collective-permute-done((bf16[256,128]{1,0:T(8,128)(2,1)}, bf16[256,128]{1,0:T(8,128)(2,1)S(1)}, u32[]{:S(2)}, u32[]{:S(2)}) %collective-permute-start) | collective-permute-done | bytes 65568 | tf_op jit(solution)/shard_map/ppermute | solution.py:191
  8.0 0.0 copy-start.1
  8.0 6.4 %all-to-all-start = ((bf16[8,64,128]{2,1,0:T(8,128)(2,1)}), bf16[8,64,128]{2,1,0:T(8,128)(2,1)S(1)}, u32[]{:S(2)}, u32[]{:S(2)}) async-start(bf16[8,64,128]{2,1,0:T(8,128)(2,1)} %bitcast.9), calls=%async_computation | async-start | bytes 262144 | tf_op jit(solution)/shard_map/all_to_all | solution.py:207
  14.4 0.0 copy-done.1
  14.4 0.0 copy-start
  14.4 3.9 %collective-permute-start.3 = (bf16[256,128]{1,0:T(8,128)(2,1)S(1)}, bf16[256,128]{1,0:T(8,128)(2,1)S(1)}, u32[]{:S(2)}, u32[]{:S(2)}) collective-permute-start(bf16[256,128]{1,0:T(8,128)(2,1)S(1)} %copy-done.1), channel_id=1, source_target_pairs={{12,0},{14,2},{8,4},{10,6},{4,8},{6,10},{0,12},{2,14},{13,1},{15,3... | collective-permute-start | bytes 196616 | tf_op jit(solution)/shard_map/ppermute | solution.py:191
  18.3 0.0 collective-permute-start.2
  18.3 1.5 %collective-permute-start.1 = (bf16[256,128]{1,0:T(8,128)(2,1)S(1)}, bf16[256,128]{1,0:T(8,128)(2,1)S(1)}, u32[]{:S(2)}, u32[]{:S(2)}) collective-permute-start(bf16[256,128]{1,0:T(8,128)(2,1)S(1)} %copy-done.1), channel_id=1, source_target_pairs={{2,0},{0,2},{6,4},{4,6},{10,8},{8,10},{14,12},{12,14},{3,1},{1,3},... | collective-permute-start | bytes 196616 | tf_op jit(solution)/shard_map/ppermute | solution.py:191
  19.8 2.0 %collective-permute-done.3.refs_3_ = bf16[256,128]{1,0:T(8,128)(2,1)S(1)} collective-permute-done((bf16[256,128]{1,0:T(8,128)(2,1)S(1)}, bf16[256,128]{1,0:T(8,128)(2,1)S(1)}, u32[]{:S(2)}, u32[]{:S(2)}) %collective-permute-start.3) | collective-permute-done | bytes 65568 | tf_op jit(solution)/shard_map/ppermute | solution.py:191
  21.8 3.2 %collective-permute-done.2.refs_2_ = bf16[256,128]{1,0:T(8,128)(2,1)S(1)} collective-permute-done((bf16[256,128]{1,0:T(8,128)(2,1)S(1)}, bf16[256,128]{1,0:T(8,128)(2,1)S(1)}, u32[]{:S(2)}, u32[]{:S(2)}) %collective-permute-start.2) | collective-permute-done | bytes 65568 | tf_op jit(solution)/shard_map/ppermute | solution.py:191
  25.0 0.0 collective-permute-done.1.refs_4_
  25.0 0.0 all-to-all-done.mine_ref
  25.0 0.0 copy-start.2
  25.0 1.5 %collective-permute-start.5 = (bf16[768,128]{1,0:T(8,128)(2,1)S(1)}, bf16[768,128]{1,0:T(8,128)(2,1)S(1)}, u32[]{:S(2)}, u32[]{:S(2)}) collective-permute-start(bf16[768,128]{1,0:T(8,128)(2,1)S(1)} %pad_maximum_fusion), channel_id=1, source_target_pairs={{2,0},{0,2},{6,4},{4,6},{10,8},{8,10},{14,12},{12,14},{3,1},{1,3},... | collective-permute-start | bytes 589832 | tf_op jit(solution)/shard_map/ppermute | solution.py:191
  26.5 0.0 collective-permute-start.4
  26.5 1.3 %collective-permute-done.4.other_ref = bf16[8,64,128]{2,1,0:T(8,128)(2,1)S(1)} collective-permute-done((bf16[8,64,128]{2,1,0:T(8,128)(2,1)S(1)}, bf16[8,64,128]{2,1,0:T(8,128)(2,1)S(1)}, u32[]{:S(2)}, u32[]{:S(2)}) %collective-permute-start.4) | collective-permute-done | bytes 131104 | tf_op jit(solution)/shard_map/ppermute | solution.py:210
  27.9 0.0 copy-done
  27.9 0.0 copy-done.2
  27.9 1.0 %prepare.1 = (bf16[1024,64]{1,0:T(8,128)(2,1)S(1)}, bf16[128,1024]{1,0:T(8,128)(2,1)S(1)}, bf16[256,128]{1,0:T(8,128)(2,1)S(1)}, f32[1,128]{1,0:T(1,128)S(1)}) custom-call(bf16[8,64,128]{2,1,0:T(8,128)(2,1)S(1)} %all-to-all-done.mine_ref, bf16[8,64,128]{2,1,0:T(8,128)(2,1)S(1)} %collective-permute-done.4.other_ref, bf16[1024,128]{1,0:T(8,128)(2,1)S(1)} %copy-done, ...), custom_call_target="tpu_custom_call" | custom-call | tf_op jit(solution)/shard_map/prepare/pallas_call | solution.py:115
  28.9 1.9 %collective-permute-done.5.refs_5_ = bf16[768,128]{1,0:T(8,128)(2,1)S(1)} collective-permute-done((bf16[768,128]{1,0:T(8,128)(2,1)S(1)}, bf16[768,128]{1,0:T(8,128)(2,1)S(1)}, u32[]{:S(2)}, u32[]{:S(2)}) %collective-permute-start.5) | collective-permute-done | bytes 196640 | tf_op jit(solution)/shard_map/ppermute | solution.py:191
  30.7 5.1 %pairs.1 = bf16[32,128,128]{2,1,0:T(8,128)(2,1)} custom-call(bf16[1024,64]{1,0:T(8,128)(2,1)S(1)} %get-tuple-element.23.left_ref, bf16[128,1024]{1,0:T(8,128)(2,1)S(1)} %get-tuple-element.24.weights_ref, f32[1,128]{1,0:T(1,128)S(1)} %get-tuple-element.25.bias_ref, bf16[256,128]{1,0:T(8,128)(2,1)S(1)} %get-tuple-element.26.refs_0_, ...), custom_call_target="tpu_custom_call" | custom-call | flops 1610612736 | bytes 1048576 | tf_op jit(solution)/shard_map/pairs/pallas_call | solution.py:170
  (1 shorter events, 0.0 us)
Async XLA Ops:
  2.5 5.5 %collective-permute-start = (bf16[256,128]{1,0:T(8,128)(2,1)}, bf16[256,128]{1,0:T(8,128)(2,1)S(1)}, u32[]{:S(2)}, u32[]{:S(2)}) collective-permute-start(bf16[256,128]{1,0:T(8,128)(2,1)} %get-tuple-element.19.own_right_ref), channel_id=1, source_target_pairs={{4,0},{6,2},{0,4},{2,6},{12,8},{14,10},{8,12},{10,14},{5,1},{7,3},... | collective-permute-start | bytes 196616 | tf_op jit(solution)/shard_map/ppermute | solution.py:191
  8.0 6.4 %copy-start.1 = (bf16[256,128]{1,0:T(8,128)(2,1)S(1)}, bf16[256,128]{1,0:T(8,128)(2,1)}, u32[]{:S(2)}) copy-start(bf16[256,128]{1,0:T(8,128)(2,1)} %get-tuple-element.19.own_right_ref) | copy-start | bytes 196612
  8.0 16.9 %all-to-all-start = ((bf16[8,64,128]{2,1,0:T(8,128)(2,1)}), bf16[8,64,128]{2,1,0:T(8,128)(2,1)S(1)}, u32[]{:S(2)}, u32[]{:S(2)}) async-start(bf16[8,64,128]{2,1,0:T(8,128)(2,1)} %bitcast.9), calls=%async_computation | async-start | bytes 262144 | tf_op jit(solution)/shard_map/all_to_all | solution.py:207
  14.4 13.4 %copy-start = (bf16[1024,128]{1,0:T(8,128)(2,1)S(1)}, bf16[1024,128]{1,0:T(8,128)(2,1)}, u32[]{:S(2)}) copy-start(bf16[1024,128]{1,0:T(8,128)(2,1)} %w_ref.1) | copy-start | bytes 786436
  14.4 7.3 %collective-permute-start.3 = (bf16[256,128]{1,0:T(8,128)(2,1)S(1)}, bf16[256,128]{1,0:T(8,128)(2,1)S(1)}, u32[]{:S(2)}, u32[]{:S(2)}) collective-permute-start(bf16[256,128]{1,0:T(8,128)(2,1)S(1)} %copy-done.1), channel_id=1, source_target_pairs={{12,0},{14,2},{8,4},{10,6},{4,8},{6,10},{0,12},{2,14},{13,1},{15,3... | collective-permute-start | bytes 196616 | tf_op jit(solution)/shard_map/ppermute | solution.py:191
  18.3 6.6 %collective-permute-start.2 = (bf16[256,128]{1,0:T(8,128)(2,1)S(1)}, bf16[256,128]{1,0:T(8,128)(2,1)S(1)}, u32[]{:S(2)}, u32[]{:S(2)}) collective-permute-start(bf16[256,128]{1,0:T(8,128)(2,1)S(1)} %copy-done.1), channel_id=1, source_target_pairs={{8,0},{10,2},{12,4},{14,6},{0,8},{2,10},{4,12},{6,14},{9,1},{11,3}... | collective-permute-start | bytes 196616 | tf_op jit(solution)/shard_map/ppermute | solution.py:191
  18.3 6.6 %collective-permute-start.1 = (bf16[256,128]{1,0:T(8,128)(2,1)S(1)}, bf16[256,128]{1,0:T(8,128)(2,1)S(1)}, u32[]{:S(2)}, u32[]{:S(2)}) collective-permute-start(bf16[256,128]{1,0:T(8,128)(2,1)S(1)} %copy-done.1), channel_id=1, source_target_pairs={{2,0},{0,2},{6,4},{4,6},{10,8},{8,10},{14,12},{12,14},{3,1},{1,3},... | collective-permute-start | bytes 196616 | tf_op jit(solution)/shard_map/ppermute | solution.py:191
  25.0 2.9 %copy-start.2 = (f32[128]{0:T(128)S(1)}, f32[128]{0:T(128)}, u32[]{:S(2)}) copy-start(f32[128]{0:T(128)} %param.17) | copy-start | bytes 1540
  25.0 5.7 %collective-permute-start.5 = (bf16[768,128]{1,0:T(8,128)(2,1)S(1)}, bf16[768,128]{1,0:T(8,128)(2,1)S(1)}, u32[]{:S(2)}, u32[]{:S(2)}) collective-permute-start(bf16[768,128]{1,0:T(8,128)(2,1)S(1)} %pad_maximum_fusion), channel_id=1, source_target_pairs={{2,0},{0,2},{6,4},{4,6},{10,8},{8,10},{14,12},{12,14},{3,1},{1,3},... | collective-permute-start | bytes 589832 | tf_op jit(solution)/shard_map/ppermute | solution.py:191
  26.5 1.3 %collective-permute-start.4 = (bf16[8,64,128]{2,1,0:T(8,128)(2,1)S(1)}, bf16[8,64,128]{2,1,0:T(8,128)(2,1)S(1)}, u32[]{:S(2)}, u32[]{:S(2)}) collective-permute-start(bf16[8,64,128]{2,1,0:T(8,128)(2,1)S(1)} %all-to-all-done.mine_ref), channel_id=1, source_target_pairs={{0,1},{1,0},{2,3},{3,2},{4,5},{5,4},{6,7},{7,6},{8,9},{9,8},{10,11... | collective-permute-start | bytes 393224 | tf_op jit(solution)/shard_map/ppermute | solution.py:210

commit v10 on v8

--- a/solution.py
+++ b/solution.py
@@ -131,17 +131,21 @@
     )(*operands)
 
 
-def pair_kernel(seqs, c, sources, left_ref, weights_ref, bias_ref, *refs):
-    right_refs, (out_ref, right_f32, right_b, outer_ref) = refs[:sources], refs[sources:]
+def pair_kernel(seqs, c, right_at, left_ref, weights_ref, bias_ref, *refs):
+    right_refs, (out_ref, right_f32, right_b, outer_ref) = refs[:-4], refs[-4:]
     rows_step = out_ref.shape[0]
     blocks = out_ref.shape[1] // LANES
+
+    def block_of(n, at):
+        array, first = right_at[n]
+        return right_refs[array][first + at:first + at + c * seqs].astype(jnp.float32)
 
     @pl.when(pl.program_id(0) == 0)
     def _():
         for b in range(blocks):
             at = b * c * seqs
             right_of = sequence_rows(
-                lambda n: right_refs[n][at:at + c * seqs].astype(jnp.float32), right_f32, c, seqs)
+                lambda n: block_of(n, at), right_f32, c, seqs)
             for e in range(c):
                 lanes = (b * c + e) * LANES
                 right_b[:, lanes:lanes + LANES] = right_of(e).astype(jnp.bfloat16)
@@ -163,15 +167,15 @@
                 out_ref[2 * p + half, b * LANES:(b + 1) * LANES, :] = mine.astype(out_ref.dtype)
 
 
-def pairs(left, weights, bias, rights, seqs, c, width):
-    sources = len(rights)
+def pairs(left, weights, bias, rights, right_at, seqs, c, width):
+    sources = len(right_at)
     z = weights.shape[0]
     rows = left.shape[0] // c
     rows_step = 8
     total = sources * seqs
     operands = (left, weights, bias, *rights)
     return pl.pallas_call(
-        functools.partial(pair_kernel, seqs, c, sources),
+        functools.partial(pair_kernel, seqs, c, right_at),
         grid=(rows // rows_step,),
         out_shape=jax.ShapeDtypeStruct((rows, width, z), jnp.bfloat16),
         in_specs=[pl.BlockSpec((rows_step * c, total), lambda i: (i, 0))] + [whole(a.shape) for a in operands[1:]],
@@ -214,16 +218,21 @@
     row_count = lax.axis_size("row")
     col_count = lax.axis_size("col")
     right, *lefts = features(alignment, ln_gain, ln_bias, w_left, b_left, w_right, b_right, row_count, col_count)
-    chips = row_count // 2
-    along = chips
-
-    near = [right] + [fetch(right, (a, 0), row_count) for a in range(1, along)]
-    far = [fetch(block, (0, 1), row_count) for block in near]
+    chips = along = row_count // 2
+    rows = right.shape[0]
+
+    line = [fetch(right, (a, 0), row_count) for a in range(1, along)]
+    across = fetch(right, (0, 1), row_count)
+    across, *held = lax.optimization_barrier((across, *line, *lefts[1:]))
+    line, lefts[1:] = held[:along - 1], held[along - 1:]
+    far = fetch(jnp.concatenate(line), (0, 1), row_count)
+
     mine = jnp.concatenate([fetch_left(left, step, row_count) for step, left in zip(half_steps(chips), lefts)])
     other = lax.ppermute(mine, "col", [(0, 1), (1, 0)])
-    left, weights, near[0], bias = prepare(mine, other, w_out, b_out, right, row_count, seqs, c)
-    rights = [(near, far)[b][half * (along // 2) + a] for half in range(2) for a, b in half_steps(chips)]
-    return pairs(left, weights, bias, rights, seqs, c, width)
+    left, weights, right, bias = prepare(mine, other, w_out, b_out, right, row_count, seqs, c)
+    places = [[(a, 0) for a in range(along)], [(along, 0)] + [(along + 1, a * rows) for a in range(along - 1)]]
+    right_at = [places[b][half * (along // 2) + a] for half in range(2) for a, b in half_steps(chips)]
+    return pairs(left, weights, bias, [right, *line, across, far], right_at, seqs, c, width)
 
 
 def solution(mesh):

time: 37.1 us -> 33.8 us (0.911)
  starting transfers between devices: 20.2 us -> 16.2 us
  waiting for transfers between devices: 7.9 us -> 8.62 us
    ppermute x4, waiting for transfers between devices: 4.48 us -> 1.24 us  [fetch_left(): return lax.ppermute(array, ('row', 'col'), moves)]
    ppermute x7 -> x5, waiting for transfers between devices: 3.42 us -> 6.48 us  [fetch(): lax.ppermute(array, 'row', [(source_at(r, step), r) for r in range(count)])]
    ppermute x4, starting transfers between devices: 6.79 us -> 4.85 us  [fetch_left(): return lax.ppermute(array, ('row', 'col'), moves)]
    ppermute x1, starting transfers between devices: 3.09 us -> 1.89 us  [on_device(): other = lax.ppermute(mine, 'col', [(0, 1), (1, 0)])]
    ppermute x7 -> x5, starting transfers between devices: 10.4 us -> 9.44 us  [fetch(): lax.ppermute(array, 'row', [(source_at(r, step), r) for r in range(count)])]
    ppermute x1, waiting for transfers between devices: 0.01 us -> 0.9 us  [on_device(): other = lax.ppermute(mine, 'col', [(0, 1), (1, 0)])]
  transfers between devices with their start and end apart: 12 -> 10, of which waited for: 5 -> 5; matrix products, arithmetic and copies ran while one was open for 0% -> 0% of each run, Pallas kernels for 3% -> 3%
where the time goes in v10:
time: 33.8 us; the launch traced here: 33.5 us
  starting transfers between devices  16.2 us (48%)
  Pallas kernels  8.63 us (26%)
  waiting for transfers between devices  8.62 us (26%)
    ppermute x5, starting transfers between devices, fetch(): lax.ppermute(array, 'row', [(source_at(r, step), r) for r in range(count)])  9.44 us
    ppermute x5, waiting for transfers between devices, fetch(): lax.ppermute(array, 'row', [(source_at(r, step), r) for r in range(count)])  6.48 us
    pallas_call x1, Pallas kernels, pairs(): pl.pallas_call(functools.partial(pair_kernel, seqs, c, right_at), grid=(r...  5.16 us
    ppermute x4, starting transfers between devices, fetch_left(): return lax.ppermute(array, ('row', 'col'), moves)  4.85 us
    pallas_call x1, Pallas kernels, features(): pl.pallas_call(functools.partial(features_kernel, 1.0 / (seqs * row_count...  2.49 us
    ppermute x1, starting transfers between devices, on_device(): other = lax.ppermute(mine, 'col', [(0, 1), (1, 0)])  1.89 us
    ppermute x4, waiting for transfers between devices, fetch_left(): return lax.ppermute(array, ('row', 'col'), moves)  1.24 us
    pallas_call x1, Pallas kernels, prepare(): pl.pallas_call(functools.partial(prepare_kernel, seqs, c), grid=(1,), out...  0.98 us
  transfers between devices with their start and end apart: 10, of which 5 were waited for; matrix products, arithmetic and copies ran while one was open for 0% of the time, Pallas kernels for 3%

profile of v10, /device:TPU:0, one launch (start us, length us, event | category | flops | bytes accessed | tf_op | source)
XLA Modules:
  0.0 33.5 jit_solution(17878123083532257902)
XLA Ops:
  0.0 2.5 %features.1 = (bf16[256,128]{1,0:T(8,128)(2,1)}, bf16[64,128]{1,0:T(8,128)(2,1)}, bf16[64,128]{1,0:T(8,128)(2,1)}, bf16[64,128]{1,0:T(8,128)(2,1)}, bf16[64,128]{1,0:T(8,128)(2,1)}) custom-call(bf16[8,128,256]{2,1,0:T(8,128)(2,1)} %x_ref.1, f32[1,256]{1,0:T(1,128)} %bitcast.10, f32[1,256]{1,0:T(1,128)} %bitcast.11, bf16[32,256]{1,0:T(8,128)(2,1)} %bitcast.8, ...), custom_call_target="tpu_custom_call" | custom-call | tf_op jit(solution)/shard_map/features/pallas_call | solution.py:68
  2.5 1.4 %collective-permute-start = (bf16[64,128]{1,0:T(8,128)(2,1)}, bf16[64,128]{1,0:T(8,128)(2,1)S(1)}, u32[]{:S(2)}, u32[]{:S(2)}) collective-permute-start(bf16[64,128]{1,0:T(8,128)(2,1)} %get-tuple-element.21), channel_id=1, source_target_pairs={{0,0},{1,8},{2,2},{3,10},{4,4},{5,12},{6,6},{7,14},{8,1},{9,9},{10... | collective-permute-start | bytes 49160 | tf_op jit(solution)/shard_map/ppermute | solution.py:212
  3.9 5.7 %collective-permute-start.4 = (bf16[256,128]{1,0:T(8,128)(2,1)}, bf16[256,128]{1,0:T(8,128)(2,1)S(1)}, u32[]{:S(2)}, u32[]{:S(2)}) collective-permute-start(bf16[256,128]{1,0:T(8,128)(2,1)} %get-tuple-element.22.own_right_ref), channel_id=1, source_target_pairs={{12,0},{14,2},{8,4},{10,6},{4,8},{6,10},{0,12},{2,14},{13,1},{15,3... | collective-permute-start | bytes 196616 | tf_op jit(solution)/shard_map/ppermute | solution.py:202
  9.6 0.0 collective-permute-start.3
  9.6 0.6 %collective-permute-start.2 = (bf16[256,128]{1,0:T(8,128)(2,1)}, bf16[256,128]{1,0:T(8,128)(2,1)S(1)}, u32[]{:S(2)}, u32[]{:S(2)}) collective-permute-start(bf16[256,128]{1,0:T(8,128)(2,1)} %get-tuple-element.22.own_right_ref), channel_id=1, source_target_pairs={{4,0},{6,2},{0,4},{2,6},{12,8},{14,10},{8,12},{10,14},{5,1},{7,3},... | collective-permute-start | bytes 196616 | tf_op jit(solution)/shard_map/ppermute | solution.py:202
  10.2 1.5 %collective-permute-start.1 = (bf16[256,128]{1,0:T(8,128)(2,1)}, bf16[256,128]{1,0:T(8,128)(2,1)S(1)}, u32[]{:S(2)}, u32[]{:S(2)}) collective-permute-start(bf16[256,128]{1,0:T(8,128)(2,1)} %get-tuple-element.22.own_right_ref), channel_id=1, source_target_pairs={{2,0},{0,2},{6,4},{4,6},{10,8},{8,10},{14,12},{12,14},{3,1},{1,3},... | collective-permute-start | bytes 196616 | tf_op jit(solution)/shard_map/ppermute | solution.py:202
  11.7 0.0 collective-permute-done
  11.7 0.3 %collective-permute-done.4.refs_3_ = bf16[256,128]{1,0:T(8,128)(2,1)S(1)} collective-permute-done((bf16[256,128]{1,0:T(8,128)(2,1)}, bf16[256,128]{1,0:T(8,128)(2,1)S(1)}, u32[]{:S(2)}, u32[]{:S(2)}) %collective-permute-start.4) | collective-permute-done | bytes 65568 | tf_op jit(solution)/shard_map/ppermute | solution.py:202
  12.1 4.6 %collective-permute-done.3.refs_2_ = bf16[256,128]{1,0:T(8,128)(2,1)S(1)} collective-permute-done((bf16[256,128]{1,0:T(8,128)(2,1)}, bf16[256,128]{1,0:T(8,128)(2,1)S(1)}, u32[]{:S(2)}, u32[]{:S(2)}) %collective-permute-start.3) | collective-permute-done | bytes 65568 | tf_op jit(solution)/shard_map/ppermute | solution.py:202
  16.7 0.0 collective-permute-done.2.refs_1_
  16.7 0.0 collective-permute-done.1.refs_4_
  16.7 0.0 collective-permute-start.5
  16.7 1.6 %collective-permute-start.6 = (bf16[64,128]{1,0:T(8,128)(2,1)S(1)}, bf16[64,128]{1,0:T(8,128)(2,1)S(1)}, u32[]{:S(2)}, u32[]{:S(2)}) collective-permute-start(bf16[64,128]{1,0:T(8,128)(2,1)S(1)} %copy-done.4), channel_id=1, source_target_pairs={{0,2},{1,10},{2,0},{3,8},{4,6},{5,14},{6,4},{7,12},{8,3},{9,11},{1... | collective-permute-start | bytes 49160 | tf_op jit(solution)/shard_map/ppermute | solution.py:212
  18.3 1.9 %collective-permute-start.7 = (bf16[64,128]{1,0:T(8,128)(2,1)S(1)}, bf16[64,128]{1,0:T(8,128)(2,1)S(1)}, u32[]{:S(2)}, u32[]{:S(2)}) collective-permute-start(bf16[64,128]{1,0:T(8,128)(2,1)S(1)} %copy-done.3), channel_id=1, source_target_pairs={{0,6},{1,14},{2,4},{3,12},{4,2},{5,10},{6,0},{7,8},{8,7},{9,15},{1... | collective-permute-start | bytes 49160 | tf_op jit(solution)/shard_map/ppermute | solution.py:212
  20.2 0.0 copy-start.1
  20.2 1.6 %collective-permute-start.9 = (bf16[768,128]{1,0:T(8,128)(2,1)S(1)}, bf16[768,128]{1,0:T(8,128)(2,1)S(1)}, u32[]{:S(2)}, u32[]{:S(2)}) collective-permute-start(bf16[768,128]{1,0:T(8,128)(2,1)S(1)} %pad_maximum_fusion), channel_id=1, source_target_pairs={{2,0},{0,2},{6,4},{4,6},{10,8},{8,10},{14,12},{12,14},{3,1},{1,3},... | collective-permute-start | bytes 589832 | tf_op jit(solution)/shard_map/ppermute | solution.py:202
  21.8 0.0 collective-permute-done.5
  21.8 0.0 collective-permute-done.6
  21.8 1.2 %collective-permute-done.7 = bf16[64,128]{1,0:T(8,128)(2,1)S(1)} collective-permute-done((bf16[64,128]{1,0:T(8,128)(2,1)S(1)}, bf16[64,128]{1,0:T(8,128)(2,1)S(1)}, u32[]{:S(2)}, u32[]{:S(2)}) %collective-permute-start.7) | collective-permute-done | bytes 16416 | tf_op jit(solution)/shard_map/ppermute | solution.py:212
  23.1 1.9 %collective-permute-start.8 = (bf16[256,128]{1,0:T(8,128)(2,1)S(1)}, bf16[256,128]{1,0:T(8,128)(2,1)S(1)}, u32[]{:S(2)}, u32[]{:S(2)}) collective-permute-start(bf16[256,128]{1,0:T(8,128)(2,1)S(1)} %constant_dynamic-update-slice_fusion.mine_ref), channel_id=1, source_target_pairs={{0,1},{1,0},{2,3},{3,2},{4,5},{5,4},{6,7},{7,6},{8,9},{9,8},{10,11... | collective-permute-start | bytes 196616 | tf_op jit(solution)/shard_map/ppermute | solution.py:231
  25.0 0.9 %collective-permute-done.8.other_ref = bf16[256,128]{1,0:T(8,128)(2,1)S(1)} collective-permute-done((bf16[256,128]{1,0:T(8,128)(2,1)S(1)}, bf16[256,128]{1,0:T(8,128)(2,1)S(1)}, u32[]{:S(2)}, u32[]{:S(2)}) %collective-permute-start.8) | collective-permute-done | bytes 65568 | tf_op jit(solution)/shard_map/ppermute | solution.py:231
  25.9 1.0 %prepare.1 = (bf16[1024,64]{1,0:T(8,128)(2,1)S(1)}, bf16[128,1024]{1,0:T(8,128)(2,1)S(1)}, bf16[256,128]{1,0:T(8,128)(2,1)S(1)}, f32[1,128]{1,0:T(1,128)S(1)}) custom-call(bf16[256,128]{1,0:T(8,128)(2,1)S(1)} %constant_dynamic-update-slice_fusion.mine_ref, bf16[256,128]{1,0:T(8,128)(2,1)S(1)} %collective-permute-done.8.other_ref, ...), custom_call_target="tpu_custom_call" | custom-call | tf_op jit(solution)/shard_map/prepare/pallas_call | solution.py:122
  26.9 1.5 %collective-permute-done.9.refs_5_ = bf16[768,128]{1,0:T(8,128)(2,1)S(1)} collective-permute-done((bf16[768,128]{1,0:T(8,128)(2,1)S(1)}, bf16[768,128]{1,0:T(8,128)(2,1)S(1)}, u32[]{:S(2)}, u32[]{:S(2)}) %collective-permute-start.9) | collective-permute-done | bytes 196640 | tf_op jit(solution)/shard_map/ppermute | solution.py:202
  28.4 5.2 %pairs.1 = bf16[32,128,128]{2,1,0:T(8,128)(2,1)} custom-call(bf16[1024,64]{1,0:T(8,128)(2,1)S(1)} %get-tuple-element.29.left_ref, bf16[128,1024]{1,0:T(8,128)(2,1)S(1)} %get-tuple-element.30.weights_ref, f32[1,128]{1,0:T(1,128)S(1)} %get-tuple-element.31.bias_ref, bf16[256,128]{1,0:T(8,128)(2,1)S(1)} %get-tuple-element.32.refs_0_, ...), custom_call_target="tpu_custom_call" | custom-call | flops 1610612736 | bytes 1048576 | tf_op jit(solution)/shard_map/pairs/pallas_call | solution.py:177
  (14 shorter events, 0.1 us)
Async XLA Ops:
  2.5 9.2 %collective-permute-start = (bf16[64,128]{1,0:T(8,128)(2,1)}, bf16[64,128]{1,0:T(8,128)(2,1)S(1)}, u32[]{:S(2)}, u32[]{:S(2)}) collective-permute-start(bf16[64,128]{1,0:T(8,128)(2,1)} %get-tuple-element.21), channel_id=1, source_target_pairs={{0,0},{1,8},{2,2},{3,10},{4,4},{5,12},{6,6},{7,14},{8,1},{9,9},{10... | collective-permute-start | bytes 49160 | tf_op jit(solution)/shard_map/ppermute | solution.py:212
  3.9 12.9 %copy-start.4 = (bf16[64,128]{1,0:T(8,128)(2,1)S(1)}, bf16[64,128]{1,0:T(8,128)(2,1)}, u32[]{:S(2)}) copy-start(bf16[64,128]{1,0:T(8,128)(2,1)} %get-tuple-element.27) | copy-start | bytes 49156
  3.9 14.5 %copy-start.3 = (bf16[64,128]{1,0:T(8,128)(2,1)S(1)}, bf16[64,128]{1,0:T(8,128)(2,1)}, u32[]{:S(2)}) copy-start(bf16[64,128]{1,0:T(8,128)(2,1)} %get-tuple-element.28) | copy-start | bytes 49156
  3.9 22.0 %copy-start = (bf16[1024,128]{1,0:T(8,128)(2,1)S(1)}, bf16[1024,128]{1,0:T(8,128)(2,1)}, u32[]{:S(2)}) copy-start(bf16[1024,128]{1,0:T(8,128)(2,1)} %w_ref.1) | copy-start | bytes 786436
  3.9 8.2 %collective-permute-start.4 = (bf16[256,128]{1,0:T(8,128)(2,1)}, bf16[256,128]{1,0:T(8,128)(2,1)S(1)}, u32[]{:S(2)}, u32[]{:S(2)}) collective-permute-start(bf16[256,128]{1,0:T(8,128)(2,1)} %get-tuple-element.22.own_right_ref), channel_id=1, source_target_pairs={{12,0},{14,2},{8,4},{10,6},{4,8},{6,10},{0,12},{2,14},{13,1},{15,3... | collective-permute-start | bytes 196616 | tf_op jit(solution)/shard_map/ppermute | solution.py:202
  9.6 7.1 %collective-permute-start.3 = (bf16[256,128]{1,0:T(8,128)(2,1)}, bf16[256,128]{1,0:T(8,128)(2,1)S(1)}, u32[]{:S(2)}, u32[]{:S(2)}) collective-permute-start(bf16[256,128]{1,0:T(8,128)(2,1)} %get-tuple-element.22.own_right_ref), channel_id=1, source_target_pairs={{8,0},{10,2},{12,4},{14,6},{0,8},{2,10},{4,12},{6,14},{9,1},{11,3}... | collective-permute-start | bytes 196616 | tf_op jit(solution)/shard_map/ppermute | solution.py:202
  9.6 7.1 %collective-permute-start.2 = (bf16[256,128]{1,0:T(8,128)(2,1)}, bf16[256,128]{1,0:T(8,128)(2,1)S(1)}, u32[]{:S(2)}, u32[]{:S(2)}) collective-permute-start(bf16[256,128]{1,0:T(8,128)(2,1)} %get-tuple-element.22.own_right_ref), channel_id=1, source_target_pairs={{4,0},{6,2},{0,4},{2,6},{12,8},{14,10},{8,12},{10,14},{5,1},{7,3},... | collective-permute-start | bytes 196616 | tf_op jit(solution)/shard_map/ppermute | solution.py:202
  10.2 6.5 %collective-permute-start.1 = (bf16[256,128]{1,0:T(8,128)(2,1)}, bf16[256,128]{1,0:T(8,128)(2,1)S(1)}, u32[]{:S(2)}, u32[]{:S(2)}) collective-permute-start(bf16[256,128]{1,0:T(8,128)(2,1)} %get-tuple-element.22.own_right_ref), channel_id=1, source_target_pairs={{2,0},{0,2},{6,4},{4,6},{10,8},{8,10},{14,12},{12,14},{3,1},{1,3},... | collective-permute-start | bytes 196616 | tf_op jit(solution)/shard_map/ppermute | solution.py:202
  16.7 5.1 %collective-permute-start.5 = (bf16[64,128]{1,0:T(8,128)(2,1)}, bf16[64,128]{1,0:T(8,128)(2,1)S(1)}, u32[]{:S(2)}, u32[]{:S(2)}) collective-permute-start(bf16[64,128]{1,0:T(8,128)(2,1)} %get-tuple-element.26), channel_id=1, source_target_pairs={{0,4},{1,12},{2,6},{3,14},{4,0},{5,8},{6,2},{7,10},{8,5},{9,13},{1... | collective-permute-start | bytes 49160 | tf_op jit(solution)/shard_map/ppermute | solution.py:212
  16.7 5.1 %collective-permute-start.6 = (bf16[64,128]{1,0:T(8,128)(2,1)S(1)}, bf16[64,128]{1,0:T(8,128)(2,1)S(1)}, u32[]{:S(2)}, u32[]{:S(2)}) collective-permute-start(bf16[64,128]{1,0:T(8,128)(2,1)S(1)} %copy-done.4), channel_id=1, source_target_pairs={{0,2},{1,10},{2,0},{3,8},{4,6},{5,14},{6,4},{7,12},{8,3},{9,11},{1... | collective-permute-start | bytes 49160 | tf_op jit(solution)/shard_map/ppermute | solution.py:212
  18.3 4.8 %collective-permute-start.7 = (bf16[64,128]{1,0:T(8,128)(2,1)S(1)}, bf16[64,128]{1,0:T(8,128)(2,1)S(1)}, u32[]{:S(2)}, u32[]{:S(2)}) collective-permute-start(bf16[64,128]{1,0:T(8,128)(2,1)S(1)} %copy-done.3), channel_id=1, source_target_pairs={{0,6},{1,14},{2,4},{3,12},{4,2},{5,10},{6,0},{7,8},{8,7},{9,15},{1... | collective-permute-start | bytes 49160 | tf_op jit(solution)/shard_map/ppermute | solution.py:212
  20.2 5.7 %copy-start.1 = (bf16[256,128]{1,0:T(8,128)(2,1)S(1)}, bf16[256,128]{1,0:T(8,128)(2,1)}, u32[]{:S(2)}) copy-start(bf16[256,128]{1,0:T(8,128)(2,1)} %get-tuple-element.22.own_right_ref) | copy-start | bytes 196612
  20.2 8.1 %collective-permute-start.9 = (bf16[768,128]{1,0:T(8,128)(2,1)S(1)}, bf16[768,128]{1,0:T(8,128)(2,1)S(1)}, u32[]{:S(2)}, u32[]{:S(2)}) collective-permute-start(bf16[768,128]{1,0:T(8,128)(2,1)S(1)} %pad_maximum_fusion), channel_id=1, source_target_pairs={{2,0},{0,2},{6,4},{4,6},{10,8},{8,10},{14,12},{12,14},{3,1},{1,3},... | collective-permute-start | bytes 589832 | tf_op jit(solution)/shard_map/ppermute | solution.py:202
  23.1 2.8 %copy-start.2 = (f32[128]{0:T(128)S(1)}, f32[128]{0:T(128)}, u32[]{:S(2)}) copy-start(f32[128]{0:T(128)} %param.17) | copy-start | bytes 1540
  23.1 2.8 %collective-permute-start.8 = (bf16[256,128]{1,0:T(8,128)(2,1)S(1)}, bf16[256,128]{1,0:T(8,128)(2,1)S(1)}, u32[]{:S(2)}, u32[]{:S(2)}) collective-permute-start(bf16[256,128]{1,0:T(8,128)(2,1)S(1)} %constant_dynamic-update-slice_fusion.mine_ref), channel_id=1, source_target_pairs={{0,1},{1,0},{2,3},{3,2},{4,5},{5,4},{6,7},{7,6},{8,9},{9,8},{10,11... | collective-permute-start | bytes 196616 | tf_op jit(solution)/shard_map/ppermute | solution.py:231

commit v11 on v10

--- a/solution.py
+++ b/solution.py
@@ -48,13 +48,23 @@
     total = (total + jnp.concatenate([bl_ref[...]] * fold, axis=1)) * scale
     for s in range(seqs):
         left_f32[pl.ds(s, quarter, stride=seqs), :] = total[s * quarter:(s + 1) * quarter]
-    right_ref, *left_refs = outs
+    own_ref, *message_refs = outs
     here = lax.axis_index("row")
-    for step, left_ref in zip(half_steps(len(left_refs)), left_refs):
-        rows = left_ref.shape[0]
-        block = source_at(here, step) % len(left_refs)
-        left_ref[...] = left_f32[pl.ds(pl.multiple_of(block * rows, rows), rows), :].astype(jnp.bfloat16)
-    right_ref[...] = right_f32[...].astype(jnp.bfloat16)
+    rows = own_ref.shape[0]
+    chips = left_f32.shape[0] // rows
+
+    def left_for(step):
+        block = source_at(here, step) % chips
+        return left_f32[pl.ds(pl.multiple_of(block * rows, rows), rows), :].astype(jnp.bfloat16)
+
+    own_ref[...] = left_for((0, 0))
+    right = right_f32[...].astype(jnp.bfloat16)
+    for step, message_ref in zip(direct_steps(chips), message_refs):
+        message_ref[:right.shape[0]] = right
+        message_ref[right.shape[0]:] = left_for(step)
+    same_half = here // chips == lax.axis_index("col")
+    for (a, b), message_ref in zip(far_steps(chips), message_refs[chips:]):
+        message_ref[...] = jnp.where(same_half, left_for((a + 1, b)), left_for((a, b)))
 
 
 def features(alignment, ln_gain, ln_bias, w_left, b_left, w_right, b_right, row_count, col_count):
@@ -62,7 +72,8 @@
     c = w_left.shape[1]
     rows = seqs * width * c // LANES
     chips = row_count // col_count
-    shapes = [(rows, LANES)] + [(rows // chips, LANES)] * chips
+    part = rows // chips
+    shapes = [(n, LANES) for n in [part] + [rows + part] * chips + [part] * (chips // 2)]
     operands = (alignment, ln_gain.reshape(1, -1), ln_bias.reshape(1, -1), w_left.T, b_left.reshape(1, -1),
                 w_right.T, b_right.reshape(1, -1))
     return pl.pallas_call(
@@ -91,17 +102,16 @@
         [flat[pl.ds(m * seqs + s, sources, stride=inner * seqs), :] for s in range(seqs)], axis=0)
 
 
-def prepare_kernel(seqs, c, mine_ref, other_ref, w_ref, bias_ref, own_right_ref,
+def prepare_kernel(seqs, c, left_at, mine_ref, other_ref, w_ref, bias_ref, own_right_ref,
                    left_ref, weights_ref, right_ref, bias_out_ref, left_f32, w_f32):
     sources, left_rows, _ = left_f32.shape
-    chips = sources // 2
-    same_half = lax.axis_index("row") // chips == lax.axis_index("col")
+    same_half = lax.axis_index("row") // (sources // 2) == lax.axis_index("col")
 
     def block(n):
-        first = n % chips * left_rows
+        first, of_same_half = left_at[n][0] * left_rows, left_at[n][1]
         mine = mine_ref[first:first + left_rows].astype(jnp.float32)
         other = other_ref[first:first + left_rows].astype(jnp.float32)
-        return jnp.where(same_half == (n < chips), mine, other)
+        return jnp.where(same_half == of_same_half, mine, other)
 
     left_of = sequence_rows(block, left_f32, left_rows // seqs, seqs)
     for k in range(left_rows // seqs):
@@ -109,18 +119,18 @@
     w_f32[...] = w_ref[...].astype(jnp.float32)
     for e in range(c):
         weights_ref[:, e * c:(e + 1) * c] = w_f32[pl.ds(e, c, stride=c), :].T.astype(jnp.bfloat16)
-    right_ref[...] = own_right_ref[...]
+    right_ref[...] = own_right_ref[:right_ref.shape[0]]
     bias_out_ref[...] = bias_ref[...]
 
 
-def prepare(mine, other, w_out, b_out, right, sources, seqs, c):
-    left_rows = mine.shape[0] * 2 // sources
+def prepare(mine, other, left_at, left_rows, w_out, b_out, right, seqs, c):
+    sources = len(left_at)
     z = w_out.shape[1]
     outs = [((left_rows // seqs * LANES, sources * seqs), jnp.bfloat16), ((z, w_out.shape[0]), jnp.bfloat16),
-            (right.shape, jnp.bfloat16), ((1, z), jnp.float32)]
+            ((right.shape[0] - left_rows, LANES), jnp.bfloat16), ((1, z), jnp.float32)]
     operands = (mine, other, w_out, b_out.reshape(1, -1), right)
     return pl.pallas_call(
-        functools.partial(prepare_kernel, seqs, c),
+        functools.partial(prepare_kernel, seqs, c, left_at),
         grid=(1,),
         out_shape=[jax.ShapeDtypeStruct(*out) for out in outs],
         in_specs=[whole(a.shape) for a in operands],
@@ -194,21 +204,27 @@
     return here ^ (2 * step[0] + step[1])
 
 
-def half_steps(chips):
-    return [(a, b) for b in range(2) for a in range(chips // 2)]
+def direct_steps(chips):
+    return [(a, 0) for a in range(1, chips)] + [(0, 1)]
+
+
+def far_steps(chips):
+    return [(a, 1) for a in range(chips // 2)]
 
 
 def fetch(array, step, count):
     return lax.ppermute(array, "row", [(source_at(r, step), r) for r in range(count)])
 
 
-def fetch_left(array, step, count):
+def fetch_far(array, step, count):
     chips = count // 2
+    a, b = step
     moves = []
     for r in range(count):
-        for core in range(2):
-            to = source_at(r % chips, step) + core * chips
-            moves.append((2 * r + core, 2 * to + (core if r // chips == core else 1 - core)))
+        half = r // chips
+        if a + 1 < chips // 2:
+            moves.append((2 * source_at(r, (a + 1, b)) + half, 2 * r + half))
+        moves.append((2 * source_at(r, (a + chips // 2, b)) + half, 2 * r + 1 - half))
     return lax.ppermute(array, ("row", "col"), moves)
 
 
@@ -217,21 +233,23 @@
     c = w_left.shape[1]
     row_count = lax.axis_size("row")
     col_count = lax.axis_size("col")
-    right, *lefts = features(alignment, ln_gain, ln_bias, w_left, b_left, w_right, b_right, row_count, col_count)
-    chips = along = row_count // 2
-    rows = right.shape[0]
-
-    line = [fetch(right, (a, 0), row_count) for a in range(1, along)]
-    across = fetch(right, (0, 1), row_count)
-    across, *held = lax.optimization_barrier((across, *line, *lefts[1:]))
-    line, lefts[1:] = held[:along - 1], held[along - 1:]
-    far = fetch(jnp.concatenate(line), (0, 1), row_count)
-
-    mine = jnp.concatenate([fetch_left(left, step, row_count) for step, left in zip(half_steps(chips), lefts)])
+    own, *messages = features(alignment, ln_gain, ln_bias, w_left, b_left, w_right, b_right, row_count, col_count)
+    along = row_count // 2
+    direct = messages[:along]
+    left_rows = own.shape[0]
+    rows = direct[0].shape[0] - left_rows
+
+    *line, across = [fetch(message, step, row_count) for step, message in zip(direct_steps(along), direct)]
+    beyond = [fetch_far(message, step, row_count) for step, message in zip(far_steps(along), messages[along:])]
+    across, *line = lax.optimization_barrier((across, *line))
+    far = fetch(jnp.concatenate([block[:rows] for block in line]), (0, 1), row_count)
+
+    mine = jnp.concatenate([own] + [block[rows:] for block in (*line, across)] + beyond)
     other = lax.ppermute(mine, "col", [(0, 1), (1, 0)])
-    left, weights, right, bias = prepare(mine, other, w_out, b_out, right, row_count, seqs, c)
-    places = [[(a, 0) for a in range(along)], [(along, 0)] + [(along + 1, a * rows) for a in range(along - 1)]]
-    right_at = [places[b][half * (along // 2) + a] for half in range(2) for a, b in half_steps(chips)]
+    left_at = [(a, True) for a in range(along + 1)]
+    left_at += [(along + a, True) if a < along // 2 else (a + 1 + along // 2, False) for a in range(1, along)]
+    left, weights, right, bias = prepare(mine, other, left_at, left_rows, w_out, b_out, direct[0], seqs, c)
+    right_at = [(a, 0) for a in range(along + 1)] + [(along + 1, a * rows) for a in range(along - 1)]
     return pairs(left, weights, bias, [right, *line, across, far], right_at, seqs, c, width)
 
 

time: 33.8 us -> 32.4 us (0.959)
  starting transfers between devices: 16.2 us -> 11 us
  local copies, waits for them, and re-layouts: 0.05 us -> 2.24 us
  waiting for transfers between devices: 8.62 us -> 9.95 us
    ppermute x5, starting transfers between devices: 9.44 us -> 6.32 us  [fetch(): lax.ppermute(array, 'row', [(source_at(r, step), r) for r in range(count)])]
    ppermute x5, waiting for transfers between devices: 6.48 us -> 8.63 us  [fetch(): lax.ppermute(array, 'row', [(source_at(r, step), r) for r in range(count)])]
    ppermute x1, starting transfers between devices: 1.89 us -> 0.07 us  [on_device(): other = lax.ppermute(mine, 'col', [(0, 1), (1, 0)])]
    unnamed x13 -> x18, local copies, waits for them, and re-layouts: 0.04 us -> 1.41 us
    ppermute x4 -> x2, waiting for transfers between devices: 1.24 us -> 0.01 us  [fetch_far(): return lax.ppermute(array, ('row', 'col'), moves)]
    slice x0 -> x4, local copies, waits for them, and re-layouts: none -> 0.82 us  [on_device(): block[:rows]]
    ppermute x1, waiting for transfers between devices: 0.9 us -> 1.31 us  [on_device(): other = lax.ppermute(mine, 'col', [(0, 1), (1, 0)])]
    ppermute x4 -> x2, starting transfers between devices: 4.85 us -> 4.62 us  [fetch_far(): return lax.ppermute(array, ('row', 'col'), moves)]
  transfers between devices with their start and end apart: 10 -> 8, of which waited for: 5 -> 5; matrix products, arithmetic and copies ran while one was open for 0% -> 3% of each run, Pallas kernels for 3% -> 3%
where the time goes in v11:
time: 32.4 us; the launch traced here: 32.1 us
  starting transfers between devices  11 us (34%)
  waiting for transfers between devices  9.95 us (31%)
  Pallas kernels  8.77 us (27%)
  local copies, waits for them, and re-layouts  2.24 us (7%)
    ppermute x5, waiting for transfers between devices, fetch(): lax.ppermute(array, 'row', [(source_at(r, step), r) for r in range(count)])  8.63 us
    ppermute x5, starting transfers between devices, fetch(): lax.ppermute(array, 'row', [(source_at(r, step), r) for r in range(count)])  6.32 us
    pallas_call x1, Pallas kernels, pairs(): pl.pallas_call(functools.partial(pair_kernel, seqs, c, right_at), grid=(r...  5.16 us
    ppermute x2, starting transfers between devices, fetch_far(): return lax.ppermute(array, ('row', 'col'), moves)  4.62 us
    pallas_call x1, Pallas kernels, features(): pl.pallas_call(functools.partial(features_kernel, 1.0 / (seqs * row_count...  2.61 us
    unnamed x18, local copies, waits for them, and re-layouts  1.41 us
    ppermute x1, waiting for transfers between devices, on_device(): other = lax.ppermute(mine, 'col', [(0, 1), (1, 0)])  1.31 us
    pallas_call x1, Pallas kernels, prepare(): pl.pallas_call(functools.partial(prepare_kernel, seqs, c, left_at), grid=...  1 us
  transfers between devices with their start and end apart: 8, of which 5 were waited for; matrix products, arithmetic and copies ran while one was open for 3% of the time, Pallas kernels for 3%

profile of v11, /device:TPU:0, one launch (start us, length us, event | category | flops | bytes accessed | tf_op | source)
XLA Modules:
  0.0 32.1 jit_solution(10646807677402539508)
XLA Ops:
  0.0 2.6 %features.1 = (bf16[64,128]{1,0:T(8,128)(2,1)}, bf16[320,128]{1,0:T(8,128)(2,1)}, bf16[320,128]{1,0:T(8,128)(2,1)}, bf16[320,128]{1,0:T(8,128)(2,1)}, bf16[320,1...) custom-call(bf16[8,128,256]{2,1,0:T(8,128)(2,1)} %x_ref.1, f32[1,256]{1,0:T(1,128)} %bitcast.10, ...), custom_call_target="tpu_custom_call" | custom-call | tf_op jit(solution)/shard_map/features/pallas_call | solution.py:79
  2.6 4.0 %collective-permute-start.4 = (bf16[64,128]{1,0:T(8,128)(2,1)}, bf16[64,128]{1,0:T(8,128)(2,1)S(1)}, u32[]{:S(2)}, u32[]{:S(2)}) collective-permute-start(bf16[64,128]{1,0:T(8,128)(2,1)} %get-tuple-element.29), channel_id=1, source_target_pairs={{6,0},{10,1},{4,2},{8,3},{2,4},{14,5},{0,6},{12,7},{15,9},{3,8},{1... | collective-permute-start | bytes 49160 | tf_op jit(solution)/shard_map/ppermute | solution.py:228
  6.6 0.5 %collective-permute-start = (bf16[320,128]{1,0:T(8,128)(2,1)}, bf16[320,128]{1,0:T(8,128)(2,1)S(1)}, u32[]{:S(2)}, u32[]{:S(2)}) collective-permute-start(bf16[320,128]{1,0:T(8,128)(2,1)} %get-tuple-element.21), channel_id=1, source_target_pairs={{2,0},{0,2},{6,4},{4,6},{10,8},{8,10},{14,12},{12,14},{3,1},{1,3},... | collective-permute-start | bytes 245768 | tf_op jit(solution)/shard_map/ppermute | solution.py:216
  7.1 1.1 %collective-permute-start.2 = (bf16[320,128]{1,0:T(8,128)(2,1)}, bf16[320,128]{1,0:T(8,128)(2,1)S(1)}, u32[]{:S(2)}, u32[]{:S(2)}) collective-permute-start(bf16[320,128]{1,0:T(8,128)(2,1)} %get-tuple-element.23), channel_id=1, source_target_pairs={{8,0},{10,2},{12,4},{14,6},{0,8},{2,10},{4,12},{6,14},{9,1},{11,3}... | collective-permute-start | bytes 245768 | tf_op jit(solution)/shard_map/ppermute | solution.py:216
  8.2 1.3 %collective-permute-start.3 = (bf16[320,128]{1,0:T(8,128)(2,1)}, bf16[320,128]{1,0:T(8,128)(2,1)S(1)}, u32[]{:S(2)}, u32[]{:S(2)}) collective-permute-start(bf16[320,128]{1,0:T(8,128)(2,1)} %get-tuple-element.24), channel_id=1, source_target_pairs={{12,0},{14,2},{8,4},{10,6},{4,8},{6,10},{0,12},{2,14},{13,1},{15,3... | collective-permute-start | bytes 245768 | tf_op jit(solution)/shard_map/ppermute | solution.py:216
  9.6 1.0 %collective-permute-start.1 = (bf16[320,128]{1,0:T(8,128)(2,1)}, bf16[320,128]{1,0:T(8,128)(2,1)S(1)}, u32[]{:S(2)}, u32[]{:S(2)}) collective-permute-start(bf16[320,128]{1,0:T(8,128)(2,1)} %get-tuple-element.22.own_right_ref), channel_id=1, source_target_pairs={{4,0},{6,2},{0,4},{2,6},{12,8},{14,10},{8,12},{10,14},{5,1},{7,3},... | collective-permute-start | bytes 245768 | tf_op jit(solution)/shard_map/ppermute | solution.py:216
  10.6 0.7 %constant_dynamic-update-slice_fusion.6 = bf16[448,128]{1,0:T(8,128)(2,1)S(1)} fusion(bf16[64,128]{1,0:T(8,128)(2,1)} %get-tuple-element.20), kind=kLoop, calls=%fused_computation.7 | loop fusion | bytes 32768
  11.3 0.6 %collective-permute-done.refs_4_ = bf16[320,128]{1,0:T(8,128)(2,1)S(1)} collective-permute-done((bf16[320,128]{1,0:T(8,128)(2,1)}, bf16[320,128]{1,0:T(8,128)(2,1)S(1)}, u32[]{:S(2)}, u32[]{:S(2)}) %collective-permute-start) | collective-permute-done | bytes 81952 | tf_op jit(solution)/shard_map/ppermute | solution.py:216
  12.0 0.7 %collective-permute-start.5 = (bf16[64,128]{1,0:T(8,128)(2,1)S(1)}, bf16[64,128]{1,0:T(8,128)(2,1)S(1)}, u32[]{:S(2)}, u32[]{:S(2)}) collective-permute-start(bf16[64,128]{1,0:T(8,128)(2,1)S(1)} %copy-done.5), channel_id=1, source_target_pairs={{14,1},{12,3},{10,5},{8,7},{7,8},{5,10},{3,12},{1,14},{30,17},{28,... | collective-permute-start | bytes 49160 | tf_op jit(solution)/shard_map/ppermute | solution.py:228
  12.6 4.1 %collective-permute-done.2.refs_2_ = bf16[320,128]{1,0:T(8,128)(2,1)S(1)} collective-permute-done((bf16[320,128]{1,0:T(8,128)(2,1)}, bf16[320,128]{1,0:T(8,128)(2,1)S(1)}, u32[]{:S(2)}, u32[]{:S(2)}) %collective-permute-start.2) | collective-permute-done | bytes 81952 | tf_op jit(solution)/shard_map/ppermute | solution.py:216
  16.7 0.0 collective-permute-done.3.refs_3_
  16.7 1.2 %collective-permute-done.1.refs_1_ = bf16[320,128]{1,0:T(8,128)(2,1)S(1)} collective-permute-done((bf16[320,128]{1,0:T(8,128)(2,1)}, bf16[320,128]{1,0:T(8,128)(2,1)S(1)}, u32[]{:S(2)}, u32[]{:S(2)}) %collective-permute-start.1) | collective-permute-done | bytes 81952 | tf_op jit(solution)/shard_map/ppermute | solution.py:216
  17.9 0.6 %copy-done.1 = bf16[320,128]{1,0:T(8,128)(2,1)} copy-done((bf16[320,128]{1,0:T(8,128)(2,1)}, bf16[320,128]{1,0:T(8,128)(2,1)S(1)}, u32[]{:S(2)}) %copy-start.1) | copy-done | bytes 81944
  18.6 0.8 %slice-done = bf16[256,128]{1,0:T(8,128)(2,1)S(1)} async-done(((bf16[320,128]{1,0:T(8,128)(2,1)}), bf16[256,128]{1,0:T(8,128)(2,1)S(1)}, s32[]{:S(2)}) %slice-start) | async-done | bytes 65560 | tf_op jit(solution)/shard_map/slice | solution.py:245
  19.4 0.0 copy-start.3
  19.4 2.3 %collective-permute-start.7 = (bf16[768,128]{1,0:T(8,128)(2,1)S(1)}, bf16[768,128]{1,0:T(8,128)(2,1)S(1)}, u32[]{:S(2)}, u32[]{:S(2)}) collective-permute-start(bf16[768,128]{1,0:T(8,128)(2,1)S(1)} %pad_maximum_fusion), channel_id=1, source_target_pairs={{2,0},{0,2},{6,4},{4,6},{10,8},{8,10},{14,12},{12,14},{3,1},{1,3},... | collective-permute-start | bytes 589832 | tf_op jit(solution)/shard_map/ppermute | solution.py:216
  21.7 0.0 collective-permute-done.4
  21.8 0.0 collective-permute-done.5
  21.8 0.0 copy-start.4
  21.8 0.1 collective-permute-start.6
  21.9 1.3 %collective-permute-done.6.other_ref = bf16[448,128]{1,0:T(8,128)(2,1)S(1)} collective-permute-done((bf16[448,128]{1,0:T(8,128)(2,1)S(1)}, bf16[448,128]{1,0:T(8,128)(2,1)S(1)}, u32[]{:S(2)}, u32[]{:S(2)}) %collective-permute-start.6) | collective-permute-done | bytes 114720 | tf_op jit(solution)/shard_map/ppermute | solution.py:248
  23.2 1.0 %prepare.1 = (bf16[1024,64]{1,0:T(8,128)(2,1)S(1)}, bf16[128,1024]{1,0:T(8,128)(2,1)S(1)}, bf16[256,128]{1,0:T(8,128)(2,1)S(1)}, f32[1,128]{1,0:T(1,128)S(1)}) custom-call(bf16[448,128]{1,0:T(8,128)(2,1)S(1)} %constant_dynamic-update-slice_fusion.mine_ref, bf16[448,128]{1,0:T(8,128)(2,1)S(1)} %collective-permute-done.6.other_ref, ...), custom_call_target="tpu_custom_call" | custom-call | tf_op jit(solution)/shard_map/prepare/pallas_call | solution.py:132
  24.2 2.7 %collective-permute-done.7.refs_5_ = bf16[768,128]{1,0:T(8,128)(2,1)S(1)} collective-permute-done((bf16[768,128]{1,0:T(8,128)(2,1)S(1)}, bf16[768,128]{1,0:T(8,128)(2,1)S(1)}, u32[]{:S(2)}, u32[]{:S(2)}) %collective-permute-start.7) | collective-permute-done | bytes 196640 | tf_op jit(solution)/shard_map/ppermute | solution.py:216
  26.9 5.2 %pairs.1 = bf16[32,128,128]{2,1,0:T(8,128)(2,1)} custom-call(bf16[1024,64]{1,0:T(8,128)(2,1)S(1)} %get-tuple-element.31.left_ref, bf16[128,1024]{1,0:T(8,128)(2,1)S(1)} %get-tuple-element.32.weights_ref, f32[1,128]{1,0:T(1,128)S(1)} %get-tuple-element.33.bias_ref, bf16[256,128]{1,0:T(8,128)(2,1)S(1)} %get-tuple-element.34.refs_0_, ...), custom_call_target="tpu_custom_call" | custom-call | flops 1610612736 | bytes 1048576 | tf_op jit(solution)/shard_map/pairs/pallas_call | solution.py:187
  (19 shorter events, 0.1 us)
Async XLA Ops:
  2.6 19.1 %collective-permute-start.4 = (bf16[64,128]{1,0:T(8,128)(2,1)}, bf16[64,128]{1,0:T(8,128)(2,1)S(1)}, u32[]{:S(2)}, u32[]{:S(2)}) collective-permute-start(bf16[64,128]{1,0:T(8,128)(2,1)} %get-tuple-element.29), channel_id=1, source_target_pairs={{6,0},{10,1},{4,2},{8,3},{2,4},{14,5},{0,6},{12,7},{15,9},{3,8},{1... | collective-permute-start | bytes 49160 | tf_op jit(solution)/shard_map/ppermute | solution.py:228
  6.6 5.4 %collective-permute-start = (bf16[320,128]{1,0:T(8,128)(2,1)}, bf16[320,128]{1,0:T(8,128)(2,1)S(1)}, u32[]{:S(2)}, u32[]{:S(2)}) collective-permute-start(bf16[320,128]{1,0:T(8,128)(2,1)} %get-tuple-element.21), channel_id=1, source_target_pairs={{2,0},{0,2},{6,4},{4,6},{10,8},{8,10},{14,12},{12,14},{3,1},{1,3},... | collective-permute-start | bytes 245768 | tf_op jit(solution)/shard_map/ppermute | solution.py:216
  7.1 9.6 %collective-permute-start.2 = (bf16[320,128]{1,0:T(8,128)(2,1)}, bf16[320,128]{1,0:T(8,128)(2,1)S(1)}, u32[]{:S(2)}, u32[]{:S(2)}) collective-permute-start(bf16[320,128]{1,0:T(8,128)(2,1)} %get-tuple-element.23), channel_id=1, source_target_pairs={{8,0},{10,2},{12,4},{14,6},{0,8},{2,10},{4,12},{6,14},{9,1},{11,3}... | collective-permute-start | bytes 245768 | tf_op jit(solution)/shard_map/ppermute | solution.py:216
  8.2 8.5 %collective-permute-start.3 = (bf16[320,128]{1,0:T(8,128)(2,1)}, bf16[320,128]{1,0:T(8,128)(2,1)S(1)}, u32[]{:S(2)}, u32[]{:S(2)}) collective-permute-start(bf16[320,128]{1,0:T(8,128)(2,1)} %get-tuple-element.24), channel_id=1, source_target_pairs={{12,0},{14,2},{8,4},{10,6},{4,8},{6,10},{0,12},{2,14},{13,1},{15,3... | collective-permute-start | bytes 245768 | tf_op jit(solution)/shard_map/ppermute | solution.py:216
  9.6 8.3 %collective-permute-start.1 = (bf16[320,128]{1,0:T(8,128)(2,1)}, bf16[320,128]{1,0:T(8,128)(2,1)S(1)}, u32[]{:S(2)}, u32[]{:S(2)}) collective-permute-start(bf16[320,128]{1,0:T(8,128)(2,1)} %get-tuple-element.22.own_right_ref), channel_id=1, source_target_pairs={{4,0},{6,2},{0,4},{2,6},{12,8},{14,10},{8,12},{10,14},{5,1},{7,3},... | collective-permute-start | bytes 245768 | tf_op jit(solution)/shard_map/ppermute | solution.py:216
  10.6 1.4 %copy-start.5 = (bf16[64,128]{1,0:T(8,128)(2,1)S(1)}, bf16[64,128]{1,0:T(8,128)(2,1)}, u32[]{:S(2)}) copy-start(bf16[64,128]{1,0:T(8,128)(2,1)} %get-tuple-element.30) | copy-start | bytes 49156
  12.0 9.8 %collective-permute-start.5 = (bf16[64,128]{1,0:T(8,128)(2,1)S(1)}, bf16[64,128]{1,0:T(8,128)(2,1)S(1)}, u32[]{:S(2)}, u32[]{:S(2)}) collective-permute-start(bf16[64,128]{1,0:T(8,128)(2,1)S(1)} %copy-done.5), channel_id=1, source_target_pairs={{14,1},{12,3},{10,5},{8,7},{7,8},{5,10},{3,12},{1,14},{30,17},{28,... | collective-permute-start | bytes 49160 | tf_op jit(solution)/shard_map/ppermute | solution.py:228
  17.9 0.6 %copy-start.1 = (bf16[320,128]{1,0:T(8,128)(2,1)}, bf16[320,128]{1,0:T(8,128)(2,1)S(1)}, u32[]{:S(2)}) copy-start(bf16[320,128]{1,0:T(8,128)(2,1)S(1)} %collective-permute-done.1.refs_1_) | copy-start | bytes 245764
  18.5 0.8 %slice-start = ((bf16[320,128]{1,0:T(8,128)(2,1)}), bf16[256,128]{1,0:T(8,128)(2,1)S(1)}, s32[]{:S(2)}) async-start(bf16[320,128]{1,0:T(8,128)(2,1)} %copy-done.1), calls=%async_computation | async-start | bytes 131072 | tf_op jit(solution)/shard_map/slice | solution.py:245
  18.6 4.6 %copy-start = (bf16[1024,128]{1,0:T(8,128)(2,1)S(1)}, bf16[1024,128]{1,0:T(8,128)(2,1)}, u32[]{:S(2)}) copy-start(bf16[1024,128]{1,0:T(8,128)(2,1)} %w_ref.1) | copy-start | bytes 786436
  19.4 3.8 %copy-start.3 = (bf16[320,128]{1,0:T(8,128)(2,1)S(1)}, bf16[320,128]{1,0:T(8,128)(2,1)}, u32[]{:S(2)}) copy-start(bf16[320,128]{1,0:T(8,128)(2,1)} %get-tuple-element.22.own_right_ref) | copy-start | bytes 245764
  19.4 7.5 %collective-permute-start.7 = (bf16[768,128]{1,0:T(8,128)(2,1)S(1)}, bf16[768,128]{1,0:T(8,128)(2,1)S(1)}, u32[]{:S(2)}, u32[]{:S(2)}) collective-permute-start(bf16[768,128]{1,0:T(8,128)(2,1)S(1)} %pad_maximum_fusion), channel_id=1, source_target_pairs={{2,0},{0,2},{6,4},{4,6},{10,8},{8,10},{14,12},{12,14},{3,1},{1,3},... | collective-permute-start | bytes 589832 | tf_op jit(solution)/shard_map/ppermute | solution.py:216
  21.8 1.4 %copy-start.4 = (f32[128]{0:T(128)S(1)}, f32[128]{0:T(128)}, u32[]{:S(2)}) copy-start(f32[128]{0:T(128)} %param.17) | copy-start | bytes 1540
  21.8 1.4 %collective-permute-start.6 = (bf16[448,128]{1,0:T(8,128)(2,1)S(1)}, bf16[448,128]{1,0:T(8,128)(2,1)S(1)}, u32[]{:S(2)}, u32[]{:S(2)}) collective-permute-start(bf16[448,128]{1,0:T(8,128)(2,1)S(1)} %constant_dynamic-update-slice_fusion.mine_ref), channel_id=1, source_target_pairs={{0,1},{1,0},{2,3},{3,2},{4,5},{5,4},{6,7},{7,6},{8,9},{9,8},{10,11... | collective-permute-start | bytes 344072 | tf_op jit(solution)/shard_map/ppermute | solution.py:248
  23.2 3.7 %copy-start.2 = (bf16[320,128]{1,0:T(8,128)(2,1)S(1)}, bf16[320,128]{1,0:T(8,128)(2,1)}, u32[]{:S(2)}) copy-start(bf16[320,128]{1,0:T(8,128)(2,1)} %copy-done.1) | copy-start | bytes 245764

commit v12 on v11

--- a/solution.py
+++ b/solution.py
@@ -239,18 +239,20 @@
     left_rows = own.shape[0]
     rows = direct[0].shape[0] - left_rows
 
-    *line, across = [fetch(message, step, row_count) for step, message in zip(direct_steps(along), direct)]
+    line = [fetch(message, step, row_count) for step, message in reversed([*zip(direct_steps(along), direct[:-1])])][::-1]
     beyond = [fetch_far(message, step, row_count) for step, message in zip(far_steps(along), messages[along:])]
-    across, *line = lax.optimization_barrier((across, *line))
-    far = fetch(jnp.concatenate([block[:rows] for block in line]), (0, 1), row_count)
-
-    mine = jnp.concatenate([own] + [block[rows:] for block in (*line, across)] + beyond)
+    beyond[0], beside = lax.optimization_barrier((beyond[0], direct[-1]))
+    across = fetch(beside, (0, 1), row_count)
+    far = [fetch(block[:rows], (0, 1), row_count) for block in reversed(line)][::-1]
+    *far[:-1], held = lax.optimization_barrier((*far[:-1], tuple(line)))
+
+    mine = jnp.concatenate([own] + [block[rows:] for block in (*held, across)] + beyond)
     other = lax.ppermute(mine, "col", [(0, 1), (1, 0)])
     left_at = [(a, True) for a in range(along + 1)]
     left_at += [(along + a, True) if a < along // 2 else (a + 1 + along // 2, False) for a in range(1, along)]
     left, weights, right, bias = prepare(mine, other, left_at, left_rows, w_out, b_out, direct[0], seqs, c)
-    right_at = [(a, 0) for a in range(along + 1)] + [(along + 1, a * rows) for a in range(along - 1)]
-    return pairs(left, weights, bias, [right, *line, across, far], right_at, seqs, c, width)
+    right_at = [(n, 0) for n in range(row_count)]
+    return pairs(left, weights, bias, [right, *line, across, *far], right_at, seqs, c, width)
 
 
 def solution(mesh):

time: 32.4 us -> 31.8 us (0.981)
  starting transfers between devices: 11 us -> 17.6 us
  waiting for transfers between devices: 9.95 us -> 5.06 us
  local copies, waits for them, and re-layouts: 2.24 us -> 0.09 us
    ppermute x5 -> x7, starting transfers between devices: 6.32 us -> 15.5 us  [fetch(): lax.ppermute(array, 'row', [(source_at(r, step), r) for r in range(count)])]
    ppermute x5 -> x7, waiting for transfers between devices: 8.63 us -> 5.05 us  [fetch(): lax.ppermute(array, 'row', [(source_at(r, step), r) for r in range(count)])]
    ppermute x2, starting transfers between devices: 4.62 us -> 2.06 us  [fetch_far(): return lax.ppermute(array, ('row', 'col'), moves)]
    unnamed x18 -> x16, local copies, waits for them, and re-layouts: 1.41 us -> 0.07 us
    ppermute x1, waiting for transfers between devices: 1.31 us -> 0.01 us  [on_device(): other = lax.ppermute(mine, 'col', [(0, 1), (1, 0)])]
    slice x4 -> x3, local copies, waits for them, and re-layouts: 0.82 us -> 0.02 us  [on_device(): block[:rows]]
  transfers between devices with their start and end apart: 8 -> 10, of which waited for: 5 -> 4; matrix products, arithmetic and copies ran while one was open for 3% -> 0% of each run, Pallas kernels for 3% -> 3%
where the time goes in v12:
time: 31.8 us; the launch traced here: 31.7 us
  starting transfers between devices  17.6 us (55%)
  Pallas kernels  8.78 us (28%)
  waiting for transfers between devices  5.06 us (16%)
    ppermute x7, starting transfers between devices, fetch(): lax.ppermute(array, 'row', [(source_at(r, step), r) for r in range(count)])  15.5 us
    pallas_call x1, Pallas kernels, pairs(): pl.pallas_call(functools.partial(pair_kernel, seqs, c, right_at), grid=(r...  5.16 us
    ppermute x7, waiting for transfers between devices, fetch(): lax.ppermute(array, 'row', [(source_at(r, step), r) for r in range(count)])  5.05 us
    pallas_call x1, Pallas kernels, features(): pl.pallas_call(functools.partial(features_kernel, 1.0 / (seqs * row_count...  2.62 us
    ppermute x2, starting transfers between devices, fetch_far(): return lax.ppermute(array, ('row', 'col'), moves)  2.06 us
    pallas_call x1, Pallas kernels, prepare(): pl.pallas_call(functools.partial(prepare_kernel, seqs, c, left_at), grid=...  1 us
  transfers between devices with their start and end apart: 10, of which 4 were waited for; matrix products, arithmetic and copies ran while one was open for 0% of the time, Pallas kernels for 3%

profile of v12, /device:TPU:0, one launch (start us, length us, event | category | flops | bytes accessed | tf_op | source)
XLA Modules:
  0.0 31.7 jit_solution(6417380655155778055)
XLA Ops:
  0.0 2.6 %features.1 = (bf16[64,128]{1,0:T(8,128)(2,1)}, bf16[320,128]{1,0:T(8,128)(2,1)}, bf16[320,128]{1,0:T(8,128)(2,1)}, bf16[320,128]{1,0:T(8,128)(2,1)}, bf16[320,1...) custom-call(bf16[8,128,256]{2,1,0:T(8,128)(2,1)} %x_ref.1, f32[1,256]{1,0:T(1,128)} %bitcast.10, ...), custom_call_target="tpu_custom_call" | custom-call | tf_op jit(solution)/shard_map/features/pallas_call | solution.py:79
  2.6 4.0 %collective-permute-start.2 = (bf16[320,128]{1,0:T(8,128)(2,1)}, bf16[320,128]{1,0:T(8,128)(2,1)S(1)}, u32[]{:S(2)}, u32[]{:S(2)}) collective-permute-start(bf16[320,128]{1,0:T(8,128)(2,1)} %get-tuple-element.25), channel_id=1, source_target_pairs={{8,0},{10,2},{12,4},{14,6},{0,8},{2,10},{4,12},{6,14},{9,1},{11,3}... | collective-permute-start | bytes 245768 | tf_op jit(solution)/shard_map/ppermute | solution.py:216
  6.7 1.6 %collective-permute-start = (bf16[320,128]{1,0:T(8,128)(2,1)}, bf16[320,128]{1,0:T(8,128)(2,1)S(1)}, u32[]{:S(2)}, u32[]{:S(2)}) collective-permute-start(bf16[320,128]{1,0:T(8,128)(2,1)} %get-tuple-element.24.own_right_ref), channel_id=1, source_target_pairs={{4,0},{6,2},{0,4},{2,6},{12,8},{14,10},{8,12},{10,14},{5,1},{7,3},... | collective-permute-start | bytes 245768 | tf_op jit(solution)/shard_map/ppermute | solution.py:216
  8.2 1.4 %collective-permute-start.5 = (bf16[64,128]{1,0:T(8,128)(2,1)}, bf16[64,128]{1,0:T(8,128)(2,1)S(1)}, u32[]{:S(2)}, u32[]{:S(2)}) collective-permute-start(bf16[64,128]{1,0:T(8,128)(2,1)} %get-tuple-element.30), channel_id=1, source_target_pairs={{6,0},{10,1},{4,2},{8,3},{2,4},{14,5},{0,6},{12,7},{15,9},{3,8},{1... | collective-permute-start | bytes 49160 | tf_op jit(solution)/shard_map/ppermute | solution.py:228
  9.6 0.7 %collective-permute-start.7 = (bf16[64,128]{1,0:T(8,128)(2,1)}, bf16[64,128]{1,0:T(8,128)(2,1)S(1)}, u32[]{:S(2)}, u32[]{:S(2)}) collective-permute-start(bf16[64,128]{1,0:T(8,128)(2,1)} %get-tuple-element.34), channel_id=1, source_target_pairs={{14,1},{12,3},{10,5},{8,7},{7,8},{5,10},{3,12},{1,14},{30,17},{28,... | collective-permute-start | bytes 49160 | tf_op jit(solution)/shard_map/ppermute | solution.py:228
  10.3 4.7 %collective-permute-start.4 = (bf16[320,128]{1,0:T(8,128)(2,1)}, bf16[320,128]{1,0:T(8,128)(2,1)S(1)}, u32[]{:S(2)}, u32[]{:S(2)}) collective-permute-start(bf16[320,128]{1,0:T(8,128)(2,1)} %get-tuple-element.26), channel_id=1, source_target_pairs={{12,0},{14,2},{8,4},{10,6},{4,8},{6,10},{0,12},{2,14},{13,1},{15,3... | collective-permute-start | bytes 245768 | tf_op jit(solution)/shard_map/ppermute | solution.py:216
  15.0 0.0 collective-permute-done.2.refs_2_
  15.0 0.0 copy-start
  15.0 1.6 %collective-permute-start.3 = (bf16[256,128]{1,0:T(8,128)(2,1)S(1)}, bf16[256,128]{1,0:T(8,128)(2,1)S(1)}, u32[]{:S(2)}, u32[]{:S(2)}) collective-permute-start(bf16[256,128]{1,0:T(8,128)(2,1)S(1)} %slice.29), channel_id=1, source_target_pairs={{2,0},{0,2},{6,4},{4,6},{10,8},{8,10},{14,12},{12,14},{3,1},{1,3},... | collective-permute-start | bytes 196616 | tf_op jit(solution)/shard_map/ppermute | solution.py:216
  16.6 0.0 collective-permute-done.refs_1_
  16.6 0.6 %collective-permute-start.1 = (bf16[256,128]{1,0:T(8,128)(2,1)S(1)}, bf16[256,128]{1,0:T(8,128)(2,1)S(1)}, u32[]{:S(2)}, u32[]{:S(2)}) collective-permute-start(bf16[256,128]{1,0:T(8,128)(2,1)S(1)} %slice.28), channel_id=1, source_target_pairs={{2,0},{0,2},{6,4},{4,6},{10,8},{8,10},{14,12},{12,14},{3,1},{1,3},... | collective-permute-start | bytes 196616 | tf_op jit(solution)/shard_map/ppermute | solution.py:216
  17.2 0.0 collective-permute-done.5
  17.2 1.6 %collective-permute-start.6 = (bf16[320,128]{1,0:T(8,128)(2,1)S(1)}, bf16[320,128]{1,0:T(8,128)(2,1)S(1)}, u32[]{:S(2)}, u32[]{:S(2)}) collective-permute-start(bf16[320,128]{1,0:T(8,128)(2,1)S(1)} %copy-done.4), channel_id=1, source_target_pairs={{2,0},{0,2},{6,4},{4,6},{10,8},{8,10},{14,12},{12,14},{3,1},{1,3},... | collective-permute-start | bytes 245768 | tf_op jit(solution)/shard_map/ppermute | solution.py:216
  18.8 0.0 collective-permute-done.4.refs_3_
  18.8 0.6 %collective-permute-done.3.refs_6_ = bf16[256,128]{1,0:T(8,128)(2,1)S(1)} collective-permute-done((bf16[256,128]{1,0:T(8,128)(2,1)S(1)}, bf16[256,128]{1,0:T(8,128)(2,1)S(1)}, u32[]{:S(2)}, u32[]{:S(2)}) %collective-permute-start.3) | collective-permute-done | bytes 65568 | tf_op jit(solution)/shard_map/ppermute | solution.py:216
  19.4 1.5 %collective-permute-done.1.refs_5_ = bf16[256,128]{1,0:T(8,128)(2,1)S(1)} collective-permute-done((bf16[256,128]{1,0:T(8,128)(2,1)S(1)}, bf16[256,128]{1,0:T(8,128)(2,1)S(1)}, u32[]{:S(2)}, u32[]{:S(2)}) %collective-permute-start.1) | collective-permute-done | bytes 65568 | tf_op jit(solution)/shard_map/ppermute | solution.py:216
  21.0 0.9 %collective-permute-done.6.refs_4_ = bf16[320,128]{1,0:T(8,128)(2,1)S(1)} collective-permute-done((bf16[320,128]{1,0:T(8,128)(2,1)S(1)}, bf16[320,128]{1,0:T(8,128)(2,1)S(1)}, u32[]{:S(2)}, u32[]{:S(2)}) %collective-permute-start.6) | collective-permute-done | bytes 81952 | tf_op jit(solution)/shard_map/ppermute | solution.py:216
  21.9 0.1 collective-permute-start.8
  21.9 0.0 copy-start.2
  22.0 1.5 %collective-permute-start.9 = (bf16[256,128]{1,0:T(8,128)(2,1)S(1)}, bf16[256,128]{1,0:T(8,128)(2,1)S(1)}, u32[]{:S(2)}, u32[]{:S(2)}) collective-permute-start(bf16[256,128]{1,0:T(8,128)(2,1)S(1)} %slice.31), channel_id=1, source_target_pairs={{2,0},{0,2},{6,4},{4,6},{10,8},{8,10},{14,12},{12,14},{3,1},{1,3},... | collective-permute-start | bytes 196616 | tf_op jit(solution)/shard_map/ppermute | solution.py:216
  23.4 0.0 collective-permute-done.8.other_ref
  23.5 1.0 %prepare.1 = (bf16[1024,64]{1,0:T(8,128)(2,1)S(1)}, bf16[128,1024]{1,0:T(8,128)(2,1)S(1)}, bf16[256,128]{1,0:T(8,128)(2,1)S(1)}, f32[1,128]{1,0:T(1,128)S(1)}) custom-call(bf16[448,128]{1,0:T(8,128)(2,1)S(1)} %constant_dynamic-update-slice_fusion.mine_ref, bf16[448,128]{1,0:T(8,128)(2,1)S(1)} %collective-permute-done.8.other_ref, ...), custom_call_target="tpu_custom_call" | custom-call | tf_op jit(solution)/shard_map/prepare/pallas_call | solution.py:132
  24.5 2.0 %collective-permute-done.9.refs_7_ = bf16[256,128]{1,0:T(8,128)(2,1)S(1)} collective-permute-done((bf16[256,128]{1,0:T(8,128)(2,1)S(1)}, bf16[256,128]{1,0:T(8,128)(2,1)S(1)}, u32[]{:S(2)}, u32[]{:S(2)}) %collective-permute-start.9) | collective-permute-done | bytes 65568 | tf_op jit(solution)/shard_map/ppermute | solution.py:216
  26.5 5.2 %pairs.1 = bf16[32,128,128]{2,1,0:T(8,128)(2,1)} custom-call(bf16[1024,64]{1,0:T(8,128)(2,1)S(1)} %get-tuple-element.35.left_ref, bf16[128,1024]{1,0:T(8,128)(2,1)S(1)} %get-tuple-element.36.weights_ref, f32[1,128]{1,0:T(1,128)S(1)} %get-tuple-element.37.bias_ref, bf16[256,128]{1,0:T(8,128)(2,1)S(1)} %get-tuple-element.38.refs_0_, ...), custom_call_target="tpu_custom_call" | custom-call | flops 1610612736 | bytes 1048576 | tf_op jit(solution)/shard_map/pairs/pallas_call | solution.py:187
  (19 shorter events, 0.1 us)
Async XLA Ops:
  2.6 12.4 %collective-permute-start.2 = (bf16[320,128]{1,0:T(8,128)(2,1)}, bf16[320,128]{1,0:T(8,128)(2,1)S(1)}, u32[]{:S(2)}, u32[]{:S(2)}) collective-permute-start(bf16[320,128]{1,0:T(8,128)(2,1)} %get-tuple-element.25), channel_id=1, source_target_pairs={{8,0},{10,2},{12,4},{14,6},{0,8},{2,10},{4,12},{6,14},{9,1},{11,3}... | collective-permute-start | bytes 245768 | tf_op jit(solution)/shard_map/ppermute | solution.py:216
  6.7 9.9 %collective-permute-start = (bf16[320,128]{1,0:T(8,128)(2,1)}, bf16[320,128]{1,0:T(8,128)(2,1)S(1)}, u32[]{:S(2)}, u32[]{:S(2)}) collective-permute-start(bf16[320,128]{1,0:T(8,128)(2,1)} %get-tuple-element.24.own_right_ref), channel_id=1, source_target_pairs={{4,0},{6,2},{0,4},{2,6},{12,8},{14,10},{8,12},{10,14},{5,1},{7,3},... | collective-permute-start | bytes 245768 | tf_op jit(solution)/shard_map/ppermute | solution.py:216
  8.2 9.0 %collective-permute-start.5 = (bf16[64,128]{1,0:T(8,128)(2,1)}, bf16[64,128]{1,0:T(8,128)(2,1)S(1)}, u32[]{:S(2)}, u32[]{:S(2)}) collective-permute-start(bf16[64,128]{1,0:T(8,128)(2,1)} %get-tuple-element.30), channel_id=1, source_target_pairs={{6,0},{10,1},{4,2},{8,3},{2,4},{14,5},{0,6},{12,7},{15,9},{3,8},{1... | collective-permute-start | bytes 49160 | tf_op jit(solution)/shard_map/ppermute | solution.py:228
  9.6 12.2 %collective-permute-start.7 = (bf16[64,128]{1,0:T(8,128)(2,1)}, bf16[64,128]{1,0:T(8,128)(2,1)S(1)}, u32[]{:S(2)}, u32[]{:S(2)}) collective-permute-start(bf16[64,128]{1,0:T(8,128)(2,1)} %get-tuple-element.34), channel_id=1, source_target_pairs={{14,1},{12,3},{10,5},{8,7},{7,8},{5,10},{3,12},{1,14},{30,17},{28,... | collective-permute-start | bytes 49160 | tf_op jit(solution)/shard_map/ppermute | solution.py:228
  10.3 8.5 %collective-permute-start.4 = (bf16[320,128]{1,0:T(8,128)(2,1)}, bf16[320,128]{1,0:T(8,128)(2,1)S(1)}, u32[]{:S(2)}, u32[]{:S(2)}) collective-permute-start(bf16[320,128]{1,0:T(8,128)(2,1)} %get-tuple-element.26), channel_id=1, source_target_pairs={{12,0},{14,2},{8,4},{10,6},{4,8},{6,10},{0,12},{2,14},{13,1},{15,3... | collective-permute-start | bytes 245768 | tf_op jit(solution)/shard_map/ppermute | solution.py:216
  15.0 2.2 %copy-start.3 = (bf16[64,128]{1,0:T(8,128)(2,1)S(1)}, bf16[64,128]{1,0:T(8,128)(2,1)}, u32[]{:S(2)}) copy-start(bf16[64,128]{1,0:T(8,128)(2,1)} %get-tuple-element.23) | copy-start | bytes 49156
  15.0 2.2 %copy-start.4 = (bf16[320,128]{1,0:T(8,128)(2,1)S(1)}, bf16[320,128]{1,0:T(8,128)(2,1)}, u32[]{:S(2)}) copy-start(bf16[320,128]{1,0:T(8,128)(2,1)} %get-tuple-element.32) | copy-start | bytes 245764
  15.0 8.4 %copy-start = (bf16[1024,128]{1,0:T(8,128)(2,1)S(1)}, bf16[1024,128]{1,0:T(8,128)(2,1)}, u32[]{:S(2)}) copy-start(bf16[1024,128]{1,0:T(8,128)(2,1)} %w_ref.1) | copy-start | bytes 786436
  15.0 4.4 %collective-permute-start.3 = (bf16[256,128]{1,0:T(8,128)(2,1)S(1)}, bf16[256,128]{1,0:T(8,128)(2,1)S(1)}, u32[]{:S(2)}, u32[]{:S(2)}) collective-permute-start(bf16[256,128]{1,0:T(8,128)(2,1)S(1)} %slice.29), channel_id=1, source_target_pairs={{2,0},{0,2},{6,4},{4,6},{10,8},{8,10},{14,12},{12,14},{3,1},{1,3},... | collective-permute-start | bytes 196616 | tf_op jit(solution)/shard_map/ppermute | solution.py:216
  16.6 4.3 %collective-permute-start.1 = (bf16[256,128]{1,0:T(8,128)(2,1)S(1)}, bf16[256,128]{1,0:T(8,128)(2,1)S(1)}, u32[]{:S(2)}, u32[]{:S(2)}) collective-permute-start(bf16[256,128]{1,0:T(8,128)(2,1)S(1)} %slice.28), channel_id=1, source_target_pairs={{2,0},{0,2},{6,4},{4,6},{10,8},{8,10},{14,12},{12,14},{3,1},{1,3},... | collective-permute-start | bytes 196616 | tf_op jit(solution)/shard_map/ppermute | solution.py:216
  17.2 4.6 %collective-permute-start.6 = (bf16[320,128]{1,0:T(8,128)(2,1)S(1)}, bf16[320,128]{1,0:T(8,128)(2,1)S(1)}, u32[]{:S(2)}, u32[]{:S(2)}) collective-permute-start(bf16[320,128]{1,0:T(8,128)(2,1)S(1)} %copy-done.4), channel_id=1, source_target_pairs={{2,0},{0,2},{6,4},{4,6},{10,8},{8,10},{14,12},{12,14},{3,1},{1,3},... | collective-permute-start | bytes 245768 | tf_op jit(solution)/shard_map/ppermute | solution.py:216
  21.8 1.6 %copy-start.1 = (bf16[320,128]{1,0:T(8,128)(2,1)S(1)}, bf16[320,128]{1,0:T(8,128)(2,1)}, u32[]{:S(2)}) copy-start(bf16[320,128]{1,0:T(8,128)(2,1)} %get-tuple-element.24.own_right_ref) | copy-start | bytes 245764
  21.9 1.6 %collective-permute-start.8 = (bf16[448,128]{1,0:T(8,128)(2,1)S(1)}, bf16[448,128]{1,0:T(8,128)(2,1)S(1)}, u32[]{:S(2)}, u32[]{:S(2)}) collective-permute-start(bf16[448,128]{1,0:T(8,128)(2,1)S(1)} %constant_dynamic-update-slice_fusion.mine_ref), channel_id=1, source_target_pairs={{0,1},{1,0},{2,3},{3,2},{4,5},{5,4},{6,7},{7,6},{8,9},{9,8},{10,11... | collective-permute-start | bytes 344072 | tf_op jit(solution)/shard_map/ppermute | solution.py:250
  21.9 1.5 %copy-start.2 = (f32[128]{0:T(128)S(1)}, f32[128]{0:T(128)}, u32[]{:S(2)}) copy-start(f32[128]{0:T(128)} %param.17) | copy-start | bytes 1540
  22.0 4.5 %collective-permute-start.9 = (bf16[256,128]{1,0:T(8,128)(2,1)S(1)}, bf16[256,128]{1,0:T(8,128)(2,1)S(1)}, u32[]{:S(2)}, u32[]{:S(2)}) collective-permute-start(bf16[256,128]{1,0:T(8,128)(2,1)S(1)} %slice.31), channel_id=1, source_target_pairs={{2,0},{0,2},{6,4},{4,6},{10,8},{8,10},{14,12},{12,14},{3,1},{1,3},... | collective-permute-start | bytes 196616 | tf_op jit(solution)/shard_map/ppermute | solution.py:216

commit v13 on v12

--- a/solution.py
+++ b/solution.py
@@ -102,8 +102,7 @@
         [flat[pl.ds(m * seqs + s, sources, stride=inner * seqs), :] for s in range(seqs)], axis=0)
 
 
-def prepare_kernel(seqs, c, left_at, mine_ref, other_ref, w_ref, bias_ref, own_right_ref,
-                   left_ref, weights_ref, right_ref, bias_out_ref, left_f32, w_f32):
+def prepare_kernel(seqs, left_at, mine_ref, other_ref, left_ref, left_f32):
     sources, left_rows, _ = left_f32.shape
     same_half = lax.axis_index("row") // (sources // 2) == lax.axis_index("col")
 
@@ -116,28 +115,44 @@
     left_of = sequence_rows(block, left_f32, left_rows // seqs, seqs)
     for k in range(left_rows // seqs):
         left_ref[k * LANES:(k + 1) * LANES] = left_of(k).T.astype(jnp.bfloat16)
+
+
+def prepare(mine, other, left_at, left_rows, seqs):
+    sources = len(left_at)
+    shape = (left_rows // seqs * LANES, sources * seqs)
+    return pl.pallas_call(
+        functools.partial(prepare_kernel, seqs, left_at),
+        grid=(1,),
+        out_shape=jax.ShapeDtypeStruct(shape, jnp.bfloat16),
+        in_specs=[whole(mine.shape), whole(other.shape)],
+        out_specs=whole(shape),
+        scratch_shapes=[pltpu.VMEM((sources, left_rows, LANES), jnp.float32)],
+        compiler_params=pltpu.CompilerParams(vmem_limit_bytes=48 * 1024 * 1024),
+        name="prepare",
+    )(mine, other)
+
+
+def constants_kernel(c, rows, w_ref, bias_ref, message_ref, weights_ref, bias_out_ref, right_ref, w_f32):
     w_f32[...] = w_ref[...].astype(jnp.float32)
     for e in range(c):
         weights_ref[:, e * c:(e + 1) * c] = w_f32[pl.ds(e, c, stride=c), :].T.astype(jnp.bfloat16)
-    right_ref[...] = own_right_ref[:right_ref.shape[0]]
     bias_out_ref[...] = bias_ref[...]
-
-
-def prepare(mine, other, left_at, left_rows, w_out, b_out, right, seqs, c):
-    sources = len(left_at)
+    right_ref[...] = message_ref[:rows]
+
+
+def constants(w_out, b_out, message, rows, c):
     z = w_out.shape[1]
-    outs = [((left_rows // seqs * LANES, sources * seqs), jnp.bfloat16), ((z, w_out.shape[0]), jnp.bfloat16),
-            ((right.shape[0] - left_rows, LANES), jnp.bfloat16), ((1, z), jnp.float32)]
-    operands = (mine, other, w_out, b_out.reshape(1, -1), right)
-    return pl.pallas_call(
-        functools.partial(prepare_kernel, seqs, c, left_at),
+    operands = (w_out, b_out.reshape(1, -1), message)
+    outs = [((z, w_out.shape[0]), jnp.bfloat16), ((1, z), jnp.float32), ((rows, LANES), jnp.bfloat16)]
+    return pl.pallas_call(
+        functools.partial(constants_kernel, c, rows),
         grid=(1,),
         out_shape=[jax.ShapeDtypeStruct(*out) for out in outs],
         in_specs=[whole(a.shape) for a in operands],
         out_specs=[whole(out[0]) for out in outs],
-        scratch_shapes=[pltpu.VMEM((sources, left_rows, LANES), jnp.float32), pltpu.VMEM(w_out.shape, jnp.float32)],
+        scratch_shapes=[pltpu.VMEM(w_out.shape, jnp.float32)],
         compiler_params=pltpu.CompilerParams(vmem_limit_bytes=48 * 1024 * 1024),
-        name="prepare",
+        name="constants",
     )(*operands)
 
 
@@ -240,17 +255,25 @@
     rows = direct[0].shape[0] - left_rows
 
     line = [fetch(message, step, row_count) for step, message in reversed([*zip(direct_steps(along), direct[:-1])])][::-1]
-    beyond = [fetch_far(message, step, row_count) for step, message in zip(far_steps(along), messages[along:])]
-    beyond[0], beside = lax.optimization_barrier((beyond[0], direct[-1]))
-    across = fetch(beside, (0, 1), row_count)
-    far = [fetch(block[:rows], (0, 1), row_count) for block in reversed(line)][::-1]
-    *far[:-1], held = lax.optimization_barrier((*far[:-1], tuple(line)))
+    across = fetch(direct[-1], (0, 1), row_count)
+    far = []
+    for block in reversed(line):
+        block, across = lax.optimization_barrier((block, across))
+        far.insert(0, fetch(block[:rows], (0, 1), row_count))
+    first, *later = messages[along:]
+    later, _ = lax.optimization_barrier((tuple(later), tuple(line)))
+    beyond = [fetch_far(message, step, row_count) for step, message in zip(far_steps(along), (first, *later))]
+
+    message, _ = lax.optimization_barrier((direct[0], line[0]))
+    weights, bias, right = constants(w_out, b_out, message, rows, c)
+    weights, bias, right, held, *far[1:] = lax.optimization_barrier((weights, bias, right, tuple(line), *far[1:]))
 
     mine = jnp.concatenate([own] + [block[rows:] for block in (*held, across)] + beyond)
     other = lax.ppermute(mine, "col", [(0, 1), (1, 0)])
+    other, far[0] = lax.optimization_barrier((other, far[0]))
     left_at = [(a, True) for a in range(along + 1)]
     left_at += [(along + a, True) if a < along // 2 else (a + 1 + along // 2, False) for a in range(1, along)]
-    left, weights, right, bias = prepare(mine, other, left_at, left_rows, w_out, b_out, direct[0], seqs, c)
+    left = prepare(mine, other, left_at, left_rows, seqs)
     right_at = [(n, 0) for n in range(row_count)]
     return pairs(left, weights, bias, [right, *line, across, *far], right_at, seqs, c, width)
 

time: 31.8 us -> 35.8 us (1.13)
  waiting for transfers between devices: 5.06 us -> 7.98 us
  local copies, waits for them, and re-layouts: 0.09 us -> 1.69 us
  starting transfers between devices: 17.6 us -> 16.9 us
    ppermute x7, starting transfers between devices: 15.5 us -> 10.6 us  [fetch(): lax.ppermute(array, 'row', [(source_at(r, step), r) for r in range(count)])]
    ppermute x1, starting transfers between devices: 0.07 us -> 4.89 us  [on_device(): other = lax.ppermute(mine, 'col', [(0, 1), (1, 0)])]
    ppermute x7, waiting for transfers between devices: 5.05 us -> 7.98 us  [fetch(): lax.ppermute(array, 'row', [(source_at(r, step), r) for r in range(count)])]
    unnamed x16 -> x14, local copies, waits for them, and re-layouts: 0.07 us -> 1.67 us
    ppermute x2, starting transfers between devices: 2.06 us -> 1.37 us  [fetch_far(): return lax.ppermute(array, ('row', 'col'), moves)]
    pallas_call x1 -> x2, Pallas kernels: 1 us -> 1.07 us  [the longest x1 0.92 us: constants(): pl.pallas_call(functools.partial(constants_kernel, c, rows), grid=(1,), o...]
  transfers between devices with their start and end apart: 10 -> 10, of which waited for: 4 -> 4; matrix products, arithmetic and copies ran while one was open for 0% -> 2% of each run, Pallas kernels for 3% -> 3%
where the time goes in v13:
time: 35.8 us; the launch traced here: 35.6 us
  starting transfers between devices  16.9 us (47%)
  Pallas kernels  8.92 us (25%)
  waiting for transfers between devices  7.98 us (22%)
  local copies, waits for them, and re-layouts  1.69 us (5%)
    ppermute x7, starting transfers between devices, fetch(): lax.ppermute(array, 'row', [(source_at(r, step), r) for r in range(count)])  10.6 us
    ppermute x7, waiting for transfers between devices, fetch(): lax.ppermute(array, 'row', [(source_at(r, step), r) for r in range(count)])  7.98 us
    pallas_call x1, Pallas kernels, pairs(): pl.pallas_call(functools.partial(pair_kernel, seqs, c, right_at), grid=(r...  5.24 us
    ppermute x1, starting transfers between devices, on_device(): other = lax.ppermute(mine, 'col', [(0, 1), (1, 0)])  4.89 us
    pallas_call x1, Pallas kernels, features(): pl.pallas_call(functools.partial(features_kernel, 1.0 / (seqs * row_count...  2.61 us
    unnamed x14, local copies, waits for them, and re-layouts  1.67 us
    ppermute x2, starting transfers between devices, fetch_far(): return lax.ppermute(array, ('row', 'col'), moves)  1.37 us
    pallas_call x1, Pallas kernels, constants(): pl.pallas_call(functools.partial(constants_kernel, c, rows), grid=(1,), o...  0.92 us
  transfers between devices with their start and end apart: 10, of which 4 were waited for; matrix products, arithmetic and copies ran while one was open for 2% of the time, Pallas kernels for 3%

profile of v13, /device:TPU:0, one launch (start us, length us, event | category | flops | bytes accessed | tf_op | source)
XLA Modules:
  0.0 35.6 jit_solution(14685477852270387255)
XLA Ops:
  0.0 2.6 %features.1 = (bf16[64,128]{1,0:T(8,128)(2,1)}, bf16[320,128]{1,0:T(8,128)(2,1)}, bf16[320,128]{1,0:T(8,128)(2,1)}, bf16[320,128]{1,0:T(8,128)(2,1)}, bf16[320,1...) custom-call(bf16[8,128,256]{2,1,0:T(8,128)(2,1)} %x_ref.1, f32[1,256]{1,0:T(1,128)} %bitcast.10, ...), custom_call_target="tpu_custom_call" | custom-call | tf_op jit(solution)/shard_map/features/pallas_call | solution.py:79
  2.6 5.1 %collective-permute-start.2 = (bf16[320,128]{1,0:T(8,128)(2,1)}, bf16[320,128]{1,0:T(8,128)(2,1)S(1)}, u32[]{:S(2)}, u32[]{:S(2)}) collective-permute-start(bf16[320,128]{1,0:T(8,128)(2,1)} %get-tuple-element.40), channel_id=1, source_target_pairs={{12,0},{14,2},{8,4},{10,6},{4,8},{6,10},{0,12},{2,14},{13,1},{15,3... | collective-permute-start | bytes 245768 | tf_op jit(solution)/shard_map/ppermute | solution.py:231
  7.7 1.5 %collective-permute-start.3 = (bf16[320,128]{1,0:T(8,128)(2,1)}, bf16[320,128]{1,0:T(8,128)(2,1)S(1)}, u32[]{:S(2)}, u32[]{:S(2)}) collective-permute-start(bf16[320,128]{1,0:T(8,128)(2,1)} %get-tuple-element.41), channel_id=1, source_target_pairs={{2,0},{0,2},{6,4},{4,6},{10,8},{8,10},{14,12},{12,14},{3,1},{1,3},... | collective-permute-start | bytes 245768 | tf_op jit(solution)/shard_map/ppermute | solution.py:231
  9.2 0.6 %collective-permute-start.6 = (bf16[64,128]{1,0:T(8,128)(2,1)}, bf16[64,128]{1,0:T(8,128)(2,1)S(1)}, u32[]{:S(2)}, u32[]{:S(2)}) collective-permute-start(bf16[64,128]{1,0:T(8,128)(2,1)} %get-tuple-element.50), channel_id=1, source_target_pairs={{6,0},{10,1},{4,2},{8,3},{2,4},{14,5},{0,6},{12,7},{15,9},{3,8},{1... | collective-permute-start | bytes 49160 | tf_op jit(solution)/shard_map/ppermute | solution.py:243
  9.8 1.4 %collective-permute-start = (bf16[320,128]{1,0:T(8,128)(2,1)}, bf16[320,128]{1,0:T(8,128)(2,1)S(1)}, u32[]{:S(2)}, u32[]{:S(2)}) collective-permute-start(bf16[320,128]{1,0:T(8,128)(2,1)} %get-tuple-element.35.message_ref), channel_id=1, source_target_pairs={{4,0},{6,2},{0,4},{2,6},{12,8},{14,10},{8,12},{10,14},{5,1},{7,3},... | collective-permute-start | bytes 245768 | tf_op jit(solution)/shard_map/ppermute | solution.py:231
  11.2 0.0 collective-permute-done.2.refs_3_
  11.2 1.2 %collective-permute-done.3.refs_4_ = bf16[320,128]{1,0:T(8,128)(2,1)S(1)} collective-permute-done((bf16[320,128]{1,0:T(8,128)(2,1)}, bf16[320,128]{1,0:T(8,128)(2,1)S(1)}, u32[]{:S(2)}, u32[]{:S(2)}) %collective-permute-start.3) | collective-permute-done | bytes 81952 | tf_op jit(solution)/shard_map/ppermute | solution.py:231
  12.4 2.8 %collective-permute-done.1.refs_2_ = bf16[320,128]{1,0:T(8,128)(2,1)S(1)} collective-permute-done((bf16[320,128]{1,0:T(8,128)(2,1)}, bf16[320,128]{1,0:T(8,128)(2,1)S(1)}, u32[]{:S(2)}, u32[]{:S(2)}) %collective-permute-start.1) | collective-permute-done | bytes 81952 | tf_op jit(solution)/shard_map/ppermute | solution.py:231
  15.2 1.4 %collective-permute-start.5 = (bf16[256,128]{1,0:T(8,128)(2,1)S(1)}, bf16[256,128]{1,0:T(8,128)(2,1)S(1)}, u32[]{:S(2)}, u32[]{:S(2)}) collective-permute-start(bf16[256,128]{1,0:T(8,128)(2,1)S(1)} %slice.22), channel_id=1, source_target_pairs={{2,0},{0,2},{6,4},{4,6},{10,8},{8,10},{14,12},{12,14},{3,1},{1,3},... | collective-permute-start | bytes 196616 | tf_op jit(solution)/shard_map/ppermute | solution.py:231
  16.7 0.7 %collective-permute-start.4 = (bf16[256,128]{1,0:T(8,128)(2,1)S(1)}, bf16[256,128]{1,0:T(8,128)(2,1)S(1)}, u32[]{:S(2)}, u32[]{:S(2)}) collective-permute-start(bf16[256,128]{1,0:T(8,128)(2,1)S(1)} %slice.21), channel_id=1, source_target_pairs={{2,0},{0,2},{6,4},{4,6},{10,8},{8,10},{14,12},{12,14},{3,1},{1,3},... | collective-permute-start | bytes 196616 | tf_op jit(solution)/shard_map/ppermute | solution.py:231
  17.3 0.7 %constant_dynamic-update-slice_fusion.6 = bf16[448,128]{1,0:T(8,128)(2,1)S(1)} fusion(bf16[64,128]{1,0:T(8,128)(2,1)} %get-tuple-element.33), kind=kLoop, calls=%fused_computation.6 | loop fusion | bytes 32768
  18.1 0.0 collective-permute-done.refs_1_
  18.1 0.8 %collective-permute-start.7 = (bf16[64,128]{1,0:T(8,128)(2,1)S(1)}, bf16[64,128]{1,0:T(8,128)(2,1)S(1)}, u32[]{:S(2)}, u32[]{:S(2)}) collective-permute-start(bf16[64,128]{1,0:T(8,128)(2,1)S(1)} %copy-done.3), channel_id=1, source_target_pairs={{14,1},{12,3},{10,5},{8,7},{7,8},{5,10},{3,12},{1,14},{30,17},{28,... | collective-permute-start | bytes 49160 | tf_op jit(solution)/shard_map/ppermute | solution.py:243
  18.9 0.0 copy-start.1
  18.9 0.9 %copy-done.1 = bf16[320,128]{1,0:T(8,128)(2,1)S(1)} copy-done((bf16[320,128]{1,0:T(8,128)(2,1)S(1)}, bf16[320,128]{1,0:T(8,128)(2,1)}, u32[]{:S(2)}) %copy-start.1) | copy-done | bytes 81944
  19.8 0.9 %constants.1 = (bf16[128,1024]{1,0:T(8,128)(2,1)S(1)}, f32[1,128]{1,0:T(1,128)S(1)}, bf16[256,128]{1,0:T(8,128)(2,1)S(1)}) custom-call(bf16[1024,128]{1,0:T(8,128)(2,1)S(1)} %copy-done, f32[1,128]{1,0:T(1,128)S(1)} %bitcast.7, bf16[320,128]{1,0:T(8,128)(2,1)S(1)} %copy-done.1), custom_call_target="tpu_custom_call" | custom-call | tf_op jit(solution)/shard_map/constants/pallas_call | solution.py:147
  20.7 0.0 collective-permute-done.5.refs_7_
  20.7 0.2 collective-permute-done.4.refs_6_
  21.0 0.0 collective-permute-done.6
  21.0 4.9 %collective-permute-start.8 = (bf16[448,128]{1,0:T(8,128)(2,1)S(1)}, bf16[448,128]{1,0:T(8,128)(2,1)S(1)}, u32[]{:S(2)}, u32[]{:S(2)}) collective-permute-start(bf16[448,128]{1,0:T(8,128)(2,1)S(1)} %constant_dynamic-update-slice_fusion.mine_ref), channel_id=1, source_target_pairs={{0,1},{1,0},{2,3},{3,2},{4,5},{5,4},{6,7},{7,6},{8,9},{9,8},{10,11... | collective-permute-start | bytes 344072 | tf_op jit(solution)/shard_map/ppermute | solution.py:272
  25.9 0.5 %collective-permute-start.9 = (bf16[256,128]{1,0:T(8,128)(2,1)S(1)}, bf16[256,128]{1,0:T(8,128)(2,1)S(1)}, u32[]{:S(2)}, u32[]{:S(2)}) collective-permute-start(bf16[256,128]{1,0:T(8,128)(2,1)S(1)} %slice.27), channel_id=1, source_target_pairs={{2,0},{0,2},{6,4},{4,6},{10,8},{8,10},{14,12},{12,14},{3,1},{1,3},... | collective-permute-start | bytes 196616 | tf_op jit(solution)/shard_map/ppermute | solution.py:231
  26.4 3.7 %collective-permute-done.9.refs_5_ = bf16[256,128]{1,0:T(8,128)(2,1)S(1)} collective-permute-done((bf16[256,128]{1,0:T(8,128)(2,1)S(1)}, bf16[256,128]{1,0:T(8,128)(2,1)S(1)}, u32[]{:S(2)}, u32[]{:S(2)}) %collective-permute-start.9) | collective-permute-done | bytes 65568 | tf_op jit(solution)/shard_map/ppermute | solution.py:231
  30.2 0.2 prepare.1.left_ref
  30.3 5.2 %pairs.1 = bf16[32,128,128]{2,1,0:T(8,128)(2,1)} custom-call(bf16[1024,64]{1,0:T(8,128)(2,1)S(1)} %prepare.1.left_ref, bf16[128,1024]{1,0:T(8,128)(2,1)S(1)} %get-tuple-element.55.weights_ref, f32[1,128]{1,0:T(1,128)S(1)} %get-tuple-element.56.bias_ref, bf16[256,128]{1,0:T(8,128)(2,1)S(1)} %get-tuple-element.57.refs_0_, ...), custom_call_target="tpu_custom_call" | custom-call | flops 1610612736 | bytes 1048576 | tf_op jit(solution)/shard_map/pairs/pallas_call | solution.py:202
  (18 shorter events, 0.1 us)
Async XLA Ops:
  2.6 16.3 %copy-start = (bf16[1024,128]{1,0:T(8,128)(2,1)S(1)}, bf16[1024,128]{1,0:T(8,128)(2,1)}, u32[]{:S(2)}) copy-start(bf16[1024,128]{1,0:T(8,128)(2,1)} %w_ref.1) | copy-start | bytes 786436
  2.6 8.6 %collective-permute-start.2 = (bf16[320,128]{1,0:T(8,128)(2,1)}, bf16[320,128]{1,0:T(8,128)(2,1)S(1)}, u32[]{:S(2)}, u32[]{:S(2)}) collective-permute-start(bf16[320,128]{1,0:T(8,128)(2,1)} %get-tuple-element.40), channel_id=1, source_target_pairs={{12,0},{14,2},{8,4},{10,6},{4,8},{6,10},{0,12},{2,14},{13,1},{15,3... | collective-permute-start | bytes 245768 | tf_op jit(solution)/shard_map/ppermute | solution.py:231
  7.7 4.7 %collective-permute-start.3 = (bf16[320,128]{1,0:T(8,128)(2,1)}, bf16[320,128]{1,0:T(8,128)(2,1)S(1)}, u32[]{:S(2)}, u32[]{:S(2)}) collective-permute-start(bf16[320,128]{1,0:T(8,128)(2,1)} %get-tuple-element.41), channel_id=1, source_target_pairs={{2,0},{0,2},{6,4},{4,6},{10,8},{8,10},{14,12},{12,14},{3,1},{1,3},... | collective-permute-start | bytes 245768 | tf_op jit(solution)/shard_map/ppermute | solution.py:231
  9.2 6.0 %collective-permute-start.1 = (bf16[320,128]{1,0:T(8,128)(2,1)}, bf16[320,128]{1,0:T(8,128)(2,1)S(1)}, u32[]{:S(2)}, u32[]{:S(2)}) collective-permute-start(bf16[320,128]{1,0:T(8,128)(2,1)} %get-tuple-element.39), channel_id=1, source_target_pairs={{8,0},{10,2},{12,4},{14,6},{0,8},{2,10},{4,12},{6,14},{9,1},{11,3}... | collective-permute-start | bytes 245768 | tf_op jit(solution)/shard_map/ppermute | solution.py:231
  9.2 11.7 %collective-permute-start.6 = (bf16[64,128]{1,0:T(8,128)(2,1)}, bf16[64,128]{1,0:T(8,128)(2,1)S(1)}, u32[]{:S(2)}, u32[]{:S(2)}) collective-permute-start(bf16[64,128]{1,0:T(8,128)(2,1)} %get-tuple-element.50), channel_id=1, source_target_pairs={{6,0},{10,1},{4,2},{8,3},{2,4},{14,5},{0,6},{12,7},{15,9},{3,8},{1... | collective-permute-start | bytes 49160 | tf_op jit(solution)/shard_map/ppermute | solution.py:243
  9.8 8.2 %collective-permute-start = (bf16[320,128]{1,0:T(8,128)(2,1)}, bf16[320,128]{1,0:T(8,128)(2,1)S(1)}, u32[]{:S(2)}, u32[]{:S(2)}) collective-permute-start(bf16[320,128]{1,0:T(8,128)(2,1)} %get-tuple-element.35.message_ref), channel_id=1, source_target_pairs={{4,0},{6,2},{0,4},{2,6},{12,8},{14,10},{8,12},{10,14},{5,1},{7,3},... | collective-permute-start | bytes 245768 | tf_op jit(solution)/shard_map/ppermute | solution.py:231
  15.2 5.5 %collective-permute-start.5 = (bf16[256,128]{1,0:T(8,128)(2,1)S(1)}, bf16[256,128]{1,0:T(8,128)(2,1)S(1)}, u32[]{:S(2)}, u32[]{:S(2)}) collective-permute-start(bf16[256,128]{1,0:T(8,128)(2,1)S(1)} %slice.22), channel_id=1, source_target_pairs={{2,0},{0,2},{6,4},{4,6},{10,8},{8,10},{14,12},{12,14},{3,1},{1,3},... | collective-permute-start | bytes 196616 | tf_op jit(solution)/shard_map/ppermute | solution.py:231
  16.7 4.3 %collective-permute-start.4 = (bf16[256,128]{1,0:T(8,128)(2,1)S(1)}, bf16[256,128]{1,0:T(8,128)(2,1)S(1)}, u32[]{:S(2)}, u32[]{:S(2)}) collective-permute-start(bf16[256,128]{1,0:T(8,128)(2,1)S(1)} %slice.21), channel_id=1, source_target_pairs={{2,0},{0,2},{6,4},{4,6},{10,8},{8,10},{14,12},{12,14},{3,1},{1,3},... | collective-permute-start | bytes 196616 | tf_op jit(solution)/shard_map/ppermute | solution.py:231
  17.3 0.7 %copy-start.3 = (bf16[64,128]{1,0:T(8,128)(2,1)S(1)}, bf16[64,128]{1,0:T(8,128)(2,1)}, u32[]{:S(2)}) copy-start(bf16[64,128]{1,0:T(8,128)(2,1)} %get-tuple-element.52) | copy-start | bytes 49156
  18.1 0.8 %copy-start.2 = (f32[128]{0:T(128)S(1)}, f32[128]{0:T(128)}, u32[]{:S(2)}) copy-start(f32[128]{0:T(128)} %param.17) | copy-start | bytes 1540
  18.1 2.9 %collective-permute-start.7 = (bf16[64,128]{1,0:T(8,128)(2,1)S(1)}, bf16[64,128]{1,0:T(8,128)(2,1)S(1)}, u32[]{:S(2)}, u32[]{:S(2)}) collective-permute-start(bf16[64,128]{1,0:T(8,128)(2,1)S(1)} %copy-done.3), channel_id=1, source_target_pairs={{14,1},{12,3},{10,5},{8,7},{7,8},{5,10},{3,12},{1,14},{30,17},{28,... | collective-permute-start | bytes 49160 | tf_op jit(solution)/shard_map/ppermute | solution.py:243
  18.9 0.9 %copy-start.1 = (bf16[320,128]{1,0:T(8,128)(2,1)S(1)}, bf16[320,128]{1,0:T(8,128)(2,1)}, u32[]{:S(2)}) copy-start(bf16[320,128]{1,0:T(8,128)(2,1)} %get-tuple-element.35.message_ref) | copy-start | bytes 245764
  21.0 9.2 %collective-permute-start.8 = (bf16[448,128]{1,0:T(8,128)(2,1)S(1)}, bf16[448,128]{1,0:T(8,128)(2,1)S(1)}, u32[]{:S(2)}, u32[]{:S(2)}) collective-permute-start(bf16[448,128]{1,0:T(8,128)(2,1)S(1)} %constant_dynamic-update-slice_fusion.mine_ref), channel_id=1, source_target_pairs={{0,1},{1,0},{2,3},{3,2},{4,5},{5,4},{6,7},{7,6},{8,9},{9,8},{10,11... | collective-permute-start | bytes 344072 | tf_op jit(solution)/shard_map/ppermute | solution.py:272
  25.9 4.3 %collective-permute-start.9 = (bf16[256,128]{1,0:T(8,128)(2,1)S(1)}, bf16[256,128]{1,0:T(8,128)(2,1)S(1)}, u32[]{:S(2)}, u32[]{:S(2)}) collective-permute-start(bf16[256,128]{1,0:T(8,128)(2,1)S(1)} %slice.27), channel_id=1, source_target_pairs={{2,0},{0,2},{6,4},{4,6},{10,8},{8,10},{14,12},{12,14},{3,1},{1,3},... | collective-permute-start | bytes 196616 | tf_op jit(solution)/shard_map/ppermute | solution.py:231

commit v14 on v13

--- a/solution.py
+++ b/solution.py
@@ -60,8 +60,13 @@
     own_ref[...] = left_for((0, 0))
     right = right_f32[...].astype(jnp.bfloat16)
     for step, message_ref in zip(direct_steps(chips), message_refs):
-        message_ref[:right.shape[0]] = right
-        message_ref[right.shape[0]:] = left_for(step)
+        first = rows if carries_far(step, chips) else 0
+        message_ref[first:first + right.shape[0]] = right
+        if first:
+            message_ref[:rows] = left_for(step)
+            message_ref[first + right.shape[0]:] = left_for((step[0], 1))
+        else:
+            message_ref[right.shape[0]:] = left_for(step)
     same_half = here // chips == lax.axis_index("col")
     for (a, b), message_ref in zip(far_steps(chips), message_refs[chips:]):
         message_ref[...] = jnp.where(same_half, left_for((a + 1, b)), left_for((a, b)))
@@ -73,7 +78,9 @@
     rows = seqs * width * c // LANES
     chips = row_count // col_count
     part = rows // chips
-    shapes = [(n, LANES) for n in [part] + [rows + part] * chips + [part] * (chips // 2)]
+    shapes = [(part, LANES)]
+    shapes += [(rows + part * (2 if carries_far(step, chips) else 1), LANES) for step in direct_steps(chips)]
+    shapes += [(part, LANES)] * len(far_steps(chips))
     operands = (alignment, ln_gain.reshape(1, -1), ln_bias.reshape(1, -1), w_left.T, b_left.reshape(1, -1),
                 w_right.T, b_right.reshape(1, -1))
     return pl.pallas_call(
@@ -224,7 +231,11 @@
 
 
 def far_steps(chips):
-    return [(a, 1) for a in range(chips // 2)]
+    return [(a, 1) for a in range(chips // 2 - 1)]
+
+
+def carries_far(step, chips):
+    return step == (chips - 1, 0)
 
 
 def fetch(array, step, count):
@@ -237,8 +248,7 @@
     moves = []
     for r in range(count):
         half = r // chips
-        if a + 1 < chips // 2:
-            moves.append((2 * source_at(r, (a + 1, b)) + half, 2 * r + half))
+        moves.append((2 * source_at(r, (a + 1, b)) + half, 2 * r + half))
         moves.append((2 * source_at(r, (a + chips // 2, b)) + half, 2 * r + 1 - half))
     return lax.ppermute(array, ("row", "col"), moves)
 
@@ -256,25 +266,25 @@
 
     line = [fetch(message, step, row_count) for step, message in reversed([*zip(direct_steps(along), direct[:-1])])][::-1]
     across = fetch(direct[-1], (0, 1), row_count)
+    beyond = [fetch_far(message, step, row_count) for step, message in zip(far_steps(along), messages[along:])]
     far = []
-    for block in reversed(line):
+    for step, block in reversed([*zip(direct_steps(along), line)]):
         block, across = lax.optimization_barrier((block, across))
-        far.insert(0, fetch(block[:rows], (0, 1), row_count))
-    first, *later = messages[along:]
-    later, _ = lax.optimization_barrier((tuple(later), tuple(line)))
-    beyond = [fetch_far(message, step, row_count) for step, message in zip(far_steps(along), (first, *later))]
+        block = block[left_rows:] if carries_far(step, along) else block[:rows]
+        far.insert(0, fetch(block, (0, 1), row_count))
 
     message, _ = lax.optimization_barrier((direct[0], line[0]))
     weights, bias, right = constants(w_out, b_out, message, rows, c)
-    weights, bias, right, held, *far[1:] = lax.optimization_barrier((weights, bias, right, tuple(line), *far[1:]))
-
-    mine = jnp.concatenate([own] + [block[rows:] for block in (*held, across)] + beyond)
+    weights, bias, right, held, far = lax.optimization_barrier((weights, bias, right, tuple(line), tuple(far)))
+    mine = jnp.concatenate([own] + [block[rows:] for block in held[:-1]] + [held[-1][:left_rows], across[rows:]]
+                           + beyond + [far[-1][rows:]])
     other = lax.ppermute(mine, "col", [(0, 1), (1, 0)])
-    other, far[0] = lax.optimization_barrier((other, far[0]))
+    half = along // 2
     left_at = [(a, True) for a in range(along + 1)]
-    left_at += [(along + a, True) if a < along // 2 else (a + 1 + along // 2, False) for a in range(1, along)]
+    left_at += [(along + a, True) if a < half else (along + 1 + a - half, False) for a in range(1, along - 1)]
+    left_at += [(along + half, True)]
     left = prepare(mine, other, left_at, left_rows, seqs)
-    right_at = [(n, 0) for n in range(row_count)]
+    right_at = [(n, left_rows if n == along - 1 else 0) for n in range(row_count)]
     return pairs(left, weights, bias, [right, *line, across, *far], right_at, seqs, c, width)
 
 

time: 35.8 us -> 29.4 us (0.82)
  starting transfers between devices: 16.9 us -> 12.4 us
  local copies, waits for them, and re-layouts: 1.69 us -> 0.72 us
  waiting for transfers between devices: 7.98 us -> 7.12 us
    ppermute x1, starting transfers between devices: 4.89 us -> 0.07 us  [on_device(): other = lax.ppermute(mine, 'col', [(0, 1), (1, 0)])]
    ppermute x7, waiting for transfers between devices: 7.98 us -> 5.81 us  [fetch(): lax.ppermute(array, 'row', [(source_at(r, step), r) for r in range(count)])]
    ppermute x1, waiting for transfers between devices: 0.01 us -> 1.31 us  [on_device(): other = lax.ppermute(mine, 'col', [(0, 1), (1, 0)])]
    unnamed x14, local copies, waits for them, and re-layouts: 1.67 us -> 0.7 us
    ppermute x7, starting transfers between devices: 10.6 us -> 11.2 us  [fetch(): lax.ppermute(array, 'row', [(source_at(r, step), r) for r in range(count)])]
    ppermute x2 -> x1, starting transfers between devices: 1.37 us -> 1.18 us  [fetch_far(): return lax.ppermute(array, ('row', 'col'), moves)]
  transfers between devices with their start and end apart: 10 -> 9, of which waited for: 4 -> 5; matrix products, arithmetic and copies ran while one was open for 2% -> 0% of each run, Pallas kernels for 3% -> 3%
where the time goes in v14:
time: 29.4 us; the launch traced here: 29.3 us
  starting transfers between devices  12.4 us (42%)
  Pallas kernels  8.91 us (30%)
  waiting for transfers between devices  7.12 us (24%)
  local copies, waits for them, and re-layouts  0.72 us (2%)
    ppermute x7, starting transfers between devices, fetch(): lax.ppermute(array, 'row', [(source_at(r, step), r) for r in range(count)])  11.2 us
    ppermute x7, waiting for transfers between devices, fetch(): lax.ppermute(array, 'row', [(source_at(r, step), r) for r in range(count)])  5.81 us
    pallas_call x1, Pallas kernels, pairs(): pl.pallas_call(functools.partial(pair_kernel, seqs, c, right_at), grid=(r...  5.23 us
    pallas_call x1, Pallas kernels, features(): pl.pallas_call(functools.partial(features_kernel, 1.0 / (seqs * row_count...  2.61 us
    ppermute x1, waiting for transfers between devices, on_device(): other = lax.ppermute(mine, 'col', [(0, 1), (1, 0)])  1.31 us
    ppermute x1, starting transfers between devices, fetch_far(): return lax.ppermute(array, ('row', 'col'), moves)  1.18 us
    pallas_call x1, Pallas kernels, constants(): pl.pallas_call(functools.partial(constants_kernel, c, rows), grid=(1,), o...  0.92 us
    unnamed x14, local copies, waits for them, and re-layouts  0.7 us
  transfers between devices with their start and end apart: 9, of which 5 were waited for; matrix products, arithmetic and copies ran while one was open for 0% of the time, Pallas kernels for 3%

profile of v14, /device:TPU:0, one launch (start us, length us, event | category | flops | bytes accessed | tf_op | source)
XLA Modules:
  0.0 29.3 jit_solution(18353493932093026844)
XLA Ops:
  0.0 2.6 %features.1 = (bf16[64,128]{1,0:T(8,128)(2,1)}, bf16[320,128]{1,0:T(8,128)(2,1)}, bf16[320,128]{1,0:T(8,128)(2,1)}, bf16[384,128]{1,0:T(8,128)(2,1)}, bf16[320,128]{1,0:T(8,128)(2,1)}, /*index=5*/bf16[64,128]{1,0:T(8,128)(2,1)}) custom-call(bf16[8,128,256]{2,1,0:T(8,128)(2,1)} %x_ref.1, f32[1,256]{1,0:T(1,128)} %bitcast.10, f32[1,256]{1,0:T(1,128)} %bitcast.11, ...), custom_call_target="tpu_custom_call" | custom-call | tf_op jit(solution)/shard_map/features/pallas_call | solution.py:86
  2.6 5.1 %collective-permute-start.2 = (bf16[384,128]{1,0:T(8,128)(2,1)}, bf16[384,128]{1,0:T(8,128)(2,1)S(1)}, u32[]{:S(2)}, u32[]{:S(2)}) collective-permute-start(bf16[384,128]{1,0:T(8,128)(2,1)} %get-tuple-element.37), channel_id=1, source_target_pairs={{12,0},{14,2},{8,4},{10,6},{4,8},{6,10},{0,12},{2,14},{13,1},{15,3... | collective-permute-start | bytes 294920 | tf_op jit(solution)/shard_map/ppermute | solution.py:242
  7.7 1.5 %collective-permute-start.3 = (bf16[320,128]{1,0:T(8,128)(2,1)}, bf16[320,128]{1,0:T(8,128)(2,1)S(1)}, u32[]{:S(2)}, u32[]{:S(2)}) collective-permute-start(bf16[320,128]{1,0:T(8,128)(2,1)} %get-tuple-element.38), channel_id=1, source_target_pairs={{2,0},{0,2},{6,4},{4,6},{10,8},{8,10},{14,12},{12,14},{3,1},{1,3},... | collective-permute-start | bytes 245768 | tf_op jit(solution)/shard_map/ppermute | solution.py:242
  9.2 0.0 collective-permute-start.1
  9.2 0.8 %collective-permute-start = (bf16[320,128]{1,0:T(8,128)(2,1)}, bf16[320,128]{1,0:T(8,128)(2,1)S(1)}, u32[]{:S(2)}, u32[]{:S(2)}) collective-permute-start(bf16[320,128]{1,0:T(8,128)(2,1)} %get-tuple-element.32.message_ref), channel_id=1, source_target_pairs={{4,0},{6,2},{0,4},{2,6},{12,8},{14,10},{8,12},{10,14},{5,1},{7,3},... | collective-permute-start | bytes 245768 | tf_op jit(solution)/shard_map/ppermute | solution.py:242
  10.0 1.2 %collective-permute-start.7 = (bf16[64,128]{1,0:T(8,128)(2,1)}, bf16[64,128]{1,0:T(8,128)(2,1)S(1)}, u32[]{:S(2)}, u32[]{:S(2)}) collective-permute-start(bf16[64,128]{1,0:T(8,128)(2,1)} %get-tuple-element.48), channel_id=1, source_target_pairs={{6,0},{10,1},{4,2},{8,3},{2,4},{14,5},{0,6},{12,7},{15,9},{3,8},{1... | collective-permute-start | bytes 49160 | tf_op jit(solution)/shard_map/ppermute | solution.py:253
  11.2 1.2 %collective-permute-done.3.refs_4_ = bf16[320,128]{1,0:T(8,128)(2,1)S(1)} collective-permute-done((bf16[320,128]{1,0:T(8,128)(2,1)}, bf16[320,128]{1,0:T(8,128)(2,1)S(1)}, u32[]{:S(2)}, u32[]{:S(2)}) %collective-permute-start.3) | collective-permute-done | bytes 81952 | tf_op jit(solution)/shard_map/ppermute | solution.py:242
  12.4 0.0 collective-permute-done.2.refs_3_
  12.4 3.1 %collective-permute-done.1.refs_2_ = bf16[320,128]{1,0:T(8,128)(2,1)S(1)} collective-permute-done((bf16[320,128]{1,0:T(8,128)(2,1)}, bf16[320,128]{1,0:T(8,128)(2,1)S(1)}, u32[]{:S(2)}, u32[]{:S(2)}) %collective-permute-start.1) | collective-permute-done | bytes 81952 | tf_op jit(solution)/shard_map/ppermute | solution.py:242
  15.5 0.0 collective-permute-done.refs_1_
  15.5 1.8 %collective-permute-start.5 = (bf16[256,128]{1,0:T(8,128)(2,1)S(1)}, bf16[256,128]{1,0:T(8,128)(2,1)S(1)}, u32[]{:S(2)}, u32[]{:S(2)}) collective-permute-start(bf16[256,128]{1,0:T(8,128)(2,1)S(1)} %slice.25), channel_id=1, source_target_pairs={{2,0},{0,2},{6,4},{4,6},{10,8},{8,10},{14,12},{12,14},{3,1},{1,3},... | collective-permute-start | bytes 196616 | tf_op jit(solution)/shard_map/ppermute | solution.py:242
  17.3 0.3 %collective-permute-start.4 = (bf16[256,128]{1,0:T(8,128)(2,1)S(1)}, bf16[256,128]{1,0:T(8,128)(2,1)S(1)}, u32[]{:S(2)}, u32[]{:S(2)}) collective-permute-start(bf16[256,128]{1,0:T(8,128)(2,1)S(1)} %slice.24), channel_id=1, source_target_pairs={{2,0},{0,2},{6,4},{4,6},{10,8},{8,10},{14,12},{12,14},{3,1},{1,3},... | collective-permute-start | bytes 196616 | tf_op jit(solution)/shard_map/ppermute | solution.py:242
  17.6 1.7 %collective-permute-start.6 = (bf16[320,128]{1,0:T(8,128)(2,1)S(1)}, bf16[320,128]{1,0:T(8,128)(2,1)S(1)}, u32[]{:S(2)}, u32[]{:S(2)}) collective-permute-start(bf16[320,128]{1,0:T(8,128)(2,1)S(1)} %slice.26), channel_id=1, source_target_pairs={{2,0},{0,2},{6,4},{4,6},{10,8},{8,10},{14,12},{12,14},{3,1},{1,3},... | collective-permute-start | bytes 245768 | tf_op jit(solution)/shard_map/ppermute | solution.py:242
  19.3 0.0 copy-done
  19.4 0.6 %copy-done.2 = f32[128]{0:T(128)S(1)} copy-done((f32[128]{0:T(128)S(1)}, f32[128]{0:T(128)}, u32[]{:S(2)}) %copy-start.2) | copy-done | bytes 536
  20.0 0.9 %constants.1 = (bf16[128,1024]{1,0:T(8,128)(2,1)S(1)}, f32[1,128]{1,0:T(1,128)S(1)}, bf16[256,128]{1,0:T(8,128)(2,1)S(1)}) custom-call(bf16[1024,128]{1,0:T(8,128)(2,1)S(1)} %copy-done, f32[1,128]{1,0:T(1,128)S(1)} %bitcast.7, bf16[320,128]{1,0:T(8,128)(2,1)S(1)} %copy-done.1), custom_call_target="tpu_custom_call" | custom-call | tf_op jit(solution)/shard_map/constants/pallas_call | solution.py:154
  20.9 0.0 collective-permute-done.5.refs_6_
  20.9 0.6 %collective-permute-done.4.refs_5_ = bf16[256,128]{1,0:T(8,128)(2,1)S(1)} collective-permute-done((bf16[256,128]{1,0:T(8,128)(2,1)S(1)}, bf16[256,128]{1,0:T(8,128)(2,1)S(1)}, u32[]{:S(2)}, u32[]{:S(2)}) %collective-permute-start.4) | collective-permute-done | bytes 65568 | tf_op jit(solution)/shard_map/ppermute | solution.py:242
  21.6 0.9 %collective-permute-done.6.refs_7_ = bf16[320,128]{1,0:T(8,128)(2,1)S(1)} collective-permute-done((bf16[320,128]{1,0:T(8,128)(2,1)S(1)}, bf16[320,128]{1,0:T(8,128)(2,1)S(1)}, u32[]{:S(2)}, u32[]{:S(2)}) %collective-permute-start.6) | collective-permute-done | bytes 81952 | tf_op jit(solution)/shard_map/ppermute | solution.py:242
  22.5 0.0 collective-permute-done.7
  22.5 0.1 collective-permute-start.8
  22.6 1.3 %collective-permute-done.8.other_ref = bf16[448,128]{1,0:T(8,128)(2,1)S(1)} collective-permute-done((bf16[448,128]{1,0:T(8,128)(2,1)S(1)}, bf16[448,128]{1,0:T(8,128)(2,1)S(1)}, u32[]{:S(2)}, u32[]{:S(2)}) %collective-permute-start.8) | collective-permute-done | bytes 114720 | tf_op jit(solution)/shard_map/ppermute | solution.py:281
  23.9 0.2 prepare.1.left_ref
  24.1 5.2 %pairs.1 = bf16[32,128,128]{2,1,0:T(8,128)(2,1)} custom-call(bf16[1024,64]{1,0:T(8,128)(2,1)S(1)} %prepare.1.left_ref, bf16[128,1024]{1,0:T(8,128)(2,1)S(1)} %get-tuple-element.50.weights_ref, f32[1,128]{1,0:T(1,128)S(1)} %get-tuple-element.51.bias_ref, bf16[256,128]{1,0:T(8,128)(2,1)S(1)} %get-tuple-element.52.refs_0_, ...), custom_call_target="tpu_custom_call" | custom-call | flops 1610612736 | bytes 1048576 | tf_op jit(solution)/shard_map/pairs/pallas_call | solution.py:209
  (16 shorter events, 0.1 us)
Async XLA Ops:
  2.6 16.7 %copy-start = (bf16[1024,128]{1,0:T(8,128)(2,1)S(1)}, bf16[1024,128]{1,0:T(8,128)(2,1)}, u32[]{:S(2)}) copy-start(bf16[1024,128]{1,0:T(8,128)(2,1)} %w_ref.1) | copy-start | bytes 786436
  2.6 9.8 %collective-permute-start.2 = (bf16[384,128]{1,0:T(8,128)(2,1)}, bf16[384,128]{1,0:T(8,128)(2,1)S(1)}, u32[]{:S(2)}, u32[]{:S(2)}) collective-permute-start(bf16[384,128]{1,0:T(8,128)(2,1)} %get-tuple-element.37), channel_id=1, source_target_pairs={{12,0},{14,2},{8,4},{10,6},{4,8},{6,10},{0,12},{2,14},{13,1},{15,3... | collective-permute-start | bytes 294920 | tf_op jit(solution)/shard_map/ppermute | solution.py:242
  7.7 4.7 %collective-permute-start.3 = (bf16[320,128]{1,0:T(8,128)(2,1)}, bf16[320,128]{1,0:T(8,128)(2,1)S(1)}, u32[]{:S(2)}, u32[]{:S(2)}) collective-permute-start(bf16[320,128]{1,0:T(8,128)(2,1)} %get-tuple-element.38), channel_id=1, source_target_pairs={{2,0},{0,2},{6,4},{4,6},{10,8},{8,10},{14,12},{12,14},{3,1},{1,3},... | collective-permute-start | bytes 245768 | tf_op jit(solution)/shard_map/ppermute | solution.py:242
  9.2 6.3 %collective-permute-start.1 = (bf16[320,128]{1,0:T(8,128)(2,1)}, bf16[320,128]{1,0:T(8,128)(2,1)S(1)}, u32[]{:S(2)}, u32[]{:S(2)}) collective-permute-start(bf16[320,128]{1,0:T(8,128)(2,1)} %get-tuple-element.36), channel_id=1, source_target_pairs={{8,0},{10,2},{12,4},{14,6},{0,8},{2,10},{4,12},{6,14},{9,1},{11,3}... | collective-permute-start | bytes 245768 | tf_op jit(solution)/shard_map/ppermute | solution.py:242
  9.2 6.3 %collective-permute-start = (bf16[320,128]{1,0:T(8,128)(2,1)}, bf16[320,128]{1,0:T(8,128)(2,1)S(1)}, u32[]{:S(2)}, u32[]{:S(2)}) collective-permute-start(bf16[320,128]{1,0:T(8,128)(2,1)} %get-tuple-element.32.message_ref), channel_id=1, source_target_pairs={{4,0},{6,2},{0,4},{2,6},{12,8},{14,10},{8,12},{10,14},{5,1},{7,3},... | collective-permute-start | bytes 245768 | tf_op jit(solution)/shard_map/ppermute | solution.py:242
  10.0 12.4 %collective-permute-start.7 = (bf16[64,128]{1,0:T(8,128)(2,1)}, bf16[64,128]{1,0:T(8,128)(2,1)S(1)}, u32[]{:S(2)}, u32[]{:S(2)}) collective-permute-start(bf16[64,128]{1,0:T(8,128)(2,1)} %get-tuple-element.48), channel_id=1, source_target_pairs={{6,0},{10,1},{4,2},{8,3},{2,4},{14,5},{0,6},{12,7},{15,9},{3,8},{1... | collective-permute-start | bytes 49160 | tf_op jit(solution)/shard_map/ppermute | solution.py:253
  15.5 3.8 %copy-start.3 = (bf16[64,128]{1,0:T(8,128)(2,1)S(1)}, bf16[64,128]{1,0:T(8,128)(2,1)}, u32[]{:S(2)}) copy-start(bf16[64,128]{1,0:T(8,128)(2,1)} %get-tuple-element.30) | copy-start | bytes 49156
  15.5 3.8 %copy-start.1 = (bf16[320,128]{1,0:T(8,128)(2,1)S(1)}, bf16[320,128]{1,0:T(8,128)(2,1)}, u32[]{:S(2)}) copy-start(bf16[320,128]{1,0:T(8,128)(2,1)} %get-tuple-element.32.message_ref) | copy-start | bytes 245764
  15.5 5.4 %collective-permute-start.5 = (bf16[256,128]{1,0:T(8,128)(2,1)S(1)}, bf16[256,128]{1,0:T(8,128)(2,1)S(1)}, u32[]{:S(2)}, u32[]{:S(2)}) collective-permute-start(bf16[256,128]{1,0:T(8,128)(2,1)S(1)} %slice.25), channel_id=1, source_target_pairs={{2,0},{0,2},{6,4},{4,6},{10,8},{8,10},{14,12},{12,14},{3,1},{1,3},... | collective-permute-start | bytes 196616 | tf_op jit(solution)/shard_map/ppermute | solution.py:242
  17.3 4.3 %collective-permute-start.4 = (bf16[256,128]{1,0:T(8,128)(2,1)S(1)}, bf16[256,128]{1,0:T(8,128)(2,1)S(1)}, u32[]{:S(2)}, u32[]{:S(2)}) collective-permute-start(bf16[256,128]{1,0:T(8,128)(2,1)S(1)} %slice.24), channel_id=1, source_target_pairs={{2,0},{0,2},{6,4},{4,6},{10,8},{8,10},{14,12},{12,14},{3,1},{1,3},... | collective-permute-start | bytes 196616 | tf_op jit(solution)/shard_map/ppermute | solution.py:242
  17.6 4.8 %collective-permute-start.6 = (bf16[320,128]{1,0:T(8,128)(2,1)S(1)}, bf16[320,128]{1,0:T(8,128)(2,1)S(1)}, u32[]{:S(2)}, u32[]{:S(2)}) collective-permute-start(bf16[320,128]{1,0:T(8,128)(2,1)S(1)} %slice.26), channel_id=1, source_target_pairs={{2,0},{0,2},{6,4},{4,6},{10,8},{8,10},{14,12},{12,14},{3,1},{1,3},... | collective-permute-start | bytes 245768 | tf_op jit(solution)/shard_map/ppermute | solution.py:242
  19.3 0.7 %copy-start.2 = (f32[128]{0:T(128)S(1)}, f32[128]{0:T(128)}, u32[]{:S(2)}) copy-start(f32[128]{0:T(128)} %param.17) | copy-start | bytes 1540
  22.5 1.4 %collective-permute-start.8 = (bf16[448,128]{1,0:T(8,128)(2,1)S(1)}, bf16[448,128]{1,0:T(8,128)(2,1)S(1)}, u32[]{:S(2)}, u32[]{:S(2)}) collective-permute-start(bf16[448,128]{1,0:T(8,128)(2,1)S(1)} %constant_dynamic-update-slice_fusion.mine_ref), channel_id=1, source_target_pairs={{0,1},{1,0},{2,3},{3,2},{4,5},{5,4},{6,7},{7,6},{8,9},{9,8},{10,11... | collective-permute-start | bytes 344072 | tf_op jit(solution)/shard_map/ppermute | solution.py:281

commit v15 on v14

--- a/solution.py
+++ b/solution.py
@@ -267,15 +267,16 @@
     line = [fetch(message, step, row_count) for step, message in reversed([*zip(direct_steps(along), direct[:-1])])][::-1]
     across = fetch(direct[-1], (0, 1), row_count)
     beyond = [fetch_far(message, step, row_count) for step, message in zip(far_steps(along), messages[along:])]
-    far = []
-    for step, block in reversed([*zip(direct_steps(along), line)]):
-        block, across = lax.optimization_barrier((block, across))
-        block = block[left_rows:] if carries_far(step, along) else block[:rows]
-        far.insert(0, fetch(block, (0, 1), row_count))
+    *near, last = line
+    last, across = lax.optimization_barrier((last, across))
+    last_far = fetch(last[left_rows:], (0, 1), row_count)
+    *near, last_far = lax.optimization_barrier((*near, last_far))
+    far = [fetch(block[:rows], (0, 1), row_count) for block in reversed(near)][::-1] + [last_far]
 
     message, _ = lax.optimization_barrier((direct[0], line[0]))
     weights, bias, right = constants(w_out, b_out, message, rows, c)
-    weights, bias, right, held, far = lax.optimization_barrier((weights, bias, right, tuple(line), tuple(far)))
+    held = [*near, last]
+    line = held
     mine = jnp.concatenate([own] + [block[rows:] for block in held[:-1]] + [held[-1][:left_rows], across[rows:]]
                            + beyond + [far[-1][rows:]])
     other = lax.ppermute(mine, "col", [(0, 1), (1, 0)])

time: 29.4 us -> 28.3 us (0.963)
  local copies, waits for them, and re-layouts: 0.72 us -> 0.09 us
    ppermute x1, waiting for transfers between devices: 1.31 us -> 0.01 us  [on_device(): other = lax.ppermute(mine, 'col', [(0, 1), (1, 0)])]
    ppermute x1, starting transfers between devices: 1.18 us -> 0.01 us  [fetch_far(): return lax.ppermute(array, ('row', 'col'), moves)]
    ppermute x7, waiting for transfers between devices: 5.81 us -> 6.82 us  [fetch(): lax.ppermute(array, 'row', [(source_at(r, step), r) for r in range(count)])]
    ppermute x7, starting transfers between devices: 11.2 us -> 12.2 us  [fetch(): lax.ppermute(array, 'row', [(source_at(r, step), r) for r in range(count)])]
    unnamed x14, local copies, waits for them, and re-layouts: 0.7 us -> 0.06 us
  transfers between devices with their start and end apart: 9 -> 9, of which waited for: 5 -> 6; matrix products, arithmetic and copies ran while one was open for 0% -> 0% of each run, Pallas kernels for 3% -> 4%
where the time goes in v15:
time: 28.3 us; the launch traced here: 28.2 us
  starting transfers between devices  12.3 us (43%)
  Pallas kernels  8.89 us (31%)
  waiting for transfers between devices  6.83 us (24%)
    ppermute x7, starting transfers between devices, fetch(): lax.ppermute(array, 'row', [(source_at(r, step), r) for r in range(count)])  12.2 us
    ppermute x7, waiting for transfers between devices, fetch(): lax.ppermute(array, 'row', [(source_at(r, step), r) for r in range(count)])  6.82 us
    pallas_call x1, Pallas kernels, pairs(): pl.pallas_call(functools.partial(pair_kernel, seqs, c, right_at), grid=(r...  5.2 us
    pallas_call x1, Pallas kernels, features(): pl.pallas_call(functools.partial(features_kernel, 1.0 / (seqs * row_count...  2.61 us
    pallas_call x1, Pallas kernels, constants(): pl.pallas_call(functools.partial(constants_kernel, c, rows), grid=(1,), o...  0.92 us
  transfers between devices with their start and end apart: 9, of which 6 were waited for; matrix products, arithmetic and copies ran while one was open for 0% of the time, Pallas kernels for 4%

profile of v15, /device:TPU:0, one launch (start us, length us, event | category | flops | bytes accessed | tf_op | source)
XLA Modules:
  0.0 28.2 jit_solution(2725675904877874664)
XLA Ops:
  0.0 2.6 %features.1 = (bf16[64,128]{1,0:T(8,128)(2,1)}, bf16[320,128]{1,0:T(8,128)(2,1)}, bf16[320,128]{1,0:T(8,128)(2,1)}, bf16[384,128]{1,0:T(8,128)(2,1)}, bf16[320,128]{1,0:T(8,128)(2,1)}, /*index=5*/bf16[64,128]{1,0:T(8,128)(2,1)}) custom-call(bf16[8,128,256]{2,1,0:T(8,128)(2,1)} %x_ref.1, f32[1,256]{1,0:T(1,128)} %bitcast.10, f32[1,256]{1,0:T(1,128)} %bitcast.11, ...), custom_call_target="tpu_custom_call" | custom-call | tf_op jit(solution)/shard_map/features/pallas_call | solution.py:86
  2.6 5.0 %collective-permute-start.2 = (bf16[384,128]{1,0:T(8,128)(2,1)}, bf16[384,128]{1,0:T(8,128)(2,1)S(1)}, u32[]{:S(2)}, u32[]{:S(2)}) collective-permute-start(bf16[384,128]{1,0:T(8,128)(2,1)} %get-tuple-element.23), channel_id=1, source_target_pairs={{12,0},{14,2},{8,4},{10,6},{4,8},{6,10},{0,12},{2,14},{13,1},{15,3... | collective-permute-start | bytes 294920 | tf_op jit(solution)/shard_map/ppermute | solution.py:242
  7.7 1.5 %collective-permute-start.3 = (bf16[320,128]{1,0:T(8,128)(2,1)}, bf16[320,128]{1,0:T(8,128)(2,1)S(1)}, u32[]{:S(2)}, u32[]{:S(2)}) collective-permute-start(bf16[320,128]{1,0:T(8,128)(2,1)} %get-tuple-element.24), channel_id=1, source_target_pairs={{2,0},{0,2},{6,4},{4,6},{10,8},{8,10},{14,12},{12,14},{3,1},{1,3},... | collective-permute-start | bytes 245768 | tf_op jit(solution)/shard_map/ppermute | solution.py:242
  9.2 0.0 collective-permute-start.5
  9.2 1.7 %collective-permute-start.1 = (bf16[320,128]{1,0:T(8,128)(2,1)}, bf16[320,128]{1,0:T(8,128)(2,1)S(1)}, u32[]{:S(2)}, u32[]{:S(2)}) collective-permute-start(bf16[320,128]{1,0:T(8,128)(2,1)} %get-tuple-element.22), channel_id=1, source_target_pairs={{8,0},{10,2},{12,4},{14,6},{0,8},{2,10},{4,12},{6,14},{9,1},{11,3}... | collective-permute-start | bytes 245768 | tf_op jit(solution)/shard_map/ppermute | solution.py:242
  10.9 0.2 collective-permute-start
  11.1 1.2 %collective-permute-done.3.refs_4_ = bf16[320,128]{1,0:T(8,128)(2,1)S(1)} collective-permute-done((bf16[320,128]{1,0:T(8,128)(2,1)}, bf16[320,128]{1,0:T(8,128)(2,1)S(1)}, u32[]{:S(2)}, u32[]{:S(2)}) %collective-permute-start.3) | collective-permute-done | bytes 81952 | tf_op jit(solution)/shard_map/ppermute | solution.py:242
  12.3 0.0 collective-permute-done.2.refs_3_
  12.3 0.0 copy-start
  12.3 1.6 %collective-permute-start.4 = (bf16[320,128]{1,0:T(8,128)(2,1)S(1)}, bf16[320,128]{1,0:T(8,128)(2,1)S(1)}, u32[]{:S(2)}, u32[]{:S(2)}) collective-permute-start(bf16[320,128]{1,0:T(8,128)(2,1)S(1)} %slice.24), channel_id=1, source_target_pairs={{2,0},{0,2},{6,4},{4,6},{10,8},{8,10},{14,12},{12,14},{3,1},{1,3},... | collective-permute-start | bytes 245768 | tf_op jit(solution)/shard_map/ppermute | solution.py:242
  13.9 1.3 %collective-permute-done.1.refs_2_ = bf16[320,128]{1,0:T(8,128)(2,1)S(1)} collective-permute-done((bf16[320,128]{1,0:T(8,128)(2,1)}, bf16[320,128]{1,0:T(8,128)(2,1)S(1)}, u32[]{:S(2)}, u32[]{:S(2)}) %collective-permute-start.1) | collective-permute-done | bytes 81952 | tf_op jit(solution)/shard_map/ppermute | solution.py:242
  15.2 0.8 %collective-permute-done.refs_1_ = bf16[320,128]{1,0:T(8,128)(2,1)S(1)} collective-permute-done((bf16[320,128]{1,0:T(8,128)(2,1)}, bf16[320,128]{1,0:T(8,128)(2,1)S(1)}, u32[]{:S(2)}, u32[]{:S(2)}) %collective-permute-start) | collective-permute-done | bytes 81952 | tf_op jit(solution)/shard_map/ppermute | solution.py:242
  16.1 0.8 %collective-permute-done.4.refs_7_ = bf16[320,128]{1,0:T(8,128)(2,1)S(1)} collective-permute-done((bf16[320,128]{1,0:T(8,128)(2,1)S(1)}, bf16[320,128]{1,0:T(8,128)(2,1)S(1)}, u32[]{:S(2)}, u32[]{:S(2)}) %collective-permute-start.4) | collective-permute-done | bytes 81952 | tf_op jit(solution)/shard_map/ppermute | solution.py:242
  16.9 0.0 collective-permute-done.5
  16.9 0.1 collective-permute-start.6
  17.0 0.0 copy-start.2
  17.0 1.6 %collective-permute-start.8 = (bf16[256,128]{1,0:T(8,128)(2,1)S(1)}, bf16[256,128]{1,0:T(8,128)(2,1)S(1)}, u32[]{:S(2)}, u32[]{:S(2)}) collective-permute-start(bf16[256,128]{1,0:T(8,128)(2,1)S(1)} %slice.31), channel_id=1, source_target_pairs={{2,0},{0,2},{6,4},{4,6},{10,8},{8,10},{14,12},{12,14},{3,1},{1,3},... | collective-permute-start | bytes 196616 | tf_op jit(solution)/shard_map/ppermute | solution.py:242
  18.6 0.5 %collective-permute-start.7 = (bf16[256,128]{1,0:T(8,128)(2,1)S(1)}, bf16[256,128]{1,0:T(8,128)(2,1)S(1)}, u32[]{:S(2)}, u32[]{:S(2)}) collective-permute-start(bf16[256,128]{1,0:T(8,128)(2,1)S(1)} %slice.30), channel_id=1, source_target_pairs={{2,0},{0,2},{6,4},{4,6},{10,8},{8,10},{14,12},{12,14},{3,1},{1,3},... | collective-permute-start | bytes 196616 | tf_op jit(solution)/shard_map/ppermute | solution.py:242
  19.1 0.9 %constants.1 = (bf16[128,1024]{1,0:T(8,128)(2,1)S(1)}, f32[1,128]{1,0:T(1,128)S(1)}, bf16[256,128]{1,0:T(8,128)(2,1)S(1)}) custom-call(bf16[1024,128]{1,0:T(8,128)(2,1)S(1)} %copy-done, f32[1,128]{1,0:T(1,128)S(1)} %bitcast.7, bf16[320,128]{1,0:T(8,128)(2,1)S(1)} %copy-done.1), custom_call_target="tpu_custom_call" | custom-call | tf_op jit(solution)/shard_map/constants/pallas_call | solution.py:154
  20.1 0.0 collective-permute-done.6.other_ref
  20.1 0.2 prepare.1.left_ref
  20.2 1.5 %collective-permute-done.8.refs_6_ = bf16[256,128]{1,0:T(8,128)(2,1)S(1)} collective-permute-done((bf16[256,128]{1,0:T(8,128)(2,1)S(1)}, bf16[256,128]{1,0:T(8,128)(2,1)S(1)}, u32[]{:S(2)}, u32[]{:S(2)}) %collective-permute-start.8) | collective-permute-done | bytes 65568 | tf_op jit(solution)/shard_map/ppermute | solution.py:242
  21.8 1.2 %collective-permute-done.7.refs_5_ = bf16[256,128]{1,0:T(8,128)(2,1)S(1)} collective-permute-done((bf16[256,128]{1,0:T(8,128)(2,1)S(1)}, bf16[256,128]{1,0:T(8,128)(2,1)S(1)}, u32[]{:S(2)}, u32[]{:S(2)}) %collective-permute-start.7) | collective-permute-done | bytes 65568 | tf_op jit(solution)/shard_map/ppermute | solution.py:242
  23.0 5.2 %pairs.1 = bf16[32,128,128]{2,1,0:T(8,128)(2,1)} custom-call(bf16[1024,64]{1,0:T(8,128)(2,1)S(1)} %prepare.1.left_ref, bf16[128,1024]{1,0:T(8,128)(2,1)S(1)} %get-tuple-element.32.weights_ref, f32[1,128]{1,0:T(1,128)S(1)} %get-tuple-element.33.bias_ref, bf16[256,128]{1,0:T(8,128)(2,1)S(1)} %get-tuple-element.34.refs_0_, ...), custom_call_target="tpu_custom_call" | custom-call | flops 1610612736 | bytes 1048576 | tf_op jit(solution)/shard_map/pairs/pallas_call | solution.py:209
  (16 shorter events, 0.1 us)
Async XLA Ops:
  2.6 9.7 %collective-permute-start.2 = (bf16[384,128]{1,0:T(8,128)(2,1)}, bf16[384,128]{1,0:T(8,128)(2,1)S(1)}, u32[]{:S(2)}, u32[]{:S(2)}) collective-permute-start(bf16[384,128]{1,0:T(8,128)(2,1)} %get-tuple-element.23), channel_id=1, source_target_pairs={{12,0},{14,2},{8,4},{10,6},{4,8},{6,10},{0,12},{2,14},{13,1},{15,3... | collective-permute-start | bytes 294920 | tf_op jit(solution)/shard_map/ppermute | solution.py:242
  7.7 4.7 %collective-permute-start.3 = (bf16[320,128]{1,0:T(8,128)(2,1)}, bf16[320,128]{1,0:T(8,128)(2,1)S(1)}, u32[]{:S(2)}, u32[]{:S(2)}) collective-permute-start(bf16[320,128]{1,0:T(8,128)(2,1)} %get-tuple-element.24), channel_id=1, source_target_pairs={{2,0},{0,2},{6,4},{4,6},{10,8},{8,10},{14,12},{12,14},{3,1},{1,3},... | collective-permute-start | bytes 245768 | tf_op jit(solution)/shard_map/ppermute | solution.py:242
  9.2 7.7 %collective-permute-start.5 = (bf16[64,128]{1,0:T(8,128)(2,1)}, bf16[64,128]{1,0:T(8,128)(2,1)S(1)}, u32[]{:S(2)}, u32[]{:S(2)}) collective-permute-start(bf16[64,128]{1,0:T(8,128)(2,1)} %get-tuple-element.29), channel_id=1, source_target_pairs={{6,0},{10,1},{4,2},{8,3},{2,4},{14,5},{0,6},{12,7},{15,9},{3,8},{1... | collective-permute-start | bytes 49160 | tf_op jit(solution)/shard_map/ppermute | solution.py:253
  9.2 6.1 %collective-permute-start.1 = (bf16[320,128]{1,0:T(8,128)(2,1)}, bf16[320,128]{1,0:T(8,128)(2,1)S(1)}, u32[]{:S(2)}, u32[]{:S(2)}) collective-permute-start(bf16[320,128]{1,0:T(8,128)(2,1)} %get-tuple-element.22), channel_id=1, source_target_pairs={{8,0},{10,2},{12,4},{14,6},{0,8},{2,10},{4,12},{6,14},{9,1},{11,3}... | collective-permute-start | bytes 245768 | tf_op jit(solution)/shard_map/ppermute | solution.py:242
  10.9 3.0 %copy-start.3 = (bf16[64,128]{1,0:T(8,128)(2,1)S(1)}, bf16[64,128]{1,0:T(8,128)(2,1)}, u32[]{:S(2)}) copy-start(bf16[64,128]{1,0:T(8,128)(2,1)} %get-tuple-element.20) | copy-start | bytes 49156
  10.9 5.1 %collective-permute-start = (bf16[320,128]{1,0:T(8,128)(2,1)}, bf16[320,128]{1,0:T(8,128)(2,1)S(1)}, u32[]{:S(2)}, u32[]{:S(2)}) collective-permute-start(bf16[320,128]{1,0:T(8,128)(2,1)} %get-tuple-element.31.message_ref), channel_id=1, source_target_pairs={{4,0},{6,2},{0,4},{2,6},{12,8},{14,10},{8,12},{10,14},{5,1},{7,3},... | collective-permute-start | bytes 245768 | tf_op jit(solution)/shard_map/ppermute | solution.py:242
  12.3 6.8 %copy-start = (bf16[1024,128]{1,0:T(8,128)(2,1)S(1)}, bf16[1024,128]{1,0:T(8,128)(2,1)}, u32[]{:S(2)}) copy-start(bf16[1024,128]{1,0:T(8,128)(2,1)} %w_ref.1) | copy-start | bytes 786436
  12.3 4.5 %collective-permute-start.4 = (bf16[320,128]{1,0:T(8,128)(2,1)S(1)}, bf16[320,128]{1,0:T(8,128)(2,1)S(1)}, u32[]{:S(2)}, u32[]{:S(2)}) collective-permute-start(bf16[320,128]{1,0:T(8,128)(2,1)S(1)} %slice.24), channel_id=1, source_target_pairs={{2,0},{0,2},{6,4},{4,6},{10,8},{8,10},{14,12},{12,14},{3,1},{1,3},... | collective-permute-start | bytes 245768 | tf_op jit(solution)/shard_map/ppermute | solution.py:242
  16.9 3.1 %collective-permute-start.6 = (bf16[448,128]{1,0:T(8,128)(2,1)S(1)}, bf16[448,128]{1,0:T(8,128)(2,1)S(1)}, u32[]{:S(2)}, u32[]{:S(2)}) collective-permute-start(bf16[448,128]{1,0:T(8,128)(2,1)S(1)} %constant_dynamic-update-slice_fusion.mine_ref), channel_id=1, source_target_pairs={{0,1},{1,0},{2,3},{3,2},{4,5},{5,4},{6,7},{7,6},{8,9},{9,8},{10,11... | collective-permute-start | bytes 344072 | tf_op jit(solution)/shard_map/ppermute | solution.py:282
  17.0 2.1 %copy-start.1 = (bf16[320,128]{1,0:T(8,128)(2,1)S(1)}, bf16[320,128]{1,0:T(8,128)(2,1)}, u32[]{:S(2)}) copy-start(bf16[320,128]{1,0:T(8,128)(2,1)} %get-tuple-element.31.message_ref) | copy-start | bytes 245764
  17.0 2.1 %copy-start.2 = (f32[128]{0:T(128)S(1)}, f32[128]{0:T(128)}, u32[]{:S(2)}) copy-start(f32[128]{0:T(128)} %param.17) | copy-start | bytes 1540
  17.0 4.7 %collective-permute-start.8 = (bf16[256,128]{1,0:T(8,128)(2,1)S(1)}, bf16[256,128]{1,0:T(8,128)(2,1)S(1)}, u32[]{:S(2)}, u32[]{:S(2)}) collective-permute-start(bf16[256,128]{1,0:T(8,128)(2,1)S(1)} %slice.31), channel_id=1, source_target_pairs={{2,0},{0,2},{6,4},{4,6},{10,8},{8,10},{14,12},{12,14},{3,1},{1,3},... | collective-permute-start | bytes 196616 | tf_op jit(solution)/shard_map/ppermute | solution.py:242
  18.6 4.4 %collective-permute-start.7 = (bf16[256,128]{1,0:T(8,128)(2,1)S(1)}, bf16[256,128]{1,0:T(8,128)(2,1)S(1)}, u32[]{:S(2)}, u32[]{:S(2)}) collective-permute-start(bf16[256,128]{1,0:T(8,128)(2,1)S(1)} %slice.30), channel_id=1, source_target_pairs={{2,0},{0,2},{6,4},{4,6},{10,8},{8,10},{14,12},{12,14},{3,1},{1,3},... | collective-permute-start | bytes 196616 | tf_op jit(solution)/shard_map/ppermute | solution.py:242

commit v16 on v15

--- a/solution.py
+++ b/solution.py
@@ -59,14 +59,14 @@
 
     own_ref[...] = left_for((0, 0))
     right = right_f32[...].astype(jnp.bfloat16)
-    for step, message_ref in zip(direct_steps(chips), message_refs):
-        first = rows if carries_far(step, chips) else 0
+    core = lax.axis_index("col")
+    for n, message_ref in enumerate(message_refs[:chips]):
+        a, b = by_core(core, *(direct_steps(chips)[m] for m in sent_by(n)))
+        first = message_ref.shape[0] - right.shape[0] - rows
+        if first:
+            message_ref[:rows] = left_for((a, b))
         message_ref[first:first + right.shape[0]] = right
-        if first:
-            message_ref[:rows] = left_for(step)
-            message_ref[first + right.shape[0]:] = left_for((step[0], 1))
-        else:
-            message_ref[right.shape[0]:] = left_for(step)
+        message_ref[first + right.shape[0]:] = left_for((a, 1) if first else (a, b))
     same_half = here // chips == lax.axis_index("col")
     for (a, b), message_ref in zip(far_steps(chips), message_refs[chips:]):
         message_ref[...] = jnp.where(same_half, left_for((a + 1, b)), left_for((a, b)))
@@ -79,7 +79,7 @@
     chips = row_count // col_count
     part = rows // chips
     shapes = [(part, LANES)]
-    shapes += [(rows + part * (2 if carries_far(step, chips) else 1), LANES) for step in direct_steps(chips)]
+    shapes += [(rows + part * (2 if n < 2 else 1), LANES) for n in range(chips)]
     shapes += [(part, LANES)] * len(far_steps(chips))
     operands = (alignment, ln_gain.reshape(1, -1), ln_bias.reshape(1, -1), w_left.T, b_left.reshape(1, -1),
                 w_right.T, b_right.reshape(1, -1))
@@ -227,19 +227,29 @@
 
 
 def direct_steps(chips):
-    return [(a, 0) for a in range(1, chips)] + [(0, 1)]
+    return [(chips - 1, 0), (0, 1)] + [(a, 0) for a in reversed(range(1, chips - 1))]
+
+
+def sent_by(n):
+    return n, n ^ 1
+
+
+def by_core(core, of_0, of_1):
+    return jax.tree.map(lambda x, y: jnp.where(core == 0, x, y), of_0, of_1)
 
 
 def far_steps(chips):
     return [(a, 1) for a in range(chips // 2 - 1)]
 
 
-def carries_far(step, chips):
-    return step == (chips - 1, 0)
-
-
 def fetch(array, step, count):
     return lax.ppermute(array, "row", [(source_at(r, step), r) for r in range(count)])
+
+
+def fetch_direct(array, n, count):
+    steps = direct_steps(count // 2)
+    moves = [(2 * source_at(r, steps[m]) + core, 2 * r + core) for r in range(count) for core, m in enumerate(sent_by(n))]
+    return lax.ppermute(array, ("row", "col"), moves)
 
 
 def fetch_far(array, step, count):
@@ -260,33 +270,32 @@
     col_count = lax.axis_size("col")
     own, *messages = features(alignment, ln_gain, ln_bias, w_left, b_left, w_right, b_right, row_count, col_count)
     along = row_count // 2
-    direct = messages[:along]
     left_rows = own.shape[0]
-    rows = direct[0].shape[0] - left_rows
-
-    line = [fetch(message, step, row_count) for step, message in reversed([*zip(direct_steps(along), direct[:-1])])][::-1]
-    across = fetch(direct[-1], (0, 1), row_count)
+    rows = messages[0].shape[0] - 2 * left_rows
+
+    core = lax.axis_index("col")
+    direct = [fetch_direct(message, n, row_count) for n, message in reversed([*enumerate(messages[:along])])][::-1]
     beyond = [fetch_far(message, step, row_count) for step, message in zip(far_steps(along), messages[along:])]
-    *near, last = line
-    last, across = lax.optimization_barrier((last, across))
+    last, across = by_core(core, (direct[0], direct[1]), (direct[1], direct[0]))
     last_far = fetch(last[left_rows:], (0, 1), row_count)
-    *near, last_far = lax.optimization_barrier((*near, last_far))
-    far = [fetch(block[:rows], (0, 1), row_count) for block in reversed(near)][::-1] + [last_far]
-
-    message, _ = lax.optimization_barrier((direct[0], line[0]))
+    *rest, last_far = lax.optimization_barrier((*direct[2:], last_far))
+    rest = [by_core(core, *(rest[m] for m in sent_by(n))) for n in range(along - 2)]
+    far = fetch(jnp.concatenate([block[:rows] for block in rest]), (0, 1), row_count)
+
+    message, _ = lax.optimization_barrier((messages[along - 1], across))
     weights, bias, right = constants(w_out, b_out, message, rows, c)
-    held = [*near, last]
-    line = held
-    mine = jnp.concatenate([own] + [block[rows:] for block in held[:-1]] + [held[-1][:left_rows], across[rows:]]
-                           + beyond + [far[-1][rows:]])
+    near = rest[::-1]
+    mine = jnp.concatenate([own] + [block[rows:] for block in near] + [last[:left_rows], across[:left_rows]]
+                           + beyond + [last_far[rows:]])
     other = lax.ppermute(mine, "col", [(0, 1), (1, 0)])
     half = along // 2
     left_at = [(a, True) for a in range(along + 1)]
     left_at += [(along + a, True) if a < half else (along + 1 + a - half, False) for a in range(1, along - 1)]
     left_at += [(along + half, True)]
     left = prepare(mine, other, left_at, left_rows, seqs)
-    right_at = [(n, left_rows if n == along - 1 else 0) for n in range(row_count)]
-    return pairs(left, weights, bias, [right, *line, across, *far], right_at, seqs, c, width)
+    right_at = [(a, 0) for a in range(along - 1)] + [(along - 1, left_rows), (along, left_rows)]
+    right_at += [(along + 1, (along - 2 - a) * rows) for a in range(1, along - 1)] + [(along + 2, 0)]
+    return pairs(left, weights, bias, [right, *near, last, across, far, last_far], right_at, seqs, c, width)
 
 
 def solution(mesh):

time: 28.3 us -> 27.7 us (0.979)
  waiting for transfers between devices: 6.83 us -> 6.03 us
  local copies, waits for them, and re-layouts: 0.09 us -> 0.64 us
  starting transfers between devices: 12.3 us -> 11.8 us
    ppermute x7 -> x2, starting transfers between devices: 12.2 us -> 3.17 us  [fetch(): lax.ppermute(array, 'row', [(source_at(r, step), r) for r in range(count)])]
    ppermute x0 -> x4, starting transfers between devices: none -> 8.53 us  [fetch_direct(): return lax.ppermute(array, ('row', 'col'), moves)]
    ppermute x7 -> x2, waiting for transfers between devices: 6.82 us -> 1.9 us  [fetch(): lax.ppermute(array, 'row', [(source_at(r, step), r) for r in range(count)])]
    ppermute x0 -> x4, waiting for transfers between devices: none -> 4.13 us  [fetch_direct(): return lax.ppermute(array, ('row', 'col'), moves)]
    unnamed x14, local copies, waits for them, and re-layouts: 0.06 us -> 0.61 us
  transfers between devices with their start and end apart: 9 -> 8, of which waited for: 6 -> 5; matrix products, arithmetic and copies ran while one was open for 0% -> 0% of each run, Pallas kernels for 4% -> 4%
where the time goes in v16:
time: 27.7 us; the launch traced here: 27.5 us
  starting transfers between devices  11.8 us (43%)
  Pallas kernels  8.9 us (32%)
  waiting for transfers between devices  6.03 us (22%)
  local copies, waits for them, and re-layouts  0.64 us (2%)
    ppermute x4, starting transfers between devices, fetch_direct(): return lax.ppermute(array, ('row', 'col'), moves)  8.53 us
    pallas_call x1, Pallas kernels, pairs(): pl.pallas_call(functools.partial(pair_kernel, seqs, c, right_at), grid=(r...  5.2 us
    ppermute x4, waiting for transfers between devices, fetch_direct(): return lax.ppermute(array, ('row', 'col'), moves)  4.13 us
    ppermute x2, starting transfers between devices, fetch(): lax.ppermute(array, 'row', [(source_at(r, step), r) for r in range(count)])  3.17 us
    pallas_call x1, Pallas kernels, features(): pl.pallas_call(functools.partial(features_kernel, 1.0 / (seqs * row_count...  2.62 us
    ppermute x2, waiting for transfers between devices, fetch(): lax.ppermute(array, 'row', [(source_at(r, step), r) for r in range(count)])  1.9 us
    pallas_call x1, Pallas kernels, constants(): pl.pallas_call(functools.partial(constants_kernel, c, rows), grid=(1,), o...  0.92 us
    unnamed x14, local copies, waits for them, and re-layouts  0.61 us
  transfers between devices with their start and end apart: 8, of which 5 were waited for; matrix products, arithmetic and copies ran while one was open for 0% of the time, Pallas kernels for 4%

profile of v16, /device:TPU:0, one launch (start us, length us, event | category | flops | bytes accessed | tf_op | source)
XLA Modules:
  0.0 27.5 jit_solution(14046403019680781049)
XLA Ops:
  0.0 2.6 %features.1 = (bf16[64,128]{1,0:T(8,128)(2,1)}, bf16[384,128]{1,0:T(8,128)(2,1)}, bf16[384,128]{1,0:T(8,128)(2,1)}, bf16[320,128]{1,0:T(8,128)(2,1)}, bf16[320,128]{1,0:T(8,128)(2,1)}, /*index=5*/bf16[64,128]{1,0:T(8,128)(2,1)}) custom-call(bf16[8,128,256]{2,1,0:T(8,128)(2,1)} %x_ref.1, f32[1,256]{1,0:T(1,128)} %bitcast.10, f32[1,256]{1,0:T(1,128)} %bitcast.11, ...), custom_call_target="tpu_custom_call" | custom-call | tf_op jit(solution)/shard_map/features/pallas_call | solution.py:86
  2.6 5.0 %collective-permute-start.2 = (bf16[384,128]{1,0:T(8,128)(2,1)}, bf16[384,128]{1,0:T(8,128)(2,1)S(1)}, u32[]{:S(2)}, u32[]{:S(2)}) collective-permute-start(bf16[384,128]{1,0:T(8,128)(2,1)} %get-tuple-element.21), channel_id=1, source_target_pairs={{12,0},{3,1},{14,2},{1,3},{8,4},{7,5},{10,6},{5,7},{4,8},{11,9},{6... | collective-permute-start | bytes 294920 | tf_op jit(solution)/shard_map/ppermute | solution.py:252
  7.7 1.5 %collective-permute-start.3 = (bf16[384,128]{1,0:T(8,128)(2,1)}, bf16[384,128]{1,0:T(8,128)(2,1)S(1)}, u32[]{:S(2)}, u32[]{:S(2)}) collective-permute-start(bf16[384,128]{1,0:T(8,128)(2,1)} %get-tuple-element.22), channel_id=1, source_target_pairs={{2,0},{13,1},{0,2},{15,3},{6,4},{9,5},{4,6},{11,7},{10,8},{5,9},{8... | collective-permute-start | bytes 294920 | tf_op jit(solution)/shard_map/ppermute | solution.py:252
  9.2 0.0 collective-permute-start.5
  9.2 1.7 %collective-permute-start = (bf16[320,128]{1,0:T(8,128)(2,1)}, bf16[320,128]{1,0:T(8,128)(2,1)S(1)}, u32[]{:S(2)}, u32[]{:S(2)}) collective-permute-start(bf16[320,128]{1,0:T(8,128)(2,1)} %get-tuple-element.19), channel_id=1, source_target_pairs={{8,0},{5,1},{10,2},{7,3},{12,4},{1,5},{14,6},{3,7},{0,8},{13,9},{2... | collective-permute-start | bytes 245768 | tf_op jit(solution)/shard_map/ppermute | solution.py:252
  10.9 0.2 collective-permute-start.1
  11.2 0.2 collective-permute-done.2
  11.3 1.2 %collective-permute-done.3 = bf16[384,128]{1,0:T(8,128)(2,1)S(1)} collective-permute-done((bf16[384,128]{1,0:T(8,128)(2,1)}, bf16[384,128]{1,0:T(8,128)(2,1)S(1)}, u32[]{:S(2)}, u32[]{:S(2)}) %collective-permute-start.3) | collective-permute-done | bytes 98336 | tf_op jit(solution)/shard_map/ppermute | solution.py:252
  12.5 1.6 %collective-permute-start.4 = (bf16[320,128]{1,0:T(8,128)(2,1)S(1)}, bf16[320,128]{1,0:T(8,128)(2,1)S(1)}, u32[]{:S(2)}, u32[]{:S(2)}) collective-permute-start(bf16[320,128]{1,0:T(8,128)(2,1)S(1)} %slice.32), channel_id=1, source_target_pairs={{2,0},{0,2},{6,4},{4,6},{10,8},{8,10},{14,12},{12,14},{3,1},{1,3},... | collective-permute-start | bytes 245768 | tf_op jit(solution)/shard_map/ppermute | solution.py:246
  14.1 2.8 %collective-permute-done = bf16[320,128]{1,0:T(8,128)(2,1)S(1)} collective-permute-done((bf16[320,128]{1,0:T(8,128)(2,1)}, bf16[320,128]{1,0:T(8,128)(2,1)S(1)}, u32[]{:S(2)}, u32[]{:S(2)}) %collective-permute-start) | collective-permute-done | bytes 81952 | tf_op jit(solution)/shard_map/ppermute | solution.py:252
  16.9 0.0 collective-permute-done.1
  16.9 0.1 collective-permute-done.4.refs_6_
  17.1 0.0 copy-start
  17.2 1.6 %collective-permute-start.7 = (bf16[512,128]{1,0:T(8,128)(2,1)S(1)}, bf16[512,128]{1,0:T(8,128)(2,1)S(1)}, u32[]{:S(2)}, u32[]{:S(2)}) collective-permute-start(bf16[512,128]{1,0:T(8,128)(2,1)S(1)} %pad_maximum_fusion), channel_id=1, source_target_pairs={{2,0},{0,2},{6,4},{4,6},{10,8},{8,10},{14,12},{12,14},{3,1},{1,3},... | collective-permute-start | bytes 393224 | tf_op jit(solution)/shard_map/ppermute | solution.py:246
  18.8 0.0 collective-permute-done.5
  18.8 0.0 copy-start.2
  18.8 0.1 collective-permute-start.6
  18.9 0.0 copy-done
  18.9 0.5 %copy-done.2 = f32[128]{0:T(128)S(1)} copy-done((f32[128]{0:T(128)S(1)}, f32[128]{0:T(128)}, u32[]{:S(2)}) %copy-start.2) | copy-done | bytes 536
  19.4 0.9 %constants.1 = (bf16[128,1024]{1,0:T(8,128)(2,1)S(1)}, f32[1,128]{1,0:T(1,128)S(1)}, bf16[256,128]{1,0:T(8,128)(2,1)S(1)}) custom-call(bf16[1024,128]{1,0:T(8,128)(2,1)S(1)} %copy-done, f32[1,128]{1,0:T(1,128)S(1)} %bitcast.7, bf16[320,128]{1,0:T(8,128)(2,1)S(1)} %copy-done.1), custom_call_target="tpu_custom_call" | custom-call | tf_op jit(solution)/shard_map/constants/pallas_call | solution.py:154
  20.4 0.0 collective-permute-done.6.other_ref
  20.4 0.2 prepare.1.left_ref
  20.5 1.8 %collective-permute-done.7.refs_5_ = bf16[512,128]{1,0:T(8,128)(2,1)S(1)} collective-permute-done((bf16[512,128]{1,0:T(8,128)(2,1)S(1)}, bf16[512,128]{1,0:T(8,128)(2,1)S(1)}, u32[]{:S(2)}, u32[]{:S(2)}) %collective-permute-start.7) | collective-permute-done | bytes 131104 | tf_op jit(solution)/shard_map/ppermute | solution.py:246
  22.3 5.2 %pairs.1 = bf16[32,128,128]{2,1,0:T(8,128)(2,1)} custom-call(bf16[1024,64]{1,0:T(8,128)(2,1)S(1)} %prepare.1.left_ref, bf16[128,1024]{1,0:T(8,128)(2,1)S(1)} %get-tuple-element.28.weights_ref, f32[1,128]{1,0:T(1,128)S(1)} %get-tuple-element.29.bias_ref, bf16[256,128]{1,0:T(8,128)(2,1)S(1)} %get-tuple-element.30.refs_0_, ...), custom_call_target="tpu_custom_call" | custom-call | flops 1610612736 | bytes 1048576 | tf_op jit(solution)/shard_map/pairs/pallas_call | solution.py:209
  (17 shorter events, 0.1 us)
Async XLA Ops:
  2.6 8.7 %collective-permute-start.2 = (bf16[384,128]{1,0:T(8,128)(2,1)}, bf16[384,128]{1,0:T(8,128)(2,1)S(1)}, u32[]{:S(2)}, u32[]{:S(2)}) collective-permute-start(bf16[384,128]{1,0:T(8,128)(2,1)} %get-tuple-element.21), channel_id=1, source_target_pairs={{12,0},{3,1},{14,2},{1,3},{8,4},{7,5},{10,6},{5,7},{4,8},{11,9},{6... | collective-permute-start | bytes 294920 | tf_op jit(solution)/shard_map/ppermute | solution.py:252
  7.7 4.8 %collective-permute-start.3 = (bf16[384,128]{1,0:T(8,128)(2,1)}, bf16[384,128]{1,0:T(8,128)(2,1)S(1)}, u32[]{:S(2)}, u32[]{:S(2)}) collective-permute-start(bf16[384,128]{1,0:T(8,128)(2,1)} %get-tuple-element.22), channel_id=1, source_target_pairs={{2,0},{13,1},{0,2},{15,3},{6,4},{9,5},{4,6},{11,7},{10,8},{5,9},{8... | collective-permute-start | bytes 294920 | tf_op jit(solution)/shard_map/ppermute | solution.py:252
  9.2 9.6 %collective-permute-start.5 = (bf16[64,128]{1,0:T(8,128)(2,1)}, bf16[64,128]{1,0:T(8,128)(2,1)S(1)}, u32[]{:S(2)}, u32[]{:S(2)}) collective-permute-start(bf16[64,128]{1,0:T(8,128)(2,1)} %get-tuple-element.25), channel_id=1, source_target_pairs={{6,0},{10,1},{4,2},{8,3},{2,4},{14,5},{0,6},{12,7},{15,9},{3,8},{1... | collective-permute-start | bytes 49160 | tf_op jit(solution)/shard_map/ppermute | solution.py:263
  9.2 7.7 %collective-permute-start = (bf16[320,128]{1,0:T(8,128)(2,1)}, bf16[320,128]{1,0:T(8,128)(2,1)S(1)}, u32[]{:S(2)}, u32[]{:S(2)}) collective-permute-start(bf16[320,128]{1,0:T(8,128)(2,1)} %get-tuple-element.19), channel_id=1, source_target_pairs={{8,0},{5,1},{10,2},{7,3},{12,4},{1,5},{14,6},{3,7},{0,8},{13,9},{2... | collective-permute-start | bytes 245768 | tf_op jit(solution)/shard_map/ppermute | solution.py:252
  10.9 6.0 %collective-permute-start.1 = (bf16[320,128]{1,0:T(8,128)(2,1)}, bf16[320,128]{1,0:T(8,128)(2,1)S(1)}, u32[]{:S(2)}, u32[]{:S(2)}) collective-permute-start(bf16[320,128]{1,0:T(8,128)(2,1)} %get-tuple-element.27.message_ref), channel_id=1, source_target_pairs={{4,0},{9,1},{6,2},{11,3},{0,4},{13,5},{2,6},{15,7},{12,8},{1,9},{1... | collective-permute-start | bytes 245768 | tf_op jit(solution)/shard_map/ppermute | solution.py:252
  12.5 1.6 %copy-start.3 = (bf16[64,128]{1,0:T(8,128)(2,1)S(1)}, bf16[64,128]{1,0:T(8,128)(2,1)}, u32[]{:S(2)}) copy-start(bf16[64,128]{1,0:T(8,128)(2,1)} %get-tuple-element.18) | copy-start | bytes 49156
  12.5 4.5 %collective-permute-start.4 = (bf16[320,128]{1,0:T(8,128)(2,1)S(1)}, bf16[320,128]{1,0:T(8,128)(2,1)S(1)}, u32[]{:S(2)}, u32[]{:S(2)}) collective-permute-start(bf16[320,128]{1,0:T(8,128)(2,1)S(1)} %slice.32), channel_id=1, source_target_pairs={{2,0},{0,2},{6,4},{4,6},{10,8},{8,10},{14,12},{12,14},{3,1},{1,3},... | collective-permute-start | bytes 245768 | tf_op jit(solution)/shard_map/ppermute | solution.py:246
  17.1 1.8 %copy-start = (bf16[1024,128]{1,0:T(8,128)(2,1)S(1)}, bf16[1024,128]{1,0:T(8,128)(2,1)}, u32[]{:S(2)}) copy-start(bf16[1024,128]{1,0:T(8,128)(2,1)} %w_ref.1) | copy-start | bytes 786436
  17.2 1.7 %copy-start.1 = (bf16[320,128]{1,0:T(8,128)(2,1)S(1)}, bf16[320,128]{1,0:T(8,128)(2,1)}, u32[]{:S(2)}) copy-start(bf16[320,128]{1,0:T(8,128)(2,1)} %get-tuple-element.27.message_ref) | copy-start | bytes 245764
  17.2 5.2 %collective-permute-start.7 = (bf16[512,128]{1,0:T(8,128)(2,1)S(1)}, bf16[512,128]{1,0:T(8,128)(2,1)S(1)}, u32[]{:S(2)}, u32[]{:S(2)}) collective-permute-start(bf16[512,128]{1,0:T(8,128)(2,1)S(1)} %pad_maximum_fusion), channel_id=1, source_target_pairs={{2,0},{0,2},{6,4},{4,6},{10,8},{8,10},{14,12},{12,14},{3,1},{1,3},... | collective-permute-start | bytes 393224 | tf_op jit(solution)/shard_map/ppermute | solution.py:246
  18.8 0.7 %copy-start.2 = (f32[128]{0:T(128)S(1)}, f32[128]{0:T(128)}, u32[]{:S(2)}) copy-start(f32[128]{0:T(128)} %param.17) | copy-start | bytes 1540
  18.8 1.6 %collective-permute-start.6 = (bf16[448,128]{1,0:T(8,128)(2,1)S(1)}, bf16[448,128]{1,0:T(8,128)(2,1)S(1)}, u32[]{:S(2)}, u32[]{:S(2)}) collective-permute-start(bf16[448,128]{1,0:T(8,128)(2,1)S(1)} %constant_dynamic-update-slice_fusion.mine_ref), channel_id=1, source_target_pairs={{0,1},{1,0},{2,3},{3,2},{4,5},{5,4},{6,7},{7,6},{8,9},{9,8},{10,11... | collective-permute-start | bytes 344072 | tf_op jit(solution)/shard_map/ppermute | solution.py:290

commit v17 on v16

--- a/solution.py
+++ b/solution.py
@@ -275,6 +275,7 @@
 
     core = lax.axis_index("col")
     direct = [fetch_direct(message, n, row_count) for n, message in reversed([*enumerate(messages[:along])])][::-1]
+    messages[along:], direct[:2] = lax.optimization_barrier((messages[along:], direct[:2]))
     beyond = [fetch_far(message, step, row_count) for step, message in zip(far_steps(along), messages[along:])]
     last, across = by_core(core, (direct[0], direct[1]), (direct[1], direct[0]))
     last_far = fetch(last[left_rows:], (0, 1), row_count)

time: 27.7 us -> 28.2 us (1.018)
  waiting for transfers between devices: 6.03 us -> 4.31 us
  starting transfers between devices: 11.8 us -> 13.2 us
  local copies, waits for them, and re-layouts: 0.64 us -> 1.36 us
    ppermute x1, starting transfers between devices: 0.01 us -> 2.68 us  [fetch_far(): return lax.ppermute(array, ('row', 'col'), moves)]
    ppermute x4, waiting for transfers between devices: 4.13 us -> 2.52 us  [fetch_direct(): return lax.ppermute(array, ('row', 'col'), moves)]
    ppermute x4, starting transfers between devices: 8.53 us -> 7.35 us  [fetch_direct(): return lax.ppermute(array, ('row', 'col'), moves)]
    unnamed x14 -> x16, local copies, waits for them, and re-layouts: 0.61 us -> 1.33 us
    ppermute x2, waiting for transfers between devices: 1.9 us -> 1.46 us  [fetch(): lax.ppermute(array, 'row', [(source_at(r, step), r) for r in range(count)])]
    ppermute x1, waiting for transfers between devices: 0.01 us -> 0.33 us  [fetch_far(): return lax.ppermute(array, ('row', 'col'), moves)]
  transfers between devices with their start and end apart: 8 -> 8, of which waited for: 5 -> 4; matrix products, arithmetic and copies ran while one was open for 0% -> 0% of each run, Pallas kernels for 4% -> 4%
where the time goes in v17:
time: 28.2 us; the launch traced here: 27.9 us
  starting transfers between devices  13.2 us (47%)
  Pallas kernels  8.88 us (31%)
  waiting for transfers between devices  4.31 us (15%)
  local copies, waits for them, and re-layouts  1.36 us (5%)
    ppermute x4, starting transfers between devices, fetch_direct(): return lax.ppermute(array, ('row', 'col'), moves)  7.35 us
    pallas_call x1, Pallas kernels, pairs(): pl.pallas_call(functools.partial(pair_kernel, seqs, c, right_at), grid=(r...  5.2 us
    ppermute x2, starting transfers between devices, fetch(): lax.ppermute(array, 'row', [(source_at(r, step), r) for r in range(count)])  3.05 us
    ppermute x1, starting transfers between devices, fetch_far(): return lax.ppermute(array, ('row', 'col'), moves)  2.68 us
    pallas_call x1, Pallas kernels, features(): pl.pallas_call(functools.partial(features_kernel, 1.0 / (seqs * row_count...  2.61 us
    ppermute x4, waiting for transfers between devices, fetch_direct(): return lax.ppermute(array, ('row', 'col'), moves)  2.52 us
    ppermute x2, waiting for transfers between devices, fetch(): lax.ppermute(array, 'row', [(source_at(r, step), r) for r in range(count)])  1.46 us
    unnamed x16, local copies, waits for them, and re-layouts  1.33 us
  transfers between devices with their start and end apart: 8, of which 4 were waited for; matrix products, arithmetic and copies ran while one was open for 0% of the time, Pallas kernels for 4%

profile of v17, /device:TPU:0, one launch (start us, length us, event | category | flops | bytes accessed | tf_op | source)
XLA Modules:
  0.0 27.9 jit_solution(7195144998818351795)
XLA Ops:
  0.0 2.6 %features.1 = (bf16[64,128]{1,0:T(8,128)(2,1)}, bf16[384,128]{1,0:T(8,128)(2,1)}, bf16[384,128]{1,0:T(8,128)(2,1)}, bf16[320,128]{1,0:T(8,128)(2,1)}, bf16[320,128]{1,0:T(8,128)(2,1)}, /*index=5*/bf16[64,128]{1,0:T(8,128)(2,1)}) custom-call(bf16[8,128,256]{2,1,0:T(8,128)(2,1)} %x_ref.1, f32[1,256]{1,0:T(1,128)} %bitcast.10, f32[1,256]{1,0:T(1,128)} %bitcast.11, ...), custom_call_target="tpu_custom_call" | custom-call | tf_op jit(solution)/shard_map/features/pallas_call | solution.py:86
  2.6 5.0 %collective-permute-start.2 = (bf16[384,128]{1,0:T(8,128)(2,1)}, bf16[384,128]{1,0:T(8,128)(2,1)S(1)}, u32[]{:S(2)}, u32[]{:S(2)}) collective-permute-start(bf16[384,128]{1,0:T(8,128)(2,1)} %get-tuple-element.25), channel_id=1, source_target_pairs={{12,0},{3,1},{14,2},{1,3},{8,4},{7,5},{10,6},{5,7},{4,8},{11,9},{6... | collective-permute-start | bytes 294920 | tf_op jit(solution)/shard_map/ppermute | solution.py:252
  7.6 1.5 %collective-permute-start.3 = (bf16[384,128]{1,0:T(8,128)(2,1)}, bf16[384,128]{1,0:T(8,128)(2,1)S(1)}, u32[]{:S(2)}, u32[]{:S(2)}) collective-permute-start(bf16[384,128]{1,0:T(8,128)(2,1)} %get-tuple-element.26), channel_id=1, source_target_pairs={{2,0},{13,1},{0,2},{15,3},{6,4},{9,5},{4,6},{11,7},{10,8},{5,9},{8... | collective-permute-start | bytes 294920 | tf_op jit(solution)/shard_map/ppermute | solution.py:252
  9.2 0.0 collective-permute-start
  9.2 0.8 %collective-permute-start.1 = (bf16[320,128]{1,0:T(8,128)(2,1)}, bf16[320,128]{1,0:T(8,128)(2,1)S(1)}, u32[]{:S(2)}, u32[]{:S(2)}) collective-permute-start(bf16[320,128]{1,0:T(8,128)(2,1)} %get-tuple-element.33.message_ref), channel_id=1, source_target_pairs={{4,0},{9,1},{6,2},{11,3},{0,4},{13,5},{2,6},{15,7},{12,8},{1,9},{1... | collective-permute-start | bytes 245768 | tf_op jit(solution)/shard_map/ppermute | solution.py:252
  10.0 1.3 %collective-permute-done.2 = bf16[384,128]{1,0:T(8,128)(2,1)S(1)} collective-permute-done((bf16[384,128]{1,0:T(8,128)(2,1)}, bf16[384,128]{1,0:T(8,128)(2,1)S(1)}, u32[]{:S(2)}, u32[]{:S(2)}) %collective-permute-start.2) | collective-permute-done | bytes 98336 | tf_op jit(solution)/shard_map/ppermute | solution.py:252
  11.3 1.2 %collective-permute-done.3 = bf16[384,128]{1,0:T(8,128)(2,1)S(1)} collective-permute-done((bf16[384,128]{1,0:T(8,128)(2,1)}, bf16[384,128]{1,0:T(8,128)(2,1)S(1)}, u32[]{:S(2)}, u32[]{:S(2)}) %collective-permute-start.3) | collective-permute-done | bytes 98336 | tf_op jit(solution)/shard_map/ppermute | solution.py:252
  12.5 0.0 copy-start.3
  12.5 1.6 %collective-permute-start.4 = (bf16[320,128]{1,0:T(8,128)(2,1)S(1)}, bf16[320,128]{1,0:T(8,128)(2,1)S(1)}, u32[]{:S(2)}, u32[]{:S(2)}) collective-permute-start(bf16[320,128]{1,0:T(8,128)(2,1)S(1)} %slice.32), channel_id=1, source_target_pairs={{2,0},{0,2},{6,4},{4,6},{10,8},{8,10},{14,12},{12,14},{3,1},{1,3},... | collective-permute-start | bytes 245768 | tf_op jit(solution)/shard_map/ppermute | solution.py:246
  14.1 0.7 %copy-done.4 = bf16[64,128]{1,0:T(8,128)(2,1)S(1)} copy-done((bf16[64,128]{1,0:T(8,128)(2,1)S(1)}, bf16[64,128]{1,0:T(8,128)(2,1)}, u32[]{:S(2)}) %copy-start.4) | copy-done | bytes 16408
  14.8 2.7 %collective-permute-start.5 = (bf16[64,128]{1,0:T(8,128)(2,1)S(1)}, bf16[64,128]{1,0:T(8,128)(2,1)S(1)}, u32[]{:S(2)}, u32[]{:S(2)}) collective-permute-start(bf16[64,128]{1,0:T(8,128)(2,1)S(1)} %copy-done.4), channel_id=1, source_target_pairs={{6,0},{10,1},{4,2},{8,3},{2,4},{14,5},{0,6},{12,7},{15,9},{3,8},{1... | collective-permute-start | bytes 49160 | tf_op jit(solution)/shard_map/ppermute | solution.py:263
  17.5 0.0 collective-permute-done
  17.5 0.0 collective-permute-done.1
  17.5 0.0 collective-permute-done.4.refs_6_
  17.6 0.0 copy-start
  17.7 1.5 %collective-permute-start.7 = (bf16[512,128]{1,0:T(8,128)(2,1)S(1)}, bf16[512,128]{1,0:T(8,128)(2,1)S(1)}, u32[]{:S(2)}, u32[]{:S(2)}) collective-permute-start(bf16[512,128]{1,0:T(8,128)(2,1)S(1)} %pad_maximum_fusion), channel_id=1, source_target_pairs={{2,0},{0,2},{6,4},{4,6},{10,8},{8,10},{14,12},{12,14},{3,1},{1,3},... | collective-permute-start | bytes 393224 | tf_op jit(solution)/shard_map/ppermute | solution.py:246
  19.1 0.3 %collective-permute-done.5 = bf16[64,128]{1,0:T(8,128)(2,1)S(1)} collective-permute-done((bf16[64,128]{1,0:T(8,128)(2,1)S(1)}, bf16[64,128]{1,0:T(8,128)(2,1)S(1)}, u32[]{:S(2)}, u32[]{:S(2)}) %collective-permute-start.5) | collective-permute-done | bytes 16416 | tf_op jit(solution)/shard_map/ppermute | solution.py:263
  19.5 0.1 collective-permute-start.6
  19.6 0.6 %copy-done.2 = f32[128]{0:T(128)S(1)} copy-done((f32[128]{0:T(128)S(1)}, f32[128]{0:T(128)}, u32[]{:S(2)}) %copy-start.2) | copy-done | bytes 536
  20.1 0.9 %constants.1 = (bf16[128,1024]{1,0:T(8,128)(2,1)S(1)}, f32[1,128]{1,0:T(1,128)S(1)}, bf16[256,128]{1,0:T(8,128)(2,1)S(1)}) custom-call(bf16[1024,128]{1,0:T(8,128)(2,1)S(1)} %copy-done, f32[1,128]{1,0:T(1,128)S(1)} %bitcast.7, bf16[320,128]{1,0:T(8,128)(2,1)S(1)} %copy-done.1), custom_call_target="tpu_custom_call" | custom-call | tf_op jit(solution)/shard_map/constants/pallas_call | solution.py:154
  21.1 0.0 collective-permute-done.6.other_ref
  21.1 0.2 prepare.1.left_ref
  21.2 1.5 %collective-permute-done.7.refs_5_ = bf16[512,128]{1,0:T(8,128)(2,1)S(1)} collective-permute-done((bf16[512,128]{1,0:T(8,128)(2,1)S(1)}, bf16[512,128]{1,0:T(8,128)(2,1)S(1)}, u32[]{:S(2)}, u32[]{:S(2)}) %collective-permute-start.7) | collective-permute-done | bytes 131104 | tf_op jit(solution)/shard_map/ppermute | solution.py:246
  22.7 5.2 %pairs.1 = bf16[32,128,128]{2,1,0:T(8,128)(2,1)} custom-call(bf16[1024,64]{1,0:T(8,128)(2,1)S(1)} %prepare.1.left_ref, bf16[128,1024]{1,0:T(8,128)(2,1)S(1)} %get-tuple-element.34.weights_ref, f32[1,128]{1,0:T(1,128)S(1)} %get-tuple-element.35.bias_ref, bf16[256,128]{1,0:T(8,128)(2,1)S(1)} %get-tuple-element.36.refs_0_, ...), custom_call_target="tpu_custom_call" | custom-call | flops 1610612736 | bytes 1048576 | tf_op jit(solution)/shard_map/pairs/pallas_call | solution.py:209
  (19 shorter events, 0.1 us)
Async XLA Ops:
  2.6 8.7 %collective-permute-start.2 = (bf16[384,128]{1,0:T(8,128)(2,1)}, bf16[384,128]{1,0:T(8,128)(2,1)S(1)}, u32[]{:S(2)}, u32[]{:S(2)}) collective-permute-start(bf16[384,128]{1,0:T(8,128)(2,1)} %get-tuple-element.25), channel_id=1, source_target_pairs={{12,0},{3,1},{14,2},{1,3},{8,4},{7,5},{10,6},{5,7},{4,8},{11,9},{6... | collective-permute-start | bytes 294920 | tf_op jit(solution)/shard_map/ppermute | solution.py:252
  7.6 4.8 %collective-permute-start.3 = (bf16[384,128]{1,0:T(8,128)(2,1)}, bf16[384,128]{1,0:T(8,128)(2,1)S(1)}, u32[]{:S(2)}, u32[]{:S(2)}) collective-permute-start(bf16[384,128]{1,0:T(8,128)(2,1)} %get-tuple-element.26), channel_id=1, source_target_pairs={{2,0},{13,1},{0,2},{15,3},{6,4},{9,5},{4,6},{11,7},{10,8},{5,9},{8... | collective-permute-start | bytes 294920 | tf_op jit(solution)/shard_map/ppermute | solution.py:252
  9.2 8.3 %collective-permute-start = (bf16[320,128]{1,0:T(8,128)(2,1)}, bf16[320,128]{1,0:T(8,128)(2,1)S(1)}, u32[]{:S(2)}, u32[]{:S(2)}) collective-permute-start(bf16[320,128]{1,0:T(8,128)(2,1)} %get-tuple-element.22), channel_id=1, source_target_pairs={{8,0},{5,1},{10,2},{7,3},{12,4},{1,5},{14,6},{3,7},{0,8},{13,9},{2... | collective-permute-start | bytes 245768 | tf_op jit(solution)/shard_map/ppermute | solution.py:252
  9.2 8.3 %collective-permute-start.1 = (bf16[320,128]{1,0:T(8,128)(2,1)}, bf16[320,128]{1,0:T(8,128)(2,1)S(1)}, u32[]{:S(2)}, u32[]{:S(2)}) collective-permute-start(bf16[320,128]{1,0:T(8,128)(2,1)} %get-tuple-element.33.message_ref), channel_id=1, source_target_pairs={{4,0},{9,1},{6,2},{11,3},{0,4},{13,5},{2,6},{15,7},{12,8},{1,9},{1... | collective-permute-start | bytes 245768 | tf_op jit(solution)/shard_map/ppermute | solution.py:252
  12.5 1.6 %copy-start.3 = (bf16[64,128]{1,0:T(8,128)(2,1)S(1)}, bf16[64,128]{1,0:T(8,128)(2,1)}, u32[]{:S(2)}) copy-start(bf16[64,128]{1,0:T(8,128)(2,1)} %get-tuple-element.21) | copy-start | bytes 49156
  12.5 5.0 %collective-permute-start.4 = (bf16[320,128]{1,0:T(8,128)(2,1)S(1)}, bf16[320,128]{1,0:T(8,128)(2,1)S(1)}, u32[]{:S(2)}, u32[]{:S(2)}) collective-permute-start(bf16[320,128]{1,0:T(8,128)(2,1)S(1)} %slice.32), channel_id=1, source_target_pairs={{2,0},{0,2},{6,4},{4,6},{10,8},{8,10},{14,12},{12,14},{3,1},{1,3},... | collective-permute-start | bytes 245768 | tf_op jit(solution)/shard_map/ppermute | solution.py:246
  14.1 0.7 %copy-start.4 = (bf16[64,128]{1,0:T(8,128)(2,1)S(1)}, bf16[64,128]{1,0:T(8,128)(2,1)}, u32[]{:S(2)}) copy-start(bf16[64,128]{1,0:T(8,128)(2,1)} %get-tuple-element.31) | copy-start | bytes 49156
  14.8 4.6 %collective-permute-start.5 = (bf16[64,128]{1,0:T(8,128)(2,1)S(1)}, bf16[64,128]{1,0:T(8,128)(2,1)S(1)}, u32[]{:S(2)}, u32[]{:S(2)}) collective-permute-start(bf16[64,128]{1,0:T(8,128)(2,1)S(1)} %copy-done.4), channel_id=1, source_target_pairs={{6,0},{10,1},{4,2},{8,3},{2,4},{14,5},{0,6},{12,7},{15,9},{3,8},{1... | collective-permute-start | bytes 49160 | tf_op jit(solution)/shard_map/ppermute | solution.py:263
  17.6 2.0 %copy-start = (bf16[1024,128]{1,0:T(8,128)(2,1)S(1)}, bf16[1024,128]{1,0:T(8,128)(2,1)}, u32[]{:S(2)}) copy-start(bf16[1024,128]{1,0:T(8,128)(2,1)} %w_ref.1) | copy-start | bytes 786436
  17.6 1.9 %copy-start.1 = (bf16[320,128]{1,0:T(8,128)(2,1)S(1)}, bf16[320,128]{1,0:T(8,128)(2,1)}, u32[]{:S(2)}) copy-start(bf16[320,128]{1,0:T(8,128)(2,1)} %get-tuple-element.33.message_ref) | copy-start | bytes 245764
  17.7 5.0 %collective-permute-start.7 = (bf16[512,128]{1,0:T(8,128)(2,1)S(1)}, bf16[512,128]{1,0:T(8,128)(2,1)S(1)}, u32[]{:S(2)}, u32[]{:S(2)}) collective-permute-start(bf16[512,128]{1,0:T(8,128)(2,1)S(1)} %pad_maximum_fusion), channel_id=1, source_target_pairs={{2,0},{0,2},{6,4},{4,6},{10,8},{8,10},{14,12},{12,14},{3,1},{1,3},... | collective-permute-start | bytes 393224 | tf_op jit(solution)/shard_map/ppermute | solution.py:246
  19.5 0.7 %copy-start.2 = (f32[128]{0:T(128)S(1)}, f32[128]{0:T(128)}, u32[]{:S(2)}) copy-start(f32[128]{0:T(128)} %param.17) | copy-start | bytes 1540
  19.5 1.6 %collective-permute-start.6 = (bf16[448,128]{1,0:T(8,128)(2,1)S(1)}, bf16[448,128]{1,0:T(8,128)(2,1)S(1)}, u32[]{:S(2)}, u32[]{:S(2)}) collective-permute-start(bf16[448,128]{1,0:T(8,128)(2,1)S(1)} %constant_dynamic-update-slice_fusion.mine_ref), channel_id=1, source_target_pairs={{0,1},{1,0},{2,3},{3,2},{4,5},{5,4},{6,7},{7,6},{8,9},{9,8},{10,11... | collective-permute-start | bytes 344072 | tf_op jit(solution)/shard_map/ppermute | solution.py:291

commit v18 on v16

--- a/solution.py
+++ b/solution.py
@@ -60,16 +60,11 @@
     own_ref[...] = left_for((0, 0))
     right = right_f32[...].astype(jnp.bfloat16)
     core = lax.axis_index("col")
-    for n, message_ref in enumerate(message_refs[:chips]):
+    for n, message_ref in enumerate(message_refs):
         a, b = by_core(core, *(direct_steps(chips)[m] for m in sent_by(n)))
-        first = message_ref.shape[0] - right.shape[0] - rows
-        if first:
-            message_ref[:rows] = left_for((a, b))
-        message_ref[first:first + right.shape[0]] = right
-        message_ref[first + right.shape[0]:] = left_for((a, 1) if first else (a, b))
-    same_half = here // chips == lax.axis_index("col")
-    for (a, b), message_ref in zip(far_steps(chips), message_refs[chips:]):
-        message_ref[...] = jnp.where(same_half, left_for((a + 1, b)), left_for((a, b)))
+        message_ref[:rows] = left_for((a, b))
+        message_ref[rows:rows + right.shape[0]] = right
+        message_ref[rows + right.shape[0]:] = left_for((a, 1))
 
 
 def features(alignment, ln_gain, ln_bias, w_left, b_left, w_right, b_right, row_count, col_count):
@@ -78,9 +73,7 @@
     rows = seqs * width * c // LANES
     chips = row_count // col_count
     part = rows // chips
-    shapes = [(part, LANES)]
-    shapes += [(rows + part * (2 if n < 2 else 1), LANES) for n in range(chips)]
-    shapes += [(part, LANES)] * len(far_steps(chips))
+    shapes = [(part, LANES)] + [(rows + 2 * part, LANES)] * chips
     operands = (alignment, ln_gain.reshape(1, -1), ln_bias.reshape(1, -1), w_left.T, b_left.reshape(1, -1),
                 w_right.T, b_right.reshape(1, -1))
     return pl.pallas_call(
@@ -109,26 +102,26 @@
         [flat[pl.ds(m * seqs + s, sources, stride=inner * seqs), :] for s in range(seqs)], axis=0)
 
 
-def prepare_kernel(seqs, left_at, mine_ref, other_ref, left_ref, left_f32):
+def prepare_kernel(seqs, mine_ref, other_ref, left_ref, left_f32):
     sources, left_rows, _ = left_f32.shape
     same_half = lax.axis_index("row") // (sources // 2) == lax.axis_index("col")
 
     def block(n):
-        first, of_same_half = left_at[n][0] * left_rows, left_at[n][1]
+        first = n * left_rows
         mine = mine_ref[first:first + left_rows].astype(jnp.float32)
         other = other_ref[first:first + left_rows].astype(jnp.float32)
-        return jnp.where(same_half == of_same_half, mine, other)
+        return jnp.where(same_half, mine, other)
 
     left_of = sequence_rows(block, left_f32, left_rows // seqs, seqs)
     for k in range(left_rows // seqs):
         left_ref[k * LANES:(k + 1) * LANES] = left_of(k).T.astype(jnp.bfloat16)
 
 
-def prepare(mine, other, left_at, left_rows, seqs):
-    sources = len(left_at)
+def prepare(mine, other, sources, seqs):
+    left_rows = mine.shape[0] // sources
     shape = (left_rows // seqs * LANES, sources * seqs)
     return pl.pallas_call(
-        functools.partial(prepare_kernel, seqs, left_at),
+        functools.partial(prepare_kernel, seqs),
         grid=(1,),
         out_shape=jax.ShapeDtypeStruct(shape, jnp.bfloat16),
         in_specs=[whole(mine.shape), whole(other.shape)],
@@ -139,20 +132,20 @@
     )(mine, other)
 
 
-def constants_kernel(c, rows, w_ref, bias_ref, message_ref, weights_ref, bias_out_ref, right_ref, w_f32):
+def constants_kernel(c, first, w_ref, bias_ref, message_ref, weights_ref, bias_out_ref, right_ref, w_f32):
     w_f32[...] = w_ref[...].astype(jnp.float32)
     for e in range(c):
         weights_ref[:, e * c:(e + 1) * c] = w_f32[pl.ds(e, c, stride=c), :].T.astype(jnp.bfloat16)
     bias_out_ref[...] = bias_ref[...]
-    right_ref[...] = message_ref[:rows]
-
-
-def constants(w_out, b_out, message, rows, c):
+    right_ref[...] = message_ref[first:first + right_ref.shape[0]]
+
+
+def constants(w_out, b_out, message, first, rows, c):
     z = w_out.shape[1]
     operands = (w_out, b_out.reshape(1, -1), message)
     outs = [((z, w_out.shape[0]), jnp.bfloat16), ((1, z), jnp.float32), ((rows, LANES), jnp.bfloat16)]
     return pl.pallas_call(
-        functools.partial(constants_kernel, c, rows),
+        functools.partial(constants_kernel, c, first),
         grid=(1,),
         out_shape=[jax.ShapeDtypeStruct(*out) for out in outs],
         in_specs=[whole(a.shape) for a in operands],
@@ -203,7 +196,7 @@
     sources = len(right_at)
     z = weights.shape[0]
     rows = left.shape[0] // c
-    rows_step = 8
+    rows_step = 16
     total = sources * seqs
     operands = (left, weights, bias, *rights)
     return pl.pallas_call(
@@ -238,10 +231,6 @@
     return jax.tree.map(lambda x, y: jnp.where(core == 0, x, y), of_0, of_1)
 
 
-def far_steps(chips):
-    return [(a, 1) for a in range(chips // 2 - 1)]
-
-
 def fetch(array, step, count):
     return lax.ppermute(array, "row", [(source_at(r, step), r) for r in range(count)])
 
@@ -249,17 +238,6 @@
 def fetch_direct(array, n, count):
     steps = direct_steps(count // 2)
     moves = [(2 * source_at(r, steps[m]) + core, 2 * r + core) for r in range(count) for core, m in enumerate(sent_by(n))]
-    return lax.ppermute(array, ("row", "col"), moves)
-
-
-def fetch_far(array, step, count):
-    chips = count // 2
-    a, b = step
-    moves = []
-    for r in range(count):
-        half = r // chips
-        moves.append((2 * source_at(r, (a + 1, b)) + half, 2 * r + half))
-        moves.append((2 * source_at(r, (a + chips // 2, b)) + half, 2 * r + 1 - half))
     return lax.ppermute(array, ("row", "col"), moves)
 
 
@@ -274,27 +252,22 @@
     rows = messages[0].shape[0] - 2 * left_rows
 
     core = lax.axis_index("col")
-    direct = [fetch_direct(message, n, row_count) for n, message in reversed([*enumerate(messages[:along])])][::-1]
-    beyond = [fetch_far(message, step, row_count) for step, message in zip(far_steps(along), messages[along:])]
+    direct = [fetch_direct(message, n, row_count) for n, message in reversed([*enumerate(messages)])][::-1]
     last, across = by_core(core, (direct[0], direct[1]), (direct[1], direct[0]))
     last_far = fetch(last[left_rows:], (0, 1), row_count)
     *rest, last_far = lax.optimization_barrier((*direct[2:], last_far))
-    rest = [by_core(core, *(rest[m] for m in sent_by(n))) for n in range(along - 2)]
-    far = fetch(jnp.concatenate([block[:rows] for block in rest]), (0, 1), row_count)
-
-    message, _ = lax.optimization_barrier((messages[along - 1], across))
-    weights, bias, right = constants(w_out, b_out, message, rows, c)
-    near = rest[::-1]
-    mine = jnp.concatenate([own] + [block[rows:] for block in near] + [last[:left_rows], across[:left_rows]]
-                           + beyond + [last_far[rows:]])
+    near = [by_core(core, *(rest[m] for m in sent_by(n))) for n in range(along - 2)][::-1]
+    far = fetch(jnp.concatenate([block[left_rows:] for block in near]), (0, 1), row_count)
+
+    message, _ = lax.optimization_barrier((messages[-1], across))
+    weights, bias, right = constants(w_out, b_out, message, left_rows, rows, c)
+    far_at = [n * (rows + left_rows) for n in range(along - 2)]
+    mine = jnp.concatenate([own] + [block[:left_rows] for block in (*near, last, across)]
+                           + [far[at + rows:at + rows + left_rows] for at in far_at] + [last_far[rows:]])
     other = lax.ppermute(mine, "col", [(0, 1), (1, 0)])
-    half = along // 2
-    left_at = [(a, True) for a in range(along + 1)]
-    left_at += [(along + a, True) if a < half else (along + 1 + a - half, False) for a in range(1, along - 1)]
-    left_at += [(along + half, True)]
-    left = prepare(mine, other, left_at, left_rows, seqs)
-    right_at = [(a, 0) for a in range(along - 1)] + [(along - 1, left_rows), (along, left_rows)]
-    right_at += [(along + 1, (along - 2 - a) * rows) for a in range(1, along - 1)] + [(along + 2, 0)]
+    left = prepare(mine, other, row_count, seqs)
+    right_at = [(0, 0)] + [(n, left_rows) for n in range(1, along + 1)]
+    right_at += [(along + 1, at) for at in far_at] + [(along + 2, 0)]
     return pairs(left, weights, bias, [right, *near, last, across, far, last_far], right_at, seqs, c, width)
 
 

time: 27.7 us -> 30.6 us (1.10)
  waiting for transfers between devices: 6.03 us -> 10.5 us
  starting transfers between devices: 11.8 us -> 10.4 us
  Pallas kernels: 8.9 us -> 8.48 us
    ppermute x2, waiting for transfers between devices: 1.9 us -> 4.88 us  [fetch(): lax.ppermute(array, 'row', [(source_at(r, step), r) for r in range(count)])]
    ppermute x4, waiting for transfers between devices: 4.13 us -> 5.61 us  [fetch_direct(): return lax.ppermute(array, ('row', 'col'), moves)]
    ppermute x4, starting transfers between devices: 8.53 us -> 7.35 us  [fetch_direct(): return lax.ppermute(array, ('row', 'col'), moves)]
    pallas_call x1, Pallas kernels: 5.2 us -> 4.79 us  [pairs(): pl.pallas_call(functools.partial(pair_kernel, seqs, c, right_at), grid=(r...]
    unnamed x14 -> x15, local copies, waits for them, and re-layouts: 0.61 us -> 0.62 us
  transfers between devices with their start and end apart: 8 -> 7, of which waited for: 5 -> 4; matrix products, arithmetic and copies ran while one was open for 0% -> 0% of each run, Pallas kernels for 4% -> 3%
where the time goes in v18:
time: 30.6 us; the launch traced here: 30.2 us
  waiting for transfers between devices  10.5 us (34%)
  starting transfers between devices  10.4 us (34%)
  Pallas kernels  8.48 us (28%)
  local copies, waits for them, and re-layouts  0.65 us (2%)
    ppermute x4, starting transfers between devices, fetch_direct(): return lax.ppermute(array, ('row', 'col'), moves)  7.35 us
    ppermute x4, waiting for transfers between devices, fetch_direct(): return lax.ppermute(array, ('row', 'col'), moves)  5.61 us
    ppermute x2, waiting for transfers between devices, fetch(): lax.ppermute(array, 'row', [(source_at(r, step), r) for r in range(count)])  4.88 us
    pallas_call x1, Pallas kernels, pairs(): pl.pallas_call(functools.partial(pair_kernel, seqs, c, right_at), grid=(r...  4.79 us
    ppermute x2, starting transfers between devices, fetch(): lax.ppermute(array, 'row', [(source_at(r, step), r) for r in range(count)])  2.99 us
    pallas_call x1, Pallas kernels, features(): pl.pallas_call(functools.partial(features_kernel, 1.0 / (seqs * row_count...  2.61 us
    pallas_call x1, Pallas kernels, constants(): pl.pallas_call(functools.partial(constants_kernel, c, first), grid=(1,),...  0.91 us
    unnamed x15, local copies, waits for them, and re-layouts  0.62 us
  transfers between devices with their start and end apart: 7, of which 4 were waited for; matrix products, arithmetic and copies ran while one was open for 0% of the time, Pallas kernels for 3%

profile of v18, /device:TPU:0, one launch (start us, length us, event | category | flops | bytes accessed | tf_op | source)
XLA Modules:
  0.0 30.2 jit_solution(1091169371767587295)
XLA Ops:
  0.0 2.6 %features.1 = (bf16[64,128]{1,0:T(8,128)(2,1)}, bf16[384,128]{1,0:T(8,128)(2,1)}, bf16[384,128]{1,0:T(8,128)(2,1)}, bf16[384,128]{1,0:T(8,128)(2,1)}, bf16[384,128]{1,0:T(8,128)(2,1)}) custom-call(bf16[8,128,256]{2,1,0:T(8,128)(2,1)} %x_ref.1, f32[1,256]{1,0:T(1,128)} %bitcast.10, f32[1,256]{1,0:T(1,128)} %bitcast.11, bf16[32,256]{1,0:T(8,128)(2,1)} %bitcast.8, ...), custom_call_target="tpu_custom_call" | custom-call | tf_op jit(solution)/shard_map/features/pallas_call | solution.py:79
  2.6 5.0 %collective-permute-start.2 = (bf16[384,128]{1,0:T(8,128)(2,1)}, bf16[384,128]{1,0:T(8,128)(2,1)S(1)}, u32[]{:S(2)}, u32[]{:S(2)}) collective-permute-start(bf16[384,128]{1,0:T(8,128)(2,1)} %get-tuple-element.20), channel_id=1, source_target_pairs={{12,0},{3,1},{14,2},{1,3},{8,4},{7,5},{10,6},{5,7},{4,8},{11,9},{6... | collective-permute-start | bytes 294920 | tf_op jit(solution)/shard_map/ppermute | solution.py:241
  7.7 1.5 %collective-permute-start.3 = (bf16[384,128]{1,0:T(8,128)(2,1)}, bf16[384,128]{1,0:T(8,128)(2,1)S(1)}, u32[]{:S(2)}, u32[]{:S(2)}) collective-permute-start(bf16[384,128]{1,0:T(8,128)(2,1)} %get-tuple-element.21), channel_id=1, source_target_pairs={{2,0},{13,1},{0,2},{15,3},{6,4},{9,5},{4,6},{11,7},{10,8},{5,9},{8... | collective-permute-start | bytes 294920 | tf_op jit(solution)/shard_map/ppermute | solution.py:241
  9.2 0.0 collective-permute-start
  9.2 0.8 %collective-permute-start.1 = (bf16[384,128]{1,0:T(8,128)(2,1)}, bf16[384,128]{1,0:T(8,128)(2,1)S(1)}, u32[]{:S(2)}, u32[]{:S(2)}) collective-permute-start(bf16[384,128]{1,0:T(8,128)(2,1)} %get-tuple-element.25.message_ref), channel_id=1, source_target_pairs={{4,0},{9,1},{6,2},{11,3},{0,4},{13,5},{2,6},{15,7},{12,8},{1,9},{1... | collective-permute-start | bytes 294920 | tf_op jit(solution)/shard_map/ppermute | solution.py:241
  10.0 1.4 %collective-permute-done.2 = bf16[384,128]{1,0:T(8,128)(2,1)S(1)} collective-permute-done((bf16[384,128]{1,0:T(8,128)(2,1)}, bf16[384,128]{1,0:T(8,128)(2,1)S(1)}, u32[]{:S(2)}, u32[]{:S(2)}) %collective-permute-start.2) | collective-permute-done | bytes 98336 | tf_op jit(solution)/shard_map/ppermute | solution.py:241
  11.3 1.2 %collective-permute-done.3 = bf16[384,128]{1,0:T(8,128)(2,1)S(1)} collective-permute-done((bf16[384,128]{1,0:T(8,128)(2,1)}, bf16[384,128]{1,0:T(8,128)(2,1)S(1)}, u32[]{:S(2)}, u32[]{:S(2)}) %collective-permute-start.3) | collective-permute-done | bytes 98336 | tf_op jit(solution)/shard_map/ppermute | solution.py:241
  12.5 0.0 copy-start.3
  12.5 1.6 %collective-permute-start.4 = (bf16[320,128]{1,0:T(8,128)(2,1)S(1)}, bf16[320,128]{1,0:T(8,128)(2,1)S(1)}, u32[]{:S(2)}, u32[]{:S(2)}) collective-permute-start(bf16[320,128]{1,0:T(8,128)(2,1)S(1)} %slice.40), channel_id=1, source_target_pairs={{2,0},{0,2},{6,4},{4,6},{10,8},{8,10},{14,12},{12,14},{3,1},{1,3},... | collective-permute-start | bytes 245768 | tf_op jit(solution)/shard_map/ppermute | solution.py:235
  14.1 0.0 copy-done.3
  14.1 3.1 %collective-permute-done = bf16[384,128]{1,0:T(8,128)(2,1)S(1)} collective-permute-done((bf16[384,128]{1,0:T(8,128)(2,1)}, bf16[384,128]{1,0:T(8,128)(2,1)S(1)}, u32[]{:S(2)}, u32[]{:S(2)}) %collective-permute-start) | collective-permute-done | bytes 98336 | tf_op jit(solution)/shard_map/ppermute | solution.py:241
  17.2 0.0 collective-permute-done.1
  17.2 0.0 collective-permute-done.4.refs_6_
  17.3 0.0 copy-start
  17.4 0.0 copy-start.1
  17.4 1.4 %collective-permute-start.5 = (bf16[640,128]{1,0:T(8,128)(2,1)S(1)}, bf16[640,128]{1,0:T(8,128)(2,1)S(1)}, u32[]{:S(2)}, u32[]{:S(2)}) collective-permute-start(bf16[640,128]{1,0:T(8,128)(2,1)S(1)} %pad_maximum_fusion), channel_id=1, source_target_pairs={{2,0},{0,2},{6,4},{4,6},{10,8},{8,10},{14,12},{12,14},{3,1},{1,3},... | collective-permute-start | bytes 491528 | tf_op jit(solution)/shard_map/ppermute | solution.py:235
  18.8 4.9 %collective-permute-done.5.refs_5_ = bf16[640,128]{1,0:T(8,128)(2,1)S(1)} collective-permute-done((bf16[640,128]{1,0:T(8,128)(2,1)S(1)}, bf16[640,128]{1,0:T(8,128)(2,1)S(1)}, u32[]{:S(2)}, u32[]{:S(2)}) %collective-permute-start.5) | collective-permute-done | bytes 163872 | tf_op jit(solution)/shard_map/ppermute | solution.py:235
  23.7 0.0 copy-start.2
  23.7 0.1 collective-permute-start.6
  23.8 0.5 %copy-done.2 = f32[128]{0:T(128)S(1)} copy-done((f32[128]{0:T(128)S(1)}, f32[128]{0:T(128)}, u32[]{:S(2)}) %copy-start.2) | copy-done | bytes 536
  24.3 0.9 %constants.1 = (bf16[128,1024]{1,0:T(8,128)(2,1)S(1)}, f32[1,128]{1,0:T(1,128)S(1)}, bf16[256,128]{1,0:T(8,128)(2,1)S(1)}) custom-call(bf16[1024,128]{1,0:T(8,128)(2,1)S(1)} %copy-done, f32[1,128]{1,0:T(1,128)S(1)} %bitcast.7, bf16[384,128]{1,0:T(8,128)(2,1)S(1)} %copy-done.1), custom_call_target="tpu_custom_call" | custom-call | tf_op jit(solution)/shard_map/constants/pallas_call | solution.py:147
  25.2 0.0 collective-permute-done.6.other_ref
  25.3 0.2 prepare.1.left_ref
  25.4 4.8 %pairs.1 = bf16[32,128,128]{2,1,0:T(8,128)(2,1)} custom-call(bf16[1024,64]{1,0:T(8,128)(2,1)S(1)} %prepare.1.left_ref, bf16[128,1024]{1,0:T(8,128)(2,1)S(1)} %get-tuple-element.26.weights_ref, f32[1,128]{1,0:T(1,128)S(1)} %get-tuple-element.27.bias_ref, bf16[256,128]{1,0:T(8,128)(2,1)S(1)} %get-tuple-element.28.refs_0_, ...), custom_call_target="tpu_custom_call" | custom-call | flops 1610612736 | bytes 1048576 | tf_op jit(solution)/shard_map/pairs/pallas_call | solution.py:202
  (16 shorter events, 0.1 us)
Async XLA Ops:
  2.6 8.7 %collective-permute-start.2 = (bf16[384,128]{1,0:T(8,128)(2,1)}, bf16[384,128]{1,0:T(8,128)(2,1)S(1)}, u32[]{:S(2)}, u32[]{:S(2)}) collective-permute-start(bf16[384,128]{1,0:T(8,128)(2,1)} %get-tuple-element.20), channel_id=1, source_target_pairs={{12,0},{3,1},{14,2},{1,3},{8,4},{7,5},{10,6},{5,7},{4,8},{11,9},{6... | collective-permute-start | bytes 294920 | tf_op jit(solution)/shard_map/ppermute | solution.py:241
  7.7 4.8 %collective-permute-start.3 = (bf16[384,128]{1,0:T(8,128)(2,1)}, bf16[384,128]{1,0:T(8,128)(2,1)S(1)}, u32[]{:S(2)}, u32[]{:S(2)}) collective-permute-start(bf16[384,128]{1,0:T(8,128)(2,1)} %get-tuple-element.21), channel_id=1, source_target_pairs={{2,0},{13,1},{0,2},{15,3},{6,4},{9,5},{4,6},{11,7},{10,8},{5,9},{8... | collective-permute-start | bytes 294920 | tf_op jit(solution)/shard_map/ppermute | solution.py:241
  9.2 8.0 %collective-permute-start = (bf16[384,128]{1,0:T(8,128)(2,1)}, bf16[384,128]{1,0:T(8,128)(2,1)S(1)}, u32[]{:S(2)}, u32[]{:S(2)}) collective-permute-start(bf16[384,128]{1,0:T(8,128)(2,1)} %get-tuple-element.18), channel_id=1, source_target_pairs={{8,0},{5,1},{10,2},{7,3},{12,4},{1,5},{14,6},{3,7},{0,8},{13,9},{2... | collective-permute-start | bytes 294920 | tf_op jit(solution)/shard_map/ppermute | solution.py:241
  9.2 8.0 %collective-permute-start.1 = (bf16[384,128]{1,0:T(8,128)(2,1)}, bf16[384,128]{1,0:T(8,128)(2,1)S(1)}, u32[]{:S(2)}, u32[]{:S(2)}) collective-permute-start(bf16[384,128]{1,0:T(8,128)(2,1)} %get-tuple-element.25.message_ref), channel_id=1, source_target_pairs={{4,0},{9,1},{6,2},{11,3},{0,4},{13,5},{2,6},{15,7},{12,8},{1,9},{1... | collective-permute-start | bytes 294920 | tf_op jit(solution)/shard_map/ppermute | solution.py:241
  12.5 1.6 %copy-start.3 = (bf16[64,128]{1,0:T(8,128)(2,1)S(1)}, bf16[64,128]{1,0:T(8,128)(2,1)}, u32[]{:S(2)}) copy-start(bf16[64,128]{1,0:T(8,128)(2,1)} %get-tuple-element.17) | copy-start | bytes 49156
  12.5 4.7 %collective-permute-start.4 = (bf16[320,128]{1,0:T(8,128)(2,1)S(1)}, bf16[320,128]{1,0:T(8,128)(2,1)S(1)}, u32[]{:S(2)}, u32[]{:S(2)}) collective-permute-start(bf16[320,128]{1,0:T(8,128)(2,1)S(1)} %slice.40), channel_id=1, source_target_pairs={{2,0},{0,2},{6,4},{4,6},{10,8},{8,10},{14,12},{12,14},{3,1},{1,3},... | collective-permute-start | bytes 245768 | tf_op jit(solution)/shard_map/ppermute | solution.py:235
  17.3 6.5 %copy-start = (bf16[1024,128]{1,0:T(8,128)(2,1)S(1)}, bf16[1024,128]{1,0:T(8,128)(2,1)}, u32[]{:S(2)}) copy-start(bf16[1024,128]{1,0:T(8,128)(2,1)} %w_ref.1) | copy-start | bytes 786436
  17.4 6.4 %copy-start.1 = (bf16[384,128]{1,0:T(8,128)(2,1)S(1)}, bf16[384,128]{1,0:T(8,128)(2,1)}, u32[]{:S(2)}) copy-start(bf16[384,128]{1,0:T(8,128)(2,1)} %get-tuple-element.25.message_ref) | copy-start | bytes 294916
  17.4 6.3 %collective-permute-start.5 = (bf16[640,128]{1,0:T(8,128)(2,1)S(1)}, bf16[640,128]{1,0:T(8,128)(2,1)S(1)}, u32[]{:S(2)}, u32[]{:S(2)}) collective-permute-start(bf16[640,128]{1,0:T(8,128)(2,1)S(1)} %pad_maximum_fusion), channel_id=1, source_target_pairs={{2,0},{0,2},{6,4},{4,6},{10,8},{8,10},{14,12},{12,14},{3,1},{1,3},... | collective-permute-start | bytes 491528 | tf_op jit(solution)/shard_map/ppermute | solution.py:235
  23.7 0.7 %copy-start.2 = (f32[128]{0:T(128)S(1)}, f32[128]{0:T(128)}, u32[]{:S(2)}) copy-start(f32[128]{0:T(128)} %param.17) | copy-start | bytes 1540
  23.7 1.6 %collective-permute-start.6 = (bf16[512,128]{1,0:T(8,128)(2,1)S(1)}, bf16[512,128]{1,0:T(8,128)(2,1)S(1)}, u32[]{:S(2)}, u32[]{:S(2)}) collective-permute-start(bf16[512,128]{1,0:T(8,128)(2,1)S(1)} %constant_dynamic-update-slice_fusion.mine_ref), channel_id=1, source_target_pairs={{0,1},{1,0},{2,3},{3,2},{4,5},{5,4},{6,7},{7,6},{8,9},{9,8},{10,11... | collective-permute-start | bytes 393224 | tf_op jit(solution)/shard_map/ppermute | solution.py:267

commit v19 on v16

--- a/solution.py
+++ b/solution.py
@@ -203,7 +203,7 @@
     sources = len(right_at)
     z = weights.shape[0]
     rows = left.shape[0] // c
-    rows_step = 8
+    rows_step = 16
     total = sources * seqs
     operands = (left, weights, bias, *rights)
     return pl.pallas_call(

time: 27.7 us -> 27.2 us (0.982)
  Pallas kernels: 8.9 us -> 8.45 us
    pallas_call x1, Pallas kernels: 5.2 us -> 4.76 us  [pairs(): pl.pallas_call(functools.partial(pair_kernel, seqs, c, right_at), grid=(r...]
where the time goes in v19:
time: 27.2 us; the launch traced here: 27.1 us
  starting transfers between devices  11.8 us (43%)
  Pallas kernels  8.45 us (31%)
  waiting for transfers between devices  6.03 us (22%)
  local copies, waits for them, and re-layouts  0.64 us (2%)
    ppermute x4, starting transfers between devices, fetch_direct(): return lax.ppermute(array, ('row', 'col'), moves)  8.53 us
    pallas_call x1, Pallas kernels, pairs(): pl.pallas_call(functools.partial(pair_kernel, seqs, c, right_at), grid=(r...  4.76 us
    ppermute x4, waiting for transfers between devices, fetch_direct(): return lax.ppermute(array, ('row', 'col'), moves)  4.13 us
    ppermute x2, starting transfers between devices, fetch(): lax.ppermute(array, 'row', [(source_at(r, step), r) for r in range(count)])  3.17 us
    pallas_call x1, Pallas kernels, features(): pl.pallas_call(functools.partial(features_kernel, 1.0 / (seqs * row_count...  2.62 us
    ppermute x2, waiting for transfers between devices, fetch(): lax.ppermute(array, 'row', [(source_at(r, step), r) for r in range(count)])  1.9 us
    pallas_call x1, Pallas kernels, constants(): pl.pallas_call(functools.partial(constants_kernel, c, rows), grid=(1,), o...  0.92 us
    unnamed x14, local copies, waits for them, and re-layouts  0.61 us
  transfers between devices with their start and end apart: 8, of which 5 were waited for; matrix products, arithmetic and copies ran while one was open for 0% of the time, Pallas kernels for 4%

profile of v19, /device:TPU:0, one launch (start us, length us, event | category | flops | bytes accessed | tf_op | source)
XLA Modules:
  0.0 27.1 jit_solution(8176782113493448066)
XLA Ops:
  0.0 2.6 %features.1 = (bf16[64,128]{1,0:T(8,128)(2,1)}, bf16[384,128]{1,0:T(8,128)(2,1)}, bf16[384,128]{1,0:T(8,128)(2,1)}, bf16[320,128]{1,0:T(8,128)(2,1)}, bf16[320,128]{1,0:T(8,128)(2,1)}, /*index=5*/bf16[64,128]{1,0:T(8,128)(2,1)}) custom-call(bf16[8,128,256]{2,1,0:T(8,128)(2,1)} %x_ref.1, f32[1,256]{1,0:T(1,128)} %bitcast.10, f32[1,256]{1,0:T(1,128)} %bitcast.11, ...), custom_call_target="tpu_custom_call" | custom-call | tf_op jit(solution)/shard_map/features/pallas_call | solution.py:86
  2.6 5.0 %collective-permute-start.2 = (bf16[384,128]{1,0:T(8,128)(2,1)}, bf16[384,128]{1,0:T(8,128)(2,1)S(1)}, u32[]{:S(2)}, u32[]{:S(2)}) collective-permute-start(bf16[384,128]{1,0:T(8,128)(2,1)} %get-tuple-element.21), channel_id=1, source_target_pairs={{12,0},{3,1},{14,2},{1,3},{8,4},{7,5},{10,6},{5,7},{4,8},{11,9},{6... | collective-permute-start | bytes 294920 | tf_op jit(solution)/shard_map/ppermute | solution.py:252
  7.7 1.5 %collective-permute-start.3 = (bf16[384,128]{1,0:T(8,128)(2,1)}, bf16[384,128]{1,0:T(8,128)(2,1)S(1)}, u32[]{:S(2)}, u32[]{:S(2)}) collective-permute-start(bf16[384,128]{1,0:T(8,128)(2,1)} %get-tuple-element.22), channel_id=1, source_target_pairs={{2,0},{13,1},{0,2},{15,3},{6,4},{9,5},{4,6},{11,7},{10,8},{5,9},{8... | collective-permute-start | bytes 294920 | tf_op jit(solution)/shard_map/ppermute | solution.py:252
  9.2 0.0 collective-permute-start.5
  9.2 1.7 %collective-permute-start = (bf16[320,128]{1,0:T(8,128)(2,1)}, bf16[320,128]{1,0:T(8,128)(2,1)S(1)}, u32[]{:S(2)}, u32[]{:S(2)}) collective-permute-start(bf16[320,128]{1,0:T(8,128)(2,1)} %get-tuple-element.19), channel_id=1, source_target_pairs={{8,0},{5,1},{10,2},{7,3},{12,4},{1,5},{14,6},{3,7},{0,8},{13,9},{2... | collective-permute-start | bytes 245768 | tf_op jit(solution)/shard_map/ppermute | solution.py:252
  10.9 0.2 collective-permute-start.1
  11.2 0.2 collective-permute-done.2
  11.3 1.2 %collective-permute-done.3 = bf16[384,128]{1,0:T(8,128)(2,1)S(1)} collective-permute-done((bf16[384,128]{1,0:T(8,128)(2,1)}, bf16[384,128]{1,0:T(8,128)(2,1)S(1)}, u32[]{:S(2)}, u32[]{:S(2)}) %collective-permute-start.3) | collective-permute-done | bytes 98336 | tf_op jit(solution)/shard_map/ppermute | solution.py:252
  12.5 1.6 %collective-permute-start.4 = (bf16[320,128]{1,0:T(8,128)(2,1)S(1)}, bf16[320,128]{1,0:T(8,128)(2,1)S(1)}, u32[]{:S(2)}, u32[]{:S(2)}) collective-permute-start(bf16[320,128]{1,0:T(8,128)(2,1)S(1)} %slice.32), channel_id=1, source_target_pairs={{2,0},{0,2},{6,4},{4,6},{10,8},{8,10},{14,12},{12,14},{3,1},{1,3},... | collective-permute-start | bytes 245768 | tf_op jit(solution)/shard_map/ppermute | solution.py:246
  14.1 2.8 %collective-permute-done = bf16[320,128]{1,0:T(8,128)(2,1)S(1)} collective-permute-done((bf16[320,128]{1,0:T(8,128)(2,1)}, bf16[320,128]{1,0:T(8,128)(2,1)S(1)}, u32[]{:S(2)}, u32[]{:S(2)}) %collective-permute-start) | collective-permute-done | bytes 81952 | tf_op jit(solution)/shard_map/ppermute | solution.py:252
  16.9 0.0 collective-permute-done.1
  16.9 0.1 collective-permute-done.4.refs_6_
  17.1 0.0 copy-start
  17.2 1.6 %collective-permute-start.7 = (bf16[512,128]{1,0:T(8,128)(2,1)S(1)}, bf16[512,128]{1,0:T(8,128)(2,1)S(1)}, u32[]{:S(2)}, u32[]{:S(2)}) collective-permute-start(bf16[512,128]{1,0:T(8,128)(2,1)S(1)} %pad_maximum_fusion), channel_id=1, source_target_pairs={{2,0},{0,2},{6,4},{4,6},{10,8},{8,10},{14,12},{12,14},{3,1},{1,3},... | collective-permute-start | bytes 393224 | tf_op jit(solution)/shard_map/ppermute | solution.py:246
  18.8 0.0 collective-permute-done.5
  18.8 0.0 copy-start.2
  18.8 0.1 collective-permute-start.6
  18.9 0.0 copy-done
  18.9 0.5 %copy-done.2 = f32[128]{0:T(128)S(1)} copy-done((f32[128]{0:T(128)S(1)}, f32[128]{0:T(128)}, u32[]{:S(2)}) %copy-start.2) | copy-done | bytes 536
  19.4 0.9 %constants.1 = (bf16[128,1024]{1,0:T(8,128)(2,1)S(1)}, f32[1,128]{1,0:T(1,128)S(1)}, bf16[256,128]{1,0:T(8,128)(2,1)S(1)}) custom-call(bf16[1024,128]{1,0:T(8,128)(2,1)S(1)} %copy-done, f32[1,128]{1,0:T(1,128)S(1)} %bitcast.7, bf16[320,128]{1,0:T(8,128)(2,1)S(1)} %copy-done.1), custom_call_target="tpu_custom_call" | custom-call | tf_op jit(solution)/shard_map/constants/pallas_call | solution.py:154
  20.4 0.0 collective-permute-done.6.other_ref
  20.4 0.2 prepare.1.left_ref
  20.5 1.8 %collective-permute-done.7.refs_5_ = bf16[512,128]{1,0:T(8,128)(2,1)S(1)} collective-permute-done((bf16[512,128]{1,0:T(8,128)(2,1)S(1)}, bf16[512,128]{1,0:T(8,128)(2,1)S(1)}, u32[]{:S(2)}, u32[]{:S(2)}) %collective-permute-start.7) | collective-permute-done | bytes 131104 | tf_op jit(solution)/shard_map/ppermute | solution.py:246
  22.3 4.8 %pairs.1 = bf16[32,128,128]{2,1,0:T(8,128)(2,1)} custom-call(bf16[1024,64]{1,0:T(8,128)(2,1)S(1)} %prepare.1.left_ref, bf16[128,1024]{1,0:T(8,128)(2,1)S(1)} %get-tuple-element.28.weights_ref, f32[1,128]{1,0:T(1,128)S(1)} %get-tuple-element.29.bias_ref, bf16[256,128]{1,0:T(8,128)(2,1)S(1)} %get-tuple-element.30.refs_0_, ...), custom_call_target="tpu_custom_call" | custom-call | flops 1610612736 | bytes 1048576 | tf_op jit(solution)/shard_map/pairs/pallas_call | solution.py:209
  (17 shorter events, 0.1 us)
Async XLA Ops:
  2.6 8.7 %collective-permute-start.2 = (bf16[384,128]{1,0:T(8,128)(2,1)}, bf16[384,128]{1,0:T(8,128)(2,1)S(1)}, u32[]{:S(2)}, u32[]{:S(2)}) collective-permute-start(bf16[384,128]{1,0:T(8,128)(2,1)} %get-tuple-element.21), channel_id=1, source_target_pairs={{12,0},{3,1},{14,2},{1,3},{8,4},{7,5},{10,6},{5,7},{4,8},{11,9},{6... | collective-permute-start | bytes 294920 | tf_op jit(solution)/shard_map/ppermute | solution.py:252
  7.7 4.8 %collective-permute-start.3 = (bf16[384,128]{1,0:T(8,128)(2,1)}, bf16[384,128]{1,0:T(8,128)(2,1)S(1)}, u32[]{:S(2)}, u32[]{:S(2)}) collective-permute-start(bf16[384,128]{1,0:T(8,128)(2,1)} %get-tuple-element.22), channel_id=1, source_target_pairs={{2,0},{13,1},{0,2},{15,3},{6,4},{9,5},{4,6},{11,7},{10,8},{5,9},{8... | collective-permute-start | bytes 294920 | tf_op jit(solution)/shard_map/ppermute | solution.py:252
  9.2 9.6 %collective-permute-start.5 = (bf16[64,128]{1,0:T(8,128)(2,1)}, bf16[64,128]{1,0:T(8,128)(2,1)S(1)}, u32[]{:S(2)}, u32[]{:S(2)}) collective-permute-start(bf16[64,128]{1,0:T(8,128)(2,1)} %get-tuple-element.25), channel_id=1, source_target_pairs={{6,0},{10,1},{4,2},{8,3},{2,4},{14,5},{0,6},{12,7},{15,9},{3,8},{1... | collective-permute-start | bytes 49160 | tf_op jit(solution)/shard_map/ppermute | solution.py:263
  9.2 7.7 %collective-permute-start = (bf16[320,128]{1,0:T(8,128)(2,1)}, bf16[320,128]{1,0:T(8,128)(2,1)S(1)}, u32[]{:S(2)}, u32[]{:S(2)}) collective-permute-start(bf16[320,128]{1,0:T(8,128)(2,1)} %get-tuple-element.19), channel_id=1, source_target_pairs={{8,0},{5,1},{10,2},{7,3},{12,4},{1,5},{14,6},{3,7},{0,8},{13,9},{2... | collective-permute-start | bytes 245768 | tf_op jit(solution)/shard_map/ppermute | solution.py:252
  10.9 6.0 %collective-permute-start.1 = (bf16[320,128]{1,0:T(8,128)(2,1)}, bf16[320,128]{1,0:T(8,128)(2,1)S(1)}, u32[]{:S(2)}, u32[]{:S(2)}) collective-permute-start(bf16[320,128]{1,0:T(8,128)(2,1)} %get-tuple-element.27.message_ref), channel_id=1, source_target_pairs={{4,0},{9,1},{6,2},{11,3},{0,4},{13,5},{2,6},{15,7},{12,8},{1,9},{1... | collective-permute-start | bytes 245768 | tf_op jit(solution)/shard_map/ppermute | solution.py:252
  12.5 1.6 %copy-start.3 = (bf16[64,128]{1,0:T(8,128)(2,1)S(1)}, bf16[64,128]{1,0:T(8,128)(2,1)}, u32[]{:S(2)}) copy-start(bf16[64,128]{1,0:T(8,128)(2,1)} %get-tuple-element.18) | copy-start | bytes 49156
  12.5 4.5 %collective-permute-start.4 = (bf16[320,128]{1,0:T(8,128)(2,1)S(1)}, bf16[320,128]{1,0:T(8,128)(2,1)S(1)}, u32[]{:S(2)}, u32[]{:S(2)}) collective-permute-start(bf16[320,128]{1,0:T(8,128)(2,1)S(1)} %slice.32), channel_id=1, source_target_pairs={{2,0},{0,2},{6,4},{4,6},{10,8},{8,10},{14,12},{12,14},{3,1},{1,3},... | collective-permute-start | bytes 245768 | tf_op jit(solution)/shard_map/ppermute | solution.py:246
  17.1 1.8 %copy-start = (bf16[1024,128]{1,0:T(8,128)(2,1)S(1)}, bf16[1024,128]{1,0:T(8,128)(2,1)}, u32[]{:S(2)}) copy-start(bf16[1024,128]{1,0:T(8,128)(2,1)} %w_ref.1) | copy-start | bytes 786436
  17.2 1.7 %copy-start.1 = (bf16[320,128]{1,0:T(8,128)(2,1)S(1)}, bf16[320,128]{1,0:T(8,128)(2,1)}, u32[]{:S(2)}) copy-start(bf16[320,128]{1,0:T(8,128)(2,1)} %get-tuple-element.27.message_ref) | copy-start | bytes 245764
  17.2 5.2 %collective-permute-start.7 = (bf16[512,128]{1,0:T(8,128)(2,1)S(1)}, bf16[512,128]{1,0:T(8,128)(2,1)S(1)}, u32[]{:S(2)}, u32[]{:S(2)}) collective-permute-start(bf16[512,128]{1,0:T(8,128)(2,1)S(1)} %pad_maximum_fusion), channel_id=1, source_target_pairs={{2,0},{0,2},{6,4},{4,6},{10,8},{8,10},{14,12},{12,14},{3,1},{1,3},... | collective-permute-start | bytes 393224 | tf_op jit(solution)/shard_map/ppermute | solution.py:246
  18.8 0.7 %copy-start.2 = (f32[128]{0:T(128)S(1)}, f32[128]{0:T(128)}, u32[]{:S(2)}) copy-start(f32[128]{0:T(128)} %param.17) | copy-start | bytes 1540
  18.8 1.6 %collective-permute-start.6 = (bf16[448,128]{1,0:T(8,128)(2,1)S(1)}, bf16[448,128]{1,0:T(8,128)(2,1)S(1)}, u32[]{:S(2)}, u32[]{:S(2)}) collective-permute-start(bf16[448,128]{1,0:T(8,128)(2,1)S(1)} %constant_dynamic-update-slice_fusion.mine_ref), channel_id=1, source_target_pairs={{0,1},{1,0},{2,3},{3,2},{4,5},{5,4},{6,7},{7,6},{8,9},{9,8},{10,11... | collective-permute-start | bytes 344072 | tf_op jit(solution)/shard_map/ppermute | solution.py:290

commit v20 on v19

--- a/solution.py
+++ b/solution.py
@@ -203,7 +203,7 @@
     sources = len(right_at)
     z = weights.shape[0]
     rows = left.shape[0] // c
-    rows_step = 16
+    rows_step = 32
     total = sources * seqs
     operands = (left, weights, bias, *rights)
     return pl.pallas_call(

time: 27.2 us -> 27.1 us (level)
  no operation moved by 1% of the time
where the time goes in v20:
time: 27.1 us; the launch traced here: 27 us
  starting transfers between devices  11.8 us (44%)
  Pallas kernels  8.36 us (31%)
  waiting for transfers between devices  6.03 us (22%)
  local copies, waits for them, and re-layouts  0.64 us (2%)
    ppermute x4, starting transfers between devices, fetch_direct(): return lax.ppermute(array, ('row', 'col'), moves)  8.53 us
    pallas_call x1, Pallas kernels, pairs(): pl.pallas_call(functools.partial(pair_kernel, seqs, c, right_at), grid=(r...  4.66 us
    ppermute x4, waiting for transfers between devices, fetch_direct(): return lax.ppermute(array, ('row', 'col'), moves)  4.13 us
    ppermute x2, starting transfers between devices, fetch(): lax.ppermute(array, 'row', [(source_at(r, step), r) for r in range(count)])  3.17 us
    pallas_call x1, Pallas kernels, features(): pl.pallas_call(functools.partial(features_kernel, 1.0 / (seqs * row_count...  2.62 us
    ppermute x2, waiting for transfers between devices, fetch(): lax.ppermute(array, 'row', [(source_at(r, step), r) for r in range(count)])  1.9 us
    pallas_call x1, Pallas kernels, constants(): pl.pallas_call(functools.partial(constants_kernel, c, rows), grid=(1,), o...  0.92 us
    unnamed x14, local copies, waits for them, and re-layouts  0.61 us
  transfers between devices with their start and end apart: 8, of which 5 were waited for; matrix products, arithmetic and copies ran while one was open for 0% of the time, Pallas kernels for 4%

profile of v20, /device:TPU:0, one launch (start us, length us, event | category | flops | bytes accessed | tf_op | source)
XLA Modules:
  0.0 27.0 jit_solution(2192452573489033613)
XLA Ops:
  0.0 2.6 %features.1 = (bf16[64,128]{1,0:T(8,128)(2,1)}, bf16[384,128]{1,0:T(8,128)(2,1)}, bf16[384,128]{1,0:T(8,128)(2,1)}, bf16[320,128]{1,0:T(8,128)(2,1)}, bf16[320,128]{1,0:T(8,128)(2,1)}, /*index=5*/bf16[64,128]{1,0:T(8,128)(2,1)}) custom-call(bf16[8,128,256]{2,1,0:T(8,128)(2,1)} %x_ref.1, f32[1,256]{1,0:T(1,128)} %bitcast.10, f32[1,256]{1,0:T(1,128)} %bitcast.11, ...), custom_call_target="tpu_custom_call" | custom-call | tf_op jit(solution)/shard_map/features/pallas_call | solution.py:86
  2.6 5.0 %collective-permute-start.2 = (bf16[384,128]{1,0:T(8,128)(2,1)}, bf16[384,128]{1,0:T(8,128)(2,1)S(1)}, u32[]{:S(2)}, u32[]{:S(2)}) collective-permute-start(bf16[384,128]{1,0:T(8,128)(2,1)} %get-tuple-element.21), channel_id=1, source_target_pairs={{12,0},{3,1},{14,2},{1,3},{8,4},{7,5},{10,6},{5,7},{4,8},{11,9},{6... | collective-permute-start | bytes 294920 | tf_op jit(solution)/shard_map/ppermute | solution.py:252
  7.7 1.5 %collective-permute-start.3 = (bf16[384,128]{1,0:T(8,128)(2,1)}, bf16[384,128]{1,0:T(8,128)(2,1)S(1)}, u32[]{:S(2)}, u32[]{:S(2)}) collective-permute-start(bf16[384,128]{1,0:T(8,128)(2,1)} %get-tuple-element.22), channel_id=1, source_target_pairs={{2,0},{13,1},{0,2},{15,3},{6,4},{9,5},{4,6},{11,7},{10,8},{5,9},{8... | collective-permute-start | bytes 294920 | tf_op jit(solution)/shard_map/ppermute | solution.py:252
  9.2 0.0 collective-permute-start.5
  9.2 1.7 %collective-permute-start = (bf16[320,128]{1,0:T(8,128)(2,1)}, bf16[320,128]{1,0:T(8,128)(2,1)S(1)}, u32[]{:S(2)}, u32[]{:S(2)}) collective-permute-start(bf16[320,128]{1,0:T(8,128)(2,1)} %get-tuple-element.19), channel_id=1, source_target_pairs={{8,0},{5,1},{10,2},{7,3},{12,4},{1,5},{14,6},{3,7},{0,8},{13,9},{2... | collective-permute-start | bytes 245768 | tf_op jit(solution)/shard_map/ppermute | solution.py:252
  10.9 0.2 collective-permute-start.1
  11.2 0.2 collective-permute-done.2
  11.3 1.2 %collective-permute-done.3 = bf16[384,128]{1,0:T(8,128)(2,1)S(1)} collective-permute-done((bf16[384,128]{1,0:T(8,128)(2,1)}, bf16[384,128]{1,0:T(8,128)(2,1)S(1)}, u32[]{:S(2)}, u32[]{:S(2)}) %collective-permute-start.3) | collective-permute-done | bytes 98336 | tf_op jit(solution)/shard_map/ppermute | solution.py:252
  12.5 1.6 %collective-permute-start.4 = (bf16[320,128]{1,0:T(8,128)(2,1)S(1)}, bf16[320,128]{1,0:T(8,128)(2,1)S(1)}, u32[]{:S(2)}, u32[]{:S(2)}) collective-permute-start(bf16[320,128]{1,0:T(8,128)(2,1)S(1)} %slice.32), channel_id=1, source_target_pairs={{2,0},{0,2},{6,4},{4,6},{10,8},{8,10},{14,12},{12,14},{3,1},{1,3},... | collective-permute-start | bytes 245768 | tf_op jit(solution)/shard_map/ppermute | solution.py:246
  14.1 0.0 copy-done.3
  14.1 2.8 %collective-permute-done = bf16[320,128]{1,0:T(8,128)(2,1)S(1)} collective-permute-done((bf16[320,128]{1,0:T(8,128)(2,1)}, bf16[320,128]{1,0:T(8,128)(2,1)S(1)}, u32[]{:S(2)}, u32[]{:S(2)}) %collective-permute-start) | collective-permute-done | bytes 81952 | tf_op jit(solution)/shard_map/ppermute | solution.py:252
  16.9 0.0 collective-permute-done.1
  16.9 0.1 collective-permute-done.4.refs_6_
  17.1 0.0 copy-start
  17.2 1.6 %collective-permute-start.7 = (bf16[512,128]{1,0:T(8,128)(2,1)S(1)}, bf16[512,128]{1,0:T(8,128)(2,1)S(1)}, u32[]{:S(2)}, u32[]{:S(2)}) collective-permute-start(bf16[512,128]{1,0:T(8,128)(2,1)S(1)} %pad_maximum_fusion), channel_id=1, source_target_pairs={{2,0},{0,2},{6,4},{4,6},{10,8},{8,10},{14,12},{12,14},{3,1},{1,3},... | collective-permute-start | bytes 393224 | tf_op jit(solution)/shard_map/ppermute | solution.py:246
  18.8 0.0 collective-permute-done.5
  18.8 0.0 copy-start.2
  18.8 0.1 collective-permute-start.6
  18.9 0.5 %copy-done.2 = f32[128]{0:T(128)S(1)} copy-done((f32[128]{0:T(128)S(1)}, f32[128]{0:T(128)}, u32[]{:S(2)}) %copy-start.2) | copy-done | bytes 536
  19.4 0.9 %constants.1 = (bf16[128,1024]{1,0:T(8,128)(2,1)S(1)}, f32[1,128]{1,0:T(1,128)S(1)}, bf16[256,128]{1,0:T(8,128)(2,1)S(1)}) custom-call(bf16[1024,128]{1,0:T(8,128)(2,1)S(1)} %copy-done, f32[1,128]{1,0:T(1,128)S(1)} %bitcast.7, bf16[320,128]{1,0:T(8,128)(2,1)S(1)} %copy-done.1), custom_call_target="tpu_custom_call" | custom-call | tf_op jit(solution)/shard_map/constants/pallas_call | solution.py:154
  20.4 0.0 collective-permute-done.6.other_ref
  20.4 0.2 prepare.1.left_ref
  20.5 1.8 %collective-permute-done.7.refs_5_ = bf16[512,128]{1,0:T(8,128)(2,1)S(1)} collective-permute-done((bf16[512,128]{1,0:T(8,128)(2,1)S(1)}, bf16[512,128]{1,0:T(8,128)(2,1)S(1)}, u32[]{:S(2)}, u32[]{:S(2)}) %collective-permute-start.7) | collective-permute-done | bytes 131104 | tf_op jit(solution)/shard_map/ppermute | solution.py:246
  22.3 4.7 %pairs.1 = bf16[32,128,128]{2,1,0:T(8,128)(2,1)} custom-call(bf16[1024,64]{1,0:T(8,128)(2,1)S(1)} %prepare.1.left_ref, bf16[128,1024]{1,0:T(8,128)(2,1)S(1)} %get-tuple-element.28.weights_ref, f32[1,128]{1,0:T(1,128)S(1)} %get-tuple-element.29.bias_ref, bf16[256,128]{1,0:T(8,128)(2,1)S(1)} %get-tuple-element.30.refs_0_, ...), custom_call_target="tpu_custom_call" | custom-call | flops 1610612736 | bytes 1048576 | tf_op jit(solution)/shard_map/pairs/pallas_call | solution.py:209
  (17 shorter events, 0.1 us)
Async XLA Ops:
  2.6 8.7 %collective-permute-start.2 = (bf16[384,128]{1,0:T(8,128)(2,1)}, bf16[384,128]{1,0:T(8,128)(2,1)S(1)}, u32[]{:S(2)}, u32[]{:S(2)}) collective-permute-start(bf16[384,128]{1,0:T(8,128)(2,1)} %get-tuple-element.21), channel_id=1, source_target_pairs={{12,0},{3,1},{14,2},{1,3},{8,4},{7,5},{10,6},{5,7},{4,8},{11,9},{6... | collective-permute-start | bytes 294920 | tf_op jit(solution)/shard_map/ppermute | solution.py:252
  7.7 4.8 %collective-permute-start.3 = (bf16[384,128]{1,0:T(8,128)(2,1)}, bf16[384,128]{1,0:T(8,128)(2,1)S(1)}, u32[]{:S(2)}, u32[]{:S(2)}) collective-permute-start(bf16[384,128]{1,0:T(8,128)(2,1)} %get-tuple-element.22), channel_id=1, source_target_pairs={{2,0},{13,1},{0,2},{15,3},{6,4},{9,5},{4,6},{11,7},{10,8},{5,9},{8... | collective-permute-start | bytes 294920 | tf_op jit(solution)/shard_map/ppermute | solution.py:252
  9.2 9.6 %collective-permute-start.5 = (bf16[64,128]{1,0:T(8,128)(2,1)}, bf16[64,128]{1,0:T(8,128)(2,1)S(1)}, u32[]{:S(2)}, u32[]{:S(2)}) collective-permute-start(bf16[64,128]{1,0:T(8,128)(2,1)} %get-tuple-element.25), channel_id=1, source_target_pairs={{6,0},{10,1},{4,2},{8,3},{2,4},{14,5},{0,6},{12,7},{15,9},{3,8},{1... | collective-permute-start | bytes 49160 | tf_op jit(solution)/shard_map/ppermute | solution.py:263
  9.2 7.7 %collective-permute-start = (bf16[320,128]{1,0:T(8,128)(2,1)}, bf16[320,128]{1,0:T(8,128)(2,1)S(1)}, u32[]{:S(2)}, u32[]{:S(2)}) collective-permute-start(bf16[320,128]{1,0:T(8,128)(2,1)} %get-tuple-element.19), channel_id=1, source_target_pairs={{8,0},{5,1},{10,2},{7,3},{12,4},{1,5},{14,6},{3,7},{0,8},{13,9},{2... | collective-permute-start | bytes 245768 | tf_op jit(solution)/shard_map/ppermute | solution.py:252
  10.9 6.0 %collective-permute-start.1 = (bf16[320,128]{1,0:T(8,128)(2,1)}, bf16[320,128]{1,0:T(8,128)(2,1)S(1)}, u32[]{:S(2)}, u32[]{:S(2)}) collective-permute-start(bf16[320,128]{1,0:T(8,128)(2,1)} %get-tuple-element.27.message_ref), channel_id=1, source_target_pairs={{4,0},{9,1},{6,2},{11,3},{0,4},{13,5},{2,6},{15,7},{12,8},{1,9},{1... | collective-permute-start | bytes 245768 | tf_op jit(solution)/shard_map/ppermute | solution.py:252
  12.5 1.6 %copy-start.3 = (bf16[64,128]{1,0:T(8,128)(2,1)S(1)}, bf16[64,128]{1,0:T(8,128)(2,1)}, u32[]{:S(2)}) copy-start(bf16[64,128]{1,0:T(8,128)(2,1)} %get-tuple-element.18) | copy-start | bytes 49156
  12.5 4.5 %collective-permute-start.4 = (bf16[320,128]{1,0:T(8,128)(2,1)S(1)}, bf16[320,128]{1,0:T(8,128)(2,1)S(1)}, u32[]{:S(2)}, u32[]{:S(2)}) collective-permute-start(bf16[320,128]{1,0:T(8,128)(2,1)S(1)} %slice.32), channel_id=1, source_target_pairs={{2,0},{0,2},{6,4},{4,6},{10,8},{8,10},{14,12},{12,14},{3,1},{1,3},... | collective-permute-start | bytes 245768 | tf_op jit(solution)/shard_map/ppermute | solution.py:246
  17.1 1.8 %copy-start = (bf16[1024,128]{1,0:T(8,128)(2,1)S(1)}, bf16[1024,128]{1,0:T(8,128)(2,1)}, u32[]{:S(2)}) copy-start(bf16[1024,128]{1,0:T(8,128)(2,1)} %w_ref.1) | copy-start | bytes 786436
  17.2 1.7 %copy-start.1 = (bf16[320,128]{1,0:T(8,128)(2,1)S(1)}, bf16[320,128]{1,0:T(8,128)(2,1)}, u32[]{:S(2)}) copy-start(bf16[320,128]{1,0:T(8,128)(2,1)} %get-tuple-element.27.message_ref) | copy-start | bytes 245764
  17.2 5.2 %collective-permute-start.7 = (bf16[512,128]{1,0:T(8,128)(2,1)S(1)}, bf16[512,128]{1,0:T(8,128)(2,1)S(1)}, u32[]{:S(2)}, u32[]{:S(2)}) collective-permute-start(bf16[512,128]{1,0:T(8,128)(2,1)S(1)} %pad_maximum_fusion), channel_id=1, source_target_pairs={{2,0},{0,2},{6,4},{4,6},{10,8},{8,10},{14,12},{12,14},{3,1},{1,3},... | collective-permute-start | bytes 393224 | tf_op jit(solution)/shard_map/ppermute | solution.py:246
  18.8 0.7 %copy-start.2 = (f32[128]{0:T(128)S(1)}, f32[128]{0:T(128)}, u32[]{:S(2)}) copy-start(f32[128]{0:T(128)} %param.17) | copy-start | bytes 1540
  18.8 1.6 %collective-permute-start.6 = (bf16[448,128]{1,0:T(8,128)(2,1)S(1)}, bf16[448,128]{1,0:T(8,128)(2,1)S(1)}, u32[]{:S(2)}, u32[]{:S(2)}) collective-permute-start(bf16[448,128]{1,0:T(8,128)(2,1)S(1)} %constant_dynamic-update-slice_fusion.mine_ref), channel_id=1, source_target_pairs={{0,1},{1,0},{2,3},{3,2},{4,5},{5,4},{6,7},{7,6},{8,9},{9,8},{10,11... | collective-permute-start | bytes 344072 | tf_op jit(solution)/shard_map/ppermute | solution.py:290
